TPU v7x, 32 devices: a whole 2x2x4 slice. The times are simulated.
32 devices in a mesh: blk: 16 (over z, x, core), dim: 2 (over y).
Axes of the slice: x: 2, y: 2, z: 4, core: 2. Of those that a mesh axis runs over, the one named last changes fastest.
Arguments:
- question_matrix: float32 [2048, 768], P('blk', 'dim'), may hold values from -20 to 20, as said below
- document_matrix: float32 [2048, 768], P('blk', 'dim'), may hold values from -0.5 to 0.5
- pool: float32 [768, 32768], P('dim', 'blk'), may hold values from -1.4 to 1.4
- hard_owner: int32 [2048, 8], P('blk'), may hold values from 0 to 15, all different within a row; in each aligned block of 128 rows (0 to 127, 128 to 255, ...) at most 128 rows name the same one
- hard_local: int32 [2048, 8], P('blk'), may hold values from 0 to 2047
Outputs:
- loss: float32 [2048], P('blk')
- question_derivative: float32 [2048, 768], P('blk', 'dim')
- document_derivative: float32 [2048, 768], P('blk', 'dim')
- grad_pool: float32 [768, 32768], P('dim', 'blk')
Inputs may be any that keep to these rules, and one draw needn't show every extreme that they name: `question_matrix`: query embeddings; some rows may be much larger than the rest. `hard_owner`: the 8 owners named in one row are different. Among the rows of one index of blk, no owner is named more than 128 times, a bound that some block reaches.
All inputs are finite; a program needn't handle non-finite values.
Results may differ from a plain program's by a relative error of at most 0.0003.
Values sent between devices are 32-bit elements; how exact they have to be, the bound alone decides.
No kernel may reach another device: no remote copies, remote signals or barrier semaphores. Data moves between devices by JAX's collectives and lax.ppermute only.
A program may use at most 64 MiB of HBM per device.

v0:
```python
import jax
import jax.numpy as jnp
from jax import lax
from jax.sharding import PartitionSpec as P

logit_divisor = 0.05


def per_device(question_matrix, document_matrix, pool, hard_owner, hard_local):
    highest_accuracy = lax.Precision.HIGHEST
    blocks = lax.axis_size("blk")
    query_rows, feature_vectors = question_matrix.shape
    negatives = hard_owner.shape[1]
    capacity = min(query_rows, 2 * query_rows * negatives // blocks)
    owners = hard_owner.reshape(-1)
    local_rows = hard_local.reshape(-1)
    owner_marks = (owners[:, None] == jnp.arange(blocks, dtype=jnp.int32)[None, :]).astype(
        jnp.int32
    )
    slot_ranks = jnp.sum(jnp.cumsum(owner_marks, axis=0) * owner_marks, axis=1) - 1
    requests = jnp.zeros((blocks, capacity), jnp.int32).at[owners, slot_ranks].set(local_rows)
    asked = lax.all_to_all(requests, "blk", split_axis=0, concat_axis=0, tiled=True)
    found = jnp.moveaxis(jnp.take(pool, asked, axis=1), 0, 2)
    fetched = lax.all_to_all(found, "blk", split_axis=0, concat_axis=0, tiled=True)
    distractor_lines = fetched[owners, slot_ranks].reshape(query_rows, negatives, feature_vectors)
    hard_part = jnp.einsum(
        "pq,pcq->pc", question_matrix, distractor_lines, precision=highest_accuracy
    )
    positive_part = jnp.sum(question_matrix * document_matrix, axis=1)
    partial_value = lax.dot_general(
        question_matrix,
        lax.all_gather(document_matrix, "blk", axis=0, tiled=True),
        (((1,), (1,)), ((), ())),
        precision=highest_accuracy,
        preferred_element_type=jnp.float32,
    )
    gathered_lines, distractor_total, matching_logit_total = lax.psum(
        (partial_value, hard_part, positive_part), "dim"
    )
    affinity_logits = gathered_lines / logit_divisor
    distractor_logits = distractor_total / logit_divisor
    row_peak = jnp.maximum(jnp.max(affinity_logits, axis=1), jnp.max(distractor_logits, axis=1))
    summed = jnp.sum(jnp.exp(affinity_logits - row_peak[:, None]), axis=1) + jnp.sum(
        jnp.exp(distractor_logits - row_peak[:, None]), axis=1
    )
    normalizer_logarithm = row_peak + jnp.log(summed)
    softmax_rows = jnp.exp(affinity_logits - normalizer_logarithm[:, None])
    distractor_coefficients = jnp.exp(distractor_logits - normalizer_logarithm[:, None])
    objective_entries = normalizer_logarithm - matching_logit_total / logit_divisor
    distractor_addend = jnp.einsum(
        "jg,jgu->ju", distractor_coefficients, distractor_lines, precision=highest_accuracy
    )
    columns = softmax_rows
    replicated_lines = jnp.dot(
        columns,
        lax.all_gather(document_matrix, "blk", axis=0, tiled=True),
        precision=highest_accuracy,
        preferred_element_type=jnp.float32,
    )
    question_derivative = (replicated_lines + distractor_addend - document_matrix) / logit_divisor
    columns = softmax_rows
    received_lines = lax.psum_scatter(
        lax.dot_general(
            columns,
            question_matrix,
            (((0,), (0,)), ((), ())),
            precision=highest_accuracy,
            preferred_element_type=jnp.float32,
        ),
        "blk",
        scatter_dimension=0,
        tiled=True,
    )
    document_derivative = (received_lines - question_matrix) / logit_divisor
    dispatched_deltas = (
        distractor_coefficients[:, :, None] * question_matrix[:, None, :] / logit_divisor
    ).reshape(-1, feature_vectors)
    outgoing = (
        jnp.zeros((blocks, capacity, feature_vectors), jnp.float32)
        .at[owners, slot_ranks]
        .set(dispatched_deltas)
    )
    arriving = lax.all_to_all(outgoing, "blk", split_axis=0, concat_axis=0, tiled=True)
    grad_pool = (
        jnp.zeros(pool.shape, jnp.float32)
        .at[:, asked.reshape(-1)]
        .add(arriving.reshape(-1, feature_vectors).T)
    )
    return (objective_entries, question_derivative, document_derivative, grad_pool)


def solution(mesh):
    placed = (P("blk", "dim"), P("blk", "dim"), P("dim", "blk"), P("blk", None), P("blk", None))
    return jax.shard_map(
        per_device,
        mesh=mesh,
        in_specs=placed,
        out_specs=(P("blk"), P("blk", "dim"), P("blk", "dim"), P("dim", "blk")),
        check_vma=False,
    )
```

profile of v0, /device:TPU:0, one launch (start us, length us, event | category | flops | bytes accessed | tf_op | source)
XLA Modules:
  0.0 284.1 jit_solution(11162234497183306623)
XLA Ops:
  9.0 4.5 %reduce-window.6 = s32[16,8,128]{2,1,0:T(8,128)S(1)} reduce-window(s32[16,8,128]{2,1,0:T(8,128)S(1)} %fusion.25, s32[]{:T(128)} %constant.20.clone.1), window={size=1x1x128 pad=0_0x0_0x127_0}, to_apply=%region_2.3 | reduce-window | flops 2080768 | bytes 131076 | tf_op jit(solution)/shard_map/reduce-window
  16.4 4.9 %scatter_custom_fusion.1 = s32[2048]{0:T(1024)} fusion(s32[1024]{0:T(1024)S(1)} %broadcast_select_fusion.1, s32[1024]{0:T(1024)S(1)} %reshape.214, s32[]{:T(128)} %constant.20.clone.1), kind=kCustom, calls=%fused_computation.57 | custom fusion | bytes 8196
  21.3 7.4 %all-to-all-start = ((s32[16,1,128]{2,1,0:T(1,128)}), s32[16,1,128]{2,1,0:T(1,128)S(1)}, u32[]{:S(2)}, u32[]{:S(2)}) async-start(s32[16,1,128]{2,1,0:T(1,128)} %bitcast.4), calls=%async_computation | async-start | bytes 16384 | tf_op jit(solution)/shard_map/all_to_all | solution.py:22
  28.6 2.4 copy.27
  31.0 3.9 %all-to-all-done = s32[16,1,128]{2,1,0:T(1,128)S(1)} async-done(((s32[16,1,128]{2,1,0:T(1,128)}), s32[16,1,128]{2,1,0:T(1,128)S(1)}, u32[]{:S(2)}, u32[]{:S(2)}) %all-to-all-start) | async-done | bytes 8224 | tf_op jit(solution)/shard_map/all_to_all | solution.py:22
  35.0 8.7 %gather_fusion = f32[2048,384]{1,0:T(8,128)} fusion(f32[384,2048]{0,1:T(8,128)S(1)} %copy.27, s32[2048]{0:T(1024)S(1)} %fusion.27), kind=kCustom, calls=%fused_computation | custom fusion | bytes 6299648 | tf_op jit(solution)/shard_map/jit(_take)/gather | solution.py:23
  43.7 3.3 %broadcast_select_fusion = f32[16,128,384]{2,1,0:T(8,128)} fusion(f32[16,128,384]{2,1,0:T(8,128)} %bitcast.55, pred[16,128]{1,0:T(8,128)(4,1)S(1)} %compare_and_fusion), kind=kLoop, calls=%fused_computation.12 | loop fusion | flops 786432 | bytes 6293504 | tf_op jit(solution)/shard_map/jit(_take)/select_n | solution.py:23
  47.0 3.9 %all-to-all-start.1 = ((f32[16,128,384]{2,1,0:T(8,128)}), f32[16,128,384]{2,1,0:T(8,128)S(1)}, u32[]{:S(2)}, u32[]{:S(2)}) async-start(f32[16,128,384]{2,1,0:T(8,128)} %broadcast_select_fusion), calls=%async_computation.1 | async-start | bytes 6291456 | tf_op jit(solution)/shard_map/all_to_all | solution.py:24
  50.9 26.9 %all-gather.2.cloned.1.call-done = f32[2048,384]{1,0:T(8,128)} async-done(((f32[128,384]{1,0:T(8,128)}), f32[2048,384]{1,0:T(8,128)}) %all-gather.2.cloned.1.call-update) | async-done | bytes 3145744 | tf_op jit(solution)/shard_map/all_gather | solution.py:32
  77.8 6.2 %fusion.32 = f32[128,2048]{1,0:T(8,128)} fusion(f32[128,384]{1,0:T(8,128)S(1)} %copy-done.2, f32[2048,384]{1,0:T(8,128)} %all-gather.2.cloned.1.call-done), kind=kOutput, calls=%fused_computation.66 | convolution fusion | flops 1207959552 | bytes 4390912 | tf_op jit(solution)/shard_map/dot_general | solution.py:30
  84.7 27.5 %all-to-all-done.1 = f32[16,128,384]{2,1,0:T(8,128)S(1)} async-done(((f32[16,128,384]{2,1,0:T(8,128)}), f32[16,128,384]{2,1,0:T(8,128)S(1)}, u32[]{:S(2)}, u32[]{:S(2)}) %all-to-all-start.1) | async-done | bytes 3145760 | tf_op jit(solution)/shard_map/all_to_all | solution.py:24
  112.2 12.5 %gather_fusion.1 = f32[1024,384]{1,0:T(8,128)} fusion(f32[16,128,384]{2,1,0:T(8,128)S(1)} %all-to-all-done.1, s32[1024]{0:T(1024)S(1)} %bitcast.53), kind=kCustom, calls=%fused_computation.1 | custom fusion | bytes 3153920 | tf_op jit(solution)/shard_map/gather | solution.py:25
  124.8 4.4 %fusion.5 = f32[128,1,8]{2,1,0:T(1,128)S(1)} fusion(f32[1024,384]{1,0:T(8,128)} %gather_fusion.1, f32[128,384,1]{1,0,2:T(8,128)S(1)} %bitcast.56), kind=kOutput, calls=%fused_computation.10 | convolution fusion | flops 4718592 | bytes 1773568 | tf_op jit(solution)/shard_map/pq,pcq->pc/dot_general | solution.py:26
  129.1 9.6 %all-reduce = (f32[128,8]{1,0:T(8,128)S(1)}, f32[128]{0:T(128)S(1)}) all-reduce(f32[128,8]{1,0:T(8,128)S(1)} %bitcast.58, f32[128]{0:T(128)} %multiply_reduce_fusion.1), channel_id=1, replica_groups=mesh['blk'=16,'dim'=2] {'dim'}, use_global_device_ids=true, to_apply=%region_6.7 | all-reduce | flops 1152 | bytes 9216 | tf_op jit(solution)/shard_map/psum | solution.py:37
  140.4 1.6 exponential_reduce_fusion
  142.7 7.2 %scatter_custom_fusion.2 = f32[2048,384]{1,0:T(8,128)} fusion(s32[1024]{0:T(1024)S(1)} %broadcast_select_fusion.1, f32[]{:T(128)} %constant.50.clone.1, f32[]{:T(128)} %constant.17.clone.1, f32[128,384]{1,0:T(8,128)S(1)} %copy-done.2, f32[1024]{0:T(1024)S(1)} %mul.26), kind=kCustom, calls=%fused_computation.7 | custom fusion | flops 786432 | bytes 3346440
  149.9 16.4 %all-to-all-start.2 = ((f32[16,128,384]{2,1,0:T(8,128)}), f32[16,128,384]{2,1,0:T(8,128)}, u32[]{:S(2)}, u32[]{:S(2)}) async-start(f32[16,128,384]{2,1,0:T(8,128)} %bitcast.54), calls=%async_computation.3 | async-start | bytes 6291456 | tf_op jit(solution)/shard_map/all_to_all | solution.py:83
  166.3 4.5 %fusion.12 = f32[2048,384]{1,0:T(8,128)} fusion(f32[128,384]{1,0:T(8,128)S(1)} %copy-done.2, f32[128,2048]{1,0:T(8,128)S(1)} %copy-done, f32[128]{0:T(128)S(1)} %get-tuple-element.19), kind=kOutput, calls=%fused_computation.21 | convolution fusion | flops 1208483840 | bytes 4391424 | tf_op jit(solution)/shard_map/dot_general | solution.py:63
  171.4 1.8 fusion.3
  173.2 4.9 %fusion.11 = f32[128,384]{1,0:T(8,128)} fusion(f32[128,384]{1,0:T(8,128)S(1)} %copy-done.3, f32[2048,384]{1,0:T(8,128)} %all-gather.2.cloned.1.call-done, f32[128,2048]{1,0:T(8,128)S(1)} %copy-done, f32[128]{0:T(128)S(1)} %get-tuple-element.19, f32[128,1,384]{2,1,0:T(1,128)S(1)} %fusion.3), kind=kOutput, calls=%fused_computation.18 | convolution fusion | flops 1208631296 | bytes 4784640 | tf_op jit(solution)/shard_map/dot_general | solution.py:54
  178.1 80.3 %reduce-scatter.2.cloned.1.call-done = f32[128,384]{1,0:T(8,128)} async-done(((f32[2048,384]{1,0:T(8,128)}), f32[128,384]{1,0:T(8,128)}) %reduce-scatter.2.cloned.1.call-update) | async-done | bytes 196624 | tf_op jit(solution)/shard_map/reduce_scatter | solution.py:62
  258.4 1.6 subtract_multiply_fusion
  260.1 15.2 %scatter_custom_fusion = f32[384,2048]{0,1:T(8,128)S(1)} fusion(s32[2048]{0:T(1024)} %bitcast.65, f32[2048,384]{1,0:T(8,128)} %bitcast.21, f32[]{:T(128)} %constant.50.clone.1), kind=kCustom, calls=%fused_computation.14 | custom fusion | flops 786432 | bytes 3146240 | tf_op jit(solution)/shard_map/scatter-add | solution.py:87
  275.2 2.4 copy.28
  (46 shorter events, 8.4 us)
Async XLA Ops:
  7.2 70.7 %all-gather.2.cloned.1.call-start = ((), (), s32[]{:S(2)}) async-start(), calls=%async_computation.4 | async-start | bytes 3342336 | tf_op jit(solution)/shard_map/all_gather | solution.py:32
  21.3 13.7 %all-to-all-start = ((s32[16,1,128]{2,1,0:T(1,128)}), s32[16,1,128]{2,1,0:T(1,128)S(1)}, u32[]{:S(2)}, u32[]{:S(2)}) async-start(s32[16,1,128]{2,1,0:T(1,128)} %bitcast.4), calls=%async_computation | async-start | bytes 16384 | tf_op jit(solution)/shard_map/all_to_all | solution.py:22
  47.0 30.8 %copy-start.2 = (f32[128,384]{1,0:T(8,128)S(1)}, f32[128,384]{1,0:T(8,128)}, u32[]{:S(2)}) copy-start(f32[128,384]{1,0:T(8,128)} %param.5) | copy-start | bytes 589828
  47.0 65.2 %all-to-all-start.1 = ((f32[16,128,384]{2,1,0:T(8,128)}), f32[16,128,384]{2,1,0:T(8,128)S(1)}, u32[]{:S(2)}, u32[]{:S(2)}) async-start(f32[16,128,384]{2,1,0:T(8,128)} %broadcast_select_fusion), calls=%async_computation.1 | async-start | bytes 6291456 | tf_op jit(solution)/shard_map/all_to_all | solution.py:24
  50.9 33.2 %copy-start.3 = (f32[128,384]{1,0:T(8,128)S(1)}, f32[128,384]{1,0:T(8,128)}, u32[]{:S(2)}) copy-start(f32[128,384]{1,0:T(8,128)} %param.6) | copy-start | bytes 589828
  50.9 88.0 %all-reduce.3.cloned.1.call-start = ((), (), s32[]{:S(2)}) async-start(), calls=%async_computation.5 | async-start | bytes 2097152 | tf_op jit(solution)/shard_map/psum | solution.py:37
  149.9 16.4 %copy-start = (f32[128,2048]{1,0:T(8,128)S(1)}, f32[128,2048]{1,0:T(8,128)}, u32[]{:S(2)}) copy-start(f32[128,2048]{1,0:T(8,128)} %all-reduce.3.cloned.1.call-done) | copy-start | bytes 3145732
  149.9 110.2 %all-to-all-start.2 = ((f32[16,128,384]{2,1,0:T(8,128)}), f32[16,128,384]{2,1,0:T(8,128)}, u32[]{:S(2)}, u32[]{:S(2)}) async-start(f32[16,128,384]{2,1,0:T(8,128)} %bitcast.54), calls=%async_computation.3 | async-start | bytes 6291456 | tf_op jit(solution)/shard_map/all_to_all | solution.py:83
  166.3 5.2 %copy-start.1 = (f32[1024,384]{1,0:T(8,128)S(1)}, f32[1024,384]{1,0:T(8,128)}, u32[]{:S(2)}) copy-start(f32[1024,384]{1,0:T(8,128)} %gather_fusion.1) | copy-start | bytes 4718596
  166.3 92.2 %reduce-scatter.2.cloned.1.call-start = ((), (), s32[]{:S(2)}) async-start(), calls=%async_computation.6 | async-start | bytes 3342336 | tf_op jit(solution)/shard_map/reduce_scatter | solution.py:62
Sparse Core Ops, SparseCore 0:
  10.3 67.5 all-gather.1
  84.2 37.2 all-reduce.2
  172.0 86.4 reduce-scatter.1
where the time goes:
time: 285 us; the launch traced here: 284 us
  waiting for transfers between devices  139 us (49%)
  other arithmetic  38.5 us (14%)
  local copies, waits for them, and re-layouts  33.2 us (12%)
  starting transfers between devices  27.7 us (10%)
  matrix products  21.7 us (8%)
  between operations  13.9 us (5%)
  blocking collectives  9.57 us (3%)
    reduce_scatter x1, waiting for transfers between devices, per_device(): lax.psum_scatter(lax.dot_general(columns, question_matrix, (((0,), (0,)),...  80.3 us
    all_to_all x1, waiting for transfers between devices, per_device(): lax.all_to_all(found, 'blk', split_axis=0, concat_axis=0, tiled=True)  27.5 us
    all_gather x1, waiting for transfers between devices, per_device(): lax.all_gather(document_matrix, 'blk', axis=0, tiled=True)  26.9 us
    all_to_all x1, starting transfers between devices, per_device(): lax.all_to_all(outgoing, 'blk', split_axis=0, concat_axis=0, tiled=True)  16.4 us
    scatter-add x1, other arithmetic, per_device(): grad_pool = jnp.zeros(pool.shape, jnp.float32).at[:, asked.reshape(-1)].a...  15.2 us
    gather x1, local copies, waits for them, and re-layouts, per_device(): fetched[owners, slot_ranks].reshape(query_rows, negatives, feature_vectors)  12.5 us
    unnamed x13, local copies, waits for them, and re-layouts  11.2 us
    psum x1, blocking collectives, per_device(): lax.psum((partial_value, hard_part, positive_part), 'dim')  9.57 us
  transfers between devices with their start and end apart: 6, of which 4 were waited for; matrix products, arithmetic and copies ran while one was open for 23% of the time, Pallas kernels for 0%

commit v1 on v0

v1 whole, which is shorter than its diff:
```python
import functools

import jax
import jax.numpy as jnp
import numpy as np
from jax import lax
from jax.experimental import pallas as pl
from jax.experimental.pallas import tpu as pltpu
from jax.sharding import PartitionSpec as P

logit_divisor = 0.05
LOWEST = -3.0e38
SLACK = 8

f32 = jnp.float32
bf16 = jnp.bfloat16


def split2(x):
    high = x.astype(bf16)
    return high, (x - high.astype(f32)).astype(bf16)


def dot(a, b, contract=((1,), (0,)), precision=None):
    return lax.dot_general(
        a, b, (contract, ((), ())), precision=precision, preferred_element_type=f32
    )


def call(body, out_shape, name, flops=0, data=1 << 20, limit=48 << 20, **kw):
    return pl.pallas_call(
        body,
        out_shape=out_shape,
        name=name,
        cost_estimate=pl.CostEstimate(flops=flops, bytes_accessed=data, transcendentals=0),
        compiler_params=pltpu.CompilerParams(vmem_limit_bytes=limit),
        **kw,
    )


def shape(*dims, dtype=f32):
    return jax.ShapeDtypeStruct(dims, dtype)


def pack_body(q_ref, owner_ref, local_ref, columns, x_ref):
    features = q_ref.shape[1]
    x_ref[:features, :] = q_ref[...].T
    x_ref[features:, :] = (owner_ref[...] * columns + local_ref[...]).astype(f32)


def prepare_body(d_ref, pool_ref, dt_ref, pool_parts_ref):
    features = d_ref.shape[1]
    high, low = split2(d_ref[...].T)
    dt_ref[:features, :] = high
    dt_ref[features:, :] = low
    values = pool_ref[...]
    high = values.astype(bf16)
    rest = values - high.astype(f32)
    middle = rest.astype(bf16)
    pool_parts_ref[:features, :] = high
    pool_parts_ref[features : 2 * features, :] = middle
    pool_parts_ref[2 * features :, :] = (rest - middle.astype(f32)).astype(bf16)


def score_body(pieces, me_ref, d_ref, pool_ref, *refs):
    part_ref, rows_ref = refs[-2:]
    rows, features = d_ref.shape
    columns = pool_ref.shape[1]
    blocks, at = [], 0
    for count in pieces:
        held = [r[...] for r in refs[at : at + count]]
        blocks.append(held[0] if count == 1 else jnp.concatenate(held, axis=0))
        at += count
    x = blocks[0] if len(blocks) == 1 else jnp.concatenate(blocks, axis=1)
    named = x[features:].astype(jnp.int32) - me_ref[0] * columns
    here = (named >= 0) & (named < columns)
    local = jnp.sum(jnp.where(here, named, 0), axis=0, keepdims=True)
    local = jnp.where(jnp.any(here, axis=0, keepdims=True), local, -1)
    x = x[:features]
    marks = lax.broadcasted_iota(jnp.int32, (columns, x.shape[1]), 0) == local
    found = dot(pool_ref[...], jnp.where(marks, 1.0, 0.0).astype(bf16))
    found = found[:features] + found[features : 2 * features] + found[2 * features :]
    scores = dot(d_ref[...], x, precision=lax.Precision.HIGHEST)
    hard = jnp.sum(x * found, axis=0, keepdims=True)
    chosen = local.astype(f32)
    for k in range(len(pieces)):
        at = slice(k * rows, (k + 1) * rows)
        part_ref[k, :rows] = scores[:, at]
        part_ref[k, rows:] = jnp.concatenate(
            [hard[:, at], chosen[:, at], jnp.zeros((SLACK - 2, rows), f32)], axis=0
        )
        rows_ref[k] = found[:, at]


def softmax_body(counts, others, dt_ref, rows_ref, part_ref, *refs):
    got, (e_ref, *sum_refs) = refs[:others], refs[others:]
    features = dt_ref.shape[0] // 2
    rows = dt_ref.shape[1]
    half = features // 2
    k = 0
    for count, sum_ref in zip(counts, sum_refs):
        for slot in range(count):
            whole = part_ref[k]
            chosen = whole[rows + 1 : rows + 2]
            for r in got:
                whole = whole + r[k]
            scores = whole[:rows] / logit_divisor
            hard = jnp.where(chosen >= 0, whole[rows : rows + 1] / logit_divisor, LOWEST)
            peak = jnp.maximum(jnp.max(scores, axis=0, keepdims=True), hard)
            e = jnp.exp(scores - peak)
            hard_e = jnp.where(chosen >= 0, jnp.exp(hard - peak), 0.0)
            total = jnp.sum(e, axis=0, keepdims=True) + hard_e
            own = lax.broadcasted_iota(jnp.int32, (rows, rows), 0) == lax.broadcasted_iota(
                jnp.int32, (rows, rows), 1
            )
            positive = jnp.sum(jnp.where(own, scores, 0.0), axis=0, keepdims=True)
            e_ref[k, :rows] = e
            e_ref[k, rows:] = jnp.concatenate(
                [hard_e, chosen, peak, total, positive, jnp.zeros((SLACK - 5, rows), f32)],
                axis=0,
            )
            high, low = split2(e)
            both = dot(dt_ref[...], high)
            sums = both[:features] + both[features:] + dot(dt_ref[:features], low)
            sums = sums + rows_ref[k] * hard_e
            for h in range(2):
                sum_ref[slot, h, :half] = sums[h * half : (h + 1) * half]
                sum_ref[slot, h, half:] = jnp.concatenate(
                    [peak, total, jnp.zeros((SLACK - 2, rows), f32)], axis=0
                )
            k += 1


def merge(terms):
    half = terms[0].shape[0] - SLACK
    peaks = [t[half : half + 1] for t in terms]
    peak = functools.reduce(jnp.maximum, peaks)
    scales = [jnp.exp(p - peak) for p in peaks]
    sums = functools.reduce(jnp.add, [t[:half] * s for t, s in zip(terms, scales)])
    total = functools.reduce(
        jnp.add, [t[half + 1 : half + 2] * s for t, s in zip(terms, scales)]
    )
    return sums, peak, total


def merged(terms):
    sums, peak, total = merge(terms)
    tail = jnp.concatenate([peak, total, jnp.zeros((SLACK - 2, peak.shape[1]), f32)], axis=0)
    return jnp.concatenate([sums, tail], axis=0)


def first_body(mine_ref, other_ref, up_ref, down_ref):
    up_ref[...] = merged([mine_ref[0, 0], other_ref[0, 0]])
    down_ref[...] = merged([mine_ref[0, 1], other_ref[0, 1]])


def step_body(halves, mine_ref, other_ref, up_in, down_in, up_ref, down_ref):
    for arrived, out, slot, first in ((up_in, up_ref, 1, 0), (down_in, down_ref, 0, 1)):
        for h in range(2):
            terms = [mine_ref[slot, h], other_ref[slot, h]]
            if not halves:
                terms.append(arrived[h])
            elif h == first:
                terms.append(arrived[...])
            out[h] = merged(terms)


def last_body(mine_ref, other_ref, up_ref, down_ref, d_ref, e_ref, dq_ref, loss_ref):
    rows, features = d_ref.shape
    half = features // 2
    for h in range(2):
        sums, peak, total = merge([mine_ref[0, h], other_ref[0, h], up_ref[h], down_ref[h]])
        at = slice(h * half, (h + 1) * half)
        if half % 128 == 0:
            dq_ref[:, at] = ((sums / total).T - d_ref[:, at]) / logit_divisor
        elif h == 0:
            held = sums / total
        else:
            held = jnp.concatenate([held, sums / total], axis=0)
            dq_ref[...] = (held.T - d_ref[...]) / logit_divisor
    log_total = peak + jnp.log(total)
    loss_ref[...] = jnp.broadcast_to(log_total - e_ref[0, 4:5], loss_ref.shape)


def stats_body(counts, table_ref, *refs):
    out_ref = refs[-1]
    slot = 0
    for ref, count in zip(refs, counts):
        for k in range(count):
            at = pl.ds(table_ref[slot], 1)
            out_ref[0, at, :] = ref[k, 2:3]
            out_ref[1, at, :] = ref[k, 3:4]
            slot += 1


def gradient_body(pieces, counts, group, table_ref, q_ref, tot_ref, *refs):
    n = len(pieces)
    x_refs, refs = refs[: sum(pieces)], refs[sum(pieces) :]
    e_refs, refs = refs[: len(counts)], refs[len(counts) :]
    dd_ref, pool_ref, scaled_ref, local_ref = refs
    rows, features = q_ref.shape

    @pl.when(pl.program_id(0) == 0)
    def _():
        where = [(b, k) for b, count in enumerate(counts) for k in range(count)]
        at, total = 0, jnp.zeros((rows, features), f32)
        for g in range(n // group):
            xs, es, hards, locals_ = [], [], [], []
            for s in range(g * group, (g + 1) * group):
                held = [r[...] for r in x_refs[at : at + pieces[s]]]
                at += pieces[s]
                x = held[0] if len(held) == 1 else jnp.concatenate(held, axis=0)
                xs.append(x[:features])
                b, k = where[s]
                e = e_refs[b][k]
                row = pl.ds(table_ref[s], 1)
                scale = jnp.exp(e[rows + 2 : rows + 3] - tot_ref[0, row, :])
                scale = scale / tot_ref[1, row, :]
                es.append(e[:rows] * scale)
                hards.append(e[rows : rows + 1] * scale)
                locals_.append(e[rows + 1 : rows + 2])
            x = jnp.concatenate(xs, axis=1)
            chance = jnp.concatenate(es, axis=1)
            total = total + dot(chance, x, ((1,), (1,)), precision=lax.Precision.HIGHEST)
            high, low = split2(x * (jnp.concatenate(hards, axis=1) / logit_divisor))
            scaled_ref[g, :features] = high
            scaled_ref[g, features:] = low
            local_ref[g] = jnp.broadcast_to(
                jnp.concatenate(locals_, axis=1).astype(jnp.int32), local_ref.shape[1:]
            )
        dd_ref[...] = (total - q_ref[...]) / logit_divisor

    width = pool_ref.shape[1]
    first = pl.program_id(0) * width
    acc = jnp.zeros((2 * features, width), f32)
    for g in range(n // group):
        local = local_ref[g, :1]
        column = first + lax.broadcasted_iota(jnp.int32, (width, local.shape[1]), 0)
        marks = jnp.where(column == local, 1.0, 0.0).astype(bf16)
        acc = acc + dot(scaled_ref[g], marks, ((1,), (1,)))
    pool_ref[...] = acc[:features] + acc[features:]


def ring_order(chips):
    if chips < 4:
        return list(range(chips))
    return list(range(0, chips, 2)) + list(range(chips - 1, 0, -2))


def per_device(question_matrix, document_matrix, pool, hard_owner, hard_local):
    n, depth = lax.axis_size("blk"), lax.axis_size("dim")
    rows, features = question_matrix.shape
    columns = pool.shape[1]
    half = features // 2
    chips = n // 2
    walk = ring_order(chips)
    reach = chips // 2
    me = lax.axis_index("blk")

    up = [(2 * a + c, 2 * b + c) for a, b in zip(walk, walk[1:] + walk[:1]) for c in range(2)]
    down = [(b, a) for a, b in up]
    across = [(i, i ^ 1) for i in range(n)]

    def send(x, perm):
        return lax.ppermute(x, "blk", perm)

    own = [[0]] + [[-t, t] for t in range(1, reach)] + [[reach], []]
    other = [[]] + own[:-1]
    slots = [(0, d) for d in own[0]]
    for b in range(1, reach + 2):
        slots += [(0, d) for d in own[b]] + [(1, d) for d in other[b]]
    place = {chip: i for i, chip in enumerate(walk)}
    table = np.zeros((n, n), np.int32)
    for i in range(n):
        for s, (swap, d) in enumerate(slots):
            chip = walk[(place[i // 2] + d) % chips]
            table[i, s] = 2 * chip + ((i % 2) ^ swap)
    table = lax.dynamic_index_in_dim(jnp.asarray(table), me, 0, keepdims=False)

    smem = pl.BlockSpec(memory_space=pltpu.SMEM)
    vmem = pl.BlockSpec(memory_space=pltpu.VMEM)

    packed = call(
        lambda q, o, l, x: pack_body(q, o, l, columns, x),
        shape(features + SLACK, rows),
        "pack",
    )(question_matrix, hard_owner.T, hard_local.T)

    arrived = [[[packed]]]
    from_up, from_down = packed, packed
    cut = half + SLACK
    for t in range(1, reach):
        from_up, from_down = send(from_up, up), send(from_down, down)
        arrived.append([[from_up], [from_down]])
    arrived.append([[send(from_up[:cut], up), send(from_down[cut:], down)]])
    arrived.append([])
    shared = [[]] + [
        [[send(piece, across) for piece in block] for block in batch] for batch in arrived[:-1]
    ]
    batches = [a + s for a, s in zip(arrived, shared)]
    pieces = [[len(block) for block in batch] for batch in batches]
    counts = [len(batch) for batch in batches]

    dt, pool_parts = call(
        prepare_body,
        (shape(2 * features, rows, dtype=bf16), shape(3 * features, columns, dtype=bf16)),
        "prepare",
        data=features * columns * 10,
    )(document_matrix, pool)

    weights, own_sums, other_sums = [], [], []
    for b, batch in enumerate(batches):
        k = counts[b]
        part, found = call(
            functools.partial(score_body, pieces[b]),
            (shape(k, rows + SLACK, rows), shape(k, features, rows)),
            "score",
            flops=2 * features * rows * k * (3 * columns + 6 * rows),
            data=features * columns * 6,
            in_specs=[smem] + [vmem] * (2 + sum(pieces[b])),
        )(
            me.reshape(1), document_matrix, pool_parts, *[piece for block in batch for piece in block]
        )
        got = [
            lax.ppermute(part, "dim", [(i, (i + s) % depth) for i in range(depth)])
            for s in range(1, depth)
        ]
        sizes = [c for c in (len(own[b]), len(other[b])) if c]
        e, *sums = call(
            functools.partial(softmax_body, sizes, len(got)),
            [shape(k, rows + SLACK, rows)] + [shape(c, 2, half + SLACK, rows) for c in sizes],
            "softmax",
            flops=6 * features * rows * rows * k,
        )(dt, found, part, *got)
        weights.append(e)
        own_sums.append(sums.pop(0) if own[b] else None)
        other_sums.append(send(sums.pop(0), across) if other[b] else None)
    other_sums = other_sums[1:]

    message = shape(half + SLACK, rows)
    wide = shape(2, half + SLACK, rows)
    going_up, going_down = call(first_body, (message, message), "first_merge")(
        own_sums[reach], other_sums[reach]
    )
    for t in range(reach - 1, 0, -1):
        going_up, going_down = call(
            functools.partial(step_body, t == reach - 1), (wide, wide), "merge"
        )(own_sums[t], other_sums[t], send(going_up, up), send(going_down, down))
    whole = pl.BlockSpec((1, SLACK, rows), lambda i: (0, rows // SLACK, 0))
    full = lambda *dims: pl.BlockSpec(dims, lambda i: (0,) * len(dims))
    sums_spec = full(1, 2, half + SLACK, rows)
    question_derivative, loss = call(
        last_body,
        (shape(rows, features), shape(SLACK, rows)),
        "finish",
        grid=(1,),
        in_specs=[sums_spec, sums_spec, full(2, half + SLACK, rows), full(2, half + SLACK, rows)]
        + [full(rows, features), whole],
        out_specs=(full(rows, features), full(SLACK, rows)),
    )(
        own_sums[0],
        other_sums[0],
        send(going_up, up),
        send(going_down, down),
        document_matrix,
        weights[0],
    )

    totals = call(
        functools.partial(stats_body, counts),
        shape(2, n, rows),
        "stats",
        grid=(1,),
        in_specs=[smem]
        + [pl.BlockSpec((c, SLACK, rows), lambda i: (0, rows // SLACK, 0)) for c in counts],
        out_specs=full(2, n, rows),
    )(table, *weights)
    step = 1
    while step < n:
        there = send(totals, [(i, i ^ step) for i in range(n)])
        peak = jnp.maximum(totals[0], there[0])
        total = totals[1] * jnp.exp(totals[0] - peak) + there[1] * jnp.exp(there[0] - peak)
        totals = jnp.stack([peak, total])
        step *= 2

    flat = [block for batch in batches for block in batch]
    group = 4
    width = 512
    document_derivative, grad_pool = call(
        functools.partial(gradient_body, [len(block) for block in flat], counts, group),
        (shape(rows, features), shape(features, columns)),
        "gradient",
        flops=2 * features * rows * n * (2 * columns + 6 * rows),
        data=features * columns * 8,
        grid=(columns // width,),
        in_specs=[smem] + [vmem] * (2 + sum(len(block) for block in flat) + len(counts)),
        out_specs=(full(rows, features), pl.BlockSpec((features, width), lambda i: (0, i))),
        scratch_shapes=[
            pltpu.VMEM((n // group, 2 * features, group * rows), bf16),
            pltpu.VMEM((n // group, SLACK, group * rows), jnp.int32),
        ],
    )(table, question_matrix, totals, *[piece for block in flat for piece in block], *weights)
    return loss[0], question_derivative, document_derivative, grad_pool


def solution(mesh):
    placed = (P("blk", "dim"), P("blk", "dim"), P("dim", "blk"), P("blk", None), P("blk", None))
    return jax.shard_map(
        per_device,
        mesh=mesh,
        in_specs=placed,
        out_specs=(P("blk"), P("blk", "dim"), P("blk", "dim"), P("dim", "blk")),
        check_vma=False,
    )
```

time: 285 us -> 118 us (0.41)
  waiting for transfers between devices: 139 us -> 30.1 us
  Pallas kernels: 0 us -> 44.8 us
  other arithmetic: 38.5 us -> 0.06 us
  local copies, waits for them, and re-layouts: 33.2 us -> 8.68 us
  matrix products: 21.7 us -> 0 us
  between operations: 13.9 us -> 1 us
  blocking collectives: 9.57 us -> 0 us
  starting transfers between devices: 27.7 us -> 32.7 us
    reduce_scatter x1 -> x0, waiting for transfers between devices: 80.3 us -> none  [per_device(): lax.psum_scatter(lax.dot_general(columns, question_matrix, (((0,), (0,)),...]
    pallas_call x0 -> x21, Pallas kernels: none -> 44.8 us  [the longest x6 24.9 us: per_device(): call(functools.partial(score_body, pieces[b]), (shape(k, rows + SLACK, ro...]
    ppermute x0 -> x40, starting transfers between devices: none -> 32.7 us  [the longest x34 26.5 us: send(): return lax.ppermute(x, 'blk', perm)]
    all_to_all x3 -> x0, waiting for transfers between devices: 31.5 us -> none  [the longest x1 27.5 us: per_device(): lax.all_to_all(found, 'blk', split_axis=0, concat_axis=0, tiled=True)]
    ppermute x0 -> x40, waiting for transfers between devices: none -> 30.1 us  [the longest x34 18.1 us: send(): return lax.ppermute(x, 'blk', perm)]
    all_to_all x3 -> x0, starting transfers between devices: 27.6 us -> none  [the longest x1 16.4 us: per_device(): lax.all_to_all(outgoing, 'blk', split_axis=0, concat_axis=0, tiled=True)]
    all_gather x1 -> x0, waiting for transfers between devices: 26.9 us -> none  [per_device(): lax.all_gather(document_matrix, 'blk', axis=0, tiled=True)]
    dot_general x5 -> x0, matrix products: 21.7 us -> none  [the longest x1 6.18 us: per_device(): lax.dot_general(question_matrix, lax.all_gather(document_matrix, 'blk', a...]
  transfers between devices with their start and end apart: 6 -> 40, of which waited for: 4 -> 11; matrix products, arithmetic and copies ran while one was open for 23% -> 1% of each run, Pallas kernels for 0% -> 36%
where the time goes in v1:
time: 118 us; the launch traced here: 117 us
  Pallas kernels  44.8 us (38%)
  starting transfers between devices  32.7 us (28%)
  waiting for transfers between devices  30.1 us (26%)
  local copies, waits for them, and re-layouts  8.68 us (7%)
    ppermute x34, starting transfers between devices, send(): return lax.ppermute(x, 'blk', perm)  26.5 us
    pallas_call x6, Pallas kernels, per_device(): call(functools.partial(score_body, pieces[b]), (shape(k, rows + SLACK, ro...  24.9 us
    ppermute x34, waiting for transfers between devices, send(): return lax.ppermute(x, 'blk', perm)  18.1 us
    ppermute x6, waiting for transfers between devices, per_device(): lax.ppermute(part, 'dim', [(i, (i + s) % depth) for i in range(depth)])  12 us
    pallas_call x1, Pallas kernels, per_device(): call(functools.partial(gradient_body, [len(block) for block in flat], cou...  11.9 us
    unnamed x20, local copies, waits for them, and re-layouts  7.47 us
    ppermute x6, starting transfers between devices, per_device(): lax.ppermute(part, 'dim', [(i, (i + s) % depth) for i in range(depth)])  6.18 us
    pallas_call x1, Pallas kernels, per_device(): call(prepare_body, (shape(2 * features, rows, dtype=bf16), shape(3 * feat...  3.69 us
  transfers between devices with their start and end apart: 40, of which 11 were waited for; matrix products, arithmetic and copies ran while one was open for 1% of the time, Pallas kernels for 36%

profile of v1, /device:TPU:0, one launch (start us, length us, event | category | flops | bytes accessed | tf_op | source)
XLA Modules:
  0.0 117.3 jit_solution(3668221674523937339)
XLA Ops:
  3.1 3.0 %collective-permute-start.2 = (f32[392,128]{1,0:T(8,128)S(1)}, f32[392,128]{1,0:T(8,128)S(1)}, u32[]{:S(2)}, u32[]{:S(2)}) collective-permute-start(f32[392,128]{1,0:T(8,128)S(1)} %pack.1.refs_0_), channel_id=1, source_target_pairs={{8,0},{10,2},{16,8},{18,10},{24,16},{26,18},{28,24},{30,26},{20,28... | collective-permute-start | bytes 602120 | tf_op jit(solution)/shard_map/ppermute | solution.py:265
  6.2 4.9 %collective-permute-done.2.refs_1_.refs_2_ = f32[392,128]{1,0:T(8,128)S(1)} collective-permute-done((f32[392,128]{1,0:T(8,128)S(1)}, f32[392,128]{1,0:T(8,128)S(1)}, u32[]{:S(2)}, u32[]{:S(2)}) %collective-permute-start.2) | collective-permute-done | bytes 200736 | tf_op jit(solution)/shard_map/ppermute | solution.py:265
  11.1 1.7 %collective-permute-start.7 = (f32[392,128]{1,0:T(8,128)S(1)}, f32[392,128]{1,0:T(8,128)S(1)}, u32[]{:S(2)}, u32[]{:S(2)}) collective-permute-start(f32[392,128]{1,0:T(8,128)S(1)} %collective-permute-done.2.refs_1_.refs_2_), channel_id=1, source_target_pairs={{8,0},{10,2},{16,8},{18,10},{24,16},{26,18},{28,24},{30,26},{20,28... | collective-permute-start | bytes 602120 | tf_op jit(solution)/shard_map/ppermute | solution.py:265
  13.7 1.9 %copy-done.3 = f32[384,2048]{1,0:T(8,128)S(1)} copy-done((f32[384,2048]{1,0:T(8,128)S(1)}, f32[384,2048]{1,0:T(8,128)}, u32[]{:S(2)}) %copy-start.3) | copy-done | bytes 3145752
  15.6 3.7 %prepare.1 = (bf16[768,128]{1,0:T(8,128)(2,1)S(1)}, bf16[1152,2048]{1,0:T(8,128)(2,1)}) custom-call(f32[128,384]{1,0:T(8,128)S(1)} %copy-done.1, f32[384,2048]{1,0:T(8,128)S(1)} %copy-done.3), custom_call_target="tpu_custom_call" | custom-call | bytes 7864320 | tf_op jit(solution)/shard_map/prepare/pallas_call | solution.py:304
  20.2 1.7 %collective-permute-start.13 = (f32[392,128]{1,0:T(8,128)S(1)}, f32[392,128]{1,0:T(8,128)S(1)}, u32[]{:S(2)}, u32[]{:S(2)}) collective-permute-start(f32[392,128]{1,0:T(8,128)S(1)} %collective-permute-done.7.refs_1_.refs_5_), channel_id=1, source_target_pairs={{8,0},{10,2},{16,8},{18,10},{24,16},{26,18},{28,24},{30,26},{20,28... | collective-permute-start | bytes 602120 | tf_op jit(solution)/shard_map/ppermute | solution.py:265
  21.8 2.3 %copy-done = bf16[1152,2048]{1,0:T(8,128)(2,1)S(1)} copy-done((bf16[1152,2048]{1,0:T(8,128)(2,1)S(1)}, bf16[1152,2048]{1,0:T(8,128)(2,1)}, u32[]{:S(2)}) %copy-start) | copy-done | bytes 4718616
  25.8 1.6 %collective-permute-start = (f32[1,136,128]{2,1,0:T(8,128)S(1)}, f32[1,136,128]{2,1,0:T(8,128)S(1)}, u32[]{:S(2)}, u32[]{:S(2)}) collective-permute-start(f32[1,136,128]{2,1,0:T(8,128)S(1)} %get-tuple-element.49.part_ref), channel_id=1, source_target_pairs={{0,1},{1,0},{2,3},{3,2},{4,5},{5,4},{6,7},{7,6},{8,9},{9,8},{10,11... | collective-permute-start | bytes 208904 | tf_op jit(solution)/shard_map/ppermute | solution.py:325
  27.3 5.4 %score.7 = (f32[3,136,128]{2,1,0:T(8,128)S(1)}, f32[3,384,128]{2,1,0:T(8,128)S(1)}) custom-call(s32[1]{0:T(128)} %bitcast.me_ref, f32[128,384]{1,0:T(8,128)S(1)} %copy-done.2, bf16[1152,2048]{1,0:T(8,128)(2,1)} %get-tuple-element.47.pool_ref, f32[392,128]{1,0:T(8,128)S(1)} %collective-permute-done.1.refs_0_.refs_1_, ...), custom_call_target="tpu_custom_call" | custom-call | flops 2038431744 | bytes 4718592 | tf_op jit(solution)/shard_map/score/pallas_call | solution.py:314
  35.4 5.6 %score.8 = (f32[4,136,128]{2,1,0:T(8,128)S(1)}, f32[4,384,128]{2,1,0:T(8,128)S(1)}) custom-call(s32[1]{0:T(128)} %bitcast.me_ref, f32[128,384]{1,0:T(8,128)S(1)} %copy-done.2, bf16[1152,2048]{1,0:T(8,128)(2,1)} %get-tuple-element.47.pool_ref, f32[392,128]{1,0:T(8,128)S(1)} %collective-permute-done.6.refs_0_.refs_4_, ...), custom_call_target="tpu_custom_call" | custom-call | flops 2717908992 | bytes 4718592 | tf_op jit(solution)/shard_map/score/pallas_call | solution.py:314
  42.4 5.5 %score.9 = (f32[4,136,128]{2,1,0:T(8,128)S(1)}, f32[4,384,128]{2,1,0:T(8,128)S(1)}) custom-call(s32[1]{0:T(128)} %bitcast.me_ref, f32[128,384]{1,0:T(8,128)S(1)} %copy-done.2, bf16[1152,2048]{1,0:T(8,128)(2,1)} %get-tuple-element.47.pool_ref, f32[392,128]{1,0:T(8,128)S(1)} %collective-permute-done.12.refs_0_.refs_8_, ...), custom_call_target="tpu_custom_call" | custom-call | flops 2717908992 | bytes 4718592 | tf_op jit(solution)/shard_map/score/pallas_call | solution.py:314
  48.3 1.7 %collective-permute-start.10 = (f32[4,136,128]{2,1,0:T(8,128)S(1)}, f32[4,136,128]{2,1,0:T(8,128)S(1)}, u32[]{:S(2)}, u32[]{:S(2)}) collective-permute-start(f32[4,136,128]{2,1,0:T(8,128)S(1)} %get-tuple-element.56.part_ref), channel_id=1, source_target_pairs={{0,1},{1,0},{2,3},{3,2},{4,5},{5,4},{6,7},{7,6},{8,9},{9,8},{10,11... | collective-permute-start | bytes 835592 | tf_op jit(solution)/shard_map/ppermute | solution.py:325
  50.4 5.4 %score.10 = (f32[3,136,128]{2,1,0:T(8,128)S(1)}, f32[3,384,128]{2,1,0:T(8,128)S(1)}) custom-call(s32[1]{0:T(128)} %bitcast.me_ref, f32[128,384]{1,0:T(8,128)S(1)} %copy-done.2, bf16[1152,2048]{1,0:T(8,128)(2,1)} %get-tuple-element.47.pool_ref, f32[200,128]{1,0:T(8,128)S(1)} %collective-permute-done.18.refs_0_.refs_12_, ...), custom_call_target="tpu_custom_call" | custom-call | flops 2038431744 | bytes 4718592 | tf_op jit(solution)/shard_map/score/pallas_call | solution.py:314
  55.7 1.7 %collective-permute-start.22 = (f32[3,136,128]{2,1,0:T(8,128)S(1)}, f32[3,136,128]{2,1,0:T(8,128)S(1)}, u32[]{:S(2)}, u32[]{:S(2)}) collective-permute-start(f32[3,136,128]{2,1,0:T(8,128)S(1)} %get-tuple-element.64.part_ref), channel_id=1, source_target_pairs={{0,1},{1,0},{2,3},{3,2},{4,5},{5,4},{6,7},{7,6},{8,9},{9,8},{10,11... | collective-permute-start | bytes 626696 | tf_op jit(solution)/shard_map/ppermute | solution.py:325
  62.4 11.0 %collective-permute-done.26.refs_0_ = f32[1,136,128]{2,1,0:T(8,128)S(1)} collective-permute-done((f32[1,136,128]{2,1,0:T(8,128)S(1)}, f32[1,136,128]{2,1,0:T(8,128)S(1)}, u32[]{:S(2)}, u32[]{:S(2)}) %collective-permute-start.26) | collective-permute-done | bytes 69664 | tf_op jit(solution)/shard_map/ppermute | solution.py:325
  78.6 1.7 %collective-permute-done.37 = f32[2,16,128]{2,1,0:T(8,128)S(1)} collective-permute-done((f32[2,16,128]{2,1,0:T(8,128)S(1)}, f32[2,16,128]{2,1,0:T(8,128)S(1)}, u32[]{:S(2)}, u32[]{:S(2)}) %collective-permute-start.37) | collective-permute-done | bytes 16416 | tf_op jit(solution)/shard_map/ppermute | solution.py:265
  80.4 1.6 %collective-permute-start.28 = (f32[200,128]{1,0:T(8,128)S(1)}, f32[200,128]{1,0:T(8,128)S(1)}, u32[]{:S(2)}, u32[]{:S(2)}) collective-permute-start(f32[200,128]{1,0:T(8,128)S(1)} %get-tuple-element.70), channel_id=1, source_target_pairs={{0,8},{2,10},{8,16},{10,18},{16,24},{18,26},{24,28},{26,30},{28,20... | collective-permute-start | bytes 307208 | tf_op jit(solution)/shard_map/ppermute | solution.py:265
  86.8 1.6 %collective-permute-start.30 = (f32[2,200,128]{2,1,0:T(8,128)S(1)}, f32[2,200,128]{2,1,0:T(8,128)S(1)}, u32[]{:S(2)}, u32[]{:S(2)}) collective-permute-start(f32[2,200,128]{2,1,0:T(8,128)S(1)} %get-tuple-element.72), channel_id=1, source_target_pairs={{0,8},{2,10},{8,16},{10,18},{16,24},{18,26},{24,28},{26,30},{28,20... | collective-permute-start | bytes 614408 | tf_op jit(solution)/shard_map/ppermute | solution.py:265
  88.9 2.7 %collective-permute-start.39 = (f32[2,16,128]{2,1,0:T(8,128)S(1)}, f32[2,16,128]{2,1,0:T(8,128)S(1)}, u32[]{:S(2)}, u32[]{:S(2)}) collective-permute-start(f32[2,16,128]{2,1,0:T(8,128)S(1)} %pad_maximum_fusion.2), channel_id=1, source_target_pairs={{0,16},{2,18},{4,20},{6,22},{8,24},{10,26},{12,28},{14,30},{16,0},... | collective-permute-start | bytes 49160 | tf_op jit(solution)/shard_map/ppermute | solution.py:265
  92.7 1.6 %collective-permute-done.31.down_in = f32[2,200,128]{2,1,0:T(8,128)S(1)} collective-permute-done((f32[2,200,128]{2,1,0:T(8,128)S(1)}, f32[2,200,128]{2,1,0:T(8,128)S(1)}, u32[]{:S(2)}, u32[]{:S(2)}) %collective-permute-start.31) | collective-permute-done | bytes 204832 | tf_op jit(solution)/shard_map/ppermute | solution.py:265
  94.4 1.7 %collective-permute-start.32 = (f32[2,200,128]{2,1,0:T(8,128)S(1)}, f32[2,200,128]{2,1,0:T(8,128)S(1)}, u32[]{:S(2)}, u32[]{:S(2)}) collective-permute-start(f32[2,200,128]{2,1,0:T(8,128)S(1)} %get-tuple-element.74), channel_id=1, source_target_pairs={{0,8},{2,10},{8,16},{10,18},{16,24},{18,26},{24,28},{26,30},{28,20... | collective-permute-start | bytes 614408 | tf_op jit(solution)/shard_map/ppermute | solution.py:265
  96.6 3.7 %collective-permute-done.32.up_in = f32[2,200,128]{2,1,0:T(8,128)S(1)} collective-permute-done((f32[2,200,128]{2,1,0:T(8,128)S(1)}, f32[2,200,128]{2,1,0:T(8,128)S(1)}, u32[]{:S(2)}, u32[]{:S(2)}) %collective-permute-start.32) | collective-permute-done | bytes 204832 | tf_op jit(solution)/shard_map/ppermute | solution.py:265
  100.3 1.6 %collective-permute-done.33.down_in = f32[2,200,128]{2,1,0:T(8,128)S(1)} collective-permute-done((f32[2,200,128]{2,1,0:T(8,128)S(1)}, f32[2,200,128]{2,1,0:T(8,128)S(1)}, u32[]{:S(2)}, u32[]{:S(2)}) %collective-permute-start.33) | collective-permute-done | bytes 204832 | tf_op jit(solution)/shard_map/ppermute | solution.py:265
  104.1 11.9 %gradient.1 = (f32[128,384]{1,0:T(8,128)}, f32[384,2048]{1,0:T(8,128)}) custom-call(s32[16]{0:T(128)S(1)} %dynamic-slice_bitcast_fusion.table_ref, f32[128,384]{1,0:T(8,128)S(1)} %copy-done.5, f32[2,16,128]{2,1,0:T(8,128)S(1)} %pad_maximum_fusion.3.tot_ref, f32[392,128]{1,0:T(8,128)S(1)} %pack.1.refs_0_, ...), custom_call_target="tpu_custom_call" | custom-call | flops 7650410496 | bytes 6291456 | tf_op jit(solution)/shard_map/gradient/pallas_call | solution.py:389
  (110 shorter events, 31.3 us)
Async XLA Ops:
  6.1 13.8 %collective-permute-start.1 = (f32[392,128]{1,0:T(8,128)S(1)}, f32[392,128]{1,0:T(8,128)S(1)}, u32[]{:S(2)}, u32[]{:S(2)}) collective-permute-start(f32[392,128]{1,0:T(8,128)S(1)} %pack.1.refs_0_), channel_id=1, source_target_pairs={{0,8},{2,10},{8,16},{10,18},{16,24},{18,26},{24,28},{26,30},{28,20... | collective-permute-start | bytes 602120 | tf_op jit(solution)/shard_map/ppermute | solution.py:265
  11.1 9.1 %collective-permute-start.7 = (f32[392,128]{1,0:T(8,128)S(1)}, f32[392,128]{1,0:T(8,128)S(1)}, u32[]{:S(2)}, u32[]{:S(2)}) collective-permute-start(f32[392,128]{1,0:T(8,128)S(1)} %collective-permute-done.2.refs_1_.refs_2_), channel_id=1, source_target_pairs={{8,0},{10,2},{16,8},{18,10},{24,16},{26,18},{28,24},{30,26},{20,28... | collective-permute-start | bytes 602120 | tf_op jit(solution)/shard_map/ppermute | solution.py:265
  12.8 13.0 %collective-permute-start.3 = (f32[392,128]{1,0:T(8,128)S(1)}, f32[392,128]{1,0:T(8,128)S(1)}, u32[]{:S(2)}, u32[]{:S(2)}) collective-permute-start(f32[392,128]{1,0:T(8,128)S(1)} %pack.1.refs_0_), channel_id=1, source_target_pairs={{0,2},{2,0},{4,6},{6,4},{8,10},{10,8},{12,14},{14,12},{16,18},{18,... | collective-permute-start | bytes 602120 | tf_op jit(solution)/shard_map/ppermute | solution.py:265
  19.3 14.0 %collective-permute-start.9 = (f32[392,128]{1,0:T(8,128)S(1)}, f32[392,128]{1,0:T(8,128)S(1)}, u32[]{:S(2)}, u32[]{:S(2)}) collective-permute-start(f32[392,128]{1,0:T(8,128)S(1)} %collective-permute-done.2.refs_1_.refs_2_), channel_id=1, source_target_pairs={{0,2},{2,0},{4,6},{6,4},{8,10},{10,8},{12,14},{14,12},{16,18},{18,... | collective-permute-start | bytes 602120 | tf_op jit(solution)/shard_map/ppermute | solution.py:265
  19.8 14.1 %collective-permute-start.8 = (f32[392,128]{1,0:T(8,128)S(1)}, f32[392,128]{1,0:T(8,128)S(1)}, u32[]{:S(2)}, u32[]{:S(2)}) collective-permute-start(f32[392,128]{1,0:T(8,128)S(1)} %collective-permute-done.1.refs_0_.refs_1_), channel_id=1, source_target_pairs={{0,2},{2,0},{4,6},{6,4},{8,10},{10,8},{12,14},{14,12},{16,18},{18,... | collective-permute-start | bytes 602120 | tf_op jit(solution)/shard_map/ppermute | solution.py:265
  19.8 12.9 %collective-permute-start.6 = (f32[392,128]{1,0:T(8,128)S(1)}, f32[392,128]{1,0:T(8,128)S(1)}, u32[]{:S(2)}, u32[]{:S(2)}) collective-permute-start(f32[392,128]{1,0:T(8,128)S(1)} %collective-permute-done.1.refs_0_.refs_1_), channel_id=1, source_target_pairs={{0,8},{2,10},{8,16},{10,18},{16,24},{18,26},{24,28},{26,30},{28,20... | collective-permute-start | bytes 602120 | tf_op jit(solution)/shard_map/ppermute | solution.py:265
  20.2 12.6 %collective-permute-start.13 = (f32[392,128]{1,0:T(8,128)S(1)}, f32[392,128]{1,0:T(8,128)S(1)}, u32[]{:S(2)}, u32[]{:S(2)}) collective-permute-start(f32[392,128]{1,0:T(8,128)S(1)} %collective-permute-done.7.refs_1_.refs_5_), channel_id=1, source_target_pairs={{8,0},{10,2},{16,8},{18,10},{24,16},{26,18},{28,24},{30,26},{20,28... | collective-permute-start | bytes 602120 | tf_op jit(solution)/shard_map/ppermute | solution.py:265
  25.8 33.3 %collective-permute-start = (f32[1,136,128]{2,1,0:T(8,128)S(1)}, f32[1,136,128]{2,1,0:T(8,128)S(1)}, u32[]{:S(2)}, u32[]{:S(2)}) collective-permute-start(f32[1,136,128]{2,1,0:T(8,128)S(1)} %get-tuple-element.49.part_ref), channel_id=1, source_target_pairs={{0,1},{1,0},{2,3},{3,2},{4,5},{5,4},{6,7},{7,6},{8,9},{9,8},{10,11... | collective-permute-start | bytes 208904 | tf_op jit(solution)/shard_map/ppermute | solution.py:325
  32.7 9.1 %collective-permute-start.15 = (f32[392,128]{1,0:T(8,128)S(1)}, f32[392,128]{1,0:T(8,128)S(1)}, u32[]{:S(2)}, u32[]{:S(2)}) collective-permute-start(f32[392,128]{1,0:T(8,128)S(1)} %collective-permute-done.7.refs_1_.refs_5_), channel_id=1, source_target_pairs={{0,2},{2,0},{4,6},{6,4},{8,10},{10,8},{12,14},{14,12},{16,18},{18,... | collective-permute-start | bytes 602120 | tf_op jit(solution)/shard_map/ppermute | solution.py:265
  32.8 9.0 %collective-permute-start.14 = (f32[392,128]{1,0:T(8,128)S(1)}, f32[392,128]{1,0:T(8,128)S(1)}, u32[]{:S(2)}, u32[]{:S(2)}) collective-permute-start(f32[392,128]{1,0:T(8,128)S(1)} %collective-permute-done.6.refs_0_.refs_4_), channel_id=1, source_target_pairs={{0,2},{2,0},{4,6},{6,4},{8,10},{10,8},{12,14},{14,12},{16,18},{18,... | collective-permute-start | bytes 602120 | tf_op jit(solution)/shard_map/ppermute | solution.py:265
  33.9 8.4 %collective-permute-start.19 = (f32[192,128]{1,0:T(8,128)S(1)}, f32[192,128]{1,0:T(8,128)S(1)}, u32[]{:S(2)}, u32[]{:S(2)}) collective-permute-start(f32[192,128]{1,0:T(8,128)S(1)} %slice.58), channel_id=1, source_target_pairs={{8,0},{10,2},{16,8},{18,10},{24,16},{26,18},{28,24},{30,26},{20,28... | collective-permute-start | bytes 294920 | tf_op jit(solution)/shard_map/ppermute | solution.py:265
  41.8 8.2 %collective-permute-start.21 = (f32[392,128]{1,0:T(8,128)S(1)}, f32[392,128]{1,0:T(8,128)S(1)}, u32[]{:S(2)}, u32[]{:S(2)}) collective-permute-start(f32[392,128]{1,0:T(8,128)S(1)} %collective-permute-done.13.refs_1_.refs_9_), channel_id=1, source_target_pairs={{0,2},{2,0},{4,6},{6,4},{8,10},{10,8},{12,14},{14,12},{16,18},{18,... | collective-permute-start | bytes 602120 | tf_op jit(solution)/shard_map/ppermute | solution.py:265
  41.8 8.5 %collective-permute-start.20 = (f32[392,128]{1,0:T(8,128)S(1)}, f32[392,128]{1,0:T(8,128)S(1)}, u32[]{:S(2)}, u32[]{:S(2)}) collective-permute-start(f32[392,128]{1,0:T(8,128)S(1)} %collective-permute-done.12.refs_0_.refs_8_), channel_id=1, source_target_pairs={{0,2},{2,0},{4,6},{6,4},{8,10},{10,8},{12,14},{14,12},{16,18},{18,... | collective-permute-start | bytes 602120 | tf_op jit(solution)/shard_map/ppermute | solution.py:265
  47.9 12.5 %collective-permute-start.4 = (f32[3,136,128]{2,1,0:T(8,128)S(1)}, f32[3,136,128]{2,1,0:T(8,128)S(1)}, u32[]{:S(2)}, u32[]{:S(2)}) collective-permute-start(f32[3,136,128]{2,1,0:T(8,128)S(1)} %get-tuple-element.52.part_ref), channel_id=1, source_target_pairs={{0,1},{1,0},{2,3},{3,2},{4,5},{5,4},{6,7},{7,6},{8,9},{9,8},{10,11... | collective-permute-start | bytes 626696 | tf_op jit(solution)/shard_map/ppermute | solution.py:325
  48.3 13.6 %collective-permute-start.10 = (f32[4,136,128]{2,1,0:T(8,128)S(1)}, f32[4,136,128]{2,1,0:T(8,128)S(1)}, u32[]{:S(2)}, u32[]{:S(2)}) collective-permute-start(f32[4,136,128]{2,1,0:T(8,128)S(1)} %get-tuple-element.56.part_ref), channel_id=1, source_target_pairs={{0,1},{1,0},{2,3},{3,2},{4,5},{5,4},{6,7},{7,6},{8,9},{9,8},{10,11... | collective-permute-start | bytes 835592 | tf_op jit(solution)/shard_map/ppermute | solution.py:325
  50.0 23.6 %collective-permute-start.16 = (f32[4,136,128]{2,1,0:T(8,128)S(1)}, f32[4,136,128]{2,1,0:T(8,128)S(1)}, u32[]{:S(2)}, u32[]{:S(2)}) collective-permute-start(f32[4,136,128]{2,1,0:T(8,128)S(1)} %get-tuple-element.60.part_ref), channel_id=1, source_target_pairs={{0,1},{1,0},{2,3},{3,2},{4,5},{5,4},{6,7},{7,6},{8,9},{9,8},{10,11... | collective-permute-start | bytes 835592 | tf_op jit(solution)/shard_map/ppermute | solution.py:325
  55.7 18.4 %collective-permute-start.22 = (f32[3,136,128]{2,1,0:T(8,128)S(1)}, f32[3,136,128]{2,1,0:T(8,128)S(1)}, u32[]{:S(2)}, u32[]{:S(2)}) collective-permute-start(f32[3,136,128]{2,1,0:T(8,128)S(1)} %get-tuple-element.64.part_ref), channel_id=1, source_target_pairs={{0,1},{1,0},{2,3},{3,2},{4,5},{5,4},{6,7},{7,6},{8,9},{9,8},{10,11... | collective-permute-start | bytes 626696 | tf_op jit(solution)/shard_map/ppermute | solution.py:325
  59.1 14.3 %collective-permute-start.26 = (f32[1,136,128]{2,1,0:T(8,128)S(1)}, f32[1,136,128]{2,1,0:T(8,128)S(1)}, u32[]{:S(2)}, u32[]{:S(2)}) collective-permute-start(f32[1,136,128]{2,1,0:T(8,128)S(1)} %get-tuple-element.68.part_ref), channel_id=1, source_target_pairs={{0,1},{1,0},{2,3},{3,2},{4,5},{5,4},{6,7},{7,6},{8,9},{9,8},{10,11... | collective-permute-start | bytes 208904 | tf_op jit(solution)/shard_map/ppermute | solution.py:325
  75.3 11.4 %collective-permute-start.23 = (f32[2,2,200,128]{3,2,1,0:T(8,128)S(1)}, f32[2,2,200,128]{3,2,1,0:T(8,128)S(1)}, u32[]{:S(2)}, u32[]{:S(2)}) collective-permute-start(f32[2,2,200,128]{3,2,1,0:T(8,128)S(1)} %get-tuple-element.65), channel_id=1, source_target_pairs={{0,2},{2,0},{4,6},{6,4},{8,10},{10,8},{12,14},{14,12},{16,18},{18,... | collective-permute-start | bytes 1228808 | tf_op jit(solution)/shard_map/ppermute | solution.py:265
  78.1 13.5 %collective-permute-start.17 = (f32[2,2,200,128]{3,2,1,0:T(8,128)S(1)}, f32[2,2,200,128]{3,2,1,0:T(8,128)S(1)}, u32[]{:S(2)}, u32[]{:S(2)}) collective-permute-start(f32[2,2,200,128]{3,2,1,0:T(8,128)S(1)} %get-tuple-element.61), channel_id=1, source_target_pairs={{0,2},{2,0},{4,6},{6,4},{8,10},{10,8},{12,14},{14,12},{16,18},{18,... | collective-permute-start | bytes 1228808 | tf_op jit(solution)/shard_map/ppermute | solution.py:265
  85.1 11.5 %collective-permute-start.11 = (f32[2,2,200,128]{3,2,1,0:T(8,128)S(1)}, f32[2,2,200,128]{3,2,1,0:T(8,128)S(1)}, u32[]{:S(2)}, u32[]{:S(2)}) collective-permute-start(f32[2,2,200,128]{3,2,1,0:T(8,128)S(1)} %get-tuple-element.57), channel_id=1, source_target_pairs={{0,2},{2,0},{4,6},{6,4},{8,10},{10,8},{12,14},{14,12},{16,18},{18,... | collective-permute-start | bytes 1228808 | tf_op jit(solution)/shard_map/ppermute | solution.py:265
  91.5 24.4 %collective-permute-start.5 = (f32[1,2,200,128]{3,2,1,0:T(8,128)S(1)}, f32[1,2,200,128]{3,2,1,0:T(8,128)S(1)}, u32[]{:S(2)}, u32[]{:S(2)}) collective-permute-start(f32[1,2,200,128]{3,2,1,0:T(8,128)S(1)} %get-tuple-element.53), channel_id=1, source_target_pairs={{0,2},{2,0},{4,6},{6,4},{8,10},{10,8},{12,14},{14,12},{16,18},{18,... | collective-permute-start | bytes 614408 | tf_op jit(solution)/shard_map/ppermute | solution.py:265
  102.0 14.0 %collective-permute-start.34 = (f32[2,200,128]{2,1,0:T(8,128)S(1)}, f32[2,200,128]{2,1,0:T(8,128)S(1)}, u32[]{:S(2)}, u32[]{:S(2)}) collective-permute-start(f32[2,200,128]{2,1,0:T(8,128)S(1)} %get-tuple-element.76), channel_id=1, source_target_pairs={{0,8},{2,10},{8,16},{10,18},{16,24},{18,26},{24,28},{26,30},{28,20... | collective-permute-start | bytes 614408 | tf_op jit(solution)/shard_map/ppermute | solution.py:265
  103.5 12.5 %collective-permute-start.35 = (f32[2,200,128]{2,1,0:T(8,128)S(1)}, f32[2,200,128]{2,1,0:T(8,128)S(1)}, u32[]{:S(2)}, u32[]{:S(2)}) collective-permute-start(f32[2,200,128]{2,1,0:T(8,128)S(1)} %get-tuple-element.77), channel_id=1, source_target_pairs={{8,0},{10,2},{16,8},{18,10},{24,16},{26,18},{28,24},{30,26},{20,28... | collective-permute-start | bytes 614408 | tf_op jit(solution)/shard_map/ppermute | solution.py:265
  (26 other events, 175.8 us)

commit v2 on v0

v2 whole, which is shorter than its diff:
```python
import functools

import jax
import jax.numpy as jnp
from jax import lax
from jax.experimental import pallas as pl
from jax.experimental.pallas import tpu as pltpu
from jax.sharding import PartitionSpec as P

logit_divisor = 0.05
LOWEST = -3.0e38
SLACK = 8

f32 = jnp.float32
bf16 = jnp.bfloat16


def split2(x):
    high = x.astype(bf16)
    return high, (x - high.astype(f32)).astype(bf16)


def dot(a, b, contract=((1,), (0,)), precision=None):
    return lax.dot_general(
        a, b, (contract, ((), ())), precision=precision, preferred_element_type=f32
    )


def call(body, out_shape, name, flops=0, data=1 << 20, limit=48 << 20, **kw):
    return pl.pallas_call(
        body,
        out_shape=out_shape,
        name=name,
        cost_estimate=pl.CostEstimate(flops=flops, bytes_accessed=data, transcendentals=0),
        compiler_params=pltpu.CompilerParams(vmem_limit_bytes=limit),
        **kw,
    )


def shape(*dims, dtype=f32):
    return jax.ShapeDtypeStruct(dims, dtype)


def pack_body(q_ref, owner_ref, local_ref, columns, x_ref):
    features = q_ref.shape[1]
    x_ref[:features, :] = q_ref[...].T
    x_ref[features:, :] = (owner_ref[...] * columns + local_ref[...]).astype(f32)


def flip_body(d_ref, dt_ref):
    dt_ref[...] = d_ref[...].T


def score_body(places, after, me_ref, d_ref, pool_ref, *refs):
    part_ref, rows_ref = refs[-2:]
    rows, features = d_ref.shape
    columns = pool_ref.shape[1]
    tile = 128
    blocks = [refs[a][...] if k is None else refs[a][k] for a, k in places]
    for k, block in enumerate(blocks):
        x = block[:features]
        named = block[features:].astype(jnp.int32) - me_ref[0] * columns
        here = (named >= 0) & (named < columns)
        local = jnp.sum(jnp.where(here, named, 0), axis=0, keepdims=True)
        owned = jnp.any(here, axis=0, keepdims=True)
        lane = jnp.broadcast_to(local % tile, (features, rows))
        found = jnp.zeros((features, rows), f32)
        for t in range(columns // tile):
            picked = jnp.take_along_axis(
                pool_ref[:, t * tile : (t + 1) * tile], lane, axis=1, mode="promise_in_bounds"
            )
            found = jnp.where(local // tile == t, picked, found)
        rows_ref[k] = found
        hard = jnp.sum(x * found, axis=0, keepdims=True)
        chosen = jnp.where(owned, local, -1).astype(f32)
        part_ref[k, rows:] = jnp.concatenate(
            [hard, chosen, jnp.zeros((SLACK - 2, rows), f32)], axis=0
        )
    x = [block[:features] for block in blocks]
    x = x[0] if len(x) == 1 else jnp.concatenate(x, axis=1)
    scores = dot(d_ref[...], x, precision=lax.Precision.HIGHEST)
    for k in range(len(blocks)):
        part_ref[k, :rows] = scores[:, k * rows : (k + 1) * rows]


def softmax_body(evens, others, dt_ref, rows_ref, part_ref, *refs):
    got, (e_ref, *sum_refs) = refs[:others], refs[others:]
    features, rows = dt_ref.shape
    count = part_ref.shape[0]
    own = lax.broadcasted_iota(jnp.int32, (rows, rows), 0) == lax.broadcasted_iota(
        jnp.int32, (rows, rows), 1
    )
    tails, es = [], []
    for k in range(count):
        whole = part_ref[k]
        chosen = whole[rows + 1 : rows + 2]
        for r in got:
            whole = whole + r[k]
        scores = whole[:rows] / logit_divisor
        hard = jnp.where(chosen >= 0, whole[rows : rows + 1] / logit_divisor, LOWEST)
        peak = jnp.maximum(jnp.max(scores, axis=0, keepdims=True), hard)
        e = jnp.exp(scores - peak)
        hard_e = jnp.where(chosen >= 0, jnp.exp(hard - peak), 0.0)
        total = jnp.sum(e, axis=0, keepdims=True) + hard_e
        positive = jnp.sum(jnp.where(own, scores, 0.0), axis=0, keepdims=True)
        e_ref[k, :rows] = e
        e_ref[k, rows:] = jnp.concatenate(
            [hard_e, chosen, peak, total, positive, jnp.zeros((SLACK - 5, rows), f32)], axis=0
        )
        es.append(e)
        tails.append((hard_e, peak, total))
    e = es[0] if count == 1 else jnp.concatenate(es, axis=1)
    sums = dot(dt_ref[...], e, precision=lax.Precision.HIGHEST)
    for k, (hard_e, peak, total) in enumerate(tails):
        at = sum_refs[0].at[k] if k < evens else sum_refs[-1].at[k - evens]
        at[:features] = sums[:, k * rows : (k + 1) * rows] + rows_ref[k] * hard_e
        at[features:] = jnp.concatenate([peak, total, jnp.zeros((SLACK - 2, rows), f32)], axis=0)


def merge(terms):
    size = terms[0].shape[0] - SLACK
    peaks = [t[size : size + 1] for t in terms]
    peak = functools.reduce(jnp.maximum, peaks)
    scales = [jnp.exp(p - peak) for p in peaks]
    sums = functools.reduce(jnp.add, [t[:size] * s for t, s in zip(terms, scales)])
    total = functools.reduce(
        jnp.add, [t[size + 1 : size + 2] * s for t, s in zip(terms, scales)]
    )
    return sums, peak, total


def merge_body(places, *refs):
    out_ref = refs[-1]
    sums, peak, total = merge([refs[i][...] if k is None else refs[i][k] for i, k in places])
    size = sums.shape[0]
    out_ref[:size] = sums
    out_ref[size:] = jnp.concatenate(
        [peak, total, jnp.zeros((SLACK - 2, peak.shape[1]), f32)], axis=0
    )


def last_body(places, d_ref, e_ref, *refs):
    dq_ref, loss_ref = refs[-2:]
    sums, peak, total = merge([refs[i][...] if k is None else refs[i][k] for i, k in places])
    dq_ref[...] = ((sums / total).T - d_ref[...]) / logit_divisor
    log_total = peak + jnp.log(total)
    loss_ref[...] = jnp.broadcast_to(log_total - e_ref[0, 4:5], loss_ref.shape)


def stats_body(places, *refs):
    out_ref = refs[-1]
    for r, (i, k) in enumerate(places):
        out_ref[0, r : r + 1] = refs[i][k, 2:3]
        out_ref[1, r : r + 1] = refs[i][k, 3:4]


def stats_merge_body(masks, own_ref, *refs):
    out_ref = refs[-1]
    n = own_ref.shape[1]
    peaks, totals = [own_ref[0]], [own_ref[1]]
    for ref, mask in zip(refs, masks):
        for values, into in ((ref[0], peaks), (ref[1], totals)):
            into.append(
                jnp.concatenate([values[r ^ mask : (r ^ mask) + 1] for r in range(n)], axis=0)
            )
    peak = functools.reduce(jnp.maximum, peaks)
    out_ref[0] = peak
    out_ref[1] = functools.reduce(
        jnp.add, [t * jnp.exp(p - peak) for p, t in zip(peaks, totals)]
    )


def gradient_body(x_places, e_places, group, q_ref, tot_ref, *refs):
    n = len(x_places)
    dd_ref, pool_ref, scaled_ref, local_ref = refs[-4:]
    rows, features = q_ref.shape
    lanes = local_ref.shape[-1]

    @pl.when(pl.program_id(0) == 0)
    def _():
        total = jnp.zeros((rows, features), f32)
        for g in range(n // group):
            xs, es, hards = [], [], []
            for r in range(g * group, (g + 1) * group):
                i, k = x_places[r]
                xs.append(refs[i][:features] if k is None else refs[i][k, :features])
                i, k = e_places[r]
                scale = jnp.exp(refs[i][k, rows + 2 : rows + 3] - tot_ref[0, r : r + 1])
                scale = scale / tot_ref[1, r : r + 1]
                es.append(refs[i][k, :rows] * scale)
                hards.append(refs[i][k, rows : rows + 1] * scale)
                chosen = jnp.broadcast_to(refs[i][k, rows + 1 : rows + 2], (lanes, rows))
                first = (r - g * group) * rows
                local_ref[g, first : first + rows] = chosen.T.astype(jnp.int32)
            x = jnp.concatenate(xs, axis=1)
            chance = jnp.concatenate(es, axis=1)
            total = total + dot(chance, x, ((1,), (1,)), precision=lax.Precision.HIGHEST)
            high, low = split2(x * (jnp.concatenate(hards, axis=1) / logit_divisor))
            scaled_ref[g, :features] = high
            scaled_ref[g, features:] = low
        dd_ref[...] = (total - q_ref[...]) / logit_divisor

    width = pool_ref.shape[1]
    first = pl.program_id(0) * width
    acc = jnp.zeros((2 * features, width), f32)
    for g in range(n // group):
        local = local_ref[g]
        column = first + lax.broadcasted_iota(jnp.int32, local.shape, 1)
        marks = jnp.concatenate(
            [
                jnp.where(local == column + t * lanes, 1.0, 0.0).astype(bf16)
                for t in range(width // lanes)
            ],
            axis=1,
        )
        acc = acc + dot(scaled_ref[g], marks)
    pool_ref[...] = acc[:features] + acc[features:]


def per_device(question_matrix, document_matrix, pool, hard_owner, hard_local):
    n, depth = lax.axis_size("blk"), lax.axis_size("dim")
    rows, features = question_matrix.shape
    columns = pool.shape[1]
    me = lax.axis_index("blk")
    smem = pl.BlockSpec(memory_space=pltpu.SMEM)
    vmem = pl.BlockSpec(memory_space=pltpu.VMEM)
    unread = pl.BlockSpec(memory_space=pl.ANY)

    def full(*dims):
        return pl.BlockSpec(dims, lambda i: (0,) * len(dims))

    def send(x, mask):
        return lax.ppermute(x, "blk", [(i, i ^ mask) for i in range(n)])

    packed = call(
        lambda q, o, l, x: pack_body(q, o, l, columns, x), shape(features + SLACK, rows), "pack"
    )(question_matrix, hard_owner.T, hard_local.T)
    far = n // 4
    x = {0: packed}
    for k in [1, 2] + list(range(3, far)):
        x[4 * k] = send(x[4 * k - 4], 4) if k % 2 and k > 1 else send(packed, 4 * k)
    for k in [0] + list(range(2, far)) + [1]:
        x[4 * k + 2] = send(x[4 * k], 2)
    waves = [[0], [2, 4]] + [[4 * k, 4 * k + 2] for k in range(2, far)] + [[6]]
    x_arrays, x_place = [], {}
    for wave in waves:
        evens = [x[r] for r in wave]
        shared = send(jnp.stack(evens) if len(wave) > 1 else evens[0], 1)
        for k, r in enumerate(wave):
            x_place[r] = (len(x_arrays) + k, None)
            x_place[r + 1] = (len(x_arrays) + len(wave), k if len(wave) > 1 else None)
        x_arrays += evens + [shared]

    dt = call(flip_body, shape(features, rows), "flip")(document_matrix)

    batches = [
        (waves[b] if b < len(waves) else [], [r + 1 for r in waves[b - 1]] if b else [])
        for b in range(len(waves) + 1)
    ]
    weights, sums, e_place, sum_place = [], [], {}, {}
    waiting = []

    def finish_batch():
        b, part, found, got = waiting.pop(0)
        evens, odds = batches[b]
        k = len(evens) + len(odds)
        e, *out = call(
            functools.partial(softmax_body, len(evens), len(got)),
            [shape(k, rows + SLACK, rows)]
            + [shape(len(half), features + SLACK, rows) for half in batches[b] if half],
            "softmax",
            flops=12 * features * rows * rows * k,
        )(dt, found, part, *got)
        for i, r in enumerate(evens + odds):
            e_place[r] = (len(weights), i)
        weights.append(e)
        if evens:
            for i, r in enumerate(evens):
                sum_place[r] = (len(sums), i)
            sums.append(out[0])
        if odds:
            for i, r in enumerate(odds):
                sum_place[r] = (len(sums), i)
            sums.append(send(out[-1], 1))

    for b, (evens, odds) in enumerate(batches):
        blocks = evens + odds
        k = len(blocks)
        used = sorted({x_place[r][0] for r in blocks})
        after = weights[-1:]
        part, found = call(
            functools.partial(
                score_body, [(used.index(x_place[r][0]), x_place[r][1]) for r in blocks], len(after)
            ),
            (shape(k, rows + SLACK, rows), shape(k, features, rows)),
            "score",
            flops=12 * features * rows * rows * k,
            data=features * columns * 4 * k,
            in_specs=[smem] + [vmem] * (2 + len(used)) + [unread] * len(after),
        )(me.reshape(1), document_matrix, pool, *[x_arrays[i] for i in used], *after)
        got = [
            lax.ppermute(part, "dim", [(i, (i + s) % depth) for i in range(depth)])
            for s in range(1, depth)
        ]
        waiting.append((b, part, found, got))
        if len(waiting) > 1:
            finish_batch()
    while waiting:
        finish_batch()

    def terms(blocks, extra):
        used = sorted({sum_place[r][0] for r in blocks})
        places = [(used.index(sum_place[r][0]), sum_place[r][1]) for r in blocks]
        places += [(len(used) + i, None) for i in range(len(extra))]
        return places, [sums[i] for i in used] + extra

    def add(blocks, extra=()):
        places, arrays = terms(blocks, list(extra))
        return call(
            functools.partial(merge_body, places), shape(features + SLACK, rows), "merge"
        )(*arrays)

    home = []
    for k in [0] + list(range(2, far)) + [1]:
        beside = send(add([4 * k + 2, 4 * k + 3]), 2)
        if k:
            home.append(send(add([4 * k, 4 * k + 1], [beside]), 4 * k))
        else:
            home.append(beside)

    totals = call(
        functools.partial(stats_body, [e_place[r] for r in range(n)]),
        shape(2, n, rows),
        "stats",
        grid=(1,),
        in_specs=[
            pl.BlockSpec((e.shape[0], SLACK, rows), lambda i: (0, rows // SLACK, 0))
            for e in weights
        ],
        out_specs=full(2, n, rows),
    )(*weights)
    for masks in ([1], [2], [4 * k for k in range(1, far)]):
        totals = call(
            functools.partial(stats_merge_body, masks), shape(2, n, rows), "stats_merge"
        )(totals, *[send(totals, mask) for mask in masks])

    group = 4
    width = 512
    e_at = len(x_arrays)
    document_derivative, grad_pool = call(
        functools.partial(
            gradient_body,
            [x_place[r] for r in range(n)],
            [(e_at + e_place[r][0], e_place[r][1]) for r in range(n)],
            group,
        ),
        (shape(rows, features), shape(features, columns)),
        "gradient",
        flops=2 * features * rows * n * (2 * columns + 6 * rows),
        data=features * columns * 8,
        grid=(columns // width,),
        in_specs=[vmem] * (2 + len(x_arrays) + len(weights)),
        out_specs=(full(rows, features), pl.BlockSpec((features, width), lambda i: (0, i))),
        scratch_shapes=[
            pltpu.VMEM((n // group, 2 * features, group * rows), bf16),
            pltpu.VMEM((n // group, group * rows, 128), jnp.int32),
        ],
    )(question_matrix, totals, *x_arrays, *weights)

    places, arrays = terms([0, 1], home)
    question_derivative, loss = call(
        functools.partial(last_body, places),
        (shape(rows, features), shape(SLACK, rows)),
        "finish",
        grid=(1,),
        in_specs=[full(rows, features)]
        + [pl.BlockSpec((1, SLACK, rows), lambda i: (0, rows // SLACK, 0))]
        + [full(*a.shape) for a in arrays],
        out_specs=(full(rows, features), full(SLACK, rows)),
    )(document_matrix, weights[0], *arrays)
    return loss[0], question_derivative, document_derivative, grad_pool


def solution(mesh):
    placed = (P("blk", "dim"), P("blk", "dim"), P("dim", "blk"), P("blk", None), P("blk", None))
    return jax.shard_map(
        per_device,
        mesh=mesh,
        in_specs=placed,
        out_specs=(P("blk"), P("blk", "dim"), P("blk", "dim"), P("dim", "blk")),
        check_vma=False,
    )
```

time: 285 us -> 121 us (0.42)
  waiting for transfers between devices: 139 us -> 42.4 us
  other arithmetic: 38.5 us -> 0.13 us
  Pallas kernels: 0 us -> 31.5 us
  local copies, waits for them, and re-layouts: 33.2 us -> 5.64 us
  matrix products: 21.7 us -> 0 us
  between operations: 13.9 us -> 0.98 us
  starting transfers between devices: 27.7 us -> 38.9 us
  blocking collectives: 9.57 us -> 0 us
    reduce_scatter x1 -> x0, waiting for transfers between devices: 80.3 us -> none  [per_device(): lax.psum_scatter(lax.dot_general(columns, question_matrix, (((0,), (0,)),...]
    ppermute x0 -> x35, waiting for transfers between devices: none -> 42.4 us  [the longest x29 31.3 us: send(): return lax.ppermute(x, 'blk', [(i, i ^ mask) for i in range(n)])]
    ppermute x0 -> x35, starting transfers between devices: none -> 38.9 us  [the longest x29 31.4 us: send(): return lax.ppermute(x, 'blk', [(i, i ^ mask) for i in range(n)])]
    all_to_all x3 -> x0, waiting for transfers between devices: 31.5 us -> none  [the longest x1 27.5 us: per_device(): lax.all_to_all(found, 'blk', split_axis=0, concat_axis=0, tiled=True)]
    pallas_call x0 -> x27, Pallas kernels: none -> 31.5 us  [the longest x6 14.7 us: per_device(): call(functools.partial(score_body, [(used.index(x_place[r][0]), x_place[r...]
    all_to_all x3 -> x0, starting transfers between devices: 27.6 us -> none  [the longest x1 16.4 us: per_device(): lax.all_to_all(outgoing, 'blk', split_axis=0, concat_axis=0, tiled=True)]
    all_gather x1 -> x0, waiting for transfers between devices: 26.9 us -> none  [per_device(): lax.all_gather(document_matrix, 'blk', axis=0, tiled=True)]
    dot_general x5 -> x0, matrix products: 21.7 us -> none  [the longest x1 6.18 us: per_device(): lax.dot_general(question_matrix, lax.all_gather(document_matrix, 'blk', a...]
  transfers between devices with their start and end apart: 6 -> 35, of which waited for: 4 -> 15; matrix products, arithmetic and copies ran while one was open for 23% -> 0% of each run, Pallas kernels for 0% -> 26%
where the time goes in v2:
time: 121 us; the launch traced here: 119 us
  waiting for transfers between devices  42.4 us (35%)
  starting transfers between devices  38.9 us (32%)
  Pallas kernels  31.5 us (26%)
  local copies, waits for them, and re-layouts  5.64 us (5%)
    ppermute x29, starting transfers between devices, send(): return lax.ppermute(x, 'blk', [(i, i ^ mask) for i in range(n)])  31.4 us
    ppermute x29, waiting for transfers between devices, send(): return lax.ppermute(x, 'blk', [(i, i ^ mask) for i in range(n)])  31.3 us
    pallas_call x6, Pallas kernels, per_device(): call(functools.partial(score_body, [(used.index(x_place[r][0]), x_place[r...  14.7 us
    pallas_call x1, Pallas kernels, per_device(): call(functools.partial(gradient_body, [x_place[r] for r in range(n)], [(e...  11.2 us
    ppermute x6, waiting for transfers between devices, per_device(): lax.ppermute(part, 'dim', [(i, (i + s) % depth) for i in range(depth)])  11.1 us
    ppermute x6, starting transfers between devices, per_device(): lax.ppermute(part, 'dim', [(i, (i + s) % depth) for i in range(depth)])  7.47 us
    unnamed x16, local copies, waits for them, and re-layouts  5.12 us
    pallas_call x6, Pallas kernels, finish_batch(): call(functools.partial(softmax_body, len(evens), len(got)), [shape(k, row...  4.06 us
  transfers between devices with their start and end apart: 35, of which 15 were waited for; matrix products, arithmetic and copies ran while one was open for 0% of the time, Pallas kernels for 26%

profile of v2, /device:TPU:0, one launch (start us, length us, event | category | flops | bytes accessed | tf_op | source)
XLA Modules:
  0.0 119.5 jit_solution(16831637114917620541)
XLA Ops:
  3.1 4.1 %collective-permute-start.7 = (f32[392,128]{1,0:T(8,128)S(1)}, f32[392,128]{1,0:T(8,128)S(1)}, u32[]{:S(2)}, u32[]{:S(2)}) collective-permute-start(f32[392,128]{1,0:T(8,128)S(1)} %pack.1.refs_0_), channel_id=1, source_target_pairs={{0,16},{2,18},{4,20},{6,22},{8,24},{10,26},{12,28},{14,30},{16,0},... | collective-permute-start | bytes 602120 | tf_op jit(solution)/shard_map/ppermute | solution.py:233
  10.2 6.3 %collective-permute-done.7.refs_1_.refs_5_ = f32[392,128]{1,0:T(8,128)S(1)} collective-permute-done((f32[392,128]{1,0:T(8,128)S(1)}, f32[392,128]{1,0:T(8,128)S(1)}, u32[]{:S(2)}, u32[]{:S(2)}) %collective-permute-start.7) | collective-permute-done | bytes 200736 | tf_op jit(solution)/shard_map/ppermute | solution.py:233
  18.8 3.9 %collective-permute-done.13.refs_1_.refs_8_ = f32[392,128]{1,0:T(8,128)S(1)} collective-permute-done((f32[392,128]{1,0:T(8,128)S(1)}, f32[392,128]{1,0:T(8,128)S(1)}, u32[]{:S(2)}, u32[]{:S(2)}) %collective-permute-start.13) | collective-permute-done | bytes 200736 | tf_op jit(solution)/shard_map/ppermute | solution.py:233
  23.9 1.9 %copy-done = f32[384,2048]{1,0:T(8,128)S(1)} copy-done((f32[384,2048]{1,0:T(8,128)S(1)}, f32[384,2048]{1,0:T(8,128)}, u32[]{:S(2)}) %copy-start) | copy-done | bytes 3145752
  27.7 1.6 %collective-permute-start = (f32[1,136,128]{2,1,0:T(8,128)S(1)}, f32[1,136,128]{2,1,0:T(8,128)S(1)}, u32[]{:S(2)}, u32[]{:S(2)}) collective-permute-start(f32[1,136,128]{2,1,0:T(8,128)S(1)} %get-tuple-element.37.part_ref), channel_id=1, source_target_pairs={{0,1},{1,0},{2,3},{3,2},{4,5},{5,4},{6,7},{7,6},{8,9},{9,8},{10,11... | collective-permute-start | bytes 208904 | tf_op jit(solution)/shard_map/ppermute | solution.py:302
  30.2 2.2 %collective-permute-done.refs_0_ = f32[1,136,128]{2,1,0:T(8,128)S(1)} collective-permute-done((f32[1,136,128]{2,1,0:T(8,128)S(1)}, f32[1,136,128]{2,1,0:T(8,128)S(1)}, u32[]{:S(2)}, u32[]{:S(2)}) %collective-permute-start) | collective-permute-done | bytes 69664 | tf_op jit(solution)/shard_map/ppermute | solution.py:302
  32.8 2.7 %score.7 = (f32[3,136,128]{2,1,0:T(8,128)S(1)}, f32[3,384,128]{2,1,0:T(8,128)S(1)}) custom-call(s32[1]{0:T(128)} %bitcast.me_ref, f32[128,384]{1,0:T(8,128)S(1)} %copy-done.3, f32[384,2048]{1,0:T(8,128)S(1)} %copy-done.1, f32[392,128]{1,0:T(8,128)S(1)} %collective-permute-done.1.refs_0_.refs_1_, f32[392,128]{1,0:T(8,128)S(1)} %collective-permute-done.2.refs_1_.refs_2_, ...), custom_call_target="tpu_custom_call" | custom-call | flops 226492416 | bytes 9437184 | tf_op jit(solution)/shard_map/score/pallas_call | solution.py:291
  37.1 3.7 %score.8 = (f32[4,136,128]{2,1,0:T(8,128)S(1)}, f32[4,384,128]{2,1,0:T(8,128)S(1)}) custom-call(s32[1]{0:T(128)} %bitcast.me_ref, f32[128,384]{1,0:T(8,128)S(1)} %copy-done.3, f32[384,2048]{1,0:T(8,128)S(1)} %copy-done.1, f32[2,392,128]{2,1,0:T(8,128)S(1)} %collective-permute-done.6.refs_0_.refs_4_, f32[392,128]{1,0:T(8,128)S(1)} %collective-permute-done.7.refs_1_.refs_5_, ...), custom_call_target="tpu_custom_call" | custom-call | flops 301989888 | bytes 12582912 | tf_op jit(solution)/shard_map/score/pallas_call | solution.py:291
  43.1 3.6 %score.9 = (f32[4,136,128]{2,1,0:T(8,128)S(1)}, f32[4,384,128]{2,1,0:T(8,128)S(1)}) custom-call(s32[1]{0:T(128)} %bitcast.me_ref, f32[128,384]{1,0:T(8,128)S(1)} %copy-done.3, f32[384,2048]{1,0:T(8,128)S(1)} %copy-done.1, f32[2,392,128]{2,1,0:T(8,128)S(1)} %collective-permute-done.12.refs_0_.refs_7_, f32[392,128]{1,0:T(8,128)S(1)} %collective-permute-done.13.refs_1_.refs_8_, ...), custom_call_target="tpu_custom_call" | custom-call | flops 301989888 | bytes 12582912 | tf_op jit(solution)/shard_map/score/pallas_call | solution.py:291
  46.7 2.0 %collective-permute-start.15 = (f32[4,136,128]{2,1,0:T(8,128)S(1)}, f32[4,136,128]{2,1,0:T(8,128)S(1)}, u32[]{:S(2)}, u32[]{:S(2)}) collective-permute-start(f32[4,136,128]{2,1,0:T(8,128)S(1)} %get-tuple-element.50.part_ref), channel_id=1, source_target_pairs={{0,1},{1,0},{2,3},{3,2},{4,5},{5,4},{6,7},{7,6},{8,9},{9,8},{10,11... | collective-permute-start | bytes 835592 | tf_op jit(solution)/shard_map/ppermute | solution.py:302
  50.5 2.7 %score.10 = (f32[3,136,128]{2,1,0:T(8,128)S(1)}, f32[3,384,128]{2,1,0:T(8,128)S(1)}) custom-call(s32[1]{0:T(128)} %bitcast.me_ref, f32[128,384]{1,0:T(8,128)S(1)} %copy-done.3, f32[384,2048]{1,0:T(8,128)S(1)} %copy-done.1, f32[2,392,128]{2,1,0:T(8,128)S(1)} %collective-permute-done.19.refs_0_.refs_10_, ...), custom_call_target="tpu_custom_call" | custom-call | flops 226492416 | bytes 9437184 | tf_op jit(solution)/shard_map/score/pallas_call | solution.py:291
  53.8 1.8 %collective-permute-done.15.refs_0_ = f32[4,136,128]{2,1,0:T(8,128)S(1)} collective-permute-done((f32[4,136,128]{2,1,0:T(8,128)S(1)}, f32[4,136,128]{2,1,0:T(8,128)S(1)}, u32[]{:S(2)}, u32[]{:S(2)}) %collective-permute-start.15) | collective-permute-done | bytes 278560 | tf_op jit(solution)/shard_map/ppermute | solution.py:302
  56.7 2.6 %collective-permute-done.21.refs_0_ = f32[3,136,128]{2,1,0:T(8,128)S(1)} collective-permute-done((f32[3,136,128]{2,1,0:T(8,128)S(1)}, f32[3,136,128]{2,1,0:T(8,128)S(1)}, u32[]{:S(2)}, u32[]{:S(2)}) %collective-permute-start.21) | collective-permute-done | bytes 208928 | tf_op jit(solution)/shard_map/ppermute | solution.py:302
  62.2 3.5 %collective-permute-done.26.refs_0_ = f32[1,136,128]{2,1,0:T(8,128)S(1)} collective-permute-done((f32[1,136,128]{2,1,0:T(8,128)S(1)}, f32[1,136,128]{2,1,0:T(8,128)S(1)}, u32[]{:S(2)}, u32[]{:S(2)}) %collective-permute-start.26) | collective-permute-done | bytes 69664 | tf_op jit(solution)/shard_map/ppermute | solution.py:302
  73.3 10.3 %collective-permute-done.31.refs_0_ = f32[2,16,128]{2,1,0:T(8,128)S(1)} collective-permute-done((f32[2,16,128]{2,1,0:T(8,128)S(1)}, f32[2,16,128]{2,1,0:T(8,128)S(1)}, u32[]{:S(2)}, u32[]{:S(2)}) %collective-permute-start.31) | collective-permute-done | bytes 16416 | tf_op jit(solution)/shard_map/ppermute | solution.py:233
  83.7 1.7 %collective-permute-start.32 = (f32[2,16,128]{2,1,0:T(8,128)S(1)}, f32[2,16,128]{2,1,0:T(8,128)S(1)}, u32[]{:S(2)}, u32[]{:S(2)}) collective-permute-start(f32[2,16,128]{2,1,0:T(8,128)S(1)} %stats_merge.4.own_ref), channel_id=1, source_target_pairs={{0,8},{2,10},{4,12},{6,14},{8,0},{10,2},{12,4},{14,6},{16,24},{18,... | collective-permute-start | bytes 49160 | tf_op jit(solution)/shard_map/ppermute | solution.py:233
  85.4 2.1 %collective-permute-done.32.refs_0_ = f32[2,16,128]{2,1,0:T(8,128)S(1)} collective-permute-done((f32[2,16,128]{2,1,0:T(8,128)S(1)}, f32[2,16,128]{2,1,0:T(8,128)S(1)}, u32[]{:S(2)}, u32[]{:S(2)}) %collective-permute-start.32) | collective-permute-done | bytes 16416 | tf_op jit(solution)/shard_map/ppermute | solution.py:233
  87.5 3.3 %collective-permute-start.33 = (f32[2,16,128]{2,1,0:T(8,128)S(1)}, f32[2,16,128]{2,1,0:T(8,128)S(1)}, u32[]{:S(2)}, u32[]{:S(2)}) collective-permute-start(f32[2,16,128]{2,1,0:T(8,128)S(1)} %stats_merge.4.own_ref), channel_id=1, source_target_pairs={{0,16},{2,18},{4,20},{6,22},{8,24},{10,26},{12,28},{14,30},{16,0},... | collective-permute-start | bytes 49160 | tf_op jit(solution)/shard_map/ppermute | solution.py:233
  90.8 1.7 %collective-permute-done.33.refs_1_ = f32[2,16,128]{2,1,0:T(8,128)S(1)} collective-permute-done((f32[2,16,128]{2,1,0:T(8,128)S(1)}, f32[2,16,128]{2,1,0:T(8,128)S(1)}, u32[]{:S(2)}, u32[]{:S(2)}) %collective-permute-start.33) | collective-permute-done | bytes 16416 | tf_op jit(solution)/shard_map/ppermute | solution.py:233
  92.5 4.1 %collective-permute-start.34 = (f32[2,16,128]{2,1,0:T(8,128)S(1)}, f32[2,16,128]{2,1,0:T(8,128)S(1)}, u32[]{:S(2)}, u32[]{:S(2)}) collective-permute-start(f32[2,16,128]{2,1,0:T(8,128)S(1)} %stats_merge.4.own_ref), channel_id=1, source_target_pairs={{0,24},{2,26},{4,28},{6,30},{8,16},{10,18},{12,20},{14,22},{16,8},... | collective-permute-start | bytes 49160 | tf_op jit(solution)/shard_map/ppermute | solution.py:233
  96.6 1.7 %collective-permute-done.34.refs_2_ = f32[2,16,128]{2,1,0:T(8,128)S(1)} collective-permute-done((f32[2,16,128]{2,1,0:T(8,128)S(1)}, f32[2,16,128]{2,1,0:T(8,128)S(1)}, u32[]{:S(2)}, u32[]{:S(2)}) %collective-permute-start.34) | collective-permute-done | bytes 16416 | tf_op jit(solution)/shard_map/ppermute | solution.py:233
  99.2 4.4 %collective-permute-start.18 = (f32[392,128]{1,0:T(8,128)S(1)}, f32[392,128]{1,0:T(8,128)S(1)}, u32[]{:S(2)}, u32[]{:S(2)}) collective-permute-start(f32[392,128]{1,0:T(8,128)S(1)} %merge.9), channel_id=1, source_target_pairs={{0,16},{2,18},{4,20},{6,22},{8,24},{10,26},{12,28},{14,30},{16,0},... | collective-permute-start | bytes 602120 | tf_op jit(solution)/shard_map/ppermute | solution.py:233
  103.8 11.2 %gradient.1 = (f32[128,384]{1,0:T(8,128)}, f32[384,2048]{1,0:T(8,128)}) custom-call(f32[128,384]{1,0:T(8,128)S(1)} %copy-done.5, f32[2,16,128]{2,1,0:T(8,128)S(1)} %stats_merge.5.tot_ref, f32[392,128]{1,0:T(8,128)S(1)} %pack.1.refs_0_, f32[392,128]{1,0:T(8,128)S(1)} %collective-permute-done.1.refs_0_.refs_1_, ...), custom_call_target="tpu_custom_call" | custom-call | flops 7650410496 | bytes 6291456 | tf_op jit(solution)/shard_map/gradient/pallas_call | solution.py:350
  115.0 3.1 %collective-permute-done.18.refs_3_ = f32[392,128]{1,0:T(8,128)S(1)} collective-permute-done((f32[392,128]{1,0:T(8,128)S(1)}, f32[392,128]{1,0:T(8,128)S(1)}, u32[]{:S(2)}, u32[]{:S(2)}) %collective-permute-start.18) | collective-permute-done | bytes 200736 | tf_op jit(solution)/shard_map/ppermute | solution.py:233
  (93 shorter events, 32.0 us)
Async XLA Ops:
  3.1 13.5 %collective-permute-start.7 = (f32[392,128]{1,0:T(8,128)S(1)}, f32[392,128]{1,0:T(8,128)S(1)}, u32[]{:S(2)}, u32[]{:S(2)}) collective-permute-start(f32[392,128]{1,0:T(8,128)S(1)} %pack.1.refs_0_), channel_id=1, source_target_pairs={{0,16},{2,18},{4,20},{6,22},{8,24},{10,26},{12,28},{14,30},{16,0},... | collective-permute-start | bytes 602120 | tf_op jit(solution)/shard_map/ppermute | solution.py:233
  7.2 11.5 %collective-permute-start.2 = (f32[392,128]{1,0:T(8,128)S(1)}, f32[392,128]{1,0:T(8,128)S(1)}, u32[]{:S(2)}, u32[]{:S(2)}) collective-permute-start(f32[392,128]{1,0:T(8,128)S(1)} %pack.1.refs_0_), channel_id=1, source_target_pairs={{0,4},{2,6},{4,0},{6,2},{8,12},{10,14},{12,8},{14,10},{16,20},{18,... | collective-permute-start | bytes 602120 | tf_op jit(solution)/shard_map/ppermute | solution.py:233
  8.7 10.0 %collective-permute-start.3 = (f32[392,128]{1,0:T(8,128)S(1)}, f32[392,128]{1,0:T(8,128)S(1)}, u32[]{:S(2)}, u32[]{:S(2)}) collective-permute-start(f32[392,128]{1,0:T(8,128)S(1)} %pack.1.refs_0_), channel_id=1, source_target_pairs={{0,8},{2,10},{4,12},{6,14},{8,0},{10,2},{12,4},{14,6},{16,24},{18,... | collective-permute-start | bytes 602120 | tf_op jit(solution)/shard_map/ppermute | solution.py:233
  17.2 12.1 %collective-permute-start.8 = (f32[392,128]{1,0:T(8,128)S(1)}, f32[392,128]{1,0:T(8,128)S(1)}, u32[]{:S(2)}, u32[]{:S(2)}) collective-permute-start(f32[392,128]{1,0:T(8,128)S(1)} %collective-permute-done.7.refs_1_.refs_5_), channel_id=1, source_target_pairs={{0,4},{2,6},{4,0},{6,2},{8,12},{10,14},{12,8},{14,10},{16,20},{18,... | collective-permute-start | bytes 602120 | tf_op jit(solution)/shard_map/ppermute | solution.py:233
  18.7 18.4 %collective-permute-start.6 = (f32[2,392,128]{2,1,0:T(8,128)S(1)}, f32[2,392,128]{2,1,0:T(8,128)S(1)}, u32[]{:S(2)}, u32[]{:S(2)}) collective-permute-start(f32[2,392,128]{2,1,0:T(8,128)S(1)} %pad_maximum_fusion), channel_id=1, source_target_pairs={{0,2},{2,0},{4,6},{6,4},{8,10},{10,8},{12,14},{14,12},{16,18},{18,... | collective-permute-start | bytes 1204232 | tf_op jit(solution)/shard_map/ppermute | solution.py:233
  22.7 7.0 %collective-permute-start.14 = (f32[392,128]{1,0:T(8,128)S(1)}, f32[392,128]{1,0:T(8,128)S(1)}, u32[]{:S(2)}, u32[]{:S(2)}) collective-permute-start(f32[392,128]{1,0:T(8,128)S(1)} %collective-permute-done.13.refs_1_.refs_8_), channel_id=1, source_target_pairs={{0,4},{2,6},{4,0},{6,2},{8,12},{10,14},{12,8},{14,10},{16,20},{18,... | collective-permute-start | bytes 602120 | tf_op jit(solution)/shard_map/ppermute | solution.py:233
  23.9 8.8 %collective-permute-start.1 = (f32[392,128]{1,0:T(8,128)S(1)}, f32[392,128]{1,0:T(8,128)S(1)}, u32[]{:S(2)}, u32[]{:S(2)}) collective-permute-start(f32[392,128]{1,0:T(8,128)S(1)} %pack.1.refs_0_), channel_id=1, source_target_pairs={{0,2},{2,0},{4,6},{6,4},{8,10},{10,8},{12,14},{14,12},{16,18},{18,... | collective-permute-start | bytes 602120 | tf_op jit(solution)/shard_map/ppermute | solution.py:233
  29.4 13.7 %collective-permute-start.12 = (f32[2,392,128]{2,1,0:T(8,128)S(1)}, f32[2,392,128]{2,1,0:T(8,128)S(1)}, u32[]{:S(2)}, u32[]{:S(2)}) collective-permute-start(f32[2,392,128]{2,1,0:T(8,128)S(1)} %pad_maximum_fusion.1), channel_id=1, source_target_pairs={{0,2},{2,0},{4,6},{6,4},{8,10},{10,8},{12,14},{14,12},{16,18},{18,... | collective-permute-start | bytes 1204232 | tf_op jit(solution)/shard_map/ppermute | solution.py:233
  29.7 20.8 %collective-permute-start.19 = (f32[2,392,128]{2,1,0:T(8,128)S(1)}, f32[2,392,128]{2,1,0:T(8,128)S(1)}, u32[]{:S(2)}, u32[]{:S(2)}) collective-permute-start(f32[2,392,128]{2,1,0:T(8,128)S(1)} %pad_maximum_fusion.2), channel_id=1, source_target_pairs={{0,2},{2,0},{4,6},{6,4},{8,10},{10,8},{12,14},{14,12},{16,18},{18,... | collective-permute-start | bytes 1204232 | tf_op jit(solution)/shard_map/ppermute | solution.py:233
  40.8 8.6 %collective-permute-start.9 = (f32[4,136,128]{2,1,0:T(8,128)S(1)}, f32[4,136,128]{2,1,0:T(8,128)S(1)}, u32[]{:S(2)}, u32[]{:S(2)}) collective-permute-start(f32[4,136,128]{2,1,0:T(8,128)S(1)} %get-tuple-element.45.part_ref), channel_id=1, source_target_pairs={{0,1},{1,0},{2,3},{3,2},{4,5},{5,4},{6,7},{7,6},{8,9},{9,8},{10,11... | collective-permute-start | bytes 835592 | tf_op jit(solution)/shard_map/ppermute | solution.py:302
  41.3 9.1 %collective-permute-start.20 = (f32[392,128]{1,0:T(8,128)S(1)}, f32[392,128]{1,0:T(8,128)S(1)}, u32[]{:S(2)}, u32[]{:S(2)}) collective-permute-start(f32[392,128]{1,0:T(8,128)S(1)} %collective-permute-done.3.refs_2_.refs_3_), channel_id=1, source_target_pairs={{0,4},{2,6},{4,0},{6,2},{8,12},{10,14},{12,8},{14,10},{16,20},{18,... | collective-permute-start | bytes 602120 | tf_op jit(solution)/shard_map/ppermute | solution.py:233
  46.7 8.9 %collective-permute-start.15 = (f32[4,136,128]{2,1,0:T(8,128)S(1)}, f32[4,136,128]{2,1,0:T(8,128)S(1)}, u32[]{:S(2)}, u32[]{:S(2)}) collective-permute-start(f32[4,136,128]{2,1,0:T(8,128)S(1)} %get-tuple-element.50.part_ref), channel_id=1, source_target_pairs={{0,1},{1,0},{2,3},{3,2},{4,5},{5,4},{6,7},{7,6},{8,9},{9,8},{10,11... | collective-permute-start | bytes 835592 | tf_op jit(solution)/shard_map/ppermute | solution.py:302
  56.6 11.6 %collective-permute-start.16 = (f32[2,392,128]{2,1,0:T(8,128)S(1)}, f32[2,392,128]{2,1,0:T(8,128)S(1)}, u32[]{:S(2)}, u32[]{:S(2)}) collective-permute-start(f32[2,392,128]{2,1,0:T(8,128)S(1)} %get-tuple-element.51), channel_id=1, source_target_pairs={{0,2},{2,0},{4,6},{6,4},{8,10},{10,8},{12,14},{14,12},{16,18},{18,... | collective-permute-start | bytes 1204232 | tf_op jit(solution)/shard_map/ppermute | solution.py:233
  60.0 9.8 %collective-permute-start.22 = (f32[2,392,128]{2,1,0:T(8,128)S(1)}, f32[2,392,128]{2,1,0:T(8,128)S(1)}, u32[]{:S(2)}, u32[]{:S(2)}) collective-permute-start(f32[2,392,128]{2,1,0:T(8,128)S(1)} %get-tuple-element.56), channel_id=1, source_target_pairs={{0,2},{2,0},{4,6},{6,4},{8,10},{10,8},{12,14},{14,12},{16,18},{18,... | collective-permute-start | bytes 1204232 | tf_op jit(solution)/shard_map/ppermute | solution.py:233
  66.1 32.2 %collective-permute-start.10 = (f32[2,392,128]{2,1,0:T(8,128)S(1)}, f32[2,392,128]{2,1,0:T(8,128)S(1)}, u32[]{:S(2)}, u32[]{:S(2)}) collective-permute-start(f32[2,392,128]{2,1,0:T(8,128)S(1)} %get-tuple-element.46), channel_id=1, source_target_pairs={{0,2},{2,0},{4,6},{6,4},{8,10},{10,8},{12,14},{14,12},{16,18},{18,... | collective-permute-start | bytes 1204232 | tf_op jit(solution)/shard_map/ppermute | solution.py:233
  67.6 31.4 %collective-permute-start.28 = (f32[392,128]{1,0:T(8,128)S(1)}, f32[392,128]{1,0:T(8,128)S(1)}, u32[]{:S(2)}, u32[]{:S(2)}) collective-permute-start(f32[392,128]{1,0:T(8,128)S(1)} %merge.12), channel_id=1, source_target_pairs={{0,4},{2,6},{4,0},{6,2},{8,12},{10,14},{12,8},{14,10},{16,20},{18,... | collective-permute-start | bytes 602120 | tf_op jit(solution)/shard_map/ppermute | solution.py:233
  68.2 30.9 %collective-permute-start.17 = (f32[392,128]{1,0:T(8,128)S(1)}, f32[392,128]{1,0:T(8,128)S(1)}, u32[]{:S(2)}, u32[]{:S(2)}) collective-permute-start(f32[392,128]{1,0:T(8,128)S(1)} %merge.8), channel_id=1, source_target_pairs={{0,4},{2,6},{4,0},{6,2},{8,12},{10,14},{12,8},{14,10},{16,20},{18,... | collective-permute-start | bytes 602120 | tf_op jit(solution)/shard_map/ppermute | solution.py:233
  69.8 33.8 %collective-permute-start.23 = (f32[392,128]{1,0:T(8,128)S(1)}, f32[392,128]{1,0:T(8,128)S(1)}, u32[]{:S(2)}, u32[]{:S(2)}) collective-permute-start(f32[392,128]{1,0:T(8,128)S(1)} %merge.10), channel_id=1, source_target_pairs={{0,4},{2,6},{4,0},{6,2},{8,12},{10,14},{12,8},{14,10},{16,20},{18,... | collective-permute-start | bytes 602120 | tf_op jit(solution)/shard_map/ppermute | solution.py:233
  71.7 11.9 %collective-permute-start.31 = (f32[2,16,128]{2,1,0:T(8,128)S(1)}, f32[2,16,128]{2,1,0:T(8,128)S(1)}, u32[]{:S(2)}, u32[]{:S(2)}) collective-permute-start(f32[2,16,128]{2,1,0:T(8,128)S(1)} %stats_merge.3.own_ref), channel_id=1, source_target_pairs={{0,4},{2,6},{4,0},{6,2},{8,12},{10,14},{12,8},{14,10},{16,20},{18,... | collective-permute-start | bytes 49160 | tf_op jit(solution)/shard_map/ppermute | solution.py:233
  98.3 16.7 %collective-permute-start.5 = (f32[1,392,128]{2,1,0:T(8,128)S(1)}, f32[1,392,128]{2,1,0:T(8,128)S(1)}, u32[]{:S(2)}, u32[]{:S(2)}) collective-permute-start(f32[1,392,128]{2,1,0:T(8,128)S(1)} %get-tuple-element.42), channel_id=1, source_target_pairs={{0,2},{2,0},{4,6},{6,4},{8,10},{10,8},{12,14},{14,12},{16,18},{18,... | collective-permute-start | bytes 602120 | tf_op jit(solution)/shard_map/ppermute | solution.py:233
  98.4 16.6 %collective-permute-start.11 = (f32[392,128]{1,0:T(8,128)S(1)}, f32[392,128]{1,0:T(8,128)S(1)}, u32[]{:S(2)}, u32[]{:S(2)}) collective-permute-start(f32[392,128]{1,0:T(8,128)S(1)} %merge.7), channel_id=1, source_target_pairs={{0,4},{2,6},{4,0},{6,2},{8,12},{10,14},{12,8},{14,10},{16,20},{18,... | collective-permute-start | bytes 602120 | tf_op jit(solution)/shard_map/ppermute | solution.py:233
  99.1 15.9 %collective-permute-start.29 = (f32[392,128]{1,0:T(8,128)S(1)}, f32[392,128]{1,0:T(8,128)S(1)}, u32[]{:S(2)}, u32[]{:S(2)}) collective-permute-start(f32[392,128]{1,0:T(8,128)S(1)} %merge.13), channel_id=1, source_target_pairs={{0,8},{2,10},{4,12},{6,14},{8,0},{10,2},{12,4},{14,6},{16,24},{18,... | collective-permute-start | bytes 602120 | tf_op jit(solution)/shard_map/ppermute | solution.py:233
  99.2 18.9 %collective-permute-start.18 = (f32[392,128]{1,0:T(8,128)S(1)}, f32[392,128]{1,0:T(8,128)S(1)}, u32[]{:S(2)}, u32[]{:S(2)}) collective-permute-start(f32[392,128]{1,0:T(8,128)S(1)} %merge.9), channel_id=1, source_target_pairs={{0,16},{2,18},{4,20},{6,22},{8,24},{10,26},{12,28},{14,30},{16,0},... | collective-permute-start | bytes 602120 | tf_op jit(solution)/shard_map/ppermute | solution.py:233
  103.7 14.4 %collective-permute-start.24 = (f32[392,128]{1,0:T(8,128)S(1)}, f32[392,128]{1,0:T(8,128)S(1)}, u32[]{:S(2)}, u32[]{:S(2)}) collective-permute-start(f32[392,128]{1,0:T(8,128)S(1)} %merge.11), channel_id=1, source_target_pairs={{0,24},{2,26},{4,28},{6,30},{8,16},{10,18},{12,20},{14,22},{16,8},... | collective-permute-start | bytes 602120 | tf_op jit(solution)/shard_map/ppermute | solution.py:233
  (19 other events, 111.2 us)

commit v3 on v2

--- a/solution.py
+++ b/solution.py
@@ -26,32 +26,59 @@
     )
 
 
-def call(body, out_shape, name, flops=0, data=1 << 20, limit=48 << 20, **kw):
-    return pl.pallas_call(
-        body,
-        out_shape=out_shape,
-        name=name,
-        cost_estimate=pl.CostEstimate(flops=flops, bytes_accessed=data, transcendentals=0),
-        compiler_params=pltpu.CompilerParams(vmem_limit_bytes=limit),
-        **kw,
-    )
+class Line:
+    def __init__(self):
+        self.last = None
+
+    def __call__(self, body, out_shape, name, arrays, in_specs=None, limit=16, **kw):
+        count = len(arrays)
+        if in_specs is None:
+            in_specs = [pl.BlockSpec(memory_space=pltpu.VMEM)] * count
+        if self.last is not None:
+            in_specs = list(in_specs) + [pl.BlockSpec(memory_space=pl.ANY)]
+            arrays = list(arrays) + [self.last]
+
+        def kernel(*refs):
+            body(*refs[:count], *refs[len(arrays) :])
+
+        out = pl.pallas_call(
+            kernel,
+            out_shape=out_shape,
+            name=name,
+            in_specs=in_specs,
+            cost_estimate=pl.CostEstimate(flops=0, bytes_accessed=0, transcendentals=0),
+            compiler_params=pltpu.CompilerParams(vmem_limit_bytes=limit << 20),
+            **kw,
+        )(*arrays)
+        self.last = out[-1] if isinstance(out, (list, tuple)) else out
+        return out
 
 
 def shape(*dims, dtype=f32):
     return jax.ShapeDtypeStruct(dims, dtype)
 
 
-def pack_body(q_ref, owner_ref, local_ref, columns, x_ref):
+def pack_body(columns, q_hbm, owner_hbm, local_hbm, x_ref, q_ref, owner_ref, local_ref, sems):
+    pairs = ((q_hbm, q_ref), (owner_hbm, owner_ref), (local_hbm, local_ref))
+    copies = [pltpu.make_async_copy(a, b, sems.at[i]) for i, (a, b) in enumerate(pairs)]
+    for copy in copies:
+        copy.start()
+    for copy in copies:
+        copy.wait()
     features = q_ref.shape[1]
     x_ref[:features, :] = q_ref[...].T
     x_ref[features:, :] = (owner_ref[...] * columns + local_ref[...]).astype(f32)
 
 
+def relay_body(*refs):
+    refs[1][...] = refs[0][...]
+
+
 def flip_body(d_ref, dt_ref):
     dt_ref[...] = d_ref[...].T
 
 
-def score_body(places, after, me_ref, d_ref, pool_ref, *refs):
+def score_body(places, me_ref, d_ref, pool_ref, *refs):
     part_ref, rows_ref = refs[-2:]
     rows, features = d_ref.shape
     columns = pool_ref.shape[1]
@@ -83,7 +110,7 @@
         part_ref[k, :rows] = scores[:, k * rows : (k + 1) * rows]
 
 
-def softmax_body(evens, others, dt_ref, rows_ref, part_ref, *refs):
+def softmax_body(others, dt_ref, rows_ref, part_ref, *refs):
     got, (e_ref, *sum_refs) = refs[:others], refs[others:]
     features, rows = dt_ref.shape
     count = part_ref.shape[0]
@@ -112,7 +139,7 @@
     e = es[0] if count == 1 else jnp.concatenate(es, axis=1)
     sums = dot(dt_ref[...], e, precision=lax.Precision.HIGHEST)
     for k, (hard_e, peak, total) in enumerate(tails):
-        at = sum_refs[0].at[k] if k < evens else sum_refs[-1].at[k - evens]
+        at = sum_refs[k]
         at[:features] = sums[:, k * rows : (k + 1) * rows] + rows_ref[k] * hard_e
         at[features:] = jnp.concatenate([peak, total, jnp.zeros((SLACK - 2, rows), f32)], axis=0)
 
@@ -129,9 +156,9 @@
     return sums, peak, total
 
 
-def merge_body(places, *refs):
+def merge_body(*refs):
     out_ref = refs[-1]
-    sums, peak, total = merge([refs[i][...] if k is None else refs[i][k] for i, k in places])
+    sums, peak, total = merge([ref[...] for ref in refs[:-1]])
     size = sums.shape[0]
     out_ref[:size] = sums
     out_ref[size:] = jnp.concatenate(
@@ -139,12 +166,12 @@
     )
 
 
-def last_body(places, d_ref, e_ref, *refs):
+def last_body(d_ref, e_ref, *refs):
     dq_ref, loss_ref = refs[-2:]
-    sums, peak, total = merge([refs[i][...] if k is None else refs[i][k] for i, k in places])
+    sums, peak, total = merge([ref[...] for ref in refs[:-2]])
     dq_ref[...] = ((sums / total).T - d_ref[...]) / logit_divisor
     log_total = peak + jnp.log(total)
-    loss_ref[...] = jnp.broadcast_to(log_total - e_ref[0, 4:5], loss_ref.shape)
+    loss_ref[...] = (log_total - e_ref[0, 4:5]).reshape(loss_ref.shape)
 
 
 def stats_body(places, *refs):
@@ -170,8 +197,9 @@
     )
 
 
-def gradient_body(x_places, e_places, group, q_ref, tot_ref, *refs):
+def gradient_body(x_places, e_places, group, *refs):
     n = len(x_places)
+    q_ref, tot_ref = refs[:2]
     dd_ref, pool_ref, scaled_ref, local_ref = refs[-4:]
     rows, features = q_ref.shape
     lanes = local_ref.shape[-1]
@@ -224,7 +252,8 @@
     me = lax.axis_index("blk")
     smem = pl.BlockSpec(memory_space=pltpu.SMEM)
     vmem = pl.BlockSpec(memory_space=pltpu.VMEM)
-    unread = pl.BlockSpec(memory_space=pl.ANY)
+    block = shape(features + SLACK, rows)
+    line = Line()
 
     def full(*dims):
         return pl.BlockSpec(dims, lambda i: (0,) * len(dims))
@@ -232,153 +261,200 @@
     def send(x, mask):
         return lax.ppermute(x, "blk", [(i, i ^ mask) for i in range(n)])
 
-    packed = call(
-        lambda q, o, l, x: pack_body(q, o, l, columns, x), shape(features + SLACK, rows), "pack"
-    )(question_matrix, hard_owner.T, hard_local.T)
     far = n // 4
-    x = {0: packed}
-    for k in [1, 2] + list(range(3, far)):
-        x[4 * k] = send(x[4 * k - 4], 4) if k % 2 and k > 1 else send(packed, 4 * k)
-    for k in [0] + list(range(2, far)) + [1]:
-        x[4 * k + 2] = send(x[4 * k], 2)
-    waves = [[0], [2, 4]] + [[4 * k, 4 * k + 2] for k in range(2, far)] + [[6]]
-    x_arrays, x_place = [], {}
-    for wave in waves:
-        evens = [x[r] for r in wave]
-        shared = send(jnp.stack(evens) if len(wave) > 1 else evens[0], 1)
-        for k, r in enumerate(wave):
-            x_place[r] = (len(x_arrays) + k, None)
-            x_place[r + 1] = (len(x_arrays) + len(wave), k if len(wave) > 1 else None)
-        x_arrays += evens + [shared]
-
-    dt = call(flip_body, shape(features, rows), "flip")(document_matrix)
-
-    batches = [
-        (waves[b] if b < len(waves) else [], [r + 1 for r in waves[b - 1]] if b else [])
-        for b in range(len(waves) + 1)
-    ]
-    weights, sums, e_place, sum_place = [], [], {}, {}
-    waiting = []
-
-    def finish_batch():
-        b, part, found, got = waiting.pop(0)
-        evens, odds = batches[b]
-        k = len(evens) + len(odds)
-        e, *out = call(
-            functools.partial(softmax_body, len(evens), len(got)),
-            [shape(k, rows + SLACK, rows)]
-            + [shape(len(half), features + SLACK, rows) for half in batches[b] if half],
-            "softmax",
-            flops=12 * features * rows * rows * k,
-        )(dt, found, part, *got)
-        for i, r in enumerate(evens + odds):
-            e_place[r] = (len(weights), i)
-        weights.append(e)
-        if evens:
-            for i, r in enumerate(evens):
-                sum_place[r] = (len(sums), i)
-            sums.append(out[0])
-        if odds:
-            for i, r in enumerate(odds):
-                sum_place[r] = (len(sums), i)
-            sums.append(send(out[-1], 1))
-
-    for b, (evens, odds) in enumerate(batches):
-        blocks = evens + odds
+    waves = [[0], [2, 4, 8]] + [[4 * k + 2, 4 * k + 4] for k in range(2, far - 1)]
+    waves += [[4 * far - 2], [6]]
+
+    x, x_arrays, x_place = {}, [], {}
+
+    def keep(array, r):
+        x[r] = array
+        x_place[r] = (len(x_arrays), None)
+        x_arrays.append(array)
+
+    def relay(r):
+        return line(relay_body, block, "relay", [x[r]])
+
+    def forward(k):
+        held = relay(4 * k)
+        if k % 2 == 0 and 2 <= k < far - 1:
+            keep(send(held, 4), 4 * k + 4)
+        keep(send(held, 2), 4 * k + 2)
+
+    def share(wave):
+        for r in wave:
+            keep(send(x[r], 1), r + 1)
+
+    weights, sums, e_place = [], {}, {}
+    waiting, stage = [], {}
+
+    def score(blocks):
         k = len(blocks)
         used = sorted({x_place[r][0] for r in blocks})
-        after = weights[-1:]
-        part, found = call(
+        part, found = line(
             functools.partial(
-                score_body, [(used.index(x_place[r][0]), x_place[r][1]) for r in blocks], len(after)
+                score_body, [(used.index(x_place[r][0]), x_place[r][1]) for r in blocks]
             ),
             (shape(k, rows + SLACK, rows), shape(k, features, rows)),
             "score",
-            flops=12 * features * rows * rows * k,
-            data=features * columns * 4 * k,
-            in_specs=[smem] + [vmem] * (2 + len(used)) + [unread] * len(after),
-        )(me.reshape(1), document_matrix, pool, *[x_arrays[i] for i in used], *after)
+            [me.reshape(1), document_matrix, pool] + [x_arrays[i] for i in used],
+            [smem] + [vmem] * (2 + len(used)),
+        )
         got = [
             lax.ppermute(part, "dim", [(i, (i + s) % depth) for i in range(depth)])
             for s in range(1, depth)
         ]
-        waiting.append((b, part, found, got))
-        if len(waiting) > 1:
-            finish_batch()
+        waiting.append((blocks, part, found, got))
+        while len(waiting) > 2:
+            softmax()
+
+    def softmax():
+        blocks, part, found, got = waiting.pop(0)
+        k = len(blocks)
+        e, *out = line(
+            functools.partial(softmax_body, len(got)),
+            [shape(k, rows + SLACK, rows)] + [block] * k,
+            "softmax",
+            [dt, found, part, *got],
+        )
+        for i, r in enumerate(blocks):
+            e_place[r] = (len(weights), i)
+        weights.append(e)
+        for r, array in zip(blocks, out):
+            sums[r] = send(array, 1) if r % 2 else array
+        ready = [k for k in groups if 4 * k + 2 in sums and 4 * k + 3 in sums]
+        for k in groups:
+            if stage.get(k) == 1:
+                inward(k)
+        for k in ready:
+            if k not in stage:
+                stage[k] = 0
+            elif stage[k] == 0:
+                beside(k)
+
+    groups = [0] + list(range(2, far)) + [1]
+    over_x, home = {}, []
+
+    def add(*terms):
+        return line(merge_body, block, "merge", list(terms))
+
+    def beside(k):
+        stage[k] = 1
+        over_x[k] = send(add(sums[4 * k + 2], sums[4 * k + 3]), 2)
+
+    def inward(k):
+        stage[k] = 2
+        whole = add(sums[4 * k], sums[4 * k + 1], over_x[k])
+        home.append(send(whole, 4 * k) if k else whole)
+
+    packed = line(
+        functools.partial(pack_body, columns),
+        block,
+        "pack",
+        [question_matrix, hard_owner.T, hard_local.T],
+        [pl.BlockSpec(memory_space=pltpu.HBM)] * 3,
+        limit=62,
+        scratch_shapes=[
+            pltpu.VMEM(question_matrix.shape, f32),
+            pltpu.VMEM(hard_owner.shape[::-1], jnp.int32),
+            pltpu.VMEM(hard_local.shape[::-1], jnp.int32),
+            pltpu.SemaphoreType.DMA((3,)),
+        ],
+    )
+    keep(packed, 0)
+    for k in [2, 1] + [k for k in range(4, far) if k % 2 == 0]:
+        keep(send(packed, 4 * k), 4 * k)
+    keep(send(packed, 2), 2)
+    keep(send(packed, 1), 1)
+    dt = line(flip_body, shape(features, rows), "flip", [document_matrix])
+    score([0, 1])
+    forward(2)
+    share(waves[1])
+    softmax()
+    score([2, 4, 8])
+    for w in range(1, len(waves) - 1):
+        upcoming = waves[w + 1]
+        odds = [r + 1 for r in waves[w]]
+        if len(upcoming) == 2:
+            forward(upcoming[1] // 4)
+        elif w == len(waves) - 3:
+            forward(1)
+        if len(odds) > 1:
+            score(odds)
+        share(upcoming)
+        if len(upcoming) > 1:
+            score(upcoming)
+        else:
+            score(upcoming + [r + 1 for r in upcoming])
     while waiting:
-        finish_batch()
-
-    def terms(blocks, extra):
-        used = sorted({sum_place[r][0] for r in blocks})
-        places = [(used.index(sum_place[r][0]), sum_place[r][1]) for r in blocks]
-        places += [(len(used) + i, None) for i in range(len(extra))]
-        return places, [sums[i] for i in used] + extra
-
-    def add(blocks, extra=()):
-        places, arrays = terms(blocks, list(extra))
-        return call(
-            functools.partial(merge_body, places), shape(features + SLACK, rows), "merge"
-        )(*arrays)
-
-    home = []
-    for k in [0] + list(range(2, far)) + [1]:
-        beside = send(add([4 * k + 2, 4 * k + 3]), 2)
-        if k:
-            home.append(send(add([4 * k, 4 * k + 1], [beside]), 4 * k))
-        else:
-            home.append(beside)
-
-    totals = call(
+        softmax()
+
+    totals = line(
         functools.partial(stats_body, [e_place[r] for r in range(n)]),
         shape(2, n, rows),
         "stats",
-        grid=(1,),
-        in_specs=[
+        weights,
+        [
             pl.BlockSpec((e.shape[0], SLACK, rows), lambda i: (0, rows // SLACK, 0))
             for e in weights
         ],
+        grid=(1,),
         out_specs=full(2, n, rows),
-    )(*weights)
-    for masks in ([1], [2], [4 * k for k in range(1, far)]):
-        totals = call(
-            functools.partial(stats_merge_body, masks), shape(2, n, rows), "stats_merge"
-        )(totals, *[send(totals, mask) for mask in masks])
+    )
+    mask = 1
+    while mask < n:
+        there = send(totals, mask)
+        if mask < 4:
+            for k in groups:
+                if stage[k] == 0:
+                    beside(k)
+        totals = line(
+            functools.partial(stats_merge_body, [mask]),
+            shape(2, n, rows),
+            "stats_merge",
+            [totals, there],
+        )
+        mask *= 2
+    for k in groups:
+        if stage[k] == 1:
+            inward(k)
 
     group = 4
     width = 512
-    e_at = len(x_arrays)
-    document_derivative, grad_pool = call(
+    e_at = 2 + len(x_arrays)
+    document_derivative, grad_pool = line(
         functools.partial(
             gradient_body,
-            [x_place[r] for r in range(n)],
+            [(x_place[r][0] + 2, x_place[r][1]) for r in range(n)],
             [(e_at + e_place[r][0], e_place[r][1]) for r in range(n)],
             group,
         ),
         (shape(rows, features), shape(features, columns)),
         "gradient",
-        flops=2 * features * rows * n * (2 * columns + 6 * rows),
-        data=features * columns * 8,
+        [question_matrix, totals, *x_arrays, *weights],
+        limit=48,
         grid=(columns // width,),
-        in_specs=[vmem] * (2 + len(x_arrays) + len(weights)),
         out_specs=(full(rows, features), pl.BlockSpec((features, width), lambda i: (0, i))),
         scratch_shapes=[
             pltpu.VMEM((n // group, 2 * features, group * rows), bf16),
             pltpu.VMEM((n // group, group * rows, 128), jnp.int32),
         ],
-    )(question_matrix, totals, *x_arrays, *weights)
-
-    places, arrays = terms([0, 1], home)
-    question_derivative, loss = call(
-        functools.partial(last_body, places),
-        (shape(rows, features), shape(SLACK, rows)),
+    )
+
+    line.last = totals
+    arrays = home
+    question_derivative, loss = line(
+        last_body,
+        (shape(rows, features), shape(rows)),
         "finish",
-        grid=(1,),
-        in_specs=[full(rows, features)]
+        [document_matrix, weights[0], *arrays],
+        [full(rows, features)]
         + [pl.BlockSpec((1, SLACK, rows), lambda i: (0, rows // SLACK, 0))]
         + [full(*a.shape) for a in arrays],
-        out_specs=(full(rows, features), full(SLACK, rows)),
-    )(document_matrix, weights[0], *arrays)
-    return loss[0], question_derivative, document_derivative, grad_pool
+        grid=(1,),
+        out_specs=(full(rows, features), full(rows)),
+    )
+    return loss, question_derivative, document_derivative, grad_pool
 
 
 def solution(mesh):

time: 121 us -> 109 us (0.901)
  waiting for transfers between devices: 42.4 us -> 30.6 us
  Pallas kernels: 31.5 us -> 33.4 us
    ppermute x29 -> x34, waiting for transfers between devices: 31.3 us -> 19 us  [send(): return lax.ppermute(x, 'blk', [(i, i ^ mask) for i in range(n)])]
    pallas_call x27 -> x34, Pallas kernels: 31.5 us -> 33.4 us  [__call__(): pl.pallas_call(kernel, out_shape=out_shape, name=name, in_specs=in_specs,...]
    ppermute x29 -> x34, starting transfers between devices: 31.4 us -> 30.1 us  [send(): return lax.ppermute(x, 'blk', [(i, i ^ mask) for i in range(n)])]
    ppermute x6 -> x7, waiting for transfers between devices: 11.1 us -> 11.6 us  [score(): lax.ppermute(part, 'dim', [(i, (i + s) % depth) for i in range(depth)])]
    unnamed x16 -> x18, local copies, waits for them, and re-layouts: 5.12 us -> 5.61 us
    ppermute x6 -> x7, starting transfers between devices: 7.47 us -> 7.8 us  [score(): lax.ppermute(part, 'dim', [(i, (i + s) % depth) for i in range(depth)])]
  transfers between devices with their start and end apart: 35 -> 41, of which waited for: 15 -> 11; matrix products, arithmetic and copies ran while one was open for 0% -> 0% of each run, Pallas kernels for 26% -> 28%
where the time goes in v3:
time: 109 us
  starting transfers between devices  37.9 us (35%)
  Pallas kernels  33.4 us (31%)
  waiting for transfers between devices  30.6 us (28%)
  local copies, waits for them, and re-layouts  5.61 us (5%)
    pallas_call x34, Pallas kernels, __call__(): pl.pallas_call(kernel, out_shape=out_shape, name=name, in_specs=in_specs,...  33.4 us
    ppermute x34, starting transfers between devices, send(): return lax.ppermute(x, 'blk', [(i, i ^ mask) for i in range(n)])  30.1 us
    ppermute x34, waiting for transfers between devices, send(): return lax.ppermute(x, 'blk', [(i, i ^ mask) for i in range(n)])  19 us
    ppermute x7, waiting for transfers between devices, score(): lax.ppermute(part, 'dim', [(i, (i + s) % depth) for i in range(depth)])  11.6 us
    ppermute x7, starting transfers between devices, score(): lax.ppermute(part, 'dim', [(i, (i + s) % depth) for i in range(depth)])  7.8 us
    unnamed x18, local copies, waits for them, and re-layouts  5.61 us
  transfers between devices with their start and end apart: 41, of which 11 were waited for; matrix products, arithmetic and copies ran while one was open for 0% of the time, Pallas kernels for 28%

profile of v3, /device:TPU:0, one launch (start us, length us, event | category | flops | bytes accessed | tf_op | source)
XLA Modules:
  0.0 108.6 jit_solution(509335643605550349)
XLA Ops:
  2.9 3.7 %collective-permute-start.2 = (f32[392,128]{1,0:T(8,128)}, f32[392,128]{1,0:T(8,128)S(1)}, u32[]{:S(2)}, u32[]{:S(2)}) collective-permute-start(f32[392,128]{1,0:T(8,128)} %pack.1.refs_1_.refs_3_.refs_2_), channel_id=1, source_target_pairs={{0,16},{2,18},{4,20},{6,22},{8,24},{10,26},{12,28},{14,30},{16,0},... | collective-permute-start | bytes 602120 | tf_op jit(solution)/shard_map/ppermute | solution.py:262
  11.7 1.9 %copy-done = f32[384,2048]{1,0:T(8,128)S(1)} copy-done((f32[384,2048]{1,0:T(8,128)S(1)}, f32[384,2048]{1,0:T(8,128)}, u32[]{:S(2)}) %copy-start) | copy-done | bytes 3145752
  15.4 1.9 %score.7 = (f32[2,136,128]{2,1,0:T(8,128)S(1)}, f32[2,384,128]{2,1,0:T(8,128)S(1)}) custom-call(s32[1]{0:T(128)} %bitcast.2.refs_0_, f32[128,384]{1,0:T(8,128)S(1)} %copy-done.3, f32[384,2048]{1,0:T(8,128)S(1)} %copy-done, f32[392,128]{1,0:T(8,128)S(1)} %copy-done.6, f32[392,128]{1,0:T(8,128)S(1)} %collective-permute-done.refs_4_.refs_6_, ...), custom_call_target="tpu_custom_call" | custom-call | tf_op jit(solution)/shard_map/score/pallas_call | solution.py:44
  20.0 3.1 %collective-permute-done.1.refs_3_ = f32[2,136,128]{2,1,0:T(8,128)S(1)} collective-permute-done((f32[2,136,128]{2,1,0:T(8,128)S(1)}, f32[2,136,128]{2,1,0:T(8,128)S(1)}, u32[]{:S(2)}, u32[]{:S(2)}) %collective-permute-start.1) | collective-permute-done | bytes 139296 | tf_op jit(solution)/shard_map/ppermute | solution.py:304
  23.6 2.7 %score.8 = (f32[3,136,128]{2,1,0:T(8,128)S(1)}, f32[3,384,128]{2,1,0:T(8,128)S(1)}) custom-call(s32[1]{0:T(128)} %bitcast.2.refs_0_, f32[128,384]{1,0:T(8,128)S(1)} %copy-done.4, f32[384,2048]{1,0:T(8,128)S(1)} %copy-done.1, f32[392,128]{1,0:T(8,128)S(1)} %collective-permute-done.2.refs_0_.refs_3_, f32[392,128]{1,0:T(8,128)S(1)} %collective-permute-done.4.refs_4_.refs_0_, ...), custom_call_target="tpu_custom_call" | custom-call | tf_op jit(solution)/shard_map/score/pallas_call | solution.py:44
  29.4 2.7 %score.9 = (f32[3,136,128]{2,1,0:T(8,128)S(1)}, f32[3,384,128]{2,1,0:T(8,128)S(1)}) custom-call(s32[1]{0:T(128)} %bitcast.2.refs_0_, f32[128,384]{1,0:T(8,128)S(1)} %copy-done.4, f32[384,2048]{1,0:T(8,128)S(1)} %copy-done.1, f32[392,128]{1,0:T(8,128)S(1)} %collective-permute-done.9.refs_3_.refs_9_, f32[392,128]{1,0:T(8,128)S(1)} %collective-permute-done.10.refs_4_.refs_10_, ...), custom_call_target="tpu_custom_call" | custom-call | tf_op jit(solution)/shard_map/score/pallas_call | solution.py:44
  34.4 1.9 %score.10 = (f32[2,136,128]{2,1,0:T(8,128)S(1)}, f32[2,384,128]{2,1,0:T(8,128)S(1)}) custom-call(s32[1]{0:T(128)} %bitcast.2.refs_0_, f32[128,384]{1,0:T(8,128)S(1)} %copy-done.4, f32[384,2048]{1,0:T(8,128)S(1)} %copy-done.1, f32[392,128]{1,0:T(8,128)S(1)} %collective-permute-done.7.refs_0_.refs_3_.refs_7_, ...), custom_call_target="tpu_custom_call" | custom-call | tf_op jit(solution)/shard_map/score/pallas_call | solution.py:44
  37.1 2.5 %collective-permute-start.21 = (f32[392,128]{1,0:T(8,128)S(1)}, f32[392,128]{1,0:T(8,128)S(1)}, u32[]{:S(2)}, u32[]{:S(2)}) collective-permute-start(f32[392,128]{1,0:T(8,128)S(1)} %relay.5.refs_5_), channel_id=1, source_target_pairs={{0,4},{2,6},{4,0},{6,2},{8,12},{10,14},{12,8},{14,10},{16,20},{18,... | collective-permute-start | bytes 602120 | tf_op jit(solution)/shard_map/ppermute | solution.py:262
  39.6 2.1 %score.11 = (f32[2,136,128]{2,1,0:T(8,128)S(1)}, f32[2,384,128]{2,1,0:T(8,128)S(1)}) custom-call(s32[1]{0:T(128)} %bitcast.2.refs_0_, f32[128,384]{1,0:T(8,128)S(1)} %copy-done.4, f32[384,2048]{1,0:T(8,128)S(1)} %copy-done.1, f32[392,128]{1,0:T(8,128)S(1)} %collective-permute-done.13.refs_3_.refs_13_, ...), custom_call_target="tpu_custom_call" | custom-call | tf_op jit(solution)/shard_map/score/pallas_call | solution.py:44
  44.9 1.9 %collective-permute-start.20 = (f32[2,136,128]{2,1,0:T(8,128)S(1)}, f32[2,136,128]{2,1,0:T(8,128)S(1)}, u32[]{:S(2)}, u32[]{:S(2)}) collective-permute-start(f32[2,136,128]{2,1,0:T(8,128)S(1)} %get-tuple-element.63.refs_2_), channel_id=1, source_target_pairs={{0,1},{1,0},{2,3},{3,2},{4,5},{5,4},{6,7},{7,6},{8,9},{9,8},{10,11... | collective-permute-start | bytes 417800 | tf_op jit(solution)/shard_map/ppermute | solution.py:304
  46.8 1.9 %score.12 = (f32[2,136,128]{2,1,0:T(8,128)S(1)}, f32[2,384,128]{2,1,0:T(8,128)S(1)}) custom-call(s32[1]{0:T(128)} %bitcast.2.refs_0_, f32[128,384]{1,0:T(8,128)S(1)} %copy-done.4, f32[384,2048]{1,0:T(8,128)S(1)} %copy-done.1, f32[392,128]{1,0:T(8,128)S(1)} %collective-permute-done.17.refs_3_.refs_12_, ...), custom_call_target="tpu_custom_call" | custom-call | tf_op jit(solution)/shard_map/score/pallas_call | solution.py:44
  48.7 2.6 %collective-permute-done.16.refs_3_ = f32[2,136,128]{2,1,0:T(8,128)S(1)} collective-permute-done((f32[2,136,128]{2,1,0:T(8,128)S(1)}, f32[2,136,128]{2,1,0:T(8,128)S(1)}, u32[]{:S(2)}, u32[]{:S(2)}) %collective-permute-start.16) | collective-permute-done | bytes 139296 | tf_op jit(solution)/shard_map/ppermute | solution.py:304
  51.8 1.8 %collective-permute-start.19 = (f32[392,128]{1,0:T(8,128)S(1)}, f32[392,128]{1,0:T(8,128)S(1)}, u32[]{:S(2)}, u32[]{:S(2)}) collective-permute-start(f32[392,128]{1,0:T(8,128)S(1)} %merge.8.refs_5_), channel_id=1, source_target_pairs={{0,4},{2,6},{4,0},{6,2},{8,12},{10,14},{12,8},{14,10},{16,20},{18,... | collective-permute-start | bytes 602120 | tf_op jit(solution)/shard_map/ppermute | solution.py:262
  53.6 1.9 %score.13 = (f32[2,136,128]{2,1,0:T(8,128)S(1)}, f32[2,384,128]{2,1,0:T(8,128)S(1)}) custom-call(s32[1]{0:T(128)} %bitcast.2.refs_0_, f32[128,384]{1,0:T(8,128)S(1)} %copy-done.4, f32[384,2048]{1,0:T(8,128)S(1)} %copy-done.1, f32[392,128]{1,0:T(8,128)S(1)} %collective-permute-done.21.refs_3_.refs_15_, ...), custom_call_target="tpu_custom_call" | custom-call | tf_op jit(solution)/shard_map/score/pallas_call | solution.py:44
  56.3 1.9 %collective-permute-start.27 = (f32[2,136,128]{2,1,0:T(8,128)S(1)}, f32[2,136,128]{2,1,0:T(8,128)S(1)}, u32[]{:S(2)}, u32[]{:S(2)}) collective-permute-start(f32[2,136,128]{2,1,0:T(8,128)S(1)} %get-tuple-element.70.refs_2_), channel_id=1, source_target_pairs={{0,1},{1,0},{2,3},{3,2},{4,5},{5,4},{6,7},{7,6},{8,9},{9,8},{10,11... | collective-permute-start | bytes 417800 | tf_op jit(solution)/shard_map/ppermute | solution.py:304
  58.3 4.4 %collective-permute-done.25.refs_3_ = f32[2,136,128]{2,1,0:T(8,128)S(1)} collective-permute-done((f32[2,136,128]{2,1,0:T(8,128)S(1)}, f32[2,136,128]{2,1,0:T(8,128)S(1)}, u32[]{:S(2)}, u32[]{:S(2)}) %collective-permute-start.25) | collective-permute-done | bytes 139296 | tf_op jit(solution)/shard_map/ppermute | solution.py:304
  66.4 3.0 %collective-permute-done.26.refs_2_ = f32[392,128]{1,0:T(8,128)S(1)} collective-permute-done((f32[392,128]{1,0:T(8,128)S(1)}, f32[392,128]{1,0:T(8,128)S(1)}, u32[]{:S(2)}, u32[]{:S(2)}) %collective-permute-start.26) | collective-permute-done | bytes 200736 | tf_op jit(solution)/shard_map/ppermute | solution.py:262
  69.9 1.8 %collective-permute-start.39 = (f32[392,128]{1,0:T(8,128)S(1)}, f32[392,128]{1,0:T(8,128)S(1)}, u32[]{:S(2)}, u32[]{:S(2)}) collective-permute-start(f32[392,128]{1,0:T(8,128)S(1)} %merge.13.refs_2_), channel_id=1, source_target_pairs={{0,4},{2,6},{4,0},{6,2},{8,12},{10,14},{12,8},{14,10},{16,20},{18,... | collective-permute-start | bytes 602120 | tf_op jit(solution)/shard_map/ppermute | solution.py:262
  73.3 6.1 %collective-permute-done.34.refs_1_ = f32[2,16,128]{2,1,0:T(8,128)S(1)} collective-permute-done((f32[2,16,128]{2,1,0:T(8,128)S(1)}, f32[2,16,128]{2,1,0:T(8,128)S(1)}, u32[]{:S(2)}, u32[]{:S(2)}) %collective-permute-start.34) | collective-permute-done | bytes 16416 | tf_op jit(solution)/shard_map/ppermute | solution.py:262
  80.3 2.9 %collective-permute-done.35.refs_1_ = f32[2,16,128]{2,1,0:T(8,128)S(1)} collective-permute-done((f32[2,16,128]{2,1,0:T(8,128)S(1)}, f32[2,16,128]{2,1,0:T(8,128)S(1)}, u32[]{:S(2)}, u32[]{:S(2)}) %collective-permute-start.35) | collective-permute-done | bytes 16416 | tf_op jit(solution)/shard_map/ppermute | solution.py:262
  83.3 3.2 %collective-permute-start.36 = (f32[2,16,128]{2,1,0:T(8,128)S(1)}, f32[2,16,128]{2,1,0:T(8,128)S(1)}, u32[]{:S(2)}, u32[]{:S(2)}) collective-permute-start(f32[2,16,128]{2,1,0:T(8,128)S(1)} %stats_merge.6.refs_0_.refs_2_), channel_id=1, source_target_pairs={{0,16},{2,18},{4,20},{6,22},{8,24},{10,26},{12,28},{14,30},{16,0},... | collective-permute-start | bytes 49160 | tf_op jit(solution)/shard_map/ppermute | solution.py:262
  86.4 3.3 %collective-permute-done.36.refs_1_ = f32[2,16,128]{2,1,0:T(8,128)S(1)} collective-permute-done((f32[2,16,128]{2,1,0:T(8,128)S(1)}, f32[2,16,128]{2,1,0:T(8,128)S(1)}, u32[]{:S(2)}, u32[]{:S(2)}) %collective-permute-start.36) | collective-permute-done | bytes 16416 | tf_op jit(solution)/shard_map/ppermute | solution.py:262
  91.4 4.4 %collective-permute-start.37 = (f32[392,128]{1,0:T(8,128)S(1)}, f32[392,128]{1,0:T(8,128)S(1)}, u32[]{:S(2)}, u32[]{:S(2)}) collective-permute-start(f32[392,128]{1,0:T(8,128)S(1)} %merge.14.refs_3_), channel_id=1, source_target_pairs={{0,24},{2,26},{4,28},{6,30},{8,16},{10,18},{12,20},{14,22},{16,8},... | collective-permute-start | bytes 602120 | tf_op jit(solution)/shard_map/ppermute | solution.py:262
  96.6 11.1 %gradient.1 = (f32[128,384]{1,0:T(8,128)}, f32[384,2048]{1,0:T(8,128)}) custom-call(f32[128,384]{1,0:T(8,128)S(1)} %copy-done.8, f32[2,16,128]{2,1,0:T(8,128)S(1)} %stats_merge.7.refs_3_.refs_6_.refs_1_, f32[392,128]{1,0:T(8,128)S(1)} %copy-done.7, f32[392,128]{1,0:T(8,128)S(1)} %collective-permute-done.2.refs_0_.refs_3_, ...), custom_call_target="tpu_custom_call" | custom-call | tf_op jit(solution)/shard_map/gradient/pallas_call | solution.py:44
  (110 shorter events, 32.9 us)
Async XLA Ops:
  2.4 9.2 %collective-permute-start = (f32[392,128]{1,0:T(8,128)}, f32[392,128]{1,0:T(8,128)S(1)}, u32[]{:S(2)}, u32[]{:S(2)}) collective-permute-start(f32[392,128]{1,0:T(8,128)} %pack.1.refs_1_.refs_3_.refs_2_), channel_id=1, source_target_pairs={{0,2},{2,0},{4,6},{6,4},{8,10},{10,8},{12,14},{14,12},{16,18},{18,... | collective-permute-start | bytes 602120 | tf_op jit(solution)/shard_map/ppermute | solution.py:262
  2.9 14.4 %collective-permute-start.2 = (f32[392,128]{1,0:T(8,128)}, f32[392,128]{1,0:T(8,128)S(1)}, u32[]{:S(2)}, u32[]{:S(2)}) collective-permute-start(f32[392,128]{1,0:T(8,128)} %pack.1.refs_1_.refs_3_.refs_2_), channel_id=1, source_target_pairs={{0,16},{2,18},{4,20},{6,22},{8,24},{10,26},{12,28},{14,30},{16,0},... | collective-permute-start | bytes 602120 | tf_op jit(solution)/shard_map/ppermute | solution.py:262
  6.6 12.8 %collective-permute-start.5 = (f32[392,128]{1,0:T(8,128)}, f32[392,128]{1,0:T(8,128)S(1)}, u32[]{:S(2)}, u32[]{:S(2)}) collective-permute-start(f32[392,128]{1,0:T(8,128)} %pack.1.refs_1_.refs_3_.refs_2_), channel_id=1, source_target_pairs={{0,4},{2,6},{4,0},{6,2},{8,12},{10,14},{12,8},{14,10},{16,20},{18,... | collective-permute-start | bytes 602120 | tf_op jit(solution)/shard_map/ppermute | solution.py:262
  8.1 11.3 %collective-permute-start.4 = (f32[392,128]{1,0:T(8,128)}, f32[392,128]{1,0:T(8,128)S(1)}, u32[]{:S(2)}, u32[]{:S(2)}) collective-permute-start(f32[392,128]{1,0:T(8,128)} %pack.1.refs_1_.refs_3_.refs_2_), channel_id=1, source_target_pairs={{0,8},{2,10},{4,12},{6,14},{8,0},{10,2},{12,4},{14,6},{16,24},{18,... | collective-permute-start | bytes 602120 | tf_op jit(solution)/shard_map/ppermute | solution.py:262
  17.3 10.5 %collective-permute-start.7 = (f32[392,128]{1,0:T(8,128)S(1)}, f32[392,128]{1,0:T(8,128)S(1)}, u32[]{:S(2)}, u32[]{:S(2)}) collective-permute-start(f32[392,128]{1,0:T(8,128)S(1)} %relay.3.refs_4_), channel_id=1, source_target_pairs={{0,8},{2,10},{4,12},{6,14},{8,0},{10,2},{12,4},{14,6},{16,24},{18,... | collective-permute-start | bytes 602120 | tf_op jit(solution)/shard_map/ppermute | solution.py:262
  19.4 10.0 %collective-permute-start.9 = (f32[392,128]{1,0:T(8,128)S(1)}, f32[392,128]{1,0:T(8,128)S(1)}, u32[]{:S(2)}, u32[]{:S(2)}) collective-permute-start(f32[392,128]{1,0:T(8,128)S(1)} %collective-permute-done.5.refs_5_), channel_id=1, source_target_pairs={{0,2},{2,0},{4,6},{6,4},{8,10},{10,8},{12,14},{14,12},{16,18},{18,... | collective-permute-start | bytes 602120 | tf_op jit(solution)/shard_map/ppermute | solution.py:262
  19.4 10.0 %collective-permute-start.10 = (f32[392,128]{1,0:T(8,128)S(1)}, f32[392,128]{1,0:T(8,128)S(1)}, u32[]{:S(2)}, u32[]{:S(2)}) collective-permute-start(f32[392,128]{1,0:T(8,128)S(1)} %collective-permute-done.4.refs_4_.refs_0_), channel_id=1, source_target_pairs={{0,2},{2,0},{4,6},{6,4},{8,10},{10,8},{12,14},{14,12},{16,18},{18,... | collective-permute-start | bytes 602120 | tf_op jit(solution)/shard_map/ppermute | solution.py:262
  19.9 9.5 %collective-permute-start.11 = (f32[392,128]{1,0:T(8,128)S(1)}, f32[392,128]{1,0:T(8,128)S(1)}, u32[]{:S(2)}, u32[]{:S(2)}) collective-permute-start(f32[392,128]{1,0:T(8,128)S(1)} %collective-permute-done.2.refs_0_.refs_3_), channel_id=1, source_target_pairs={{0,2},{2,0},{4,6},{6,4},{8,10},{10,8},{12,14},{14,12},{16,18},{18,... | collective-permute-start | bytes 602120 | tf_op jit(solution)/shard_map/ppermute | solution.py:262
  26.3 10.0 %collective-permute-start.6 = (f32[3,136,128]{2,1,0:T(8,128)S(1)}, f32[3,136,128]{2,1,0:T(8,128)S(1)}, u32[]{:S(2)}, u32[]{:S(2)}) collective-permute-start(f32[3,136,128]{2,1,0:T(8,128)S(1)} %get-tuple-element.51.refs_2_), channel_id=1, source_target_pairs={{0,1},{1,0},{2,3},{3,2},{4,5},{5,4},{6,7},{7,6},{8,9},{9,8},{10,11... | collective-permute-start | bytes 626696 | tf_op jit(solution)/shard_map/ppermute | solution.py:304
  32.1 9.6 %collective-permute-start.12 = (f32[3,136,128]{2,1,0:T(8,128)S(1)}, f32[3,136,128]{2,1,0:T(8,128)S(1)}, u32[]{:S(2)}, u32[]{:S(2)}) collective-permute-start(f32[3,136,128]{2,1,0:T(8,128)S(1)} %get-tuple-element.55.refs_2_), channel_id=1, source_target_pairs={{0,1},{1,0},{2,3},{3,2},{4,5},{5,4},{6,7},{7,6},{8,9},{9,8},{10,11... | collective-permute-start | bytes 626696 | tf_op jit(solution)/shard_map/ppermute | solution.py:304
  37.1 7.7 %collective-permute-start.21 = (f32[392,128]{1,0:T(8,128)S(1)}, f32[392,128]{1,0:T(8,128)S(1)}, u32[]{:S(2)}, u32[]{:S(2)}) collective-permute-start(f32[392,128]{1,0:T(8,128)S(1)} %relay.5.refs_5_), channel_id=1, source_target_pairs={{0,4},{2,6},{4,0},{6,2},{8,12},{10,14},{12,8},{14,10},{16,20},{18,... | collective-permute-start | bytes 602120 | tf_op jit(solution)/shard_map/ppermute | solution.py:262
  42.4 9.3 %collective-permute-start.15 = (f32[392,128]{1,0:T(8,128)S(1)}, f32[392,128]{1,0:T(8,128)S(1)}, u32[]{:S(2)}, u32[]{:S(2)}) collective-permute-start(f32[392,128]{1,0:T(8,128)S(1)} %get-tuple-element.58), channel_id=1, source_target_pairs={{0,2},{2,0},{4,6},{6,4},{8,10},{10,8},{12,14},{14,12},{16,18},{18,... | collective-permute-start | bytes 602120 | tf_op jit(solution)/shard_map/ppermute | solution.py:262
  44.8 8.9 %collective-permute-start.22 = (f32[392,128]{1,0:T(8,128)S(1)}, f32[392,128]{1,0:T(8,128)S(1)}, u32[]{:S(2)}, u32[]{:S(2)}) collective-permute-start(f32[392,128]{1,0:T(8,128)S(1)} %collective-permute-done.21.refs_3_.refs_15_), channel_id=1, source_target_pairs={{0,2},{2,0},{4,6},{6,4},{8,10},{10,8},{12,14},{14,12},{16,18},{18,... | collective-permute-start | bytes 602120 | tf_op jit(solution)/shard_map/ppermute | solution.py:262
  44.9 10.6 %collective-permute-start.20 = (f32[2,136,128]{2,1,0:T(8,128)S(1)}, f32[2,136,128]{2,1,0:T(8,128)S(1)}, u32[]{:S(2)}, u32[]{:S(2)}) collective-permute-start(f32[2,136,128]{2,1,0:T(8,128)S(1)} %get-tuple-element.63.refs_2_), channel_id=1, source_target_pairs={{0,1},{1,0},{2,3},{3,2},{4,5},{5,4},{6,7},{7,6},{8,9},{9,8},{10,11... | collective-permute-start | bytes 417800 | tf_op jit(solution)/shard_map/ppermute | solution.py:304
  46.8 11.4 %collective-permute-start.3 = (f32[392,128]{1,0:T(8,128)S(1)}, f32[392,128]{1,0:T(8,128)S(1)}, u32[]{:S(2)}, u32[]{:S(2)}) collective-permute-start(f32[392,128]{1,0:T(8,128)S(1)} %get-tuple-element.49.refs_6_), channel_id=1, source_target_pairs={{0,2},{2,0},{4,6},{6,4},{8,10},{10,8},{12,14},{14,12},{16,18},{18,... | collective-permute-start | bytes 602120 | tf_op jit(solution)/shard_map/ppermute | solution.py:262
  56.3 8.9 %collective-permute-start.27 = (f32[2,136,128]{2,1,0:T(8,128)S(1)}, f32[2,136,128]{2,1,0:T(8,128)S(1)}, u32[]{:S(2)}, u32[]{:S(2)}) collective-permute-start(f32[2,136,128]{2,1,0:T(8,128)S(1)} %get-tuple-element.70.refs_2_), channel_id=1, source_target_pairs={{0,1},{1,0},{2,3},{3,2},{4,5},{5,4},{6,7},{7,6},{8,9},{9,8},{10,11... | collective-permute-start | bytes 417800 | tf_op jit(solution)/shard_map/ppermute | solution.py:304
  58.2 8.1 %collective-permute-start.23 = (f32[392,128]{1,0:T(8,128)S(1)}, f32[392,128]{1,0:T(8,128)S(1)}, u32[]{:S(2)}, u32[]{:S(2)}) collective-permute-start(f32[392,128]{1,0:T(8,128)S(1)} %get-tuple-element.60.refs_5_), channel_id=1, source_target_pairs={{0,2},{2,0},{4,6},{6,4},{8,10},{10,8},{12,14},{14,12},{16,18},{18,... | collective-permute-start | bytes 602120 | tf_op jit(solution)/shard_map/ppermute | solution.py:262
  65.8 30.0 %collective-permute-start.38 = (f32[392,128]{1,0:T(8,128)S(1)}, f32[392,128]{1,0:T(8,128)S(1)}, u32[]{:S(2)}, u32[]{:S(2)}) collective-permute-start(f32[392,128]{1,0:T(8,128)S(1)} %get-tuple-element.81), channel_id=1, source_target_pairs={{0,2},{2,0},{4,6},{6,4},{8,10},{10,8},{12,14},{14,12},{16,18},{18,... | collective-permute-start | bytes 602120 | tf_op jit(solution)/shard_map/ppermute | solution.py:262
  66.3 25.0 %collective-permute-start.29 = (f32[392,128]{1,0:T(8,128)S(1)}, f32[392,128]{1,0:T(8,128)S(1)}, u32[]{:S(2)}, u32[]{:S(2)}) collective-permute-start(f32[392,128]{1,0:T(8,128)S(1)} %get-tuple-element.65.refs_3_), channel_id=1, source_target_pairs={{0,2},{2,0},{4,6},{6,4},{8,10},{10,8},{12,14},{14,12},{16,18},{18,... | collective-permute-start | bytes 602120 | tf_op jit(solution)/shard_map/ppermute | solution.py:262
  69.5 21.8 %collective-permute-start.31 = (f32[392,128]{1,0:T(8,128)S(1)}, f32[392,128]{1,0:T(8,128)S(1)}, u32[]{:S(2)}, u32[]{:S(2)}) collective-permute-start(f32[392,128]{1,0:T(8,128)S(1)} %merge.12.refs_7_), channel_id=1, source_target_pairs={{0,4},{2,6},{4,0},{6,2},{8,12},{10,14},{12,8},{14,10},{16,20},{18,... | collective-permute-start | bytes 602120 | tf_op jit(solution)/shard_map/ppermute | solution.py:262
  69.9 25.9 %collective-permute-start.39 = (f32[392,128]{1,0:T(8,128)S(1)}, f32[392,128]{1,0:T(8,128)S(1)}, u32[]{:S(2)}, u32[]{:S(2)}) collective-permute-start(f32[392,128]{1,0:T(8,128)S(1)} %merge.13.refs_2_), channel_id=1, source_target_pairs={{0,4},{2,6},{4,0},{6,2},{8,12},{10,14},{12,8},{14,10},{16,20},{18,... | collective-permute-start | bytes 602120 | tf_op jit(solution)/shard_map/ppermute | solution.py:262
  89.7 18.0 %collective-permute-start.28 = (f32[392,128]{1,0:T(8,128)S(1)}, f32[392,128]{1,0:T(8,128)S(1)}, u32[]{:S(2)}, u32[]{:S(2)}) collective-permute-start(f32[392,128]{1,0:T(8,128)S(1)} %merge.11.refs_2_), channel_id=1, source_target_pairs={{0,16},{2,18},{4,20},{6,22},{8,24},{10,26},{12,28},{14,30},{16,0},... | collective-permute-start | bytes 602120 | tf_op jit(solution)/shard_map/ppermute | solution.py:262
  91.4 16.3 %collective-permute-start.37 = (f32[392,128]{1,0:T(8,128)S(1)}, f32[392,128]{1,0:T(8,128)S(1)}, u32[]{:S(2)}, u32[]{:S(2)}) collective-permute-start(f32[392,128]{1,0:T(8,128)S(1)} %merge.14.refs_3_), channel_id=1, source_target_pairs={{0,24},{2,26},{4,28},{6,30},{8,16},{10,18},{12,20},{14,22},{16,8},... | collective-permute-start | bytes 602120 | tf_op jit(solution)/shard_map/ppermute | solution.py:262
  95.9 11.8 %collective-permute-start.40 = (f32[392,128]{1,0:T(8,128)S(1)}, f32[392,128]{1,0:T(8,128)S(1)}, u32[]{:S(2)}, u32[]{:S(2)}) collective-permute-start(f32[392,128]{1,0:T(8,128)S(1)} %merge.15.refs_25_), channel_id=1, source_target_pairs={{0,8},{2,10},{4,12},{6,14},{8,0},{10,2},{12,4},{14,6},{16,24},{18,... | collective-permute-start | bytes 602120 | tf_op jit(solution)/shard_map/ppermute | solution.py:262
  (26 other events, 184.9 us)

commit v4 on v3

--- a/solution.py
+++ b/solution.py
@@ -9,6 +9,7 @@
 
 logit_divisor = 0.05
 LOWEST = -3.0e38
+COST = 3.7e6
 SLACK = 8
 
 f32 = jnp.float32
@@ -30,7 +31,7 @@
     def __init__(self):
         self.last = None
 
-    def __call__(self, body, out_shape, name, arrays, in_specs=None, limit=16, **kw):
+    def __call__(self, body, out_shape, name, arrays, us, in_specs=None, limit=16, **kw):
         count = len(arrays)
         if in_specs is None:
             in_specs = [pl.BlockSpec(memory_space=pltpu.VMEM)] * count
@@ -46,7 +47,9 @@
             out_shape=out_shape,
             name=name,
             in_specs=in_specs,
-            cost_estimate=pl.CostEstimate(flops=0, bytes_accessed=0, transcendentals=0),
+            cost_estimate=pl.CostEstimate(
+                flops=0, bytes_accessed=int(us * COST), transcendentals=0
+            ),
             compiler_params=pltpu.CompilerParams(vmem_limit_bytes=limit << 20),
             **kw,
         )(*arrays)
@@ -262,9 +265,6 @@
         return lax.ppermute(x, "blk", [(i, i ^ mask) for i in range(n)])
 
     far = n // 4
-    waves = [[0], [2, 4, 8]] + [[4 * k + 2, 4 * k + 4] for k in range(2, far - 1)]
-    waves += [[4 * far - 2], [6]]
-
     x, x_arrays, x_place = {}, [], {}
 
     def keep(array, r):
@@ -273,16 +273,16 @@
         x_arrays.append(array)
 
     def relay(r):
-        return line(relay_body, block, "relay", [x[r]])
+        x_arrays[x_place[r][0]] = x[r] = line(relay_body, block, "relay", [x[r]], 0.05)
 
     def forward(k):
-        held = relay(4 * k)
-        if k % 2 == 0 and 2 <= k < far - 1:
-            keep(send(held, 4), 4 * k + 4)
-        keep(send(held, 2), 4 * k + 2)
-
-    def share(wave):
-        for r in wave:
+        relay(4 * k)
+        if k % 2 == 0 and k + 1 < far:
+            keep(send(x[4 * k], 4), 4 * k + 4)
+        keep(send(x[4 * k], 2), 4 * k + 2)
+
+    def share(*blocks):
+        for r in blocks:
             keep(send(x[r], 1), r + 1)
 
     weights, sums, e_place = [], {}, {}
@@ -298,6 +298,7 @@
             (shape(k, rows + SLACK, rows), shape(k, features, rows)),
             "score",
             [me.reshape(1), document_matrix, pool] + [x_arrays[i] for i in used],
+            0.9 * k,
             [smem] + [vmem] * (2 + len(used)),
         )
         got = [
@@ -305,8 +306,6 @@
             for s in range(1, depth)
         ]
         waiting.append((blocks, part, found, got))
-        while len(waiting) > 2:
-            softmax()
 
     def softmax():
         blocks, part, found, got = waiting.pop(0)
@@ -316,34 +315,23 @@
             [shape(k, rows + SLACK, rows)] + [block] * k,
             "softmax",
             [dt, found, part, *got],
+            0.25 * k,
         )
         for i, r in enumerate(blocks):
             e_place[r] = (len(weights), i)
         weights.append(e)
         for r, array in zip(blocks, out):
             sums[r] = send(array, 1) if r % 2 else array
-        ready = [k for k in groups if 4 * k + 2 in sums and 4 * k + 3 in sums]
-        for k in groups:
-            if stage.get(k) == 1:
-                inward(k)
-        for k in ready:
-            if k not in stage:
-                stage[k] = 0
-            elif stage[k] == 0:
-                beside(k)
-
-    groups = [0] + list(range(2, far)) + [1]
+
     over_x, home = {}, []
 
     def add(*terms):
-        return line(merge_body, block, "merge", list(terms))
+        return line(merge_body, block, "merge", list(terms), 0.05)
 
     def beside(k):
-        stage[k] = 1
         over_x[k] = send(add(sums[4 * k + 2], sums[4 * k + 3]), 2)
 
     def inward(k):
-        stage[k] = 2
         whole = add(sums[4 * k], sums[4 * k + 1], over_x[k])
         home.append(send(whole, 4 * k) if k else whole)
 
@@ -352,6 +340,7 @@
         block,
         "pack",
         [question_matrix, hard_owner.T, hard_local.T],
+        1.8,
         [pl.BlockSpec(memory_space=pltpu.HBM)] * 3,
         limit=62,
         scratch_shapes=[
@@ -366,34 +355,45 @@
         keep(send(packed, 4 * k), 4 * k)
     keep(send(packed, 2), 2)
     keep(send(packed, 1), 1)
-    dt = line(flip_body, shape(features, rows), "flip", [document_matrix])
+    dt = line(flip_body, shape(features, rows), "flip", [document_matrix], 0.1)
     score([0, 1])
+    relay(2)
     forward(2)
-    share(waves[1])
+    forward(1)
+    share(2, 4, 8)
     softmax()
     score([2, 4, 8])
-    for w in range(1, len(waves) - 1):
-        upcoming = waves[w + 1]
-        odds = [r + 1 for r in waves[w]]
-        if len(upcoming) == 2:
-            forward(upcoming[1] // 4)
-        elif w == len(waves) - 3:
-            forward(1)
-        if len(odds) > 1:
-            score(odds)
-        share(upcoming)
-        if len(upcoming) > 1:
-            score(upcoming)
+    relay(10)
+    if far > 3:
+        forward(3)
+    share(10, 6)
+    score([3, 5, 9])
+    softmax()
+    relay(6)
+    score([10, 6, 11, 7])
+    softmax()
+    for k in range(3, far):
+        if k + 1 < far:
+            forward(k + 1)
+        share(4 * k, 4 * k + 2)
+        score([4 * k, 4 * k + 2, 4 * k + 1, 4 * k + 3])
+        if k == 3:
+            beside(0)
+        softmax()
+        if k == 3:
+            beside(2)
+            beside(1)
         else:
-            score(upcoming + [r + 1 for r in upcoming])
-    while waiting:
-        softmax()
+            beside(k - 1)
+    inward(0)
+    softmax()
 
     totals = line(
         functools.partial(stats_body, [e_place[r] for r in range(n)]),
         shape(2, n, rows),
         "stats",
         weights,
+        0.05,
         [
             pl.BlockSpec((e.shape[0], SLACK, rows), lambda i: (0, rows // SLACK, 0))
             for e in weights
@@ -404,20 +404,23 @@
     mask = 1
     while mask < n:
         there = send(totals, mask)
-        if mask < 4:
-            for k in groups:
-                if stage[k] == 0:
-                    beside(k)
         totals = line(
             functools.partial(stats_merge_body, [mask]),
             shape(2, n, rows),
             "stats_merge",
             [totals, there],
-        )
+            0.05,
+        )
+        if mask == 2 and far > 3:
+            inward(2)
+        if mask == 1:
+            beside(far - 1)
+        if mask == 4:
+            inward(1)
+            for k in range(3, far - 1):
+                inward(k)
         mask *= 2
-    for k in groups:
-        if stage[k] == 1:
-            inward(k)
+    inward(far - 1)
 
     group = 4
     width = 512
@@ -432,6 +435,7 @@
         (shape(rows, features), shape(features, columns)),
         "gradient",
         [question_matrix, totals, *x_arrays, *weights],
+        11.0,
         limit=48,
         grid=(columns // width,),
         out_specs=(full(rows, features), pl.BlockSpec((features, width), lambda i: (0, i))),
@@ -448,6 +452,7 @@
         (shape(rows, features), shape(rows)),
         "finish",
         [document_matrix, weights[0], *arrays],
+        0.8,
         [full(rows, features)]
         + [pl.BlockSpec((1, SLACK, rows), lambda i: (0, rows // SLACK, 0))]
         + [full(*a.shape) for a in arrays],

time: 109 us -> 93.9 us (0.86)
  waiting for transfers between devices: 30.6 us -> 24 us
  starting transfers between devices: 37.9 us -> 31.4 us
  local copies, waits for them, and re-layouts: 5.61 us -> 3.76 us
    ppermute x7 -> x5, waiting for transfers between devices: 11.6 us -> 2.07 us  [score(): lax.ppermute(part, 'dim', [(i, (i + s) % depth) for i in range(depth)])]
    ppermute x34, starting transfers between devices: 30.1 us -> 25.6 us  [send(): return lax.ppermute(x, 'blk', [(i, i ^ mask) for i in range(n)])]
    ppermute x34, waiting for transfers between devices: 19 us -> 21.9 us  [send(): return lax.ppermute(x, 'blk', [(i, i ^ mask) for i in range(n)])]
    ppermute x7 -> x5, starting transfers between devices: 7.8 us -> 5.84 us  [score(): lax.ppermute(part, 'dim', [(i, (i + s) % depth) for i in range(depth)])]
    unnamed x18 -> x14, local copies, waits for them, and re-layouts: 5.61 us -> 3.76 us
    pallas_call x34 -> x33, Pallas kernels: 33.4 us -> 33.5 us  [__call__(): pl.pallas_call(kernel, out_shape=out_shape, name=name, in_specs=in_specs,...]
  transfers between devices with their start and end apart: 41 -> 39, of which waited for: 11 -> 15; matrix products, arithmetic and copies ran while one was open for 0% -> 0% of each run, Pallas kernels for 28% -> 32%
where the time goes in v4:
time: 93.9 us; the launch traced here: 93.7 us
  Pallas kernels  33.5 us (36%)
  starting transfers between devices  31.4 us (33%)
  waiting for transfers between devices  24 us (26%)
  local copies, waits for them, and re-layouts  3.76 us (4%)
  between operations  1 us (1%)
    pallas_call x33, Pallas kernels, __call__(): pl.pallas_call(kernel, out_shape=out_shape, name=name, in_specs=in_specs,...  33.5 us
    ppermute x34, starting transfers between devices, send(): return lax.ppermute(x, 'blk', [(i, i ^ mask) for i in range(n)])  25.6 us
    ppermute x34, waiting for transfers between devices, send(): return lax.ppermute(x, 'blk', [(i, i ^ mask) for i in range(n)])  21.9 us
    ppermute x5, starting transfers between devices, score(): lax.ppermute(part, 'dim', [(i, (i + s) % depth) for i in range(depth)])  5.84 us
    unnamed x14, local copies, waits for them, and re-layouts  3.76 us
    ppermute x5, waiting for transfers between devices, score(): lax.ppermute(part, 'dim', [(i, (i + s) % depth) for i in range(depth)])  2.07 us
  transfers between devices with their start and end apart: 39, of which 15 were waited for; matrix products, arithmetic and copies ran while one was open for 0% of the time, Pallas kernels for 32%

profile of v4, /device:TPU:0, one launch (start us, length us, event | category | flops | bytes accessed | tf_op | source)
XLA Modules:
  0.0 93.7 jit_solution(6390683009291466418)
XLA Ops:
  0.6 1.8 %pack.1.refs_1_.refs_3_.refs_2_ = f32[392,128]{1,0:T(8,128)} custom-call(f32[128,384]{1,0:T(8,128)} %refs_0_.7, s32[8,128]{1,0:T(8,128)} %bitcast.3, s32[8,128]{1,0:T(8,128)} %bitcast.4), custom_call_target="tpu_custom_call" | custom-call | bytes 6660000 | tf_op jit(solution)/shard_map/pack/pallas_call | solution.py:45
  2.9 2.6 %collective-permute-start.4 = (f32[392,128]{1,0:T(8,128)}, f32[392,128]{1,0:T(8,128)S(1)}, u32[]{:S(2)}, u32[]{:S(2)}) collective-permute-start(f32[392,128]{1,0:T(8,128)} %pack.1.refs_1_.refs_3_.refs_2_), channel_id=1, source_target_pairs={{0,4},{2,6},{4,0},{6,2},{8,12},{10,14},{12,8},{14,10},{16,20},{18,... | collective-permute-start | bytes 602120 | tf_op jit(solution)/shard_map/ppermute | solution.py:265
  5.5 2.6 %collective-permute-start.3 = (f32[392,128]{1,0:T(8,128)}, f32[392,128]{1,0:T(8,128)S(1)}, u32[]{:S(2)}, u32[]{:S(2)}) collective-permute-start(f32[392,128]{1,0:T(8,128)} %pack.1.refs_1_.refs_3_.refs_2_), channel_id=1, source_target_pairs={{0,16},{2,18},{4,20},{6,22},{8,24},{10,26},{12,28},{14,30},{16,0},... | collective-permute-start | bytes 602120 | tf_op jit(solution)/shard_map/ppermute | solution.py:265
  8.1 1.6 %collective-permute-start.2 = (f32[392,128]{1,0:T(8,128)}, f32[392,128]{1,0:T(8,128)S(1)}, u32[]{:S(2)}, u32[]{:S(2)}) collective-permute-start(f32[392,128]{1,0:T(8,128)} %pack.1.refs_1_.refs_3_.refs_2_), channel_id=1, source_target_pairs={{0,8},{2,10},{4,12},{6,14},{8,0},{10,2},{12,4},{14,6},{16,24},{18,... | collective-permute-start | bytes 602120 | tf_op jit(solution)/shard_map/ppermute | solution.py:265
  11.7 1.9 %copy-done = f32[384,2048]{1,0:T(8,128)S(1)} copy-done((f32[384,2048]{1,0:T(8,128)S(1)}, f32[384,2048]{1,0:T(8,128)}, u32[]{:S(2)}) %copy-start) | copy-done | bytes 3145752
  13.5 1.9 %score.5 = (f32[2,136,128]{2,1,0:T(8,128)S(1)}, f32[2,384,128]{2,1,0:T(8,128)S(1)}) custom-call(s32[1]{0:T(128)} %bitcast.2.refs_0_, f32[128,384]{1,0:T(8,128)S(1)} %copy-done.2, f32[384,2048]{1,0:T(8,128)S(1)} %copy-done, f32[392,128]{1,0:T(8,128)S(1)} %copy-done.4, f32[392,128]{1,0:T(8,128)S(1)} %collective-permute-done.refs_4_.refs_6_, ...), custom_call_target="tpu_custom_call" | custom-call | bytes 6660000 | tf_op jit(solution)/shard_map/score/pallas_call | solution.py:45
  15.5 1.6 %collective-permute-start.1 = (f32[2,136,128]{2,1,0:T(8,128)S(1)}, f32[2,136,128]{2,1,0:T(8,128)S(1)}, u32[]{:S(2)}, u32[]{:S(2)}) collective-permute-start(f32[2,136,128]{2,1,0:T(8,128)S(1)} %get-tuple-element.40.refs_2_), channel_id=1, source_target_pairs={{0,1},{1,0},{2,3},{3,2},{4,5},{5,4},{6,7},{7,6},{8,9},{9,8},{10,11... | collective-permute-start | bytes 417800 | tf_op jit(solution)/shard_map/ppermute | solution.py:305
  22.0 4.2 %collective-permute-done.13.refs_0_ = f32[392,128]{1,0:T(8,128)S(1)} collective-permute-done((f32[392,128]{1,0:T(8,128)S(1)}, f32[392,128]{1,0:T(8,128)S(1)}, u32[]{:S(2)}, u32[]{:S(2)}) %collective-permute-start.13) | collective-permute-done | bytes 200736 | tf_op jit(solution)/shard_map/ppermute | solution.py:265
  26.8 2.9 %score.6 = (f32[3,136,128]{2,1,0:T(8,128)S(1)}, f32[3,384,128]{2,1,0:T(8,128)S(1)}) custom-call(s32[1]{0:T(128)} %bitcast.2.refs_0_, f32[128,384]{1,0:T(8,128)S(1)} %copy-done.3, f32[384,2048]{1,0:T(8,128)S(1)} %copy-done.1, f32[392,128]{1,0:T(8,128)S(1)} %relay.7.refs_1_.refs_3_, f32[392,128]{1,0:T(8,128)S(1)} %relay.8.refs_4_, ...), custom_call_target="tpu_custom_call" | custom-call | bytes 9990000 | tf_op jit(solution)/shard_map/score/pallas_call | solution.py:45
  29.7 1.6 %collective-permute-start.6 = (f32[3,136,128]{2,1,0:T(8,128)S(1)}, f32[3,136,128]{2,1,0:T(8,128)S(1)}, u32[]{:S(2)}, u32[]{:S(2)}) collective-permute-start(f32[3,136,128]{2,1,0:T(8,128)S(1)} %get-tuple-element.45.refs_2_), channel_id=1, source_target_pairs={{0,1},{1,0},{2,3},{3,2},{4,5},{5,4},{6,7},{7,6},{8,9},{9,8},{10,11... | collective-permute-start | bytes 626696 | tf_op jit(solution)/shard_map/ppermute | solution.py:305
  32.5 2.8 %score.7 = (f32[3,136,128]{2,1,0:T(8,128)S(1)}, f32[3,384,128]{2,1,0:T(8,128)S(1)}) custom-call(s32[1]{0:T(128)} %bitcast.2.refs_0_, f32[128,384]{1,0:T(8,128)S(1)} %copy-done.3, f32[384,2048]{1,0:T(8,128)S(1)} %copy-done.1, f32[392,128]{1,0:T(8,128)S(1)} %collective-permute-done.7.refs_3_.refs_10_, f32[392,128]{1,0:T(8,128)S(1)} %collective-permute-done.8.refs_4_.refs_11_, ...), custom_call_target="tpu_custom_call" | custom-call | bytes 9990000 | tf_op jit(solution)/shard_map/score/pallas_call | solution.py:45
  38.1 4.0 %score.8 = (f32[4,136,128]{2,1,0:T(8,128)S(1)}, f32[4,384,128]{2,1,0:T(8,128)S(1)}) custom-call(s32[1]{0:T(128)} %bitcast.2.refs_0_, f32[128,384]{1,0:T(8,128)S(1)} %copy-done.3, f32[384,2048]{1,0:T(8,128)S(1)} %copy-done.1, f32[392,128]{1,0:T(8,128)S(1)} %relay.9.refs_1_.refs_3_.refs_8_, f32[392,128]{1,0:T(8,128)S(1)} %relay.11.refs_4_.refs_7_.refs_9_, ...), custom_call_target="tpu_custom_call" | custom-call | bytes 13320000 | tf_op jit(solution)/shard_map/score/pallas_call | solution.py:45
  42.1 2.0 %collective-permute-start.21 = (f32[4,136,128]{2,1,0:T(8,128)S(1)}, f32[4,136,128]{2,1,0:T(8,128)S(1)}, u32[]{:S(2)}, u32[]{:S(2)}) collective-permute-start(f32[4,136,128]{2,1,0:T(8,128)S(1)} %get-tuple-element.54.refs_2_), channel_id=1, source_target_pairs={{0,1},{1,0},{2,3},{3,2},{4,5},{5,4},{6,7},{7,6},{8,9},{9,8},{10,11... | collective-permute-start | bytes 835592 | tf_op jit(solution)/shard_map/ppermute | solution.py:305
  45.8 3.8 %score.9 = (f32[4,136,128]{2,1,0:T(8,128)S(1)}, f32[4,384,128]{2,1,0:T(8,128)S(1)}) custom-call(s32[1]{0:T(128)} %bitcast.2.refs_0_, f32[128,384]{1,0:T(8,128)S(1)} %copy-done.3, f32[384,2048]{1,0:T(8,128)S(1)} %copy-done.1, f32[392,128]{1,0:T(8,128)S(1)} %relay.10.refs_6_.refs_3_.refs_7_, f32[392,128]{1,0:T(8,128)S(1)} %collective-permute-done.17.refs_4_.refs_13_, ...), custom_call_target="tpu_custom_call" | custom-call | bytes 13320000 | tf_op jit(solution)/shard_map/score/pallas_call | solution.py:45
  53.4 5.9 %collective-permute-done.20.refs_2_ = f32[392,128]{1,0:T(8,128)S(1)} collective-permute-done((f32[392,128]{1,0:T(8,128)S(1)}, f32[392,128]{1,0:T(8,128)S(1)}, u32[]{:S(2)}, u32[]{:S(2)}) %collective-permute-start.20) | collective-permute-done | bytes 200736 | tf_op jit(solution)/shard_map/ppermute | solution.py:265
  62.7 1.6 %collective-permute-start.28 = (f32[2,16,128]{2,1,0:T(8,128)S(1)}, f32[2,16,128]{2,1,0:T(8,128)S(1)}, u32[]{:S(2)}, u32[]{:S(2)}) collective-permute-start(f32[2,16,128]{2,1,0:T(8,128)S(1)} %stats_merge.4.refs_2_.refs_0_), channel_id=1, source_target_pairs={{0,4},{2,6},{4,0},{6,2},{8,12},{10,14},{12,8},{14,10},{16,20},{18,... | collective-permute-start | bytes 49160 | tf_op jit(solution)/shard_map/ppermute | solution.py:265
  65.1 3.9 %collective-permute-done.28.refs_1_ = f32[2,16,128]{2,1,0:T(8,128)S(1)} collective-permute-done((f32[2,16,128]{2,1,0:T(8,128)S(1)}, f32[2,16,128]{2,1,0:T(8,128)S(1)}, u32[]{:S(2)}, u32[]{:S(2)}) %collective-permute-start.28) | collective-permute-done | bytes 16416 | tf_op jit(solution)/shard_map/ppermute | solution.py:265
  69.5 1.5 %collective-permute-start.33 = (f32[2,16,128]{2,1,0:T(8,128)S(1)}, f32[2,16,128]{2,1,0:T(8,128)S(1)}, u32[]{:S(2)}, u32[]{:S(2)}) collective-permute-start(f32[2,16,128]{2,1,0:T(8,128)S(1)} %stats_merge.5.refs_3_.refs_0_), channel_id=1, source_target_pairs={{0,8},{2,10},{4,12},{6,14},{8,0},{10,2},{12,4},{14,6},{16,24},{18,... | collective-permute-start | bytes 49160 | tf_op jit(solution)/shard_map/ppermute | solution.py:265
  71.1 2.2 %collective-permute-done.33.refs_1_ = f32[2,16,128]{2,1,0:T(8,128)S(1)} collective-permute-done((f32[2,16,128]{2,1,0:T(8,128)S(1)}, f32[2,16,128]{2,1,0:T(8,128)S(1)}, u32[]{:S(2)}, u32[]{:S(2)}) %collective-permute-start.33) | collective-permute-done | bytes 16416 | tf_op jit(solution)/shard_map/ppermute | solution.py:265
  73.3 1.8 %collective-permute-start.37 = (f32[2,16,128]{2,1,0:T(8,128)S(1)}, f32[2,16,128]{2,1,0:T(8,128)S(1)}, u32[]{:S(2)}, u32[]{:S(2)}) collective-permute-start(f32[2,16,128]{2,1,0:T(8,128)S(1)} %stats_merge.6.refs_3_.refs_0_), channel_id=1, source_target_pairs={{0,16},{2,18},{4,20},{6,22},{8,24},{10,26},{12,28},{14,30},{16,0},... | collective-permute-start | bytes 49160 | tf_op jit(solution)/shard_map/ppermute | solution.py:265
  76.4 1.5 %collective-permute-start.34 = (f32[392,128]{1,0:T(8,128)S(1)}, f32[392,128]{1,0:T(8,128)S(1)}, u32[]{:S(2)}, u32[]{:S(2)}) collective-permute-start(f32[392,128]{1,0:T(8,128)S(1)} %merge.14.refs_2_), channel_id=1, source_target_pairs={{0,8},{2,10},{4,12},{6,14},{8,0},{10,2},{12,4},{14,6},{16,24},{18,... | collective-permute-start | bytes 602120 | tf_op jit(solution)/shard_map/ppermute | solution.py:265
  77.9 2.0 %collective-permute-done.37.refs_1_ = f32[2,16,128]{2,1,0:T(8,128)S(1)} collective-permute-done((f32[2,16,128]{2,1,0:T(8,128)S(1)}, f32[2,16,128]{2,1,0:T(8,128)S(1)}, u32[]{:S(2)}, u32[]{:S(2)}) %collective-permute-start.37) | collective-permute-done | bytes 16416 | tf_op jit(solution)/shard_map/ppermute | solution.py:265
  80.1 1.6 %collective-permute-start.38 = (f32[392,128]{1,0:T(8,128)S(1)}, f32[392,128]{1,0:T(8,128)S(1)}, u32[]{:S(2)}, u32[]{:S(2)}) collective-permute-start(f32[392,128]{1,0:T(8,128)S(1)} %merge.15.refs_23_), channel_id=1, source_target_pairs={{0,24},{2,26},{4,28},{6,30},{8,16},{10,18},{12,20},{14,22},{16,8},... | collective-permute-start | bytes 602120 | tf_op jit(solution)/shard_map/ppermute | solution.py:265
  81.7 11.1 %gradient.1 = (f32[128,384]{1,0:T(8,128)}, f32[384,2048]{1,0:T(8,128)}) custom-call(f32[128,384]{1,0:T(8,128)S(1)} %copy-done.6, f32[2,16,128]{2,1,0:T(8,128)S(1)} %stats_merge.7.refs_3_.refs_6_.refs_1_, f32[392,128]{1,0:T(8,128)S(1)} %copy-done.5, f32[392,128]{1,0:T(8,128)S(1)} %relay.7.refs_1_.refs_3_, f32[392,128]{1,0:T(8,128)S(1)} %relay.8.refs_4_, ...), custom_call_target="tpu_custom_call" | custom-call | bytes 40700000 | tf_op jit(solution)/shard_map/gradient/pallas_call | solution.py:45
  (101 shorter events, 24.4 us)
Async XLA Ops:
  2.4 9.2 %collective-permute-start = (f32[392,128]{1,0:T(8,128)}, f32[392,128]{1,0:T(8,128)S(1)}, u32[]{:S(2)}, u32[]{:S(2)}) collective-permute-start(f32[392,128]{1,0:T(8,128)} %pack.1.refs_1_.refs_3_.refs_2_), channel_id=1, source_target_pairs={{0,2},{2,0},{4,6},{6,4},{8,10},{10,8},{12,14},{14,12},{16,18},{18,... | collective-permute-start | bytes 602120 | tf_op jit(solution)/shard_map/ppermute | solution.py:265
  2.9 14.1 %collective-permute-start.4 = (f32[392,128]{1,0:T(8,128)}, f32[392,128]{1,0:T(8,128)S(1)}, u32[]{:S(2)}, u32[]{:S(2)}) collective-permute-start(f32[392,128]{1,0:T(8,128)} %pack.1.refs_1_.refs_3_.refs_2_), channel_id=1, source_target_pairs={{0,4},{2,6},{4,0},{6,2},{8,12},{10,14},{12,8},{14,10},{16,20},{18,... | collective-permute-start | bytes 602120 | tf_op jit(solution)/shard_map/ppermute | solution.py:265
  5.5 12.6 %collective-permute-start.3 = (f32[392,128]{1,0:T(8,128)}, f32[392,128]{1,0:T(8,128)S(1)}, u32[]{:S(2)}, u32[]{:S(2)}) collective-permute-start(f32[392,128]{1,0:T(8,128)} %pack.1.refs_1_.refs_3_.refs_2_), channel_id=1, source_target_pairs={{0,16},{2,18},{4,20},{6,22},{8,24},{10,26},{12,28},{14,30},{16,0},... | collective-permute-start | bytes 602120 | tf_op jit(solution)/shard_map/ppermute | solution.py:265
  8.1 10.2 %collective-permute-start.2 = (f32[392,128]{1,0:T(8,128)}, f32[392,128]{1,0:T(8,128)S(1)}, u32[]{:S(2)}, u32[]{:S(2)}) collective-permute-start(f32[392,128]{1,0:T(8,128)} %pack.1.refs_1_.refs_3_.refs_2_), channel_id=1, source_target_pairs={{0,8},{2,10},{4,12},{6,14},{8,0},{10,2},{12,4},{14,6},{16,24},{18,... | collective-permute-start | bytes 602120 | tf_op jit(solution)/shard_map/ppermute | solution.py:265
  18.3 8.0 %collective-permute-start.13 = (f32[392,128]{1,0:T(8,128)S(1)}, f32[392,128]{1,0:T(8,128)S(1)}, u32[]{:S(2)}, u32[]{:S(2)}) collective-permute-start(f32[392,128]{1,0:T(8,128)S(1)} %relay.8.refs_4_), channel_id=1, source_target_pairs={{0,4},{2,6},{4,0},{6,2},{8,12},{10,14},{12,8},{14,10},{16,20},{18,... | collective-permute-start | bytes 602120 | tf_op jit(solution)/shard_map/ppermute | solution.py:265
  18.8 10.8 %collective-permute-start.11 = (f32[392,128]{1,0:T(8,128)S(1)}, f32[392,128]{1,0:T(8,128)S(1)}, u32[]{:S(2)}, u32[]{:S(2)}) collective-permute-start(f32[392,128]{1,0:T(8,128)S(1)} %relay.7.refs_1_.refs_3_), channel_id=1, source_target_pairs={{0,4},{2,6},{4,0},{6,2},{8,12},{10,14},{12,8},{14,10},{16,20},{18,... | collective-permute-start | bytes 602120 | tf_op jit(solution)/shard_map/ppermute | solution.py:265
  20.4 10.9 %collective-permute-start.8 = (f32[392,128]{1,0:T(8,128)S(1)}, f32[392,128]{1,0:T(8,128)S(1)}, u32[]{:S(2)}, u32[]{:S(2)}) collective-permute-start(f32[392,128]{1,0:T(8,128)S(1)} %relay.8.refs_4_), channel_id=1, source_target_pairs={{0,2},{2,0},{4,6},{6,4},{8,10},{10,8},{12,14},{14,12},{16,18},{18,... | collective-permute-start | bytes 602120 | tf_op jit(solution)/shard_map/ppermute | solution.py:265
  20.4 11.2 %collective-permute-start.10 = (f32[392,128]{1,0:T(8,128)S(1)}, f32[392,128]{1,0:T(8,128)S(1)}, u32[]{:S(2)}, u32[]{:S(2)}) collective-permute-start(f32[392,128]{1,0:T(8,128)S(1)} %relay.7.refs_1_.refs_3_), channel_id=1, source_target_pairs={{0,8},{2,10},{4,12},{6,14},{8,0},{10,2},{12,4},{14,6},{16,24},{18,... | collective-permute-start | bytes 602120 | tf_op jit(solution)/shard_map/ppermute | solution.py:265
  21.8 10.1 %collective-permute-start.9 = (f32[392,128]{1,0:T(8,128)S(1)}, f32[392,128]{1,0:T(8,128)S(1)}, u32[]{:S(2)}, u32[]{:S(2)}) collective-permute-start(f32[392,128]{1,0:T(8,128)S(1)} %relay.7.refs_1_.refs_3_), channel_id=1, source_target_pairs={{0,2},{2,0},{4,6},{6,4},{8,10},{10,8},{12,14},{14,12},{16,18},{18,... | collective-permute-start | bytes 602120 | tf_op jit(solution)/shard_map/ppermute | solution.py:265
  29.7 7.6 %collective-permute-start.6 = (f32[3,136,128]{2,1,0:T(8,128)S(1)}, f32[3,136,128]{2,1,0:T(8,128)S(1)}, u32[]{:S(2)}, u32[]{:S(2)}) collective-permute-start(f32[3,136,128]{2,1,0:T(8,128)S(1)} %get-tuple-element.45.refs_2_), channel_id=1, source_target_pairs={{0,1},{1,0},{2,3},{3,2},{4,5},{5,4},{6,7},{7,6},{8,9},{9,8},{10,11... | collective-permute-start | bytes 626696 | tf_op jit(solution)/shard_map/ppermute | solution.py:305
  31.3 6.8 %collective-permute-start.15 = (f32[392,128]{1,0:T(8,128)S(1)}, f32[392,128]{1,0:T(8,128)S(1)}, u32[]{:S(2)}, u32[]{:S(2)}) collective-permute-start(f32[392,128]{1,0:T(8,128)S(1)} %collective-permute-done.13.refs_0_), channel_id=1, source_target_pairs={{0,2},{2,0},{4,6},{6,4},{8,10},{10,8},{12,14},{14,12},{16,18},{18,... | collective-permute-start | bytes 602120 | tf_op jit(solution)/shard_map/ppermute | solution.py:265
  31.9 12.1 %collective-permute-start.17 = (f32[392,128]{1,0:T(8,128)S(1)}, f32[392,128]{1,0:T(8,128)S(1)}, u32[]{:S(2)}, u32[]{:S(2)}) collective-permute-start(f32[392,128]{1,0:T(8,128)S(1)} %relay.10.refs_6_.refs_3_.refs_7_), channel_id=1, source_target_pairs={{0,4},{2,6},{4,0},{6,2},{8,12},{10,14},{12,8},{14,10},{16,20},{18,... | collective-permute-start | bytes 602120 | tf_op jit(solution)/shard_map/ppermute | solution.py:265
  35.4 9.2 %collective-permute-start.12 = (f32[3,136,128]{2,1,0:T(8,128)S(1)}, f32[3,136,128]{2,1,0:T(8,128)S(1)}, u32[]{:S(2)}, u32[]{:S(2)}) collective-permute-start(f32[3,136,128]{2,1,0:T(8,128)S(1)} %get-tuple-element.48.refs_2_), channel_id=1, source_target_pairs={{0,1},{1,0},{2,3},{3,2},{4,5},{5,4},{6,7},{7,6},{8,9},{9,8},{10,11... | collective-permute-start | bytes 626696 | tf_op jit(solution)/shard_map/ppermute | solution.py:305
  42.1 8.4 %collective-permute-start.21 = (f32[4,136,128]{2,1,0:T(8,128)S(1)}, f32[4,136,128]{2,1,0:T(8,128)S(1)}, u32[]{:S(2)}, u32[]{:S(2)}) collective-permute-start(f32[4,136,128]{2,1,0:T(8,128)S(1)} %get-tuple-element.54.refs_2_), channel_id=1, source_target_pairs={{0,1},{1,0},{2,3},{3,2},{4,5},{5,4},{6,7},{7,6},{8,9},{9,8},{10,11... | collective-permute-start | bytes 835592 | tf_op jit(solution)/shard_map/ppermute | solution.py:305
  49.6 9.9 %collective-permute-start.26 = (f32[4,136,128]{2,1,0:T(8,128)S(1)}, f32[4,136,128]{2,1,0:T(8,128)S(1)}, u32[]{:S(2)}, u32[]{:S(2)}) collective-permute-start(f32[4,136,128]{2,1,0:T(8,128)S(1)} %get-tuple-element.62.refs_2_), channel_id=1, source_target_pairs={{0,1},{1,0},{2,3},{3,2},{4,5},{5,4},{6,7},{7,6},{8,9},{9,8},{10,11... | collective-permute-start | bytes 835592 | tf_op jit(solution)/shard_map/ppermute | solution.py:305
  52.0 7.3 %collective-permute-start.20 = (f32[392,128]{1,0:T(8,128)S(1)}, f32[392,128]{1,0:T(8,128)S(1)}, u32[]{:S(2)}, u32[]{:S(2)}) collective-permute-start(f32[392,128]{1,0:T(8,128)S(1)} %merge.8.refs_4_), channel_id=1, source_target_pairs={{0,4},{2,6},{4,0},{6,2},{8,12},{10,14},{12,8},{14,10},{16,20},{18,... | collective-permute-start | bytes 602120 | tf_op jit(solution)/shard_map/ppermute | solution.py:265
  60.9 8.6 %collective-permute-start.25 = (f32[392,128]{1,0:T(8,128)S(1)}, f32[392,128]{1,0:T(8,128)S(1)}, u32[]{:S(2)}, u32[]{:S(2)}) collective-permute-start(f32[392,128]{1,0:T(8,128)S(1)} %merge.9.refs_2_), channel_id=1, source_target_pairs={{0,4},{2,6},{4,0},{6,2},{8,12},{10,14},{12,8},{14,10},{16,20},{18,... | collective-permute-start | bytes 602120 | tf_op jit(solution)/shard_map/ppermute | solution.py:265
  64.3 10.8 %collective-permute-start.31 = (f32[392,128]{1,0:T(8,128)S(1)}, f32[392,128]{1,0:T(8,128)S(1)}, u32[]{:S(2)}, u32[]{:S(2)}) collective-permute-start(f32[392,128]{1,0:T(8,128)S(1)} %get-tuple-element.67), channel_id=1, source_target_pairs={{0,2},{2,0},{4,6},{6,4},{8,10},{10,8},{12,14},{14,12},{16,18},{18,... | collective-permute-start | bytes 602120 | tf_op jit(solution)/shard_map/ppermute | solution.py:265
  64.3 12.0 %collective-permute-start.32 = (f32[392,128]{1,0:T(8,128)S(1)}, f32[392,128]{1,0:T(8,128)S(1)}, u32[]{:S(2)}, u32[]{:S(2)}) collective-permute-start(f32[392,128]{1,0:T(8,128)S(1)} %merge.10.refs_3_), channel_id=1, source_target_pairs={{0,4},{2,6},{4,0},{6,2},{8,12},{10,14},{12,8},{14,10},{16,20},{18,... | collective-permute-start | bytes 602120 | tf_op jit(solution)/shard_map/ppermute | solution.py:265
  64.8 15.2 %collective-permute-start.35 = (f32[392,128]{1,0:T(8,128)S(1)}, f32[392,128]{1,0:T(8,128)S(1)}, u32[]{:S(2)}, u32[]{:S(2)}) collective-permute-start(f32[392,128]{1,0:T(8,128)S(1)} %get-tuple-element.69), channel_id=1, source_target_pairs={{0,2},{2,0},{4,6},{6,4},{8,10},{10,8},{12,14},{14,12},{16,18},{18,... | collective-permute-start | bytes 602120 | tf_op jit(solution)/shard_map/ppermute | solution.py:265
  69.0 11.0 %collective-permute-start.36 = (f32[392,128]{1,0:T(8,128)S(1)}, f32[392,128]{1,0:T(8,128)S(1)}, u32[]{:S(2)}, u32[]{:S(2)}) collective-permute-start(f32[392,128]{1,0:T(8,128)S(1)} %merge.12.refs_2_), channel_id=1, source_target_pairs={{0,4},{2,6},{4,0},{6,2},{8,12},{10,14},{12,8},{14,10},{16,20},{18,... | collective-permute-start | bytes 602120 | tf_op jit(solution)/shard_map/ppermute | solution.py:265
  75.1 17.7 %collective-permute-start.30 = (f32[392,128]{1,0:T(8,128)S(1)}, f32[392,128]{1,0:T(8,128)S(1)}, u32[]{:S(2)}, u32[]{:S(2)}) collective-permute-start(f32[392,128]{1,0:T(8,128)S(1)} %merge.13.refs_2_), channel_id=1, source_target_pairs={{0,16},{2,18},{4,20},{6,22},{8,24},{10,26},{12,28},{14,30},{16,0},... | collective-permute-start | bytes 602120 | tf_op jit(solution)/shard_map/ppermute | solution.py:265
  76.4 16.4 %collective-permute-start.34 = (f32[392,128]{1,0:T(8,128)S(1)}, f32[392,128]{1,0:T(8,128)S(1)}, u32[]{:S(2)}, u32[]{:S(2)}) collective-permute-start(f32[392,128]{1,0:T(8,128)S(1)} %merge.14.refs_2_), channel_id=1, source_target_pairs={{0,8},{2,10},{4,12},{6,14},{8,0},{10,2},{12,4},{14,6},{16,24},{18,... | collective-permute-start | bytes 602120 | tf_op jit(solution)/shard_map/ppermute | solution.py:265
  80.1 12.7 %collective-permute-start.38 = (f32[392,128]{1,0:T(8,128)S(1)}, f32[392,128]{1,0:T(8,128)S(1)}, u32[]{:S(2)}, u32[]{:S(2)}) collective-permute-start(f32[392,128]{1,0:T(8,128)S(1)} %merge.15.refs_23_), channel_id=1, source_target_pairs={{0,24},{2,26},{4,28},{6,30},{8,16},{10,18},{12,20},{14,22},{16,8},... | collective-permute-start | bytes 602120 | tf_op jit(solution)/shard_map/ppermute | solution.py:265
  (22 other events, 132.7 us)

commit v5 on v4

--- a/solution.py
+++ b/solution.py
@@ -74,7 +74,8 @@
 
 
 def relay_body(*refs):
-    refs[1][...] = refs[0][...]
+    for k, ref in enumerate(refs[:-1]):
+        refs[-1][k] = ref[...]
 
 
 def flip_body(d_ref, dt_ref):
@@ -113,7 +114,7 @@
         part_ref[k, :rows] = scores[:, k * rows : (k + 1) * rows]
 
 
-def softmax_body(others, dt_ref, rows_ref, part_ref, *refs):
+def softmax_body(evens, others, dt_ref, rows_ref, part_ref, *refs):
     got, (e_ref, *sum_refs) = refs[:others], refs[others:]
     features, rows = dt_ref.shape
     count = part_ref.shape[0]
@@ -142,7 +143,7 @@
     e = es[0] if count == 1 else jnp.concatenate(es, axis=1)
     sums = dot(dt_ref[...], e, precision=lax.Precision.HIGHEST)
     for k, (hard_e, peak, total) in enumerate(tails):
-        at = sum_refs[k]
+        at = sum_refs[k] if k < evens else sum_refs[-1].at[k - evens]
         at[:features] = sums[:, k * rows : (k + 1) * rows] + rows_ref[k] * hard_e
         at[features:] = jnp.concatenate([peak, total, jnp.zeros((SLACK - 2, rows), f32)], axis=0)
 
@@ -159,9 +160,9 @@
     return sums, peak, total
 
 
-def merge_body(*refs):
+def merge_body(places, *refs):
     out_ref = refs[-1]
-    sums, peak, total = merge([ref[...] for ref in refs[:-1]])
+    sums, peak, total = merge([r[...] if k is None else r[k] for r, k in zip(refs, places)])
     size = sums.shape[0]
     out_ref[:size] = sums
     out_ref[size:] = jnp.concatenate(
@@ -202,14 +203,17 @@
 
 def gradient_body(x_places, e_places, group, *refs):
     n = len(x_places)
-    q_ref, tot_ref = refs[:2]
+    tot_ref = refs[0]
     dd_ref, pool_ref, scaled_ref, local_ref = refs[-4:]
-    rows, features = q_ref.shape
+    rows, features = dd_ref.shape
     lanes = local_ref.shape[-1]
 
     @pl.when(pl.program_id(0) == 0)
     def _():
-        total = jnp.zeros((rows, features), f32)
+        own = lax.broadcasted_iota(jnp.int32, (rows, rows), 0) == lax.broadcasted_iota(
+            jnp.int32, (rows, rows), 1
+        )
+        total = jnp.zeros((features, rows), f32)
         for g in range(n // group):
             xs, es, hards = [], [], []
             for r in range(g * group, (g + 1) * group):
@@ -218,18 +222,23 @@
                 i, k = e_places[r]
                 scale = jnp.exp(refs[i][k, rows + 2 : rows + 3] - tot_ref[0, r : r + 1])
                 scale = scale / tot_ref[1, r : r + 1]
-                es.append(refs[i][k, :rows] * scale)
+                e = refs[i][k, :rows] * scale
+                es.append(e if r else jnp.where(own, e - 1.0, e))
                 hards.append(refs[i][k, rows : rows + 1] * scale)
                 chosen = jnp.broadcast_to(refs[i][k, rows + 1 : rows + 2], (lanes, rows))
                 first = (r - g * group) * rows
                 local_ref[g, first : first + rows] = chosen.T.astype(jnp.int32)
             x = jnp.concatenate(xs, axis=1)
             chance = jnp.concatenate(es, axis=1)
-            total = total + dot(chance, x, ((1,), (1,)), precision=lax.Precision.HIGHEST)
+            high, low = split2(x)
+            c_high, c_low = split2(chance)
+            both = dot(jnp.concatenate([high, low], axis=0), c_high, ((1,), (1,)))
+            total = total + both[:features] + both[features:]
+            total = total + dot(high, c_low, ((1,), (1,)))
             high, low = split2(x * (jnp.concatenate(hards, axis=1) / logit_divisor))
             scaled_ref[g, :features] = high
             scaled_ref[g, features:] = low
-        dd_ref[...] = (total - q_ref[...]) / logit_divisor
+        dd_ref[...] = total.T / logit_divisor
 
     width = pool_ref.shape[1]
     first = pl.program_id(0) * width
@@ -267,13 +276,17 @@
     far = n // 4
     x, x_arrays, x_place = {}, [], {}
 
-    def keep(array, r):
-        x[r] = array
-        x_place[r] = (len(x_arrays), None)
+    def keep(array, *blocks):
+        for k, r in enumerate(blocks):
+            x[r] = array
+            x_place[r] = (len(x_arrays), k if array.ndim == 3 else None)
         x_arrays.append(array)
 
+    def pass_on(array):
+        return line(lambda a, out: out.__setitem__(..., a[...]), block, "relay", [array], 0.05)
+
     def relay(r):
-        x_arrays[x_place[r][0]] = x[r] = line(relay_body, block, "relay", [x[r]], 0.05)
+        x_arrays[x_place[r][0]] = x[r] = pass_on(x[r])
 
     def forward(k):
         relay(4 * k)
@@ -284,6 +297,11 @@
     def share(*blocks):
         for r in blocks:
             keep(send(x[r], 1), r + 1)
+
+    def share_all(*blocks):
+        out = shape(len(blocks), features + SLACK, rows)
+        held = line(relay_body, out, "relay", [x[r] for r in blocks], 0.05)
+        keep(send(held, 1), *[r + 1 for r in blocks])
 
     weights, sums, e_place = [], {}, {}
     waiting, stage = [], {}
@@ -310,9 +328,13 @@
     def softmax():
         blocks, part, found, got = waiting.pop(0)
         k = len(blocks)
+        odds = [r for r in blocks if r % 2]
+        evens = k - len(odds)
         e, *out = line(
-            functools.partial(softmax_body, len(got)),
-            [shape(k, rows + SLACK, rows)] + [block] * k,
+            functools.partial(softmax_body, evens, len(got)),
+            [shape(k, rows + SLACK, rows)]
+            + [block] * evens
+            + [shape(len(odds), features + SLACK, rows)] * (len(odds) > 0),
             "softmax",
             [dt, found, part, *got],
             0.25 * k,
@@ -320,19 +342,29 @@
         for i, r in enumerate(blocks):
             e_place[r] = (len(weights), i)
         weights.append(e)
-        for r, array in zip(blocks, out):
-            sums[r] = send(array, 1) if r % 2 else array
+        for r, array in zip(blocks, out[:evens]):
+            sums[r] = (array, None)
+        if odds:
+            shared = send(out[-1], 1)
+            for i, r in enumerate(odds):
+                sums[r] = (shared, i)
 
     over_x, home = {}, []
 
     def add(*terms):
-        return line(merge_body, block, "merge", list(terms), 0.05)
+        arrays = [array for array, k in terms]
+        places = [k for array, k in terms]
+        return line(functools.partial(merge_body, places), block, "merge", arrays, 0.05)
+
+    def pair(*blocks):
+        for r in blocks:
+            sums[r] = (add(sums[r], sums[r + 1]), None)
 
     def beside(k):
-        over_x[k] = send(add(sums[4 * k + 2], sums[4 * k + 3]), 2)
+        over_x[k] = send(sums[4 * k + 2][0], 2)
 
     def inward(k):
-        whole = add(sums[4 * k], sums[4 * k + 1], over_x[k])
+        whole = add(sums[4 * k], (over_x[k], None))
         home.append(send(whole, 4 * k) if k else whole)
 
     packed = line(
@@ -357,35 +389,40 @@
     keep(send(packed, 1), 1)
     dt = line(flip_body, shape(features, rows), "flip", [document_matrix], 0.1)
     score([0, 1])
-    relay(2)
     forward(2)
     forward(1)
-    share(2, 4, 8)
+    relay(2)
+    share_all(2, 4, 8)
     softmax()
     score([2, 4, 8])
     relay(10)
-    if far > 3:
-        forward(3)
+    forward(3)
+    score([3, 5, 9])
+    relay(6)
     share(10, 6)
-    score([3, 5, 9])
     softmax()
-    relay(6)
     score([10, 6, 11, 7])
+    relay(14)
+    share(12, 14)
     softmax()
     for k in range(3, far):
         if k + 1 < far:
             forward(k + 1)
-        share(4 * k, 4 * k + 2)
         score([4 * k, 4 * k + 2, 4 * k + 1, 4 * k + 3])
+        if k + 1 < far:
+            relay(4 * k + 6)
+            share(4 * k + 4, 4 * k + 6)
         if k == 3:
-            beside(0)
+            pair(0, 2, 4, 8)
         softmax()
         if k == 3:
+            pair(10)
             beside(2)
+            pair(6)
             beside(1)
         else:
+            pair(4 * k - 2, 4 * k - 4)
             beside(k - 1)
-    inward(0)
     softmax()
 
     totals = line(
@@ -404,6 +441,8 @@
     mask = 1
     while mask < n:
         there = send(totals, mask)
+        if mask == 1:
+            inward(2)
         totals = line(
             functools.partial(stats_merge_body, [mask]),
             shape(2, n, rows),
@@ -411,30 +450,31 @@
             [totals, there],
             0.05,
         )
-        if mask == 2 and far > 3:
-            inward(2)
-        if mask == 1:
+        if mask == 2:
+            inward(1)
+            pair(4 * far - 2)
             beside(far - 1)
+            beside(0)
+            pair(4 * far - 4)
         if mask == 4:
-            inward(1)
-            for k in range(3, far - 1):
+            for k in range(3, far):
                 inward(k)
         mask *= 2
-    inward(far - 1)
+    sums[0] = (add(sums[0], (home.pop(0), None)), None)
 
     group = 4
     width = 512
-    e_at = 2 + len(x_arrays)
+    e_at = 1 + len(x_arrays)
     document_derivative, grad_pool = line(
         functools.partial(
             gradient_body,
-            [(x_place[r][0] + 2, x_place[r][1]) for r in range(n)],
+            [(x_place[r][0] + 1, x_place[r][1]) for r in range(n)],
             [(e_at + e_place[r][0], e_place[r][1]) for r in range(n)],
             group,
         ),
         (shape(rows, features), shape(features, columns)),
         "gradient",
-        [question_matrix, totals, *x_arrays, *weights],
+        [totals, *x_arrays, *weights],
         11.0,
         limit=48,
         grid=(columns // width,),
@@ -446,6 +486,7 @@
     )
 
     line.last = totals
+    inward(0)
     arrays = home
     question_derivative, loss = line(
         last_body,

time: 93.9 us -> 109 us (1.16)
  waiting for transfers between devices: 24 us -> 37.1 us
  local copies, waits for them, and re-layouts: 3.76 us -> 5.61 us
  starting transfers between devices: 31.4 us -> 32.9 us
  Pallas kernels: 33.5 us -> 32.4 us
    ppermute x5, waiting for transfers between devices: 2.07 us -> 12.7 us  [score(): lax.ppermute(part, 'dim', [(i, (i + s) % depth) for i in range(depth)])]
    ppermute x34 -> x28, waiting for transfers between devices: 21.9 us -> 24.4 us  [send(): return lax.ppermute(x, 'blk', [(i, i ^ mask) for i in range(n)])]
    unnamed x14 -> x16, local copies, waits for them, and re-layouts: 3.76 us -> 5.61 us
    pallas_call x33 -> x40, Pallas kernels: 33.5 us -> 32.4 us  [__call__(): pl.pallas_call(kernel, out_shape=out_shape, name=name, in_specs=in_specs,...]
    ppermute x34 -> x28, starting transfers between devices: 25.6 us -> 26.1 us  [send(): return lax.ppermute(x, 'blk', [(i, i ^ mask) for i in range(n)])]
  transfers between devices with their start and end apart: 39 -> 33, of which waited for: 15 -> 11; matrix products, arithmetic and copies ran while one was open for 0% -> 0% of each run, Pallas kernels for 32% -> 25%
where the time goes in v5:
time: 109 us
  waiting for transfers between devices  37.1 us (34%)
  starting transfers between devices  32.9 us (30%)
  Pallas kernels  32.4 us (30%)
  local copies, waits for them, and re-layouts  5.61 us (5%)
  between operations  1.13 us (1%)
    pallas_call x40, Pallas kernels, __call__(): pl.pallas_call(kernel, out_shape=out_shape, name=name, in_specs=in_specs,...  32.4 us
    ppermute x28, starting transfers between devices, send(): return lax.ppermute(x, 'blk', [(i, i ^ mask) for i in range(n)])  26.1 us
    ppermute x28, waiting for transfers between devices, send(): return lax.ppermute(x, 'blk', [(i, i ^ mask) for i in range(n)])  24.4 us
    ppermute x5, waiting for transfers between devices, score(): lax.ppermute(part, 'dim', [(i, (i + s) % depth) for i in range(depth)])  12.7 us
    ppermute x5, starting transfers between devices, score(): lax.ppermute(part, 'dim', [(i, (i + s) % depth) for i in range(depth)])  6.85 us
    unnamed x16, local copies, waits for them, and re-layouts  5.61 us
  transfers between devices with their start and end apart: 33, of which 11 were waited for; matrix products, arithmetic and copies ran while one was open for 0% of the time, Pallas kernels for 25%

profile of v5, /device:TPU:0, one launch (start us, length us, event | category | flops | bytes accessed | tf_op | source)
XLA Modules:
  0.0 109.2 jit_solution(6271940511278393359)
XLA Ops:
  0.6 1.8 %pack.1.refs_1_.refs_3_ = f32[392,128]{1,0:T(8,128)} custom-call(f32[128,384]{1,0:T(8,128)} %refs_0_.3, s32[8,128]{1,0:T(8,128)} %bitcast.3, s32[8,128]{1,0:T(8,128)} %bitcast.4), custom_call_target="tpu_custom_call" | custom-call | bytes 6660000 | tf_op jit(solution)/shard_map/pack/pallas_call | solution.py:45
  2.9 3.7 %collective-permute-start.4 = (f32[392,128]{1,0:T(8,128)}, f32[392,128]{1,0:T(8,128)S(1)}, u32[]{:S(2)}, u32[]{:S(2)}) collective-permute-start(f32[392,128]{1,0:T(8,128)} %pack.1.refs_1_.refs_3_), channel_id=1, source_target_pairs={{0,16},{2,18},{4,20},{6,22},{8,24},{10,26},{12,28},{14,30},{16,0},... | collective-permute-start | bytes 602120 | tf_op jit(solution)/shard_map/ppermute | solution.py:274
  6.6 1.6 %collective-permute-start.3 = (f32[392,128]{1,0:T(8,128)}, f32[392,128]{1,0:T(8,128)S(1)}, u32[]{:S(2)}, u32[]{:S(2)}) collective-permute-start(f32[392,128]{1,0:T(8,128)} %pack.1.refs_1_.refs_3_), channel_id=1, source_target_pairs={{0,8},{2,10},{4,12},{6,14},{8,0},{10,2},{12,4},{14,6},{16,24},{18,... | collective-permute-start | bytes 602120 | tf_op jit(solution)/shard_map/ppermute | solution.py:274
  11.7 1.9 %copy-done = f32[384,2048]{1,0:T(8,128)S(1)} copy-done((f32[384,2048]{1,0:T(8,128)S(1)}, f32[384,2048]{1,0:T(8,128)}, u32[]{:S(2)}) %copy-start) | copy-done | bytes 3145752
  15.4 2.0 %score.5 = (f32[2,136,128]{2,1,0:T(8,128)S(1)}, f32[2,384,128]{2,1,0:T(8,128)S(1)}) custom-call(s32[1]{0:T(128)} %bitcast.2.refs_0_, f32[128,384]{1,0:T(8,128)S(1)} %copy-done.3, f32[384,2048]{1,0:T(8,128)S(1)} %copy-done, f32[392,128]{1,0:T(8,128)S(1)} %copy-done.6, f32[392,128]{1,0:T(8,128)S(1)} %collective-permute-done.refs_4_.refs_5_, ...), custom_call_target="tpu_custom_call" | custom-call | bytes 6660000 | tf_op jit(solution)/shard_map/score/pallas_call | solution.py:45
  22.3 3.7 %collective-permute-done.1.refs_3_ = f32[2,136,128]{2,1,0:T(8,128)S(1)} collective-permute-done((f32[2,136,128]{2,1,0:T(8,128)S(1)}, f32[2,136,128]{2,1,0:T(8,128)S(1)}, u32[]{:S(2)}, u32[]{:S(2)}) %collective-permute-start.1) | collective-permute-done | bytes 139296 | tf_op jit(solution)/shard_map/ppermute | solution.py:323
  26.5 2.8 %score.6 = (f32[3,136,128]{2,1,0:T(8,128)S(1)}, f32[3,384,128]{2,1,0:T(8,128)S(1)}) custom-call(s32[1]{0:T(128)} %bitcast.2.refs_0_, f32[128,384]{1,0:T(8,128)S(1)} %copy-done.4, f32[384,2048]{1,0:T(8,128)S(1)} %copy-done.1, f32[392,128]{1,0:T(8,128)S(1)} %relay.8.refs_1_.refs_2_.refs_3_, f32[392,128]{1,0:T(8,128)S(1)} %relay.9.refs_1_.refs_4_.refs_3_, ...), custom_call_target="tpu_custom_call" | custom-call | bytes 9990000 | tf_op jit(solution)/shard_map/score/pallas_call | solution.py:45
  29.3 1.6 %collective-permute-start.5 = (f32[3,136,128]{2,1,0:T(8,128)S(1)}, f32[3,136,128]{2,1,0:T(8,128)S(1)}, u32[]{:S(2)}, u32[]{:S(2)}) collective-permute-start(f32[3,136,128]{2,1,0:T(8,128)S(1)} %get-tuple-element.40.refs_2_), channel_id=1, source_target_pairs={{0,1},{1,0},{2,3},{3,2},{4,5},{5,4},{6,7},{7,6},{8,9},{9,8},{10,11... | collective-permute-start | bytes 626696 | tf_op jit(solution)/shard_map/ppermute | solution.py:323
  31.0 2.8 %score.7 = (f32[3,136,128]{2,1,0:T(8,128)S(1)}, f32[3,384,128]{2,1,0:T(8,128)S(1)}) custom-call(s32[1]{0:T(128)} %bitcast.2.refs_0_, f32[128,384]{1,0:T(8,128)S(1)} %copy-done.4, f32[384,2048]{1,0:T(8,128)S(1)} %copy-done.1, f32[3,392,128]{2,1,0:T(8,128)S(1)} %collective-permute-done.7.refs_3_.refs_9_, f32[392,128]{1,0:T(8,128)S(1)} %relay.13.refs_4_.refs_3_.refs_6_), custom_call_target="tpu_custom_call" | custom-call | bytes 9990000 | tf_op jit(solution)/shard_map/score/pallas_call | solution.py:45
  37.2 4.0 %score.8 = (f32[4,136,128]{2,1,0:T(8,128)S(1)}, f32[4,384,128]{2,1,0:T(8,128)S(1)}) custom-call(s32[1]{0:T(128)} %bitcast.2.refs_0_, f32[128,384]{1,0:T(8,128)S(1)} %copy-done.4, f32[384,2048]{1,0:T(8,128)S(1)} %copy-done.1, f32[392,128]{1,0:T(8,128)S(1)} %relay.12.refs_1_.refs_3_.refs_7_, f32[392,128]{1,0:T(8,128)S(1)} %relay.14.refs_4_.refs_8_, ...), custom_call_target="tpu_custom_call" | custom-call | bytes 13320000 | tf_op jit(solution)/shard_map/score/pallas_call | solution.py:45
  42.8 1.6 %collective-permute-start.18 = (f32[4,136,128]{2,1,0:T(8,128)S(1)}, f32[4,136,128]{2,1,0:T(8,128)S(1)}, u32[]{:S(2)}, u32[]{:S(2)}) collective-permute-start(f32[4,136,128]{2,1,0:T(8,128)S(1)} %get-tuple-element.50.refs_2_), channel_id=1, source_target_pairs={{0,1},{1,0},{2,3},{3,2},{4,5},{5,4},{6,7},{7,6},{8,9},{9,8},{10,11... | collective-permute-start | bytes 835592 | tf_op jit(solution)/shard_map/ppermute | solution.py:323
  46.1 3.8 %score.9 = (f32[4,136,128]{2,1,0:T(8,128)S(1)}, f32[4,384,128]{2,1,0:T(8,128)S(1)}) custom-call(s32[1]{0:T(128)} %bitcast.2.refs_0_, f32[128,384]{1,0:T(8,128)S(1)} %copy-done.4, f32[384,2048]{1,0:T(8,128)S(1)} %copy-done.1, f32[392,128]{1,0:T(8,128)S(1)} %relay.13.refs_4_.refs_3_.refs_6_, f32[392,128]{1,0:T(8,128)S(1)} %relay.15.refs_4_.refs_10_, ...), custom_call_target="tpu_custom_call" | custom-call | bytes 13320000 | tf_op jit(solution)/shard_map/score/pallas_call | solution.py:45
  50.1 1.7 %collective-permute-done.18.refs_3_ = f32[4,136,128]{2,1,0:T(8,128)S(1)} collective-permute-done((f32[4,136,128]{2,1,0:T(8,128)S(1)}, f32[4,136,128]{2,1,0:T(8,128)S(1)}, u32[]{:S(2)}, u32[]{:S(2)}) %collective-permute-start.18) | collective-permute-done | bytes 278560 | tf_op jit(solution)/shard_map/ppermute | solution.py:323
  52.8 1.6 %collective-permute-start.21 = (f32[4,136,128]{2,1,0:T(8,128)S(1)}, f32[4,136,128]{2,1,0:T(8,128)S(1)}, u32[]{:S(2)}, u32[]{:S(2)}) collective-permute-start(f32[4,136,128]{2,1,0:T(8,128)S(1)} %get-tuple-element.57.refs_2_), channel_id=1, source_target_pairs={{0,1},{1,0},{2,3},{3,2},{4,5},{5,4},{6,7},{7,6},{8,9},{9,8},{10,11... | collective-permute-start | bytes 835592 | tf_op jit(solution)/shard_map/ppermute | solution.py:323
  54.6 7.3 %collective-permute-done.21.refs_3_ = f32[4,136,128]{2,1,0:T(8,128)S(1)} collective-permute-done((f32[4,136,128]{2,1,0:T(8,128)S(1)}, f32[4,136,128]{2,1,0:T(8,128)S(1)}, u32[]{:S(2)}, u32[]{:S(2)}) %collective-permute-start.21) | collective-permute-done | bytes 278560 | tf_op jit(solution)/shard_map/ppermute | solution.py:323
  62.9 1.6 %collective-permute-start.23 = (f32[392,128]{1,0:T(8,128)S(1)}, f32[392,128]{1,0:T(8,128)S(1)}, u32[]{:S(2)}, u32[]{:S(2)}) collective-permute-start(f32[392,128]{1,0:T(8,128)S(1)} %merge.17.refs_2_), channel_id=1, source_target_pairs={{0,4},{2,6},{4,0},{6,2},{8,12},{10,14},{12,8},{14,10},{16,20},{18,... | collective-permute-start | bytes 602120 | tf_op jit(solution)/shard_map/ppermute | solution.py:274
  65.1 5.7 %collective-permute-done.23.refs_1_ = f32[392,128]{1,0:T(8,128)S(1)} collective-permute-done((f32[392,128]{1,0:T(8,128)S(1)}, f32[392,128]{1,0:T(8,128)S(1)}, u32[]{:S(2)}, u32[]{:S(2)}) %collective-permute-start.23) | collective-permute-done | bytes 200736 | tf_op jit(solution)/shard_map/ppermute | solution.py:274
  70.8 1.6 %collective-permute-start.24 = (f32[2,16,128]{2,1,0:T(8,128)S(1)}, f32[2,16,128]{2,1,0:T(8,128)S(1)}, u32[]{:S(2)}, u32[]{:S(2)}) collective-permute-start(f32[2,16,128]{2,1,0:T(8,128)S(1)} %stats_merge.4.refs_0_.refs_2_), channel_id=1, source_target_pairs={{0,4},{2,6},{4,0},{6,2},{8,12},{10,14},{12,8},{14,10},{16,20},{18,... | collective-permute-start | bytes 49160 | tf_op jit(solution)/shard_map/ppermute | solution.py:274
  72.4 2.6 %collective-permute-done.24.refs_1_ = f32[2,16,128]{2,1,0:T(8,128)S(1)} collective-permute-done((f32[2,16,128]{2,1,0:T(8,128)S(1)}, f32[2,16,128]{2,1,0:T(8,128)S(1)}, u32[]{:S(2)}, u32[]{:S(2)}) %collective-permute-start.24) | collective-permute-done | bytes 16416 | tf_op jit(solution)/shard_map/ppermute | solution.py:274
  78.2 1.6 %collective-permute-start.30 = (f32[392,128]{1,0:T(8,128)S(1)}, f32[392,128]{1,0:T(8,128)S(1)}, u32[]{:S(2)}, u32[]{:S(2)}) collective-permute-start(f32[392,128]{1,0:T(8,128)S(1)} %merge.19.refs_2_), channel_id=1, source_target_pairs={{0,16},{2,18},{4,20},{6,22},{8,24},{10,26},{12,28},{14,30},{16,0},... | collective-permute-start | bytes 602120 | tf_op jit(solution)/shard_map/ppermute | solution.py:274
  79.8 1.7 %collective-permute-start.25 = (f32[392,128]{1,0:T(8,128)S(1)}, f32[392,128]{1,0:T(8,128)S(1)}, u32[]{:S(2)}, u32[]{:S(2)}) collective-permute-start(f32[392,128]{1,0:T(8,128)S(1)} %merge.20.refs_2_), channel_id=1, source_target_pairs={{0,8},{2,10},{4,12},{6,14},{8,0},{10,2},{12,4},{14,6},{16,24},{18,... | collective-permute-start | bytes 602120 | tf_op jit(solution)/shard_map/ppermute | solution.py:274
  83.1 2.1 %collective-permute-start.29 = (f32[392,128]{1,0:T(8,128)S(1)}, f32[392,128]{1,0:T(8,128)S(1)}, u32[]{:S(2)}, u32[]{:S(2)}) collective-permute-start(f32[392,128]{1,0:T(8,128)S(1)} %merge.23.refs_2_), channel_id=1, source_target_pairs={{0,24},{2,26},{4,28},{6,30},{8,16},{10,18},{12,20},{14,22},{16,8},... | collective-permute-start | bytes 602120 | tf_op jit(solution)/shard_map/ppermute | solution.py:274
  85.6 12.8 %collective-permute-done.31.refs_1_ = f32[2,16,128]{2,1,0:T(8,128)S(1)} collective-permute-done((f32[2,16,128]{2,1,0:T(8,128)S(1)}, f32[2,16,128]{2,1,0:T(8,128)S(1)}, u32[]{:S(2)}, u32[]{:S(2)}) %collective-permute-start.31) | collective-permute-done | bytes 16416 | tf_op jit(solution)/shard_map/ppermute | solution.py:274
  98.5 9.8 %gradient.1 = (f32[128,384]{1,0:T(8,128)}, f32[384,2048]{1,0:T(8,128)}) custom-call(f32[2,16,128]{2,1,0:T(8,128)S(1)} %stats_merge.7.refs_2_.refs_0_, f32[392,128]{1,0:T(8,128)S(1)} %copy-done.7, f32[392,128]{1,0:T(8,128)S(1)} %relay.8.refs_1_.refs_2_.refs_3_, f32[392,128]{1,0:T(8,128)S(1)} %relay.9.refs_1_.refs_4_.refs_3_, ...), custom_call_target="tpu_custom_call" | custom-call | bytes 40700000 | tf_op jit(solution)/shard_map/gradient/pallas_call | solution.py:45
  (98 shorter events, 26.9 us)
Async XLA Ops:
  2.4 9.2 %collective-permute-start = (f32[392,128]{1,0:T(8,128)}, f32[392,128]{1,0:T(8,128)S(1)}, u32[]{:S(2)}, u32[]{:S(2)}) collective-permute-start(f32[392,128]{1,0:T(8,128)} %pack.1.refs_1_.refs_3_), channel_id=1, source_target_pairs={{0,2},{2,0},{4,6},{6,4},{8,10},{10,8},{12,14},{14,12},{16,18},{18,... | collective-permute-start | bytes 602120 | tf_op jit(solution)/shard_map/ppermute | solution.py:274
  2.9 14.5 %collective-permute-start.4 = (f32[392,128]{1,0:T(8,128)}, f32[392,128]{1,0:T(8,128)S(1)}, u32[]{:S(2)}, u32[]{:S(2)}) collective-permute-start(f32[392,128]{1,0:T(8,128)} %pack.1.refs_1_.refs_3_), channel_id=1, source_target_pairs={{0,16},{2,18},{4,20},{6,22},{8,24},{10,26},{12,28},{14,30},{16,0},... | collective-permute-start | bytes 602120 | tf_op jit(solution)/shard_map/ppermute | solution.py:274
  6.6 10.8 %collective-permute-start.3 = (f32[392,128]{1,0:T(8,128)}, f32[392,128]{1,0:T(8,128)S(1)}, u32[]{:S(2)}, u32[]{:S(2)}) collective-permute-start(f32[392,128]{1,0:T(8,128)} %pack.1.refs_1_.refs_3_), channel_id=1, source_target_pairs={{0,8},{2,10},{4,12},{6,14},{8,0},{10,2},{12,4},{14,6},{16,24},{18,... | collective-permute-start | bytes 602120 | tf_op jit(solution)/shard_map/ppermute | solution.py:274
  8.2 9.3 %collective-permute-start.2 = (f32[392,128]{1,0:T(8,128)}, f32[392,128]{1,0:T(8,128)S(1)}, u32[]{:S(2)}, u32[]{:S(2)}) collective-permute-start(f32[392,128]{1,0:T(8,128)} %pack.1.refs_1_.refs_3_), channel_id=1, source_target_pairs={{0,4},{2,6},{4,0},{6,2},{8,12},{10,14},{12,8},{14,10},{16,20},{18,... | collective-permute-start | bytes 602120 | tf_op jit(solution)/shard_map/ppermute | solution.py:274
  17.5 13.4 %collective-permute-start.7 = (f32[3,392,128]{2,1,0:T(8,128)S(1)}, f32[3,392,128]{2,1,0:T(8,128)S(1)}, u32[]{:S(2)}, u32[]{:S(2)}) collective-permute-start(f32[3,392,128]{2,1,0:T(8,128)S(1)} %relay.11.refs_4_), channel_id=1, source_target_pairs={{0,2},{2,0},{4,6},{6,4},{8,10},{10,8},{12,14},{14,12},{16,18},{18,... | collective-permute-start | bytes 1806344 | tf_op jit(solution)/shard_map/ppermute | solution.py:274
  17.6 13.3 %collective-permute-start.9 = (f32[392,128]{1,0:T(8,128)S(1)}, f32[392,128]{1,0:T(8,128)S(1)}, u32[]{:S(2)}, u32[]{:S(2)}) collective-permute-start(f32[392,128]{1,0:T(8,128)S(1)} %relay.8.refs_1_.refs_2_.refs_3_), channel_id=1, source_target_pairs={{0,4},{2,6},{4,0},{6,2},{8,12},{10,14},{12,8},{14,10},{16,20},{18,... | collective-permute-start | bytes 602120 | tf_op jit(solution)/shard_map/ppermute | solution.py:274
  18.8 12.2 %collective-permute-start.8 = (f32[392,128]{1,0:T(8,128)S(1)}, f32[392,128]{1,0:T(8,128)S(1)}, u32[]{:S(2)}, u32[]{:S(2)}) collective-permute-start(f32[392,128]{1,0:T(8,128)S(1)} %relay.8.refs_1_.refs_2_.refs_3_), channel_id=1, source_target_pairs={{0,8},{2,10},{4,12},{6,14},{8,0},{10,2},{12,4},{14,6},{16,24},{18,... | collective-permute-start | bytes 602120 | tf_op jit(solution)/shard_map/ppermute | solution.py:274
  20.2 14.2 %collective-permute-start.6 = (f32[392,128]{1,0:T(8,128)S(1)}, f32[392,128]{1,0:T(8,128)S(1)}, u32[]{:S(2)}, u32[]{:S(2)}) collective-permute-start(f32[392,128]{1,0:T(8,128)S(1)} %relay.9.refs_1_.refs_4_.refs_3_), channel_id=1, source_target_pairs={{0,4},{2,6},{4,0},{6,2},{8,12},{10,14},{12,8},{14,10},{16,20},{18,... | collective-permute-start | bytes 602120 | tf_op jit(solution)/shard_map/ppermute | solution.py:274
  29.3 7.1 %collective-permute-start.5 = (f32[3,136,128]{2,1,0:T(8,128)S(1)}, f32[3,136,128]{2,1,0:T(8,128)S(1)}, u32[]{:S(2)}, u32[]{:S(2)}) collective-permute-start(f32[3,136,128]{2,1,0:T(8,128)S(1)} %get-tuple-element.40.refs_2_), channel_id=1, source_target_pairs={{0,1},{1,0},{2,3},{3,2},{4,5},{5,4},{6,7},{7,6},{8,9},{9,8},{10,11... | collective-permute-start | bytes 626696 | tf_op jit(solution)/shard_map/ppermute | solution.py:323
  33.8 8.2 %collective-permute-start.10 = (f32[3,136,128]{2,1,0:T(8,128)S(1)}, f32[3,136,128]{2,1,0:T(8,128)S(1)}, u32[]{:S(2)}, u32[]{:S(2)}) collective-permute-start(f32[3,136,128]{2,1,0:T(8,128)S(1)} %get-tuple-element.43.refs_2_), channel_id=1, source_target_pairs={{0,1},{1,0},{2,3},{3,2},{4,5},{5,4},{6,7},{7,6},{8,9},{9,8},{10,11... | collective-permute-start | bytes 626696 | tf_op jit(solution)/shard_map/ppermute | solution.py:323
  35.0 7.0 %collective-permute-start.11 = (f32[392,128]{1,0:T(8,128)S(1)}, f32[392,128]{1,0:T(8,128)S(1)}, u32[]{:S(2)}, u32[]{:S(2)}) collective-permute-start(f32[392,128]{1,0:T(8,128)S(1)} %relay.13.refs_4_.refs_3_.refs_6_), channel_id=1, source_target_pairs={{0,4},{2,6},{4,0},{6,2},{8,12},{10,14},{12,8},{14,10},{16,20},{18,... | collective-permute-start | bytes 602120 | tf_op jit(solution)/shard_map/ppermute | solution.py:274
  42.7 7.3 %collective-permute-start.14 = (f32[3,392,128]{2,1,0:T(8,128)S(1)}, f32[3,392,128]{2,1,0:T(8,128)S(1)}, u32[]{:S(2)}, u32[]{:S(2)}) collective-permute-start(f32[3,392,128]{2,1,0:T(8,128)S(1)} %get-tuple-element.46.refs_7_), channel_id=1, source_target_pairs={{0,2},{2,0},{4,6},{6,4},{8,10},{10,8},{12,14},{14,12},{16,18},{18,... | collective-permute-start | bytes 1806344 | tf_op jit(solution)/shard_map/ppermute | solution.py:274
  42.8 9.1 %collective-permute-start.18 = (f32[4,136,128]{2,1,0:T(8,128)S(1)}, f32[4,136,128]{2,1,0:T(8,128)S(1)}, u32[]{:S(2)}, u32[]{:S(2)}) collective-permute-start(f32[4,136,128]{2,1,0:T(8,128)S(1)} %get-tuple-element.50.refs_2_), channel_id=1, source_target_pairs={{0,1},{1,0},{2,3},{3,2},{4,5},{5,4},{6,7},{7,6},{8,9},{9,8},{10,11... | collective-permute-start | bytes 835592 | tf_op jit(solution)/shard_map/ppermute | solution.py:323
  52.8 9.1 %collective-permute-start.21 = (f32[4,136,128]{2,1,0:T(8,128)S(1)}, f32[4,136,128]{2,1,0:T(8,128)S(1)}, u32[]{:S(2)}, u32[]{:S(2)}) collective-permute-start(f32[4,136,128]{2,1,0:T(8,128)S(1)} %get-tuple-element.57.refs_2_), channel_id=1, source_target_pairs={{0,1},{1,0},{2,3},{3,2},{4,5},{5,4},{6,7},{7,6},{8,9},{9,8},{10,11... | collective-permute-start | bytes 835592 | tf_op jit(solution)/shard_map/ppermute | solution.py:323
  62.8 12.2 %collective-permute-start.26 = (f32[2,392,128]{2,1,0:T(8,128)S(1)}, f32[2,392,128]{2,1,0:T(8,128)S(1)}, u32[]{:S(2)}, u32[]{:S(2)}) collective-permute-start(f32[2,392,128]{2,1,0:T(8,128)S(1)} %get-tuple-element.59.refs_5_), channel_id=1, source_target_pairs={{0,2},{2,0},{4,6},{6,4},{8,10},{10,8},{12,14},{14,12},{16,18},{18,... | collective-permute-start | bytes 1204232 | tf_op jit(solution)/shard_map/ppermute | solution.py:274
  62.9 7.9 %collective-permute-start.23 = (f32[392,128]{1,0:T(8,128)S(1)}, f32[392,128]{1,0:T(8,128)S(1)}, u32[]{:S(2)}, u32[]{:S(2)}) collective-permute-start(f32[392,128]{1,0:T(8,128)S(1)} %merge.17.refs_2_), channel_id=1, source_target_pairs={{0,4},{2,6},{4,0},{6,2},{8,12},{10,14},{12,8},{14,10},{16,20},{18,... | collective-permute-start | bytes 602120 | tf_op jit(solution)/shard_map/ppermute | solution.py:274
  64.4 10.5 %collective-permute-start.20 = (f32[392,128]{1,0:T(8,128)S(1)}, f32[392,128]{1,0:T(8,128)S(1)}, u32[]{:S(2)}, u32[]{:S(2)}) collective-permute-start(f32[392,128]{1,0:T(8,128)S(1)} %merge.18.refs_4_), channel_id=1, source_target_pairs={{0,4},{2,6},{4,0},{6,2},{8,12},{10,14},{12,8},{14,10},{16,20},{18,... | collective-permute-start | bytes 602120 | tf_op jit(solution)/shard_map/ppermute | solution.py:274
  65.0 5.8 %collective-permute-start.22 = (f32[2,16,128]{2,1,0:T(8,128)S(1)}, f32[2,16,128]{2,1,0:T(8,128)S(1)}, u32[]{:S(2)}, u32[]{:S(2)}) collective-permute-start(f32[2,16,128]{2,1,0:T(8,128)S(1)} %stats.1.refs_2_.refs_0_), channel_id=1, source_target_pairs={{0,2},{2,0},{4,6},{6,4},{8,10},{10,8},{12,14},{14,12},{16,18},{18,... | collective-permute-start | bytes 49160 | tf_op jit(solution)/shard_map/ppermute | solution.py:274
  75.1 8.0 %collective-permute-start.27 = (f32[392,128]{1,0:T(8,128)S(1)}, f32[392,128]{1,0:T(8,128)S(1)}, u32[]{:S(2)}, u32[]{:S(2)}) collective-permute-start(f32[392,128]{1,0:T(8,128)S(1)} %merge.21.refs_2_), channel_id=1, source_target_pairs={{0,4},{2,6},{4,0},{6,2},{8,12},{10,14},{12,8},{14,10},{16,20},{18,... | collective-permute-start | bytes 602120 | tf_op jit(solution)/shard_map/ppermute | solution.py:274
  77.2 31.0 %collective-permute-start.32 = (f32[392,128]{1,0:T(8,128)S(1)}, f32[392,128]{1,0:T(8,128)S(1)}, u32[]{:S(2)}, u32[]{:S(2)}) collective-permute-start(f32[392,128]{1,0:T(8,128)S(1)} %merge.14.refs_2_), channel_id=1, source_target_pairs={{0,4},{2,6},{4,0},{6,2},{8,12},{10,14},{12,8},{14,10},{16,20},{18,... | collective-permute-start | bytes 602120 | tf_op jit(solution)/shard_map/ppermute | solution.py:274
  78.2 20.2 %collective-permute-start.30 = (f32[392,128]{1,0:T(8,128)S(1)}, f32[392,128]{1,0:T(8,128)S(1)}, u32[]{:S(2)}, u32[]{:S(2)}) collective-permute-start(f32[392,128]{1,0:T(8,128)S(1)} %merge.19.refs_2_), channel_id=1, source_target_pairs={{0,16},{2,18},{4,20},{6,22},{8,24},{10,26},{12,28},{14,30},{16,0},... | collective-permute-start | bytes 602120 | tf_op jit(solution)/shard_map/ppermute | solution.py:274
  79.8 28.5 %collective-permute-start.25 = (f32[392,128]{1,0:T(8,128)S(1)}, f32[392,128]{1,0:T(8,128)S(1)}, u32[]{:S(2)}, u32[]{:S(2)}) collective-permute-start(f32[392,128]{1,0:T(8,128)S(1)} %merge.20.refs_2_), channel_id=1, source_target_pairs={{0,8},{2,10},{4,12},{6,14},{8,0},{10,2},{12,4},{14,6},{16,24},{18,... | collective-permute-start | bytes 602120 | tf_op jit(solution)/shard_map/ppermute | solution.py:274
  83.1 25.2 %collective-permute-start.29 = (f32[392,128]{1,0:T(8,128)S(1)}, f32[392,128]{1,0:T(8,128)S(1)}, u32[]{:S(2)}, u32[]{:S(2)}) collective-permute-start(f32[392,128]{1,0:T(8,128)S(1)} %merge.23.refs_2_), channel_id=1, source_target_pairs={{0,24},{2,26},{4,28},{6,30},{8,16},{10,18},{12,20},{14,22},{16,8},... | collective-permute-start | bytes 602120 | tf_op jit(solution)/shard_map/ppermute | solution.py:274
  85.3 13.1 %collective-permute-start.31 = (f32[2,16,128]{2,1,0:T(8,128)S(1)}, f32[2,16,128]{2,1,0:T(8,128)S(1)}, u32[]{:S(2)}, u32[]{:S(2)}) collective-permute-start(f32[2,16,128]{2,1,0:T(8,128)S(1)} %stats_merge.6.refs_2_.refs_0_), channel_id=1, source_target_pairs={{0,16},{2,18},{4,20},{6,22},{8,24},{10,26},{12,28},{14,30},{16,0},... | collective-permute-start | bytes 49160 | tf_op jit(solution)/shard_map/ppermute | solution.py:274
  (17 other events, 87.0 us)

commit v6 on v5

--- a/solution.py
+++ b/solution.py
@@ -330,11 +330,12 @@
         k = len(blocks)
         odds = [r for r in blocks if r % 2]
         evens = k - len(odds)
+        stacked = len(odds) > 2
         e, *out = line(
-            functools.partial(softmax_body, evens, len(got)),
+            functools.partial(softmax_body, evens if stacked else k, len(got)),
             [shape(k, rows + SLACK, rows)]
-            + [block] * evens
-            + [shape(len(odds), features + SLACK, rows)] * (len(odds) > 0),
+            + [block] * (evens if stacked else k)
+            + [shape(len(odds), features + SLACK, rows)] * stacked,
             "softmax",
             [dt, found, part, *got],
             0.25 * k,
@@ -344,10 +345,9 @@
         weights.append(e)
         for r, array in zip(blocks, out[:evens]):
             sums[r] = (array, None)
-        if odds:
-            shared = send(out[-1], 1)
-            for i, r in enumerate(odds):
-                sums[r] = (shared, i)
+        shared = send(out[-1], 1) if stacked else None
+        for i, r in enumerate(odds):
+            sums[r] = (shared, i) if stacked else (send(out[evens + i], 1), None)
 
     over_x, home = {}, []
 
@@ -393,8 +393,8 @@
     forward(1)
     relay(2)
     share_all(2, 4, 8)
+    score([2, 4, 8])
     softmax()
-    score([2, 4, 8])
     relay(10)
     forward(3)
     score([3, 5, 9])
@@ -424,6 +424,7 @@
             pair(4 * k - 2, 4 * k - 4)
             beside(k - 1)
     softmax()
+    over_x[2] = pass_on(over_x[2])
 
     totals = line(
         functools.partial(stats_body, [e_place[r] for r in range(n)]),
@@ -438,11 +439,13 @@
         grid=(1,),
         out_specs=full(2, n, rows),
     )
-    mask = 1
-    while mask < n:
+    masks = [1] + [4 << i for i in reversed(range(far.bit_length() - 1))] + [2]
+    for mask in masks:
         there = send(totals, mask)
-        if mask == 1:
+        if mask == 2:
+            pair(4 * far - 4)
             inward(2)
+            inward(1)
         totals = line(
             functools.partial(stats_merge_body, [mask]),
             shape(2, n, rows),
@@ -450,17 +453,15 @@
             [totals, there],
             0.05,
         )
-        if mask == 2:
-            inward(1)
+        if mask == 2 * far:
+            over_x[1] = pass_on(over_x[1])
+        if mask == 1:
             pair(4 * far - 2)
             beside(far - 1)
-            beside(0)
-            pair(4 * far - 4)
-        if mask == 4:
-            for k in range(3, far):
-                inward(k)
-        mask *= 2
-    sums[0] = (add(sums[0], (home.pop(0), None)), None)
+    sums[2] = (pass_on(sums[2][0]), None)
+    beside(0)
+    for k in range(3, far):
+        inward(k)
 
     group = 4
     width = 512

time: 109 us -> 89.4 us (0.82)
  waiting for transfers between devices: 37.1 us -> 14.7 us
  starting transfers between devices: 32.9 us -> 35.4 us
    ppermute x28 -> x30, waiting for transfers between devices: 24.4 us -> 10.2 us  [send(): return lax.ppermute(x, 'blk', [(i, i ^ mask) for i in range(n)])]
    ppermute x5, waiting for transfers between devices: 12.7 us -> 4.56 us  [score(): lax.ppermute(part, 'dim', [(i, (i + s) % depth) for i in range(depth)])]
    ppermute x28 -> x30, starting transfers between devices: 26.1 us -> 29.3 us  [send(): return lax.ppermute(x, 'blk', [(i, i ^ mask) for i in range(n)])]
    pallas_call x40 -> x42, Pallas kernels: 32.4 us -> 32.3 us  [__call__(): pl.pallas_call(kernel, out_shape=out_shape, name=name, in_specs=in_specs,...]
  transfers between devices with their start and end apart: 33 -> 35, of which waited for: 11 -> 12; matrix products, arithmetic and copies ran while one was open for 0% -> 0% of each run, Pallas kernels for 25% -> 32%
where the time goes in v6:
time: 89.4 us; the launch traced here: 89.1 us
  starting transfers between devices  35.4 us (40%)
  Pallas kernels  32.3 us (36%)
  waiting for transfers between devices  14.7 us (16%)
  local copies, waits for them, and re-layouts  5.61 us (6%)
  between operations  1.08 us (1%)
    pallas_call x42, Pallas kernels, __call__(): pl.pallas_call(kernel, out_shape=out_shape, name=name, in_specs=in_specs,...  32.3 us
    ppermute x30, starting transfers between devices, send(): return lax.ppermute(x, 'blk', [(i, i ^ mask) for i in range(n)])  29.3 us
    ppermute x30, waiting for transfers between devices, send(): return lax.ppermute(x, 'blk', [(i, i ^ mask) for i in range(n)])  10.2 us
    ppermute x5, starting transfers between devices, score(): lax.ppermute(part, 'dim', [(i, (i + s) % depth) for i in range(depth)])  6.04 us
    unnamed x16, local copies, waits for them, and re-layouts  5.61 us
    ppermute x5, waiting for transfers between devices, score(): lax.ppermute(part, 'dim', [(i, (i + s) % depth) for i in range(depth)])  4.56 us
  transfers between devices with their start and end apart: 35, of which 12 were waited for; matrix products, arithmetic and copies ran while one was open for 0% of the time, Pallas kernels for 32%

profile of v6, /device:TPU:0, one launch (start us, length us, event | category | flops | bytes accessed | tf_op | source)
XLA Modules:
  0.0 89.1 jit_solution(4666295554232007101)
XLA Ops:
  0.6 1.8 %pack.1.refs_1_.refs_3_ = f32[392,128]{1,0:T(8,128)} custom-call(f32[128,384]{1,0:T(8,128)} %refs_0_.3, s32[8,128]{1,0:T(8,128)} %bitcast.3, s32[8,128]{1,0:T(8,128)} %bitcast.4), custom_call_target="tpu_custom_call" | custom-call | bytes 6660000 | tf_op jit(solution)/shard_map/pack/pallas_call | solution.py:45
  2.9 3.7 %collective-permute-start.2 = (f32[392,128]{1,0:T(8,128)}, f32[392,128]{1,0:T(8,128)S(1)}, u32[]{:S(2)}, u32[]{:S(2)}) collective-permute-start(f32[392,128]{1,0:T(8,128)} %pack.1.refs_1_.refs_3_), channel_id=1, source_target_pairs={{0,16},{2,18},{4,20},{6,22},{8,24},{10,26},{12,28},{14,30},{16,0},... | collective-permute-start | bytes 602120 | tf_op jit(solution)/shard_map/ppermute | solution.py:274
  6.6 1.6 %collective-permute-start.3 = (f32[392,128]{1,0:T(8,128)}, f32[392,128]{1,0:T(8,128)S(1)}, u32[]{:S(2)}, u32[]{:S(2)}) collective-permute-start(f32[392,128]{1,0:T(8,128)} %pack.1.refs_1_.refs_3_), channel_id=1, source_target_pairs={{0,8},{2,10},{4,12},{6,14},{8,0},{10,2},{12,4},{14,6},{16,24},{18,... | collective-permute-start | bytes 602120 | tf_op jit(solution)/shard_map/ppermute | solution.py:274
  8.2 1.5 %collective-permute-start.4 = (f32[392,128]{1,0:T(8,128)}, f32[392,128]{1,0:T(8,128)S(1)}, u32[]{:S(2)}, u32[]{:S(2)}) collective-permute-start(f32[392,128]{1,0:T(8,128)} %pack.1.refs_1_.refs_3_), channel_id=1, source_target_pairs={{0,4},{2,6},{4,0},{6,2},{8,12},{10,14},{12,8},{14,10},{16,20},{18,... | collective-permute-start | bytes 602120 | tf_op jit(solution)/shard_map/ppermute | solution.py:274
  11.7 1.9 %copy-done = f32[384,2048]{1,0:T(8,128)S(1)} copy-done((f32[384,2048]{1,0:T(8,128)S(1)}, f32[384,2048]{1,0:T(8,128)}, u32[]{:S(2)}) %copy-start) | copy-done | bytes 3145752
  15.4 2.0 %score.5 = (f32[2,136,128]{2,1,0:T(8,128)S(1)}, f32[2,384,128]{2,1,0:T(8,128)S(1)}) custom-call(s32[1]{0:T(128)} %bitcast.2.refs_0_, f32[128,384]{1,0:T(8,128)S(1)} %copy-done.3, f32[384,2048]{1,0:T(8,128)S(1)} %copy-done, f32[392,128]{1,0:T(8,128)S(1)} %copy-done.6, f32[392,128]{1,0:T(8,128)S(1)} %collective-permute-done.refs_4_.refs_5_, ...), custom_call_target="tpu_custom_call" | custom-call | bytes 6660000 | tf_op jit(solution)/shard_map/score/pallas_call | solution.py:45
  20.8 1.5 %collective-permute-start.1 = (f32[2,136,128]{2,1,0:T(8,128)S(1)}, f32[2,136,128]{2,1,0:T(8,128)S(1)}, u32[]{:S(2)}, u32[]{:S(2)}) collective-permute-start(f32[2,136,128]{2,1,0:T(8,128)S(1)} %get-tuple-element.38.refs_2_), channel_id=1, source_target_pairs={{0,1},{1,0},{2,3},{3,2},{4,5},{5,4},{6,7},{7,6},{8,9},{9,8},{10,11... | collective-permute-start | bytes 417800 | tf_op jit(solution)/shard_map/ppermute | solution.py:323
  22.3 2.8 %score.6 = (f32[3,136,128]{2,1,0:T(8,128)S(1)}, f32[3,384,128]{2,1,0:T(8,128)S(1)}) custom-call(s32[1]{0:T(128)} %bitcast.2.refs_0_, f32[128,384]{1,0:T(8,128)S(1)} %copy-done.4, f32[384,2048]{1,0:T(8,128)S(1)} %copy-done.1, f32[392,128]{1,0:T(8,128)S(1)} %relay.11.refs_1_.refs_2_.refs_3_, f32[392,128]{1,0:T(8,128)S(1)} %relay.12.refs_1_.refs_4_.refs_3_, ...), custom_call_target="tpu_custom_call" | custom-call | bytes 9990000 | tf_op jit(solution)/shard_map/score/pallas_call | solution.py:45
  25.9 1.5 %collective-permute-start.5 = (f32[3,136,128]{2,1,0:T(8,128)S(1)}, f32[3,136,128]{2,1,0:T(8,128)S(1)}, u32[]{:S(2)}, u32[]{:S(2)}) collective-permute-start(f32[3,136,128]{2,1,0:T(8,128)S(1)} %get-tuple-element.41.refs_2_), channel_id=1, source_target_pairs={{0,1},{1,0},{2,3},{3,2},{4,5},{5,4},{6,7},{7,6},{8,9},{9,8},{10,11... | collective-permute-start | bytes 626696 | tf_op jit(solution)/shard_map/ppermute | solution.py:323
  28.1 2.8 %score.7 = (f32[3,136,128]{2,1,0:T(8,128)S(1)}, f32[3,384,128]{2,1,0:T(8,128)S(1)}) custom-call(s32[1]{0:T(128)} %bitcast.2.refs_0_, f32[128,384]{1,0:T(8,128)S(1)} %copy-done.4, f32[384,2048]{1,0:T(8,128)S(1)} %copy-done.1, f32[3,392,128]{2,1,0:T(8,128)S(1)} %collective-permute-done.7.refs_3_.refs_9_, f32[392,128]{1,0:T(8,128)S(1)} %relay.16.refs_4_.refs_3_.refs_6_), custom_call_target="tpu_custom_call" | custom-call | bytes 9990000 | tf_op jit(solution)/shard_map/score/pallas_call | solution.py:45
  32.1 1.5 %collective-permute-start.11 = (f32[392,128]{1,0:T(8,128)S(1)}, f32[392,128]{1,0:T(8,128)S(1)}, u32[]{:S(2)}, u32[]{:S(2)}) collective-permute-start(f32[392,128]{1,0:T(8,128)S(1)} %relay.16.refs_4_.refs_3_.refs_6_), channel_id=1, source_target_pairs={{0,4},{2,6},{4,0},{6,2},{8,12},{10,14},{12,8},{14,10},{16,20},{18,... | collective-permute-start | bytes 602120 | tf_op jit(solution)/shard_map/ppermute | solution.py:274
  34.3 4.0 %score.8 = (f32[4,136,128]{2,1,0:T(8,128)S(1)}, f32[4,384,128]{2,1,0:T(8,128)S(1)}) custom-call(s32[1]{0:T(128)} %bitcast.2.refs_0_, f32[128,384]{1,0:T(8,128)S(1)} %copy-done.4, f32[384,2048]{1,0:T(8,128)S(1)} %copy-done.1, f32[392,128]{1,0:T(8,128)S(1)} %relay.15.refs_1_.refs_3_.refs_7_, f32[392,128]{1,0:T(8,128)S(1)} %relay.17.refs_4_.refs_8_, ...), custom_call_target="tpu_custom_call" | custom-call | bytes 13320000 | tf_op jit(solution)/shard_map/score/pallas_call | solution.py:45
  39.9 1.6 %collective-permute-start.18 = (f32[4,136,128]{2,1,0:T(8,128)S(1)}, f32[4,136,128]{2,1,0:T(8,128)S(1)}, u32[]{:S(2)}, u32[]{:S(2)}) collective-permute-start(f32[4,136,128]{2,1,0:T(8,128)S(1)} %get-tuple-element.52.refs_2_), channel_id=1, source_target_pairs={{0,1},{1,0},{2,3},{3,2},{4,5},{5,4},{6,7},{7,6},{8,9},{9,8},{10,11... | collective-permute-start | bytes 835592 | tf_op jit(solution)/shard_map/ppermute | solution.py:323
  43.2 3.8 %score.9 = (f32[4,136,128]{2,1,0:T(8,128)S(1)}, f32[4,384,128]{2,1,0:T(8,128)S(1)}) custom-call(s32[1]{0:T(128)} %bitcast.2.refs_0_, f32[128,384]{1,0:T(8,128)S(1)} %copy-done.4, f32[384,2048]{1,0:T(8,128)S(1)} %copy-done.1, f32[392,128]{1,0:T(8,128)S(1)} %relay.16.refs_4_.refs_3_.refs_6_, f32[392,128]{1,0:T(8,128)S(1)} %relay.18.refs_4_.refs_10_, ...), custom_call_target="tpu_custom_call" | custom-call | bytes 13320000 | tf_op jit(solution)/shard_map/score/pallas_call | solution.py:45
  51.4 1.6 %collective-permute-start.20 = (f32[392,128]{1,0:T(8,128)S(1)}, f32[392,128]{1,0:T(8,128)S(1)}, u32[]{:S(2)}, u32[]{:S(2)}) collective-permute-start(f32[392,128]{1,0:T(8,128)S(1)} %merge.16.refs_2_), channel_id=1, source_target_pairs={{0,4},{2,6},{4,0},{6,2},{8,12},{10,14},{12,8},{14,10},{16,20},{18,... | collective-permute-start | bytes 602120 | tf_op jit(solution)/shard_map/ppermute | solution.py:274
  53.0 2.8 %collective-permute-done.21.refs_3_ = f32[4,136,128]{2,1,0:T(8,128)S(1)} collective-permute-done((f32[4,136,128]{2,1,0:T(8,128)S(1)}, f32[4,136,128]{2,1,0:T(8,128)S(1)}, u32[]{:S(2)}, u32[]{:S(2)}) %collective-permute-start.21) | collective-permute-done | bytes 278560 | tf_op jit(solution)/shard_map/ppermute | solution.py:323
  56.8 1.6 %collective-permute-start.28 = (f32[392,128]{1,0:T(8,128)S(1)}, f32[392,128]{1,0:T(8,128)S(1)}, u32[]{:S(2)}, u32[]{:S(2)}) collective-permute-start(f32[392,128]{1,0:T(8,128)S(1)} %merge.17.refs_4_), channel_id=1, source_target_pairs={{0,4},{2,6},{4,0},{6,2},{8,12},{10,14},{12,8},{14,10},{16,20},{18,... | collective-permute-start | bytes 602120 | tf_op jit(solution)/shard_map/ppermute | solution.py:274
  59.9 1.6 %collective-permute-start.31 = (f32[392,128]{1,0:T(8,128)S(1)}, f32[392,128]{1,0:T(8,128)S(1)}, u32[]{:S(2)}, u32[]{:S(2)}) collective-permute-start(f32[392,128]{1,0:T(8,128)S(1)} %merge.18.refs_2_), channel_id=1, source_target_pairs={{0,4},{2,6},{4,0},{6,2},{8,12},{10,14},{12,8},{14,10},{16,20},{18,... | collective-permute-start | bytes 602120 | tf_op jit(solution)/shard_map/ppermute | solution.py:274
  61.4 2.4 %collective-permute-start.25 = (f32[2,16,128]{2,1,0:T(8,128)S(1)}, f32[2,16,128]{2,1,0:T(8,128)S(1)}, u32[]{:S(2)}, u32[]{:S(2)}) collective-permute-start(f32[2,16,128]{2,1,0:T(8,128)S(1)} %stats_merge.4.refs_2_.refs_0_), channel_id=1, source_target_pairs={{0,16},{2,18},{4,20},{6,22},{8,24},{10,26},{12,28},{14,30},{16,0},... | collective-permute-start | bytes 49160 | tf_op jit(solution)/shard_map/ppermute | solution.py:274
  63.8 2.5 %collective-permute-done.25.refs_1_ = f32[2,16,128]{2,1,0:T(8,128)S(1)} collective-permute-done((f32[2,16,128]{2,1,0:T(8,128)S(1)}, f32[2,16,128]{2,1,0:T(8,128)S(1)}, u32[]{:S(2)}, u32[]{:S(2)}) %collective-permute-start.25) | collective-permute-done | bytes 16416 | tf_op jit(solution)/shard_map/ppermute | solution.py:274
  66.9 3.2 %collective-permute-done.27.refs_1_ = f32[2,16,128]{2,1,0:T(8,128)S(1)} collective-permute-done((f32[2,16,128]{2,1,0:T(8,128)S(1)}, f32[2,16,128]{2,1,0:T(8,128)S(1)}, u32[]{:S(2)}, u32[]{:S(2)}) %collective-permute-start.27) | collective-permute-done | bytes 16416 | tf_op jit(solution)/shard_map/ppermute | solution.py:274
  70.6 2.4 %collective-permute-start.29 = (f32[392,128]{1,0:T(8,128)S(1)}, f32[392,128]{1,0:T(8,128)S(1)}, u32[]{:S(2)}, u32[]{:S(2)}) collective-permute-start(f32[392,128]{1,0:T(8,128)S(1)} %merge.20.refs_2_), channel_id=1, source_target_pairs={{0,16},{2,18},{4,20},{6,22},{8,24},{10,26},{12,28},{14,30},{16,0},... | collective-permute-start | bytes 602120 | tf_op jit(solution)/shard_map/ppermute | solution.py:274
  75.5 2.9 %collective-permute-start.33 = (f32[392,128]{1,0:T(8,128)S(1)}, f32[392,128]{1,0:T(8,128)S(1)}, u32[]{:S(2)}, u32[]{:S(2)}) collective-permute-start(f32[392,128]{1,0:T(8,128)S(1)} %merge.22.refs_20_), channel_id=1, source_target_pairs={{0,24},{2,26},{4,28},{6,30},{8,16},{10,18},{12,20},{14,22},{16,8},... | collective-permute-start | bytes 602120 | tf_op jit(solution)/shard_map/ppermute | solution.py:274
  78.4 9.7 %gradient.1 = (f32[128,384]{1,0:T(8,128)}, f32[384,2048]{1,0:T(8,128)}) custom-call(f32[2,16,128]{2,1,0:T(8,128)S(1)} %stats_merge.7.refs_1_.refs_2_.refs_0_, f32[392,128]{1,0:T(8,128)S(1)} %copy-done.7, f32[392,128]{1,0:T(8,128)S(1)} %relay.11.refs_1_.refs_2_.refs_3_, f32[392,128]{1,0:T(8,128)S(1)} %relay.12.refs_1_.refs_4_.refs_3_, ...), custom_call_target="tpu_custom_call" | custom-call | bytes 40700000 | tf_op jit(solution)/shard_map/gradient/pallas_call | solution.py:45
  (104 shorter events, 25.6 us)
Async XLA Ops:
  2.4 9.2 %collective-permute-start = (f32[392,128]{1,0:T(8,128)}, f32[392,128]{1,0:T(8,128)S(1)}, u32[]{:S(2)}, u32[]{:S(2)}) collective-permute-start(f32[392,128]{1,0:T(8,128)} %pack.1.refs_1_.refs_3_), channel_id=1, source_target_pairs={{0,2},{2,0},{4,6},{6,4},{8,10},{10,8},{12,14},{14,12},{16,18},{18,... | collective-permute-start | bytes 602120 | tf_op jit(solution)/shard_map/ppermute | solution.py:274
  2.9 14.4 %collective-permute-start.2 = (f32[392,128]{1,0:T(8,128)}, f32[392,128]{1,0:T(8,128)S(1)}, u32[]{:S(2)}, u32[]{:S(2)}) collective-permute-start(f32[392,128]{1,0:T(8,128)} %pack.1.refs_1_.refs_3_), channel_id=1, source_target_pairs={{0,16},{2,18},{4,20},{6,22},{8,24},{10,26},{12,28},{14,30},{16,0},... | collective-permute-start | bytes 602120 | tf_op jit(solution)/shard_map/ppermute | solution.py:274
  6.6 10.8 %collective-permute-start.3 = (f32[392,128]{1,0:T(8,128)}, f32[392,128]{1,0:T(8,128)S(1)}, u32[]{:S(2)}, u32[]{:S(2)}) collective-permute-start(f32[392,128]{1,0:T(8,128)} %pack.1.refs_1_.refs_3_), channel_id=1, source_target_pairs={{0,8},{2,10},{4,12},{6,14},{8,0},{10,2},{12,4},{14,6},{16,24},{18,... | collective-permute-start | bytes 602120 | tf_op jit(solution)/shard_map/ppermute | solution.py:274
  8.2 9.3 %collective-permute-start.4 = (f32[392,128]{1,0:T(8,128)}, f32[392,128]{1,0:T(8,128)S(1)}, u32[]{:S(2)}, u32[]{:S(2)}) collective-permute-start(f32[392,128]{1,0:T(8,128)} %pack.1.refs_1_.refs_3_), channel_id=1, source_target_pairs={{0,4},{2,6},{4,0},{6,2},{8,12},{10,14},{12,8},{14,10},{16,20},{18,... | collective-permute-start | bytes 602120 | tf_op jit(solution)/shard_map/ppermute | solution.py:274
  17.5 10.5 %collective-permute-start.7 = (f32[3,392,128]{2,1,0:T(8,128)S(1)}, f32[3,392,128]{2,1,0:T(8,128)S(1)}, u32[]{:S(2)}, u32[]{:S(2)}) collective-permute-start(f32[3,392,128]{2,1,0:T(8,128)S(1)} %relay.14.refs_6_), channel_id=1, source_target_pairs={{0,2},{2,0},{4,6},{6,4},{8,10},{10,8},{12,14},{14,12},{16,18},{18,... | collective-permute-start | bytes 1806344 | tf_op jit(solution)/shard_map/ppermute | solution.py:274
  17.6 10.4 %collective-permute-start.9 = (f32[392,128]{1,0:T(8,128)S(1)}, f32[392,128]{1,0:T(8,128)S(1)}, u32[]{:S(2)}, u32[]{:S(2)}) collective-permute-start(f32[392,128]{1,0:T(8,128)S(1)} %relay.11.refs_1_.refs_2_.refs_3_), channel_id=1, source_target_pairs={{0,4},{2,6},{4,0},{6,2},{8,12},{10,14},{12,8},{14,10},{16,20},{18,... | collective-permute-start | bytes 602120 | tf_op jit(solution)/shard_map/ppermute | solution.py:274
  18.8 9.2 %collective-permute-start.8 = (f32[392,128]{1,0:T(8,128)S(1)}, f32[392,128]{1,0:T(8,128)S(1)}, u32[]{:S(2)}, u32[]{:S(2)}) collective-permute-start(f32[392,128]{1,0:T(8,128)S(1)} %relay.11.refs_1_.refs_2_.refs_3_), channel_id=1, source_target_pairs={{0,8},{2,10},{4,12},{6,14},{8,0},{10,2},{12,4},{14,6},{16,24},{18,... | collective-permute-start | bytes 602120 | tf_op jit(solution)/shard_map/ppermute | solution.py:274
  20.2 11.2 %collective-permute-start.6 = (f32[392,128]{1,0:T(8,128)S(1)}, f32[392,128]{1,0:T(8,128)S(1)}, u32[]{:S(2)}, u32[]{:S(2)}) collective-permute-start(f32[392,128]{1,0:T(8,128)S(1)} %relay.12.refs_1_.refs_4_.refs_3_), channel_id=1, source_target_pairs={{0,4},{2,6},{4,0},{6,2},{8,12},{10,14},{12,8},{14,10},{16,20},{18,... | collective-permute-start | bytes 602120 | tf_op jit(solution)/shard_map/ppermute | solution.py:274
  20.8 5.2 %collective-permute-start.1 = (f32[2,136,128]{2,1,0:T(8,128)S(1)}, f32[2,136,128]{2,1,0:T(8,128)S(1)}, u32[]{:S(2)}, u32[]{:S(2)}) collective-permute-start(f32[2,136,128]{2,1,0:T(8,128)S(1)} %get-tuple-element.38.refs_2_), channel_id=1, source_target_pairs={{0,1},{1,0},{2,3},{3,2},{4,5},{5,4},{6,7},{7,6},{8,9},{9,8},{10,11... | collective-permute-start | bytes 417800 | tf_op jit(solution)/shard_map/ppermute | solution.py:323
  25.9 7.6 %collective-permute-start.5 = (f32[3,136,128]{2,1,0:T(8,128)S(1)}, f32[3,136,128]{2,1,0:T(8,128)S(1)}, u32[]{:S(2)}, u32[]{:S(2)}) collective-permute-start(f32[3,136,128]{2,1,0:T(8,128)S(1)} %get-tuple-element.41.refs_2_), channel_id=1, source_target_pairs={{0,1},{1,0},{2,3},{3,2},{4,5},{5,4},{6,7},{7,6},{8,9},{9,8},{10,11... | collective-permute-start | bytes 626696 | tf_op jit(solution)/shard_map/ppermute | solution.py:323
  30.9 8.2 %collective-permute-start.10 = (f32[3,136,128]{2,1,0:T(8,128)S(1)}, f32[3,136,128]{2,1,0:T(8,128)S(1)}, u32[]{:S(2)}, u32[]{:S(2)}) collective-permute-start(f32[3,136,128]{2,1,0:T(8,128)S(1)} %get-tuple-element.45.refs_2_), channel_id=1, source_target_pairs={{0,1},{1,0},{2,3},{3,2},{4,5},{5,4},{6,7},{7,6},{8,9},{9,8},{10,11... | collective-permute-start | bytes 626696 | tf_op jit(solution)/shard_map/ppermute | solution.py:323
  32.1 7.0 %collective-permute-start.11 = (f32[392,128]{1,0:T(8,128)S(1)}, f32[392,128]{1,0:T(8,128)S(1)}, u32[]{:S(2)}, u32[]{:S(2)}) collective-permute-start(f32[392,128]{1,0:T(8,128)S(1)} %relay.16.refs_4_.refs_3_.refs_6_), channel_id=1, source_target_pairs={{0,4},{2,6},{4,0},{6,2},{8,12},{10,14},{12,8},{14,10},{16,20},{18,... | collective-permute-start | bytes 602120 | tf_op jit(solution)/shard_map/ppermute | solution.py:274
  39.8 8.1 %collective-permute-start.14 = (f32[3,392,128]{2,1,0:T(8,128)S(1)}, f32[3,392,128]{2,1,0:T(8,128)S(1)}, u32[]{:S(2)}, u32[]{:S(2)}) collective-permute-start(f32[3,392,128]{2,1,0:T(8,128)S(1)} %get-tuple-element.47.refs_7_), channel_id=1, source_target_pairs={{0,2},{2,0},{4,6},{6,4},{8,10},{10,8},{12,14},{14,12},{16,18},{18,... | collective-permute-start | bytes 1806344 | tf_op jit(solution)/shard_map/ppermute | solution.py:274
  39.9 9.1 %collective-permute-start.18 = (f32[4,136,128]{2,1,0:T(8,128)S(1)}, f32[4,136,128]{2,1,0:T(8,128)S(1)}, u32[]{:S(2)}, u32[]{:S(2)}) collective-permute-start(f32[4,136,128]{2,1,0:T(8,128)S(1)} %get-tuple-element.52.refs_2_), channel_id=1, source_target_pairs={{0,1},{1,0},{2,3},{3,2},{4,5},{5,4},{6,7},{7,6},{8,9},{9,8},{10,11... | collective-permute-start | bytes 835592 | tf_op jit(solution)/shard_map/ppermute | solution.py:323
  41.9 5.9 %collective-permute-start.15 = (f32[392,128]{1,0:T(8,128)S(1)}, f32[392,128]{1,0:T(8,128)S(1)}, u32[]{:S(2)}, u32[]{:S(2)}) collective-permute-start(f32[392,128]{1,0:T(8,128)S(1)} %get-tuple-element.42.refs_1_), channel_id=1, source_target_pairs={{0,2},{2,0},{4,6},{6,4},{8,10},{10,8},{12,14},{14,12},{16,18},{18,... | collective-permute-start | bytes 602120 | tf_op jit(solution)/shard_map/ppermute | solution.py:274
  47.0 8.9 %collective-permute-start.21 = (f32[4,136,128]{2,1,0:T(8,128)S(1)}, f32[4,136,128]{2,1,0:T(8,128)S(1)}, u32[]{:S(2)}, u32[]{:S(2)}) collective-permute-start(f32[4,136,128]{2,1,0:T(8,128)S(1)} %get-tuple-element.56.refs_2_), channel_id=1, source_target_pairs={{0,1},{1,0},{2,3},{3,2},{4,5},{5,4},{6,7},{7,6},{8,9},{9,8},{10,11... | collective-permute-start | bytes 835592 | tf_op jit(solution)/shard_map/ppermute | solution.py:323
  51.4 7.1 %collective-permute-start.20 = (f32[392,128]{1,0:T(8,128)S(1)}, f32[392,128]{1,0:T(8,128)S(1)}, u32[]{:S(2)}, u32[]{:S(2)}) collective-permute-start(f32[392,128]{1,0:T(8,128)S(1)} %merge.16.refs_2_), channel_id=1, source_target_pairs={{0,4},{2,6},{4,0},{6,2},{8,12},{10,14},{12,8},{14,10},{16,20},{18,... | collective-permute-start | bytes 602120 | tf_op jit(solution)/shard_map/ppermute | solution.py:274
  56.8 10.0 %collective-permute-start.28 = (f32[392,128]{1,0:T(8,128)S(1)}, f32[392,128]{1,0:T(8,128)S(1)}, u32[]{:S(2)}, u32[]{:S(2)}) collective-permute-start(f32[392,128]{1,0:T(8,128)S(1)} %merge.17.refs_4_), channel_id=1, source_target_pairs={{0,4},{2,6},{4,0},{6,2},{8,12},{10,14},{12,8},{14,10},{16,20},{18,... | collective-permute-start | bytes 602120 | tf_op jit(solution)/shard_map/ppermute | solution.py:274
  58.7 11.8 %collective-permute-start.23 = (f32[392,128]{1,0:T(8,128)S(1)}, f32[392,128]{1,0:T(8,128)S(1)}, u32[]{:S(2)}, u32[]{:S(2)}) collective-permute-start(f32[392,128]{1,0:T(8,128)S(1)} %get-tuple-element.60), channel_id=1, source_target_pairs={{0,2},{2,0},{4,6},{6,4},{8,10},{10,8},{12,14},{14,12},{16,18},{18,... | collective-permute-start | bytes 602120 | tf_op jit(solution)/shard_map/ppermute | solution.py:274
  59.9 15.6 %collective-permute-start.31 = (f32[392,128]{1,0:T(8,128)S(1)}, f32[392,128]{1,0:T(8,128)S(1)}, u32[]{:S(2)}, u32[]{:S(2)}) collective-permute-start(f32[392,128]{1,0:T(8,128)S(1)} %merge.18.refs_2_), channel_id=1, source_target_pairs={{0,4},{2,6},{4,0},{6,2},{8,12},{10,14},{12,8},{14,10},{16,20},{18,... | collective-permute-start | bytes 602120 | tf_op jit(solution)/shard_map/ppermute | solution.py:274
  70.6 17.6 %collective-permute-start.29 = (f32[392,128]{1,0:T(8,128)S(1)}, f32[392,128]{1,0:T(8,128)S(1)}, u32[]{:S(2)}, u32[]{:S(2)}) collective-permute-start(f32[392,128]{1,0:T(8,128)S(1)} %merge.20.refs_2_), channel_id=1, source_target_pairs={{0,16},{2,18},{4,20},{6,22},{8,24},{10,26},{12,28},{14,30},{16,0},... | collective-permute-start | bytes 602120 | tf_op jit(solution)/shard_map/ppermute | solution.py:274
  74.0 14.2 %collective-permute-start.34 = (f32[392,128]{1,0:T(8,128)S(1)}, f32[392,128]{1,0:T(8,128)S(1)}, u32[]{:S(2)}, u32[]{:S(2)}) collective-permute-start(f32[392,128]{1,0:T(8,128)S(1)} %relay.21.refs_2_), channel_id=1, source_target_pairs={{0,4},{2,6},{4,0},{6,2},{8,12},{10,14},{12,8},{14,10},{16,20},{18,... | collective-permute-start | bytes 602120 | tf_op jit(solution)/shard_map/ppermute | solution.py:274
  74.7 13.6 %collective-permute-start.30 = (f32[392,128]{1,0:T(8,128)S(1)}, f32[392,128]{1,0:T(8,128)S(1)}, u32[]{:S(2)}, u32[]{:S(2)}) collective-permute-start(f32[392,128]{1,0:T(8,128)S(1)} %merge.21.refs_2_), channel_id=1, source_target_pairs={{0,8},{2,10},{4,12},{6,14},{8,0},{10,2},{12,4},{14,6},{16,24},{18,... | collective-permute-start | bytes 602120 | tf_op jit(solution)/shard_map/ppermute | solution.py:274
  75.5 12.7 %collective-permute-start.33 = (f32[392,128]{1,0:T(8,128)S(1)}, f32[392,128]{1,0:T(8,128)S(1)}, u32[]{:S(2)}, u32[]{:S(2)}) collective-permute-start(f32[392,128]{1,0:T(8,128)S(1)} %merge.22.refs_20_), channel_id=1, source_target_pairs={{0,24},{2,26},{4,28},{6,30},{8,16},{10,18},{12,20},{14,22},{16,8},... | collective-permute-start | bytes 602120 | tf_op jit(solution)/shard_map/ppermute | solution.py:274
  (19 other events, 69.3 us)

commit v7 on v6

--- a/solution.py
+++ b/solution.py
@@ -53,7 +53,7 @@
             compiler_params=pltpu.CompilerParams(vmem_limit_bytes=limit << 20),
             **kw,
         )(*arrays)
-        self.last = out[-1] if isinstance(out, (list, tuple)) else out
+        self.last = min(jax.tree.leaves(out), key=lambda array: array.size)
         return out
 
 
@@ -73,6 +73,10 @@
     x_ref[features:, :] = (owner_ref[...] * columns + local_ref[...]).astype(f32)
 
 
+def settle_body(out_ref):
+    out_ref[...] = jnp.zeros_like(out_ref)
+
+
 def relay_body(*refs):
     for k, ref in enumerate(refs[:-1]):
         refs[-1][k] = ref[...]
@@ -83,7 +87,8 @@
 
 
 def score_body(places, me_ref, d_ref, pool_ref, *refs):
-    part_ref, rows_ref = refs[-2:]
+    part_ref, rows_ref, token_ref = refs[-3:]
+    token_ref[...] = jnp.zeros_like(token_ref)
     rows, features = d_ref.shape
     columns = pool_ref.shape[1]
     tile = 128
@@ -168,6 +173,21 @@
     out_ref[size:] = jnp.concatenate(
         [peak, total, jnp.zeros((SLACK - 2, peak.shape[1]), f32)], axis=0
     )
+
+
+def merge_all_body(places, *refs):
+    out_ref = refs[-1]
+    size = out_ref.shape[1] - SLACK
+    for slot, terms in enumerate(places):
+        terms = [refs[i][...] if k is None else refs[i][k] for i, k in terms]
+        if len(terms) == 1:
+            out_ref[slot] = terms[0]
+        else:
+            sums, peak, total = merge(terms)
+            out_ref[slot, :size] = sums
+            out_ref[slot, size:] = jnp.concatenate(
+                [peak, total, jnp.zeros((SLACK - 2, peak.shape[1]), f32)], axis=0
+            )
 
 
 def last_body(d_ref, e_ref, *refs):
@@ -306,18 +326,19 @@
     weights, sums, e_place = [], {}, {}
     waiting, stage = [], {}
 
-    def score(blocks):
+    def score(blocks, limit=16):
         k = len(blocks)
         used = sorted({x_place[r][0] for r in blocks})
-        part, found = line(
+        part, found, token = line(
             functools.partial(
                 score_body, [(used.index(x_place[r][0]), x_place[r][1]) for r in blocks]
             ),
-            (shape(k, rows + SLACK, rows), shape(k, features, rows)),
+            (shape(k, rows + SLACK, rows), shape(k, features, rows), shape(SLACK, rows)),
             "score",
             [me.reshape(1), document_matrix, pool] + [x_arrays[i] for i in used],
             0.9 * k,
             [smem] + [vmem] * (2 + len(used)),
+            limit=limit,
         )
         got = [
             lax.ppermute(part, "dim", [(i, (i + s) % depth) for i in range(depth)])
@@ -361,10 +382,21 @@
             sums[r] = (add(sums[r], sums[r + 1]), None)
 
     def beside(k):
-        over_x[k] = send(sums[4 * k + 2][0], 2)
+        over_x[k] = (send(sums[4 * k + 2][0], 2), None)
+
+    def beside_all(*blocks):
+        arrays, places = [], []
+        for terms in blocks:
+            places.append([(len(arrays) + i, sums[r][1]) for i, r in enumerate(terms)])
+            arrays += [sums[r][0] for r in terms]
+        out = shape(len(blocks), features + SLACK, rows)
+        held = line(functools.partial(merge_all_body, places), out, "merge", arrays, 0.1)
+        shared = send(held, 2)
+        for i, terms in enumerate(blocks):
+            over_x[terms[0] // 4] = (shared, i)
 
     def inward(k):
-        whole = add(sums[4 * k], (over_x[k], None))
+        whole = add(sums[4 * k], over_x[k])
         home.append(send(whole, 4 * k) if k else whole)
 
     packed = line(
@@ -387,8 +419,9 @@
         keep(send(packed, 4 * k), 4 * k)
     keep(send(packed, 2), 2)
     keep(send(packed, 1), 1)
-    dt = line(flip_body, shape(features, rows), "flip", [document_matrix], 0.1)
-    score([0, 1])
+    dt = line(flip_body, shape(features, rows), "flip", [document_matrix], 0.1, limit=62)
+    score([0, 1], limit=60)
+    line(settle_body, shape(SLACK, rows), "settle", [], 0.05)
     forward(2)
     forward(1)
     relay(2)
@@ -424,7 +457,7 @@
             pair(4 * k - 2, 4 * k - 4)
             beside(k - 1)
     softmax()
-    over_x[2] = pass_on(over_x[2])
+    over_x[2] = (pass_on(over_x[2][0]), None)
 
     totals = line(
         functools.partial(stats_body, [e_place[r] for r in range(n)]),
@@ -454,7 +487,7 @@
             0.05,
         )
         if mask == 2 * far:
-            over_x[1] = pass_on(over_x[1])
+            over_x[1] = (pass_on(over_x[1][0]), None)
         if mask == 1:
             pair(4 * far - 2)
             beside(far - 1)

time: 89.4 us -> 90.5 us (1.012)
  Pallas kernels: 32.3 us -> 37.1 us
  local copies, waits for them, and re-layouts: 5.61 us -> 1.4 us
    pallas_call x42 -> x43, Pallas kernels: 32.3 us -> 37.1 us  [__call__(): pl.pallas_call(kernel, out_shape=out_shape, name=name, in_specs=in_specs,...]
    unnamed x16 -> x18, local copies, waits for them, and re-layouts: 5.61 us -> 1.4 us
  transfers between devices with their start and end apart: 35 -> 35, of which waited for: 12 -> 12; matrix products, arithmetic and copies ran while one was open for 0% -> 0% of each run, Pallas kernels for 32% -> 37%
where the time goes in v7:
time: 90.5 us; the launch traced here: 90.3 us
  Pallas kernels  37.1 us (41%)
  starting transfers between devices  36 us (40%)
  waiting for transfers between devices  14.7 us (16%)
  local copies, waits for them, and re-layouts  1.4 us (2%)
  between operations  1.08 us (1%)
    pallas_call x43, Pallas kernels, __call__(): pl.pallas_call(kernel, out_shape=out_shape, name=name, in_specs=in_specs,...  37.1 us
    ppermute x30, starting transfers between devices, send(): return lax.ppermute(x, 'blk', [(i, i ^ mask) for i in range(n)])  30 us
    ppermute x30, waiting for transfers between devices, send(): return lax.ppermute(x, 'blk', [(i, i ^ mask) for i in range(n)])  9.36 us
    ppermute x5, starting transfers between devices, score(): lax.ppermute(part, 'dim', [(i, (i + s) % depth) for i in range(depth)])  6.04 us
    ppermute x5, waiting for transfers between devices, score(): lax.ppermute(part, 'dim', [(i, (i + s) % depth) for i in range(depth)])  5.35 us
  transfers between devices with their start and end apart: 35, of which 12 were waited for; matrix products, arithmetic and copies ran while one was open for 0% of the time, Pallas kernels for 37%

profile of v7, /device:TPU:0, one launch (start us, length us, event | category | flops | bytes accessed | tf_op | source)
XLA Modules:
  0.0 90.3 jit_solution(8935648274214941025)
XLA Ops:
  0.6 1.8 %pack.1.refs_1_.refs_3_ = f32[392,128]{1,0:T(8,128)} custom-call(f32[128,384]{1,0:T(8,128)} %refs_0_.3, s32[8,128]{1,0:T(8,128)} %bitcast.3, s32[8,128]{1,0:T(8,128)} %bitcast.4), custom_call_target="tpu_custom_call" | custom-call | bytes 6660000 | tf_op jit(solution)/shard_map/pack/pallas_call | solution.py:45
  2.9 3.7 %collective-permute-start.2 = (f32[392,128]{1,0:T(8,128)}, f32[392,128]{1,0:T(8,128)}, u32[]{:S(2)}, u32[]{:S(2)}) collective-permute-start(f32[392,128]{1,0:T(8,128)} %pack.1.refs_1_.refs_3_), channel_id=1, source_target_pairs={{0,16},{2,18},{4,20},{6,22},{8,24},{10,26},{12,28},{14,30},{16,0},... | collective-permute-start | bytes 602120 | tf_op jit(solution)/shard_map/ppermute | solution.py:294
  6.6 1.6 %collective-permute-start.3 = (f32[392,128]{1,0:T(8,128)}, f32[392,128]{1,0:T(8,128)S(1)}, u32[]{:S(2)}, u32[]{:S(2)}) collective-permute-start(f32[392,128]{1,0:T(8,128)} %pack.1.refs_1_.refs_3_), channel_id=1, source_target_pairs={{0,8},{2,10},{4,12},{6,14},{8,0},{10,2},{12,4},{14,6},{16,24},{18,... | collective-permute-start | bytes 602120 | tf_op jit(solution)/shard_map/ppermute | solution.py:294
  8.2 1.5 %collective-permute-start.4 = (f32[392,128]{1,0:T(8,128)}, f32[392,128]{1,0:T(8,128)S(1)}, u32[]{:S(2)}, u32[]{:S(2)}) collective-permute-start(f32[392,128]{1,0:T(8,128)} %pack.1.refs_1_.refs_3_), channel_id=1, source_target_pairs={{0,4},{2,6},{4,0},{6,2},{8,12},{10,14},{12,8},{14,10},{16,20},{18,... | collective-permute-start | bytes 602120 | tf_op jit(solution)/shard_map/ppermute | solution.py:294
  9.7 1.7 %flip.1.refs_5_.refs_0_ = f32[384,128]{1,0:T(8,128)} custom-call(f32[128,384]{1,0:T(8,128)} %refs_0_.5, f32[392,128]{1,0:T(8,128)} %pack.1.refs_1_.refs_3_), custom_call_target="tpu_custom_call" | custom-call | bytes 370000 | tf_op jit(solution)/shard_map/flip/pallas_call | solution.py:45
  12.1 4.8 %score.5 = (f32[2,136,128]{2,1,0:T(8,128)}, f32[2,384,128]{2,1,0:T(8,128)}, f32[8,128]{1,0:T(8,128)}) custom-call(s32[1]{0:T(128)} %bitcast.2.refs_0_, f32[128,384]{1,0:T(8,128)} %refs_0_.5, f32[384,2048]{1,0:T(8,128)} %refs_2_.9, f32[392,128]{1,0:T(8,128)} %pack.1.refs_1_.refs_3_, f32[392,128]{1,0:T(8,128)} %copy-done.4, f32[384,128]{1,0:T(8,128)} %flip.1.refs_5_.refs_0_), custom_call_target="tpu_custom_call" | custom-call | bytes 6660000 | tf_op jit(solution)/shard_map/score/pallas_call | solution.py:45
  21.2 1.5 %collective-permute-start.1 = (f32[2,136,128]{2,1,0:T(8,128)}, f32[2,136,128]{2,1,0:T(8,128)S(1)}, u32[]{:S(2)}, u32[]{:S(2)}) collective-permute-start(f32[2,136,128]{2,1,0:T(8,128)} %get-tuple-element.43.refs_2_), channel_id=1, source_target_pairs={{0,1},{1,0},{2,3},{3,2},{4,5},{5,4},{6,7},{7,6},{8,9},{9,8},{10,11... | collective-permute-start | bytes 417800 | tf_op jit(solution)/shard_map/ppermute | solution.py:344
  22.8 2.7 %score.6 = (f32[3,136,128]{2,1,0:T(8,128)S(1)}, f32[3,384,128]{2,1,0:T(8,128)S(1)}, f32[8,128]{1,0:T(8,128)S(1)}) custom-call(s32[1]{0:T(128)} %bitcast.2.refs_0_, f32[128,384]{1,0:T(8,128)S(1)} %copy-done.1, f32[384,2048]{1,0:T(8,128)S(1)} %copy-done, f32[392,128]{1,0:T(8,128)S(1)} %relay.11.refs_1_.refs_2_.refs_3_, ...), custom_call_target="tpu_custom_call" | custom-call | bytes 9990000 | tf_op jit(solution)/shard_map/score/pallas_call | solution.py:45
  25.5 1.1 %collective-permute-done.1.refs_3_ = f32[2,136,128]{2,1,0:T(8,128)S(1)} collective-permute-done((f32[2,136,128]{2,1,0:T(8,128)}, f32[2,136,128]{2,1,0:T(8,128)S(1)}, u32[]{:S(2)}, u32[]{:S(2)}) %collective-permute-start.1) | collective-permute-done | bytes 139296 | tf_op jit(solution)/shard_map/ppermute | solution.py:344
  26.6 1.5 %collective-permute-start.5 = (f32[3,136,128]{2,1,0:T(8,128)S(1)}, f32[3,136,128]{2,1,0:T(8,128)S(1)}, u32[]{:S(2)}, u32[]{:S(2)}) collective-permute-start(f32[3,136,128]{2,1,0:T(8,128)S(1)} %get-tuple-element.48.refs_2_), channel_id=1, source_target_pairs={{0,1},{1,0},{2,3},{3,2},{4,5},{5,4},{6,7},{7,6},{8,9},{9,8},{10,11... | collective-permute-start | bytes 626696 | tf_op jit(solution)/shard_map/ppermute | solution.py:344
  28.8 2.7 %score.7 = (f32[3,136,128]{2,1,0:T(8,128)S(1)}, f32[3,384,128]{2,1,0:T(8,128)S(1)}, f32[8,128]{1,0:T(8,128)S(1)}) custom-call(s32[1]{0:T(128)} %bitcast.2.refs_0_, f32[128,384]{1,0:T(8,128)S(1)} %copy-done.1, f32[384,2048]{1,0:T(8,128)S(1)} %copy-done, f32[3,392,128]{2,1,0:T(8,128)S(1)} %collective-permute-done.7.refs_3_.refs_9_, ...), custom_call_target="tpu_custom_call" | custom-call | bytes 9990000 | tf_op jit(solution)/shard_map/score/pallas_call | solution.py:45
  34.5 3.8 %score.8 = (f32[4,136,128]{2,1,0:T(8,128)S(1)}, f32[4,384,128]{2,1,0:T(8,128)S(1)}, f32[8,128]{1,0:T(8,128)S(1)}) custom-call(s32[1]{0:T(128)} %bitcast.2.refs_0_, f32[128,384]{1,0:T(8,128)S(1)} %copy-done.1, f32[384,2048]{1,0:T(8,128)S(1)} %copy-done, f32[392,128]{1,0:T(8,128)S(1)} %relay.15.refs_1_.refs_3_.refs_7_, f32[392,128]{1,0:T(8,128)S(1)} %relay.17.refs_4_.refs_8_, ...), custom_call_target="tpu_custom_call" | custom-call | bytes 13320000 | tf_op jit(solution)/shard_map/score/pallas_call | solution.py:45
  38.3 1.4 %collective-permute-done.11.refs_0_ = f32[392,128]{1,0:T(8,128)S(1)} collective-permute-done((f32[392,128]{1,0:T(8,128)S(1)}, f32[392,128]{1,0:T(8,128)S(1)}, u32[]{:S(2)}, u32[]{:S(2)}) %collective-permute-start.11) | collective-permute-done | bytes 200736 | tf_op jit(solution)/shard_map/ppermute | solution.py:294
  40.5 1.6 %collective-permute-start.18 = (f32[4,136,128]{2,1,0:T(8,128)S(1)}, f32[4,136,128]{2,1,0:T(8,128)S(1)}, u32[]{:S(2)}, u32[]{:S(2)}) collective-permute-start(f32[4,136,128]{2,1,0:T(8,128)S(1)} %get-tuple-element.62.refs_2_), channel_id=1, source_target_pairs={{0,1},{1,0},{2,3},{3,2},{4,5},{5,4},{6,7},{7,6},{8,9},{9,8},{10,11... | collective-permute-start | bytes 835592 | tf_op jit(solution)/shard_map/ppermute | solution.py:344
  43.8 3.6 %score.9 = (f32[4,136,128]{2,1,0:T(8,128)S(1)}, f32[4,384,128]{2,1,0:T(8,128)S(1)}, f32[8,128]{1,0:T(8,128)S(1)}) custom-call(s32[1]{0:T(128)} %bitcast.2.refs_0_, f32[128,384]{1,0:T(8,128)S(1)} %copy-done.1, f32[384,2048]{1,0:T(8,128)S(1)} %copy-done, f32[392,128]{1,0:T(8,128)S(1)} %relay.16.refs_4_.refs_3_.refs_6_, f32[392,128]{1,0:T(8,128)S(1)} %relay.18.refs_4_.refs_10_, ...), custom_call_target="tpu_custom_call" | custom-call | bytes 13320000 | tf_op jit(solution)/shard_map/score/pallas_call | solution.py:45
  53.2 3.1 %collective-permute-done.21.refs_3_ = f32[4,136,128]{2,1,0:T(8,128)S(1)} collective-permute-done((f32[4,136,128]{2,1,0:T(8,128)S(1)}, f32[4,136,128]{2,1,0:T(8,128)S(1)}, u32[]{:S(2)}, u32[]{:S(2)}) %collective-permute-start.21) | collective-permute-done | bytes 278560 | tf_op jit(solution)/shard_map/ppermute | solution.py:344
  57.3 1.1 %collective-permute-start.28 = (f32[392,128]{1,0:T(8,128)S(1)}, f32[392,128]{1,0:T(8,128)S(1)}, u32[]{:S(2)}, u32[]{:S(2)}) collective-permute-start(f32[392,128]{1,0:T(8,128)S(1)} %merge.17.refs_4_), channel_id=1, source_target_pairs={{0,4},{2,6},{4,0},{6,2},{8,12},{10,14},{12,8},{14,10},{16,20},{18,... | collective-permute-start | bytes 602120 | tf_op jit(solution)/shard_map/ppermute | solution.py:294
  61.6 3.4 %collective-permute-start.25 = (f32[2,16,128]{2,1,0:T(8,128)S(1)}, f32[2,16,128]{2,1,0:T(8,128)S(1)}, u32[]{:S(2)}, u32[]{:S(2)}) collective-permute-start(f32[2,16,128]{2,1,0:T(8,128)S(1)} %stats_merge.4.refs_2_.refs_0_), channel_id=1, source_target_pairs={{0,16},{2,18},{4,20},{6,22},{8,24},{10,26},{12,28},{14,30},{16,0},... | collective-permute-start | bytes 49160 | tf_op jit(solution)/shard_map/ppermute | solution.py:294
  65.0 1.7 %collective-permute-done.25.refs_1_ = f32[2,16,128]{2,1,0:T(8,128)S(1)} collective-permute-done((f32[2,16,128]{2,1,0:T(8,128)S(1)}, f32[2,16,128]{2,1,0:T(8,128)S(1)}, u32[]{:S(2)}, u32[]{:S(2)}) %collective-permute-start.25) | collective-permute-done | bytes 16416 | tf_op jit(solution)/shard_map/ppermute | solution.py:294
  67.8 2.7 %collective-permute-done.27.refs_1_ = f32[2,16,128]{2,1,0:T(8,128)S(1)} collective-permute-done((f32[2,16,128]{2,1,0:T(8,128)S(1)}, f32[2,16,128]{2,1,0:T(8,128)S(1)}, u32[]{:S(2)}, u32[]{:S(2)}) %collective-permute-start.27) | collective-permute-done | bytes 16416 | tf_op jit(solution)/shard_map/ppermute | solution.py:294
  71.3 2.9 %collective-permute-start.29 = (f32[392,128]{1,0:T(8,128)S(1)}, f32[392,128]{1,0:T(8,128)S(1)}, u32[]{:S(2)}, u32[]{:S(2)}) collective-permute-start(f32[392,128]{1,0:T(8,128)S(1)} %merge.20.refs_2_), channel_id=1, source_target_pairs={{0,16},{2,18},{4,20},{6,22},{8,24},{10,26},{12,28},{14,30},{16,0},... | collective-permute-start | bytes 602120 | tf_op jit(solution)/shard_map/ppermute | solution.py:294
  74.4 1.5 %collective-permute-start.34 = (f32[392,128]{1,0:T(8,128)S(1)}, f32[392,128]{1,0:T(8,128)S(1)}, u32[]{:S(2)}, u32[]{:S(2)}) collective-permute-start(f32[392,128]{1,0:T(8,128)S(1)} %relay.21.refs_2_), channel_id=1, source_target_pairs={{0,4},{2,6},{4,0},{6,2},{8,12},{10,14},{12,8},{14,10},{16,20},{18,... | collective-permute-start | bytes 602120 | tf_op jit(solution)/shard_map/ppermute | solution.py:294
  76.8 2.9 %collective-permute-start.33 = (f32[392,128]{1,0:T(8,128)S(1)}, f32[392,128]{1,0:T(8,128)S(1)}, u32[]{:S(2)}, u32[]{:S(2)}) collective-permute-start(f32[392,128]{1,0:T(8,128)S(1)} %merge.22.refs_20_), channel_id=1, source_target_pairs={{0,24},{2,26},{4,28},{6,30},{8,16},{10,18},{12,20},{14,22},{16,8},... | collective-permute-start | bytes 602120 | tf_op jit(solution)/shard_map/ppermute | solution.py:294
  79.7 9.7 %gradient.1 = (f32[128,384]{1,0:T(8,128)}, f32[384,2048]{1,0:T(8,128)}) custom-call(f32[2,16,128]{2,1,0:T(8,128)S(1)} %stats_merge.7.refs_1_.refs_2_.refs_0_, f32[392,128]{1,0:T(8,128)S(1)} %copy-done.3, f32[392,128]{1,0:T(8,128)S(1)} %relay.11.refs_1_.refs_2_.refs_3_, f32[392,128]{1,0:T(8,128)S(1)} %relay.12.refs_1_.refs_4_.refs_3_, ...), custom_call_target="tpu_custom_call" | custom-call | bytes 40700000 | tf_op jit(solution)/shard_map/gradient/pallas_call | solution.py:45
  (107 shorter events, 25.2 us)
Async XLA Ops:
  2.4 9.0 %collective-permute-start = (f32[392,128]{1,0:T(8,128)}, f32[392,128]{1,0:T(8,128)S(1)}, u32[]{:S(2)}, u32[]{:S(2)}) collective-permute-start(f32[392,128]{1,0:T(8,128)} %pack.1.refs_1_.refs_3_), channel_id=1, source_target_pairs={{0,2},{2,0},{4,6},{6,4},{8,10},{10,8},{12,14},{14,12},{16,18},{18,... | collective-permute-start | bytes 602120 | tf_op jit(solution)/shard_map/ppermute | solution.py:294
  2.9 14.6 %collective-permute-start.2 = (f32[392,128]{1,0:T(8,128)}, f32[392,128]{1,0:T(8,128)}, u32[]{:S(2)}, u32[]{:S(2)}) collective-permute-start(f32[392,128]{1,0:T(8,128)} %pack.1.refs_1_.refs_3_), channel_id=1, source_target_pairs={{0,16},{2,18},{4,20},{6,22},{8,24},{10,26},{12,28},{14,30},{16,0},... | collective-permute-start | bytes 602120 | tf_op jit(solution)/shard_map/ppermute | solution.py:294
  6.6 11.9 %collective-permute-start.3 = (f32[392,128]{1,0:T(8,128)}, f32[392,128]{1,0:T(8,128)S(1)}, u32[]{:S(2)}, u32[]{:S(2)}) collective-permute-start(f32[392,128]{1,0:T(8,128)} %pack.1.refs_1_.refs_3_), channel_id=1, source_target_pairs={{0,8},{2,10},{4,12},{6,14},{8,0},{10,2},{12,4},{14,6},{16,24},{18,... | collective-permute-start | bytes 602120 | tf_op jit(solution)/shard_map/ppermute | solution.py:294
  8.2 10.4 %collective-permute-start.4 = (f32[392,128]{1,0:T(8,128)}, f32[392,128]{1,0:T(8,128)S(1)}, u32[]{:S(2)}, u32[]{:S(2)}) collective-permute-start(f32[392,128]{1,0:T(8,128)} %pack.1.refs_1_.refs_3_), channel_id=1, source_target_pairs={{0,4},{2,6},{4,0},{6,2},{8,12},{10,14},{12,8},{14,10},{16,20},{18,... | collective-permute-start | bytes 602120 | tf_op jit(solution)/shard_map/ppermute | solution.py:294
  18.6 10.1 %collective-permute-start.7 = (f32[3,392,128]{2,1,0:T(8,128)S(1)}, f32[3,392,128]{2,1,0:T(8,128)S(1)}, u32[]{:S(2)}, u32[]{:S(2)}) collective-permute-start(f32[3,392,128]{2,1,0:T(8,128)S(1)} %relay.14.refs_6_), channel_id=1, source_target_pairs={{0,2},{2,0},{4,6},{6,4},{8,10},{10,8},{12,14},{14,12},{16,18},{18,... | collective-permute-start | bytes 1806344 | tf_op jit(solution)/shard_map/ppermute | solution.py:294
  18.7 10.0 %collective-permute-start.9 = (f32[392,128]{1,0:T(8,128)S(1)}, f32[392,128]{1,0:T(8,128)S(1)}, u32[]{:S(2)}, u32[]{:S(2)}) collective-permute-start(f32[392,128]{1,0:T(8,128)S(1)} %relay.11.refs_1_.refs_2_.refs_3_), channel_id=1, source_target_pairs={{0,4},{2,6},{4,0},{6,2},{8,12},{10,14},{12,8},{14,10},{16,20},{18,... | collective-permute-start | bytes 602120 | tf_op jit(solution)/shard_map/ppermute | solution.py:294
  19.7 9.0 %collective-permute-start.8 = (f32[392,128]{1,0:T(8,128)S(1)}, f32[392,128]{1,0:T(8,128)S(1)}, u32[]{:S(2)}, u32[]{:S(2)}) collective-permute-start(f32[392,128]{1,0:T(8,128)S(1)} %relay.11.refs_1_.refs_2_.refs_3_), channel_id=1, source_target_pairs={{0,8},{2,10},{4,12},{6,14},{8,0},{10,2},{12,4},{14,6},{16,24},{18,... | collective-permute-start | bytes 602120 | tf_op jit(solution)/shard_map/ppermute | solution.py:294
  20.3 11.8 %collective-permute-start.6 = (f32[392,128]{1,0:T(8,128)S(1)}, f32[392,128]{1,0:T(8,128)S(1)}, u32[]{:S(2)}, u32[]{:S(2)}) collective-permute-start(f32[392,128]{1,0:T(8,128)S(1)} %relay.12.refs_1_.refs_4_.refs_3_), channel_id=1, source_target_pairs={{0,4},{2,6},{4,0},{6,2},{8,12},{10,14},{12,8},{14,10},{16,20},{18,... | collective-permute-start | bytes 602120 | tf_op jit(solution)/shard_map/ppermute | solution.py:294
  21.2 5.4 %collective-permute-start.1 = (f32[2,136,128]{2,1,0:T(8,128)}, f32[2,136,128]{2,1,0:T(8,128)S(1)}, u32[]{:S(2)}, u32[]{:S(2)}) collective-permute-start(f32[2,136,128]{2,1,0:T(8,128)} %get-tuple-element.43.refs_2_), channel_id=1, source_target_pairs={{0,1},{1,0},{2,3},{3,2},{4,5},{5,4},{6,7},{7,6},{8,9},{9,8},{10,11... | collective-permute-start | bytes 417800 | tf_op jit(solution)/shard_map/ppermute | solution.py:344
  26.6 7.1 %collective-permute-start.5 = (f32[3,136,128]{2,1,0:T(8,128)S(1)}, f32[3,136,128]{2,1,0:T(8,128)S(1)}, u32[]{:S(2)}, u32[]{:S(2)}) collective-permute-start(f32[3,136,128]{2,1,0:T(8,128)S(1)} %get-tuple-element.48.refs_2_), channel_id=1, source_target_pairs={{0,1},{1,0},{2,3},{3,2},{4,5},{5,4},{6,7},{7,6},{8,9},{9,8},{10,11... | collective-permute-start | bytes 626696 | tf_op jit(solution)/shard_map/ppermute | solution.py:344
  31.5 8.2 %collective-permute-start.10 = (f32[3,136,128]{2,1,0:T(8,128)S(1)}, f32[3,136,128]{2,1,0:T(8,128)S(1)}, u32[]{:S(2)}, u32[]{:S(2)}) collective-permute-start(f32[3,136,128]{2,1,0:T(8,128)S(1)} %get-tuple-element.52.refs_2_), channel_id=1, source_target_pairs={{0,1},{1,0},{2,3},{3,2},{4,5},{5,4},{6,7},{7,6},{8,9},{9,8},{10,11... | collective-permute-start | bytes 626696 | tf_op jit(solution)/shard_map/ppermute | solution.py:344
  32.7 7.0 %collective-permute-start.11 = (f32[392,128]{1,0:T(8,128)S(1)}, f32[392,128]{1,0:T(8,128)S(1)}, u32[]{:S(2)}, u32[]{:S(2)}) collective-permute-start(f32[392,128]{1,0:T(8,128)S(1)} %relay.16.refs_4_.refs_3_.refs_6_), channel_id=1, source_target_pairs={{0,4},{2,6},{4,0},{6,2},{8,12},{10,14},{12,8},{14,10},{16,20},{18,... | collective-permute-start | bytes 602120 | tf_op jit(solution)/shard_map/ppermute | solution.py:294
  40.4 7.9 %collective-permute-start.14 = (f32[3,392,128]{2,1,0:T(8,128)S(1)}, f32[3,392,128]{2,1,0:T(8,128)S(1)}, u32[]{:S(2)}, u32[]{:S(2)}) collective-permute-start(f32[3,392,128]{2,1,0:T(8,128)S(1)} %get-tuple-element.55), channel_id=1, source_target_pairs={{0,2},{2,0},{4,6},{6,4},{8,10},{10,8},{12,14},{14,12},{16,18},{18,... | collective-permute-start | bytes 1806344 | tf_op jit(solution)/shard_map/ppermute | solution.py:294
  40.5 9.1 %collective-permute-start.18 = (f32[4,136,128]{2,1,0:T(8,128)S(1)}, f32[4,136,128]{2,1,0:T(8,128)S(1)}, u32[]{:S(2)}, u32[]{:S(2)}) collective-permute-start(f32[4,136,128]{2,1,0:T(8,128)S(1)} %get-tuple-element.62.refs_2_), channel_id=1, source_target_pairs={{0,1},{1,0},{2,3},{3,2},{4,5},{5,4},{6,7},{7,6},{8,9},{9,8},{10,11... | collective-permute-start | bytes 835592 | tf_op jit(solution)/shard_map/ppermute | solution.py:344
  42.6 5.7 %collective-permute-start.15 = (f32[392,128]{1,0:T(8,128)S(1)}, f32[392,128]{1,0:T(8,128)S(1)}, u32[]{:S(2)}, u32[]{:S(2)}) collective-permute-start(f32[392,128]{1,0:T(8,128)S(1)} %get-tuple-element.58), channel_id=1, source_target_pairs={{0,2},{2,0},{4,6},{6,4},{8,10},{10,8},{12,14},{14,12},{16,18},{18,... | collective-permute-start | bytes 602120 | tf_op jit(solution)/shard_map/ppermute | solution.py:294
  47.4 8.9 %collective-permute-start.21 = (f32[4,136,128]{2,1,0:T(8,128)S(1)}, f32[4,136,128]{2,1,0:T(8,128)S(1)}, u32[]{:S(2)}, u32[]{:S(2)}) collective-permute-start(f32[4,136,128]{2,1,0:T(8,128)S(1)} %get-tuple-element.66.refs_2_), channel_id=1, source_target_pairs={{0,1},{1,0},{2,3},{3,2},{4,5},{5,4},{6,7},{7,6},{8,9},{9,8},{10,11... | collective-permute-start | bytes 835592 | tf_op jit(solution)/shard_map/ppermute | solution.py:344
  52.0 7.1 %collective-permute-start.20 = (f32[392,128]{1,0:T(8,128)S(1)}, f32[392,128]{1,0:T(8,128)S(1)}, u32[]{:S(2)}, u32[]{:S(2)}) collective-permute-start(f32[392,128]{1,0:T(8,128)S(1)} %merge.16.refs_2_), channel_id=1, source_target_pairs={{0,4},{2,6},{4,0},{6,2},{8,12},{10,14},{12,8},{14,10},{16,20},{18,... | collective-permute-start | bytes 602120 | tf_op jit(solution)/shard_map/ppermute | solution.py:294
  57.3 10.5 %collective-permute-start.28 = (f32[392,128]{1,0:T(8,128)S(1)}, f32[392,128]{1,0:T(8,128)S(1)}, u32[]{:S(2)}, u32[]{:S(2)}) collective-permute-start(f32[392,128]{1,0:T(8,128)S(1)} %merge.17.refs_4_), channel_id=1, source_target_pairs={{0,4},{2,6},{4,0},{6,2},{8,12},{10,14},{12,8},{14,10},{16,20},{18,... | collective-permute-start | bytes 602120 | tf_op jit(solution)/shard_map/ppermute | solution.py:294
  59.3 12.0 %collective-permute-start.23 = (f32[392,128]{1,0:T(8,128)S(1)}, f32[392,128]{1,0:T(8,128)S(1)}, u32[]{:S(2)}, u32[]{:S(2)}) collective-permute-start(f32[392,128]{1,0:T(8,128)S(1)} %get-tuple-element.70), channel_id=1, source_target_pairs={{0,2},{2,0},{4,6},{6,4},{8,10},{10,8},{12,14},{14,12},{16,18},{18,... | collective-permute-start | bytes 602120 | tf_op jit(solution)/shard_map/ppermute | solution.py:294
  60.5 16.2 %collective-permute-start.31 = (f32[392,128]{1,0:T(8,128)S(1)}, f32[392,128]{1,0:T(8,128)S(1)}, u32[]{:S(2)}, u32[]{:S(2)}) collective-permute-start(f32[392,128]{1,0:T(8,128)S(1)} %merge.18.refs_2_), channel_id=1, source_target_pairs={{0,4},{2,6},{4,0},{6,2},{8,12},{10,14},{12,8},{14,10},{16,20},{18,... | collective-permute-start | bytes 602120 | tf_op jit(solution)/shard_map/ppermute | solution.py:294
  71.3 18.1 %collective-permute-start.29 = (f32[392,128]{1,0:T(8,128)S(1)}, f32[392,128]{1,0:T(8,128)S(1)}, u32[]{:S(2)}, u32[]{:S(2)}) collective-permute-start(f32[392,128]{1,0:T(8,128)S(1)} %merge.20.refs_2_), channel_id=1, source_target_pairs={{0,16},{2,18},{4,20},{6,22},{8,24},{10,26},{12,28},{14,30},{16,0},... | collective-permute-start | bytes 602120 | tf_op jit(solution)/shard_map/ppermute | solution.py:294
  74.4 15.0 %collective-permute-start.34 = (f32[392,128]{1,0:T(8,128)S(1)}, f32[392,128]{1,0:T(8,128)S(1)}, u32[]{:S(2)}, u32[]{:S(2)}) collective-permute-start(f32[392,128]{1,0:T(8,128)S(1)} %relay.21.refs_2_), channel_id=1, source_target_pairs={{0,4},{2,6},{4,0},{6,2},{8,12},{10,14},{12,8},{14,10},{16,20},{18,... | collective-permute-start | bytes 602120 | tf_op jit(solution)/shard_map/ppermute | solution.py:294
  75.9 13.6 %collective-permute-start.30 = (f32[392,128]{1,0:T(8,128)S(1)}, f32[392,128]{1,0:T(8,128)S(1)}, u32[]{:S(2)}, u32[]{:S(2)}) collective-permute-start(f32[392,128]{1,0:T(8,128)S(1)} %merge.21.refs_2_), channel_id=1, source_target_pairs={{0,8},{2,10},{4,12},{6,14},{8,0},{10,2},{12,4},{14,6},{16,24},{18,... | collective-permute-start | bytes 602120 | tf_op jit(solution)/shard_map/ppermute | solution.py:294
  76.8 12.7 %collective-permute-start.33 = (f32[392,128]{1,0:T(8,128)S(1)}, f32[392,128]{1,0:T(8,128)S(1)}, u32[]{:S(2)}, u32[]{:S(2)}) collective-permute-start(f32[392,128]{1,0:T(8,128)S(1)} %merge.22.refs_20_), channel_id=1, source_target_pairs={{0,24},{2,26},{4,28},{6,30},{8,16},{10,18},{12,20},{14,22},{16,8},... | collective-permute-start | bytes 602120 | tf_op jit(solution)/shard_map/ppermute | solution.py:294
  (20 other events, 121.8 us)

commit v8 on v7

--- a/solution.py
+++ b/solution.py
@@ -53,7 +53,7 @@
             compiler_params=pltpu.CompilerParams(vmem_limit_bytes=limit << 20),
             **kw,
         )(*arrays)
-        self.last = min(jax.tree.leaves(out), key=lambda array: array.size)
+        self.last = out[-1] if isinstance(out, (list, tuple)) else out
         return out
 
 
@@ -73,10 +73,6 @@
     x_ref[features:, :] = (owner_ref[...] * columns + local_ref[...]).astype(f32)
 
 
-def settle_body(out_ref):
-    out_ref[...] = jnp.zeros_like(out_ref)
-
-
 def relay_body(*refs):
     for k, ref in enumerate(refs[:-1]):
         refs[-1][k] = ref[...]
@@ -87,8 +83,7 @@
 
 
 def score_body(places, me_ref, d_ref, pool_ref, *refs):
-    part_ref, rows_ref, token_ref = refs[-3:]
-    token_ref[...] = jnp.zeros_like(token_ref)
+    part_ref, rows_ref = refs[-2:]
     rows, features = d_ref.shape
     columns = pool_ref.shape[1]
     tile = 128
@@ -326,19 +321,18 @@
     weights, sums, e_place = [], {}, {}
     waiting, stage = [], {}
 
-    def score(blocks, limit=16):
+    def score(blocks):
         k = len(blocks)
         used = sorted({x_place[r][0] for r in blocks})
-        part, found, token = line(
+        part, found = line(
             functools.partial(
                 score_body, [(used.index(x_place[r][0]), x_place[r][1]) for r in blocks]
             ),
-            (shape(k, rows + SLACK, rows), shape(k, features, rows), shape(SLACK, rows)),
+            (shape(k, rows + SLACK, rows), shape(k, features, rows)),
             "score",
             [me.reshape(1), document_matrix, pool] + [x_arrays[i] for i in used],
             0.9 * k,
             [smem] + [vmem] * (2 + len(used)),
-            limit=limit,
         )
         got = [
             lax.ppermute(part, "dim", [(i, (i + s) % depth) for i in range(depth)])
@@ -419,9 +413,8 @@
         keep(send(packed, 4 * k), 4 * k)
     keep(send(packed, 2), 2)
     keep(send(packed, 1), 1)
-    dt = line(flip_body, shape(features, rows), "flip", [document_matrix], 0.1, limit=62)
-    score([0, 1], limit=60)
-    line(settle_body, shape(SLACK, rows), "settle", [], 0.05)
+    dt = line(flip_body, shape(features, rows), "flip", [document_matrix], 0.1)
+    score([0, 1])
     forward(2)
     forward(1)
     relay(2)
@@ -434,8 +427,8 @@
     relay(6)
     share(10, 6)
     softmax()
+    relay(14)
     score([10, 6, 11, 7])
-    relay(14)
     share(12, 14)
     softmax()
     for k in range(3, far):
@@ -447,17 +440,14 @@
             share(4 * k + 4, 4 * k + 6)
         if k == 3:
             pair(0, 2, 4, 8)
+            beside(0)
         softmax()
         if k == 3:
-            pair(10)
-            beside(2)
-            pair(6)
-            beside(1)
+            beside_all((10, 11), (6, 7))
         else:
             pair(4 * k - 2, 4 * k - 4)
             beside(k - 1)
     softmax()
-    over_x[2] = (pass_on(over_x[2][0]), None)
 
     totals = line(
         functools.partial(stats_body, [e_place[r] for r in range(n)]),
@@ -486,13 +476,9 @@
             [totals, there],
             0.05,
         )
-        if mask == 2 * far:
-            over_x[1] = (pass_on(over_x[1][0]), None)
         if mask == 1:
             pair(4 * far - 2)
             beside(far - 1)
-    sums[2] = (pass_on(sums[2][0]), None)
-    beside(0)
     for k in range(3, far):
         inward(k)
 

time: 90.5 us -> 91.5 us (1.011)
  Pallas kernels: 37.1 us -> 32.4 us
  local copies, waits for them, and re-layouts: 1.4 us -> 5.61 us
  waiting for transfers between devices: 14.7 us -> 18.7 us
  starting transfers between devices: 36 us -> 33 us
    ppermute x30 -> x29, waiting for transfers between devices: 9.36 us -> 14.5 us  [send(): return lax.ppermute(x, 'blk', [(i, i ^ mask) for i in range(n)])]
    pallas_call x43 -> x38, Pallas kernels: 37.1 us -> 32.4 us  [__call__(): pl.pallas_call(kernel, out_shape=out_shape, name=name, in_specs=in_specs,...]
    unnamed x18 -> x16, local copies, waits for them, and re-layouts: 1.4 us -> 5.61 us
    ppermute x30 -> x29, starting transfers between devices: 30 us -> 27 us  [send(): return lax.ppermute(x, 'blk', [(i, i ^ mask) for i in range(n)])]
    ppermute x5, waiting for transfers between devices: 5.35 us -> 4.25 us  [score(): lax.ppermute(part, 'dim', [(i, (i + s) % depth) for i in range(depth)])]
  transfers between devices with their start and end apart: 35 -> 34, of which waited for: 12 -> 12; matrix products, arithmetic and copies ran while one was open for 0% -> 0% of each run, Pallas kernels for 37% -> 32%
where the time goes in v8:
time: 91.5 us; the launch traced here: 90.8 us
  starting transfers between devices  33 us (36%)
  Pallas kernels  32.4 us (35%)
  waiting for transfers between devices  18.7 us (20%)
  local copies, waits for them, and re-layouts  5.61 us (6%)
  between operations  1.06 us (1%)
    pallas_call x38, Pallas kernels, __call__(): pl.pallas_call(kernel, out_shape=out_shape, name=name, in_specs=in_specs,...  32.4 us
    ppermute x29, starting transfers between devices, send(): return lax.ppermute(x, 'blk', [(i, i ^ mask) for i in range(n)])  27 us
    ppermute x29, waiting for transfers between devices, send(): return lax.ppermute(x, 'blk', [(i, i ^ mask) for i in range(n)])  14.5 us
    ppermute x5, starting transfers between devices, score(): lax.ppermute(part, 'dim', [(i, (i + s) % depth) for i in range(depth)])  6.04 us
    unnamed x16, local copies, waits for them, and re-layouts  5.61 us
    ppermute x5, waiting for transfers between devices, score(): lax.ppermute(part, 'dim', [(i, (i + s) % depth) for i in range(depth)])  4.25 us
  transfers between devices with their start and end apart: 34, of which 12 were waited for; matrix products, arithmetic and copies ran while one was open for 0% of the time, Pallas kernels for 32%

profile of v8, /device:TPU:0, one launch (start us, length us, event | category | flops | bytes accessed | tf_op | source)
XLA Modules:
  0.0 90.8 jit_solution(13549477295835434622)
XLA Ops:
  0.6 1.8 %pack.1.refs_1_.refs_3_ = f32[392,128]{1,0:T(8,128)} custom-call(f32[128,384]{1,0:T(8,128)} %refs_0_.3, s32[8,128]{1,0:T(8,128)} %bitcast.3, s32[8,128]{1,0:T(8,128)} %bitcast.4), custom_call_target="tpu_custom_call" | custom-call | bytes 6660000 | tf_op jit(solution)/shard_map/pack/pallas_call | solution.py:45
  2.9 3.7 %collective-permute-start.2 = (f32[392,128]{1,0:T(8,128)}, f32[392,128]{1,0:T(8,128)S(1)}, u32[]{:S(2)}, u32[]{:S(2)}) collective-permute-start(f32[392,128]{1,0:T(8,128)} %pack.1.refs_1_.refs_3_), channel_id=1, source_target_pairs={{0,16},{2,18},{4,20},{6,22},{8,24},{10,26},{12,28},{14,30},{16,0},... | collective-permute-start | bytes 602120 | tf_op jit(solution)/shard_map/ppermute | solution.py:289
  6.6 1.6 %collective-permute-start.3 = (f32[392,128]{1,0:T(8,128)}, f32[392,128]{1,0:T(8,128)S(1)}, u32[]{:S(2)}, u32[]{:S(2)}) collective-permute-start(f32[392,128]{1,0:T(8,128)} %pack.1.refs_1_.refs_3_), channel_id=1, source_target_pairs={{0,8},{2,10},{4,12},{6,14},{8,0},{10,2},{12,4},{14,6},{16,24},{18,... | collective-permute-start | bytes 602120 | tf_op jit(solution)/shard_map/ppermute | solution.py:289
  8.2 1.5 %collective-permute-start.4 = (f32[392,128]{1,0:T(8,128)}, f32[392,128]{1,0:T(8,128)S(1)}, u32[]{:S(2)}, u32[]{:S(2)}) collective-permute-start(f32[392,128]{1,0:T(8,128)} %pack.1.refs_1_.refs_3_), channel_id=1, source_target_pairs={{0,4},{2,6},{4,0},{6,2},{8,12},{10,14},{12,8},{14,10},{16,20},{18,... | collective-permute-start | bytes 602120 | tf_op jit(solution)/shard_map/ppermute | solution.py:289
  11.7 1.9 %copy-done = f32[384,2048]{1,0:T(8,128)S(1)} copy-done((f32[384,2048]{1,0:T(8,128)S(1)}, f32[384,2048]{1,0:T(8,128)}, u32[]{:S(2)}) %copy-start) | copy-done | bytes 3145752
  15.4 2.0 %score.5 = (f32[2,136,128]{2,1,0:T(8,128)S(1)}, f32[2,384,128]{2,1,0:T(8,128)S(1)}) custom-call(s32[1]{0:T(128)} %bitcast.2.refs_0_, f32[128,384]{1,0:T(8,128)S(1)} %copy-done.3, f32[384,2048]{1,0:T(8,128)S(1)} %copy-done, f32[392,128]{1,0:T(8,128)S(1)} %copy-done.6, f32[392,128]{1,0:T(8,128)S(1)} %collective-permute-done.refs_4_.refs_5_, ...), custom_call_target="tpu_custom_call" | custom-call | bytes 6660000 | tf_op jit(solution)/shard_map/score/pallas_call | solution.py:45
  20.8 1.5 %collective-permute-start.1 = (f32[2,136,128]{2,1,0:T(8,128)S(1)}, f32[2,136,128]{2,1,0:T(8,128)S(1)}, u32[]{:S(2)}, u32[]{:S(2)}) collective-permute-start(f32[2,136,128]{2,1,0:T(8,128)S(1)} %get-tuple-element.38.refs_2_), channel_id=1, source_target_pairs={{0,1},{1,0},{2,3},{3,2},{4,5},{5,4},{6,7},{7,6},{8,9},{9,8},{10,11... | collective-permute-start | bytes 417800 | tf_op jit(solution)/shard_map/ppermute | solution.py:338
  22.3 2.8 %score.6 = (f32[3,136,128]{2,1,0:T(8,128)S(1)}, f32[3,384,128]{2,1,0:T(8,128)S(1)}) custom-call(s32[1]{0:T(128)} %bitcast.2.refs_0_, f32[128,384]{1,0:T(8,128)S(1)} %copy-done.4, f32[384,2048]{1,0:T(8,128)S(1)} %copy-done.1, f32[392,128]{1,0:T(8,128)S(1)} %relay.8.refs_1_.refs_2_.refs_3_, f32[392,128]{1,0:T(8,128)S(1)} %relay.9.refs_1_.refs_4_.refs_3_, ...), custom_call_target="tpu_custom_call" | custom-call | bytes 9990000 | tf_op jit(solution)/shard_map/score/pallas_call | solution.py:45
  25.9 1.5 %collective-permute-start.5 = (f32[3,136,128]{2,1,0:T(8,128)S(1)}, f32[3,136,128]{2,1,0:T(8,128)S(1)}, u32[]{:S(2)}, u32[]{:S(2)}) collective-permute-start(f32[3,136,128]{2,1,0:T(8,128)S(1)} %get-tuple-element.41.refs_2_), channel_id=1, source_target_pairs={{0,1},{1,0},{2,3},{3,2},{4,5},{5,4},{6,7},{7,6},{8,9},{9,8},{10,11... | collective-permute-start | bytes 626696 | tf_op jit(solution)/shard_map/ppermute | solution.py:338
  28.1 2.8 %score.7 = (f32[3,136,128]{2,1,0:T(8,128)S(1)}, f32[3,384,128]{2,1,0:T(8,128)S(1)}) custom-call(s32[1]{0:T(128)} %bitcast.2.refs_0_, f32[128,384]{1,0:T(8,128)S(1)} %copy-done.4, f32[384,2048]{1,0:T(8,128)S(1)} %copy-done.1, f32[3,392,128]{2,1,0:T(8,128)S(1)} %collective-permute-done.7.refs_3_.refs_9_, f32[392,128]{1,0:T(8,128)S(1)} %relay.13.refs_4_.refs_3_.refs_6_), custom_call_target="tpu_custom_call" | custom-call | bytes 9990000 | tf_op jit(solution)/shard_map/score/pallas_call | solution.py:45
  34.0 4.9 %collective-permute-done.13.refs_0_ = f32[392,128]{1,0:T(8,128)S(1)} collective-permute-done((f32[392,128]{1,0:T(8,128)S(1)}, f32[392,128]{1,0:T(8,128)S(1)}, u32[]{:S(2)}, u32[]{:S(2)}) %collective-permute-start.13) | collective-permute-done | bytes 200736 | tf_op jit(solution)/shard_map/ppermute | solution.py:289
  38.9 4.0 %score.8 = (f32[4,136,128]{2,1,0:T(8,128)S(1)}, f32[4,384,128]{2,1,0:T(8,128)S(1)}) custom-call(s32[1]{0:T(128)} %bitcast.2.refs_0_, f32[128,384]{1,0:T(8,128)S(1)} %copy-done.4, f32[384,2048]{1,0:T(8,128)S(1)} %copy-done.1, f32[392,128]{1,0:T(8,128)S(1)} %relay.12.refs_1_.refs_3_.refs_7_, f32[392,128]{1,0:T(8,128)S(1)} %relay.14.refs_4_.refs_8_, ...), custom_call_target="tpu_custom_call" | custom-call | bytes 13320000 | tf_op jit(solution)/shard_map/score/pallas_call | solution.py:45
  43.7 1.6 %collective-permute-start.18 = (f32[4,136,128]{2,1,0:T(8,128)S(1)}, f32[4,136,128]{2,1,0:T(8,128)S(1)}, u32[]{:S(2)}, u32[]{:S(2)}) collective-permute-start(f32[4,136,128]{2,1,0:T(8,128)S(1)} %get-tuple-element.52.refs_2_), channel_id=1, source_target_pairs={{0,1},{1,0},{2,3},{3,2},{4,5},{5,4},{6,7},{7,6},{8,9},{9,8},{10,11... | collective-permute-start | bytes 835592 | tf_op jit(solution)/shard_map/ppermute | solution.py:338
  47.0 3.8 %score.9 = (f32[4,136,128]{2,1,0:T(8,128)S(1)}, f32[4,384,128]{2,1,0:T(8,128)S(1)}) custom-call(s32[1]{0:T(128)} %bitcast.2.refs_0_, f32[128,384]{1,0:T(8,128)S(1)} %copy-done.4, f32[384,2048]{1,0:T(8,128)S(1)} %copy-done.1, f32[392,128]{1,0:T(8,128)S(1)} %relay.13.refs_4_.refs_3_.refs_6_, f32[392,128]{1,0:T(8,128)S(1)} %relay.15.refs_7_.refs_4_.refs_10_, ...), custom_call_target="tpu_custom_call" | custom-call | bytes 13320000 | tf_op jit(solution)/shard_map/score/pallas_call | solution.py:45
  55.6 1.6 %collective-permute-start.21 = (f32[2,392,128]{2,1,0:T(8,128)S(1)}, f32[2,392,128]{2,1,0:T(8,128)S(1)}, u32[]{:S(2)}, u32[]{:S(2)}) collective-permute-start(f32[2,392,128]{2,1,0:T(8,128)S(1)} %merge.15.refs_4_), channel_id=1, source_target_pairs={{0,4},{2,6},{4,0},{6,2},{8,12},{10,14},{12,8},{14,10},{16,20},{18,... | collective-permute-start | bytes 1204232 | tf_op jit(solution)/shard_map/ppermute | solution.py:289
  57.1 2.6 %collective-permute-done.22.refs_3_ = f32[4,136,128]{2,1,0:T(8,128)S(1)} collective-permute-done((f32[4,136,128]{2,1,0:T(8,128)S(1)}, f32[4,136,128]{2,1,0:T(8,128)S(1)}, u32[]{:S(2)}, u32[]{:S(2)}) %collective-permute-start.22) | collective-permute-done | bytes 278560 | tf_op jit(solution)/shard_map/ppermute | solution.py:338
  62.2 1.6 %collective-permute-start.30 = (f32[392,128]{1,0:T(8,128)S(1)}, f32[392,128]{1,0:T(8,128)S(1)}, u32[]{:S(2)}, u32[]{:S(2)}) collective-permute-start(f32[392,128]{1,0:T(8,128)S(1)} %merge.16.refs_2_), channel_id=1, source_target_pairs={{0,4},{2,6},{4,0},{6,2},{8,12},{10,14},{12,8},{14,10},{16,20},{18,... | collective-permute-start | bytes 602120 | tf_op jit(solution)/shard_map/ppermute | solution.py:289
  63.8 2.4 %collective-permute-start.25 = (f32[2,16,128]{2,1,0:T(8,128)S(1)}, f32[2,16,128]{2,1,0:T(8,128)S(1)}, u32[]{:S(2)}, u32[]{:S(2)}) collective-permute-start(f32[2,16,128]{2,1,0:T(8,128)S(1)} %stats_merge.4.refs_2_.refs_0_), channel_id=1, source_target_pairs={{0,16},{2,18},{4,20},{6,22},{8,24},{10,26},{12,28},{14,30},{16,0},... | collective-permute-start | bytes 49160 | tf_op jit(solution)/shard_map/ppermute | solution.py:289
  66.1 2.5 %collective-permute-done.25.refs_1_ = f32[2,16,128]{2,1,0:T(8,128)S(1)} collective-permute-done((f32[2,16,128]{2,1,0:T(8,128)S(1)}, f32[2,16,128]{2,1,0:T(8,128)S(1)}, u32[]{:S(2)}, u32[]{:S(2)}) %collective-permute-start.25) | collective-permute-done | bytes 16416 | tf_op jit(solution)/shard_map/ppermute | solution.py:289
  69.2 3.2 %collective-permute-done.27.refs_1_ = f32[2,16,128]{2,1,0:T(8,128)S(1)} collective-permute-done((f32[2,16,128]{2,1,0:T(8,128)S(1)}, f32[2,16,128]{2,1,0:T(8,128)S(1)}, u32[]{:S(2)}, u32[]{:S(2)}) %collective-permute-start.27) | collective-permute-done | bytes 16416 | tf_op jit(solution)/shard_map/ppermute | solution.py:289
  72.8 1.7 %collective-permute-start.33 = (f32[392,128]{1,0:T(8,128)S(1)}, f32[392,128]{1,0:T(8,128)S(1)}, u32[]{:S(2)}, u32[]{:S(2)}) collective-permute-start(f32[392,128]{1,0:T(8,128)S(1)} %merge.12.refs_2_), channel_id=1, source_target_pairs={{0,4},{2,6},{4,0},{6,2},{8,12},{10,14},{12,8},{14,10},{16,20},{18,... | collective-permute-start | bytes 602120 | tf_op jit(solution)/shard_map/ppermute | solution.py:289
  74.6 2.2 %collective-permute-start.28 = (f32[392,128]{1,0:T(8,128)S(1)}, f32[392,128]{1,0:T(8,128)S(1)}, u32[]{:S(2)}, u32[]{:S(2)}) collective-permute-start(f32[392,128]{1,0:T(8,128)S(1)} %merge.18.refs_2_), channel_id=1, source_target_pairs={{0,16},{2,18},{4,20},{6,22},{8,24},{10,26},{12,28},{14,30},{16,0},... | collective-permute-start | bytes 602120 | tf_op jit(solution)/shard_map/ppermute | solution.py:289
  77.3 2.0 %collective-permute-start.32 = (f32[392,128]{1,0:T(8,128)S(1)}, f32[392,128]{1,0:T(8,128)S(1)}, u32[]{:S(2)}, u32[]{:S(2)}) collective-permute-start(f32[392,128]{1,0:T(8,128)S(1)} %merge.20.refs_20_), channel_id=1, source_target_pairs={{0,24},{2,26},{4,28},{6,30},{8,16},{10,18},{12,20},{14,22},{16,8},... | collective-permute-start | bytes 602120 | tf_op jit(solution)/shard_map/ppermute | solution.py:289
  79.3 9.8 %gradient.1 = (f32[128,384]{1,0:T(8,128)}, f32[384,2048]{1,0:T(8,128)}) custom-call(f32[2,16,128]{2,1,0:T(8,128)S(1)} %stats_merge.7.refs_2_.refs_0_, f32[392,128]{1,0:T(8,128)S(1)} %copy-done.7, f32[392,128]{1,0:T(8,128)S(1)} %relay.8.refs_1_.refs_2_.refs_3_, f32[392,128]{1,0:T(8,128)S(1)} %relay.9.refs_1_.refs_4_.refs_3_, ...), custom_call_target="tpu_custom_call" | custom-call | bytes 40700000 | tf_op jit(solution)/shard_map/gradient/pallas_call | solution.py:45
  (98 shorter events, 25.1 us)
Async XLA Ops:
  2.4 9.2 %collective-permute-start = (f32[392,128]{1,0:T(8,128)}, f32[392,128]{1,0:T(8,128)S(1)}, u32[]{:S(2)}, u32[]{:S(2)}) collective-permute-start(f32[392,128]{1,0:T(8,128)} %pack.1.refs_1_.refs_3_), channel_id=1, source_target_pairs={{0,2},{2,0},{4,6},{6,4},{8,10},{10,8},{12,14},{14,12},{16,18},{18,... | collective-permute-start | bytes 602120 | tf_op jit(solution)/shard_map/ppermute | solution.py:289
  2.9 14.4 %collective-permute-start.2 = (f32[392,128]{1,0:T(8,128)}, f32[392,128]{1,0:T(8,128)S(1)}, u32[]{:S(2)}, u32[]{:S(2)}) collective-permute-start(f32[392,128]{1,0:T(8,128)} %pack.1.refs_1_.refs_3_), channel_id=1, source_target_pairs={{0,16},{2,18},{4,20},{6,22},{8,24},{10,26},{12,28},{14,30},{16,0},... | collective-permute-start | bytes 602120 | tf_op jit(solution)/shard_map/ppermute | solution.py:289
  6.6 10.8 %collective-permute-start.3 = (f32[392,128]{1,0:T(8,128)}, f32[392,128]{1,0:T(8,128)S(1)}, u32[]{:S(2)}, u32[]{:S(2)}) collective-permute-start(f32[392,128]{1,0:T(8,128)} %pack.1.refs_1_.refs_3_), channel_id=1, source_target_pairs={{0,8},{2,10},{4,12},{6,14},{8,0},{10,2},{12,4},{14,6},{16,24},{18,... | collective-permute-start | bytes 602120 | tf_op jit(solution)/shard_map/ppermute | solution.py:289
  8.2 9.3 %collective-permute-start.4 = (f32[392,128]{1,0:T(8,128)}, f32[392,128]{1,0:T(8,128)S(1)}, u32[]{:S(2)}, u32[]{:S(2)}) collective-permute-start(f32[392,128]{1,0:T(8,128)} %pack.1.refs_1_.refs_3_), channel_id=1, source_target_pairs={{0,4},{2,6},{4,0},{6,2},{8,12},{10,14},{12,8},{14,10},{16,20},{18,... | collective-permute-start | bytes 602120 | tf_op jit(solution)/shard_map/ppermute | solution.py:289
  17.5 10.5 %collective-permute-start.7 = (f32[3,392,128]{2,1,0:T(8,128)S(1)}, f32[3,392,128]{2,1,0:T(8,128)S(1)}, u32[]{:S(2)}, u32[]{:S(2)}) collective-permute-start(f32[3,392,128]{2,1,0:T(8,128)S(1)} %relay.11.refs_6_), channel_id=1, source_target_pairs={{0,2},{2,0},{4,6},{6,4},{8,10},{10,8},{12,14},{14,12},{16,18},{18,... | collective-permute-start | bytes 1806344 | tf_op jit(solution)/shard_map/ppermute | solution.py:289
  17.6 10.4 %collective-permute-start.9 = (f32[392,128]{1,0:T(8,128)S(1)}, f32[392,128]{1,0:T(8,128)S(1)}, u32[]{:S(2)}, u32[]{:S(2)}) collective-permute-start(f32[392,128]{1,0:T(8,128)S(1)} %relay.8.refs_1_.refs_2_.refs_3_), channel_id=1, source_target_pairs={{0,4},{2,6},{4,0},{6,2},{8,12},{10,14},{12,8},{14,10},{16,20},{18,... | collective-permute-start | bytes 602120 | tf_op jit(solution)/shard_map/ppermute | solution.py:289
  18.8 9.2 %collective-permute-start.8 = (f32[392,128]{1,0:T(8,128)S(1)}, f32[392,128]{1,0:T(8,128)S(1)}, u32[]{:S(2)}, u32[]{:S(2)}) collective-permute-start(f32[392,128]{1,0:T(8,128)S(1)} %relay.8.refs_1_.refs_2_.refs_3_), channel_id=1, source_target_pairs={{0,8},{2,10},{4,12},{6,14},{8,0},{10,2},{12,4},{14,6},{16,24},{18,... | collective-permute-start | bytes 602120 | tf_op jit(solution)/shard_map/ppermute | solution.py:289
  20.2 12.7 %collective-permute-start.6 = (f32[392,128]{1,0:T(8,128)S(1)}, f32[392,128]{1,0:T(8,128)S(1)}, u32[]{:S(2)}, u32[]{:S(2)}) collective-permute-start(f32[392,128]{1,0:T(8,128)S(1)} %relay.9.refs_1_.refs_4_.refs_3_), channel_id=1, source_target_pairs={{0,4},{2,6},{4,0},{6,2},{8,12},{10,14},{12,8},{14,10},{16,20},{18,... | collective-permute-start | bytes 602120 | tf_op jit(solution)/shard_map/ppermute | solution.py:289
  25.9 7.3 %collective-permute-start.5 = (f32[3,136,128]{2,1,0:T(8,128)S(1)}, f32[3,136,128]{2,1,0:T(8,128)S(1)}, u32[]{:S(2)}, u32[]{:S(2)}) collective-permute-start(f32[3,136,128]{2,1,0:T(8,128)S(1)} %get-tuple-element.41.refs_2_), channel_id=1, source_target_pairs={{0,1},{1,0},{2,3},{3,2},{4,5},{5,4},{6,7},{7,6},{8,9},{9,8},{10,11... | collective-permute-start | bytes 626696 | tf_op jit(solution)/shard_map/ppermute | solution.py:338
  30.9 12.0 %collective-permute-start.10 = (f32[3,136,128]{2,1,0:T(8,128)S(1)}, f32[3,136,128]{2,1,0:T(8,128)S(1)}, u32[]{:S(2)}, u32[]{:S(2)}) collective-permute-start(f32[3,136,128]{2,1,0:T(8,128)S(1)} %get-tuple-element.45.refs_2_), channel_id=1, source_target_pairs={{0,1},{1,0},{2,3},{3,2},{4,5},{5,4},{6,7},{7,6},{8,9},{9,8},{10,11... | collective-permute-start | bytes 626696 | tf_op jit(solution)/shard_map/ppermute | solution.py:338
  31.5 7.4 %collective-permute-start.11 = (f32[392,128]{1,0:T(8,128)S(1)}, f32[392,128]{1,0:T(8,128)S(1)}, u32[]{:S(2)}, u32[]{:S(2)}) collective-permute-start(f32[392,128]{1,0:T(8,128)S(1)} %relay.12.refs_1_.refs_3_.refs_7_), channel_id=1, source_target_pairs={{0,2},{2,0},{4,6},{6,4},{8,10},{10,8},{12,14},{14,12},{16,18},{18,... | collective-permute-start | bytes 602120 | tf_op jit(solution)/shard_map/ppermute | solution.py:289
  31.5 7.4 %collective-permute-start.13 = (f32[392,128]{1,0:T(8,128)S(1)}, f32[392,128]{1,0:T(8,128)S(1)}, u32[]{:S(2)}, u32[]{:S(2)}) collective-permute-start(f32[392,128]{1,0:T(8,128)S(1)} %relay.13.refs_4_.refs_3_.refs_6_), channel_id=1, source_target_pairs={{0,4},{2,6},{4,0},{6,2},{8,12},{10,14},{12,8},{14,10},{16,20},{18,... | collective-permute-start | bytes 602120 | tf_op jit(solution)/shard_map/ppermute | solution.py:289
  33.0 5.9 %collective-permute-start.12 = (f32[392,128]{1,0:T(8,128)S(1)}, f32[392,128]{1,0:T(8,128)S(1)}, u32[]{:S(2)}, u32[]{:S(2)}) collective-permute-start(f32[392,128]{1,0:T(8,128)S(1)} %relay.14.refs_4_.refs_8_), channel_id=1, source_target_pairs={{0,2},{2,0},{4,6},{6,4},{8,10},{10,8},{12,14},{14,12},{16,18},{18,... | collective-permute-start | bytes 602120 | tf_op jit(solution)/shard_map/ppermute | solution.py:289
  43.6 8.1 %collective-permute-start.14 = (f32[3,392,128]{2,1,0:T(8,128)S(1)}, f32[3,392,128]{2,1,0:T(8,128)S(1)}, u32[]{:S(2)}, u32[]{:S(2)}) collective-permute-start(f32[3,392,128]{2,1,0:T(8,128)S(1)} %get-tuple-element.47.refs_7_), channel_id=1, source_target_pairs={{0,2},{2,0},{4,6},{6,4},{8,10},{10,8},{12,14},{14,12},{16,18},{18,... | collective-permute-start | bytes 1806344 | tf_op jit(solution)/shard_map/ppermute | solution.py:289
  43.7 9.1 %collective-permute-start.18 = (f32[4,136,128]{2,1,0:T(8,128)S(1)}, f32[4,136,128]{2,1,0:T(8,128)S(1)}, u32[]{:S(2)}, u32[]{:S(2)}) collective-permute-start(f32[4,136,128]{2,1,0:T(8,128)S(1)} %get-tuple-element.52.refs_2_), channel_id=1, source_target_pairs={{0,1},{1,0},{2,3},{3,2},{4,5},{5,4},{6,7},{7,6},{8,9},{9,8},{10,11... | collective-permute-start | bytes 835592 | tf_op jit(solution)/shard_map/ppermute | solution.py:338
  45.8 5.9 %collective-permute-start.15 = (f32[392,128]{1,0:T(8,128)S(1)}, f32[392,128]{1,0:T(8,128)S(1)}, u32[]{:S(2)}, u32[]{:S(2)}) collective-permute-start(f32[392,128]{1,0:T(8,128)S(1)} %get-tuple-element.42.refs_1_), channel_id=1, source_target_pairs={{0,2},{2,0},{4,6},{6,4},{8,10},{10,8},{12,14},{14,12},{16,18},{18,... | collective-permute-start | bytes 602120 | tf_op jit(solution)/shard_map/ppermute | solution.py:289
  50.8 8.9 %collective-permute-start.22 = (f32[4,136,128]{2,1,0:T(8,128)S(1)}, f32[4,136,128]{2,1,0:T(8,128)S(1)}, u32[]{:S(2)}, u32[]{:S(2)}) collective-permute-start(f32[4,136,128]{2,1,0:T(8,128)S(1)} %get-tuple-element.57.refs_2_), channel_id=1, source_target_pairs={{0,1},{1,0},{2,3},{3,2},{4,5},{5,4},{6,7},{7,6},{8,9},{9,8},{10,11... | collective-permute-start | bytes 835592 | tf_op jit(solution)/shard_map/ppermute | solution.py:338
  55.6 19.0 %collective-permute-start.21 = (f32[2,392,128]{2,1,0:T(8,128)S(1)}, f32[2,392,128]{2,1,0:T(8,128)S(1)}, u32[]{:S(2)}, u32[]{:S(2)}) collective-permute-start(f32[2,392,128]{2,1,0:T(8,128)S(1)} %merge.15.refs_4_), channel_id=1, source_target_pairs={{0,4},{2,6},{4,0},{6,2},{8,12},{10,14},{12,8},{14,10},{16,20},{18,... | collective-permute-start | bytes 1204232 | tf_op jit(solution)/shard_map/ppermute | solution.py:289
  61.2 13.2 %collective-permute-start.23 = (f32[392,128]{1,0:T(8,128)S(1)}, f32[392,128]{1,0:T(8,128)S(1)}, u32[]{:S(2)}, u32[]{:S(2)}) collective-permute-start(f32[392,128]{1,0:T(8,128)S(1)} %get-tuple-element.59), channel_id=1, source_target_pairs={{0,2},{2,0},{4,6},{6,4},{8,10},{10,8},{12,14},{14,12},{16,18},{18,... | collective-permute-start | bytes 602120 | tf_op jit(solution)/shard_map/ppermute | solution.py:289
  62.2 15.0 %collective-permute-start.30 = (f32[392,128]{1,0:T(8,128)S(1)}, f32[392,128]{1,0:T(8,128)S(1)}, u32[]{:S(2)}, u32[]{:S(2)}) collective-permute-start(f32[392,128]{1,0:T(8,128)S(1)} %merge.16.refs_2_), channel_id=1, source_target_pairs={{0,4},{2,6},{4,0},{6,2},{8,12},{10,14},{12,8},{14,10},{16,20},{18,... | collective-permute-start | bytes 602120 | tf_op jit(solution)/shard_map/ppermute | solution.py:289
  72.8 6.5 %collective-permute-start.33 = (f32[392,128]{1,0:T(8,128)S(1)}, f32[392,128]{1,0:T(8,128)S(1)}, u32[]{:S(2)}, u32[]{:S(2)}) collective-permute-start(f32[392,128]{1,0:T(8,128)S(1)} %merge.12.refs_2_), channel_id=1, source_target_pairs={{0,4},{2,6},{4,0},{6,2},{8,12},{10,14},{12,8},{14,10},{16,20},{18,... | collective-permute-start | bytes 602120 | tf_op jit(solution)/shard_map/ppermute | solution.py:289
  74.6 15.3 %collective-permute-start.28 = (f32[392,128]{1,0:T(8,128)S(1)}, f32[392,128]{1,0:T(8,128)S(1)}, u32[]{:S(2)}, u32[]{:S(2)}) collective-permute-start(f32[392,128]{1,0:T(8,128)S(1)} %merge.18.refs_2_), channel_id=1, source_target_pairs={{0,16},{2,18},{4,20},{6,22},{8,24},{10,26},{12,28},{14,30},{16,0},... | collective-permute-start | bytes 602120 | tf_op jit(solution)/shard_map/ppermute | solution.py:289
  76.9 13.1 %collective-permute-start.29 = (f32[392,128]{1,0:T(8,128)S(1)}, f32[392,128]{1,0:T(8,128)S(1)}, u32[]{:S(2)}, u32[]{:S(2)}) collective-permute-start(f32[392,128]{1,0:T(8,128)S(1)} %merge.19.refs_2_), channel_id=1, source_target_pairs={{0,8},{2,10},{4,12},{6,14},{8,0},{10,2},{12,4},{14,6},{16,24},{18,... | collective-permute-start | bytes 602120 | tf_op jit(solution)/shard_map/ppermute | solution.py:289
  77.3 12.6 %collective-permute-start.32 = (f32[392,128]{1,0:T(8,128)S(1)}, f32[392,128]{1,0:T(8,128)S(1)}, u32[]{:S(2)}, u32[]{:S(2)}) collective-permute-start(f32[392,128]{1,0:T(8,128)S(1)} %merge.20.refs_20_), channel_id=1, source_target_pairs={{0,24},{2,26},{4,28},{6,30},{8,16},{10,18},{12,20},{14,22},{16,8},... | collective-permute-start | bytes 602120 | tf_op jit(solution)/shard_map/ppermute | solution.py:289
  (18 other events, 65.9 us)

commit v9 on v8

--- a/solution.py
+++ b/solution.py
@@ -82,8 +82,12 @@
     dt_ref[...] = d_ref[...].T
 
 
-def score_body(places, me_ref, d_ref, pool_ref, *refs):
+def score_body(places, early, me_ref, d_ref, pool_ref, *refs):
     part_ref, rows_ref = refs[-2:]
+    if early:
+        early_part_ref, early_rows_ref = refs[-4:-2]
+        part_ref[len(places) :] = early_part_ref[...]
+        rows_ref[len(places) :] = early_rows_ref[...]
     rows, features = d_ref.shape
     columns = pool_ref.shape[1]
     tile = 128
@@ -321,19 +325,28 @@
     weights, sums, e_place = [], {}, {}
     waiting, stage = [], {}
 
-    def score(blocks):
-        k = len(blocks)
+    held = []
+
+    def score(blocks, hold=False):
+        early = held.pop() if held else ([], ())
+        k = len(blocks) + len(early[0])
         used = sorted({x_place[r][0] for r in blocks})
         part, found = line(
             functools.partial(
-                score_body, [(used.index(x_place[r][0]), x_place[r][1]) for r in blocks]
+                score_body,
+                [(used.index(x_place[r][0]), x_place[r][1]) for r in blocks],
+                len(early[0]),
             ),
             (shape(k, rows + SLACK, rows), shape(k, features, rows)),
             "score",
-            [me.reshape(1), document_matrix, pool] + [x_arrays[i] for i in used],
-            0.9 * k,
-            [smem] + [vmem] * (2 + len(used)),
-        )
+            [me.reshape(1), document_matrix, pool] + [x_arrays[i] for i in used] + [*early[1]],
+            0.9 * len(blocks),
+            [smem] + [vmem] * (2 + len(used) + len(early[1])),
+        )
+        blocks = blocks + early[0]
+        if hold:
+            held.append((blocks, (part, found)))
+            return
         got = [
             lax.ppermute(part, "dim", [(i, (i + s) % depth) for i in range(depth)])
             for s in range(1, depth)
@@ -414,21 +427,20 @@
     keep(send(packed, 2), 2)
     keep(send(packed, 1), 1)
     dt = line(flip_body, shape(features, rows), "flip", [document_matrix], 0.1)
-    score([0, 1])
+    score([0, 1], hold=True)
     forward(2)
     forward(1)
     relay(2)
     share_all(2, 4, 8)
     score([2, 4, 8])
-    softmax()
     relay(10)
     forward(3)
     score([3, 5, 9])
     relay(6)
     share(10, 6)
     softmax()
+    score([10, 6, 11, 7])
     relay(14)
-    score([10, 6, 11, 7])
     share(12, 14)
     softmax()
     for k in range(3, far):
@@ -512,10 +524,10 @@
         last_body,
         (shape(rows, features), shape(rows)),
         "finish",
-        [document_matrix, weights[0], *arrays],
+        [document_matrix, weights[e_place[0][0]], *arrays],
         0.8,
         [full(rows, features)]
-        + [pl.BlockSpec((1, SLACK, rows), lambda i: (0, rows // SLACK, 0))]
+        + [pl.BlockSpec((1, SLACK, rows), lambda i: (e_place[0][1], rows // SLACK, 0))]
         + [full(*a.shape) for a in arrays],
         grid=(1,),
         out_specs=(full(rows, features), full(rows)),

time: 91.5 us -> 88.4 us (0.966)
  waiting for transfers between devices: 18.7 us -> 16.6 us
    ppermute x29, waiting for transfers between devices: 14.5 us -> 10.2 us  [send(): return lax.ppermute(x, 'blk', [(i, i ^ mask) for i in range(n)])]
    ppermute x5 -> x4, waiting for transfers between devices: 4.25 us -> 6.41 us  [score(): lax.ppermute(part, 'dim', [(i, (i + s) % depth) for i in range(depth)])]
    ppermute x5 -> x4, starting transfers between devices: 6.04 us -> 5.6 us  [score(): lax.ppermute(part, 'dim', [(i, (i + s) % depth) for i in range(depth)])]
    pallas_call x38 -> x37, Pallas kernels: 32.4 us -> 32.1 us  [__call__(): pl.pallas_call(kernel, out_shape=out_shape, name=name, in_specs=in_specs,...]
  transfers between devices with their start and end apart: 34 -> 33, of which waited for: 12 -> 13; matrix products, arithmetic and copies ran while one was open for 0% -> 0% of each run, Pallas kernels for 32% -> 33%
where the time goes in v9:
time: 88.4 us; the launch traced here: 87.7 us
  starting transfers between devices  32.3 us (37%)
  Pallas kernels  32.1 us (36%)
  waiting for transfers between devices  16.6 us (19%)
  local copies, waits for them, and re-layouts  5.61 us (6%)
  between operations  1.06 us (1%)
    pallas_call x37, Pallas kernels, __call__(): pl.pallas_call(kernel, out_shape=out_shape, name=name, in_specs=in_specs,...  32.1 us
    ppermute x29, starting transfers between devices, send(): return lax.ppermute(x, 'blk', [(i, i ^ mask) for i in range(n)])  26.7 us
    ppermute x29, waiting for transfers between devices, send(): return lax.ppermute(x, 'blk', [(i, i ^ mask) for i in range(n)])  10.2 us
    ppermute x4, waiting for transfers between devices, score(): lax.ppermute(part, 'dim', [(i, (i + s) % depth) for i in range(depth)])  6.41 us
    unnamed x16, local copies, waits for them, and re-layouts  5.61 us
    ppermute x4, starting transfers between devices, score(): lax.ppermute(part, 'dim', [(i, (i + s) % depth) for i in range(depth)])  5.6 us
  transfers between devices with their start and end apart: 33, of which 13 were waited for; matrix products, arithmetic and copies ran while one was open for 0% of the time, Pallas kernels for 33%

profile of v9, /device:TPU:0, one launch (start us, length us, event | category | flops | bytes accessed | tf_op | source)
XLA Modules:
  0.0 87.7 jit_solution(4925177380079858537)
XLA Ops:
  0.6 1.8 %pack.1.refs_1_.refs_3_ = f32[392,128]{1,0:T(8,128)} custom-call(f32[128,384]{1,0:T(8,128)} %refs_0_.3, s32[8,128]{1,0:T(8,128)} %bitcast.3, s32[8,128]{1,0:T(8,128)} %bitcast.4), custom_call_target="tpu_custom_call" | custom-call | bytes 6660000 | tf_op jit(solution)/shard_map/pack/pallas_call | solution.py:45
  2.9 3.7 %collective-permute-start = (f32[392,128]{1,0:T(8,128)}, f32[392,128]{1,0:T(8,128)S(1)}, u32[]{:S(2)}, u32[]{:S(2)}) collective-permute-start(f32[392,128]{1,0:T(8,128)} %pack.1.refs_1_.refs_3_), channel_id=1, source_target_pairs={{0,16},{2,18},{4,20},{6,22},{8,24},{10,26},{12,28},{14,30},{16,0},... | collective-permute-start | bytes 602120 | tf_op jit(solution)/shard_map/ppermute | solution.py:293
  6.6 1.6 %collective-permute-start.2 = (f32[392,128]{1,0:T(8,128)}, f32[392,128]{1,0:T(8,128)S(1)}, u32[]{:S(2)}, u32[]{:S(2)}) collective-permute-start(f32[392,128]{1,0:T(8,128)} %pack.1.refs_1_.refs_3_), channel_id=1, source_target_pairs={{0,8},{2,10},{4,12},{6,14},{8,0},{10,2},{12,4},{14,6},{16,24},{18,... | collective-permute-start | bytes 602120 | tf_op jit(solution)/shard_map/ppermute | solution.py:293
  8.2 1.5 %collective-permute-start.3 = (f32[392,128]{1,0:T(8,128)}, f32[392,128]{1,0:T(8,128)S(1)}, u32[]{:S(2)}, u32[]{:S(2)}) collective-permute-start(f32[392,128]{1,0:T(8,128)} %pack.1.refs_1_.refs_3_), channel_id=1, source_target_pairs={{0,4},{2,6},{4,0},{6,2},{8,12},{10,14},{12,8},{14,10},{16,20},{18,... | collective-permute-start | bytes 602120 | tf_op jit(solution)/shard_map/ppermute | solution.py:293
  11.7 1.9 %copy-done = f32[384,2048]{1,0:T(8,128)S(1)} copy-done((f32[384,2048]{1,0:T(8,128)S(1)}, f32[384,2048]{1,0:T(8,128)}, u32[]{:S(2)}) %copy-start) | copy-done | bytes 3145752
  15.4 2.0 %score.5 = (f32[2,136,128]{2,1,0:T(8,128)S(1)}, f32[2,384,128]{2,1,0:T(8,128)S(1)}) custom-call(s32[1]{0:T(128)} %bitcast.2.refs_0_, f32[128,384]{1,0:T(8,128)S(1)} %copy-done.3, f32[384,2048]{1,0:T(8,128)S(1)} %copy-done, f32[392,128]{1,0:T(8,128)S(1)} %copy-done.6, f32[392,128]{1,0:T(8,128)S(1)} %collective-permute-done.1.refs_4_.refs_5_, ...), custom_call_target="tpu_custom_call" | custom-call | bytes 6660000 | tf_op jit(solution)/shard_map/score/pallas_call | solution.py:45
  20.8 2.9 %score.6 = (f32[5,136,128]{2,1,0:T(8,128)S(1)}, f32[5,384,128]{2,1,0:T(8,128)S(1)}) custom-call(s32[1]{0:T(128)} %bitcast.2.refs_0_, f32[128,384]{1,0:T(8,128)S(1)} %copy-done.4, f32[384,2048]{1,0:T(8,128)S(1)} %copy-done.1, f32[392,128]{1,0:T(8,128)S(1)} %relay.8.refs_1_.refs_2_.refs_3_, f32[392,128]{1,0:T(8,128)S(1)} %relay.9.refs_1_.refs_4_.refs_3_, ...), custom_call_target="tpu_custom_call" | custom-call | bytes 9990000 | tf_op jit(solution)/shard_map/score/pallas_call | solution.py:45
  23.6 1.6 %collective-permute-start.4 = (f32[5,136,128]{2,1,0:T(8,128)S(1)}, f32[5,136,128]{2,1,0:T(8,128)S(1)}, u32[]{:S(2)}, u32[]{:S(2)}) collective-permute-start(f32[5,136,128]{2,1,0:T(8,128)S(1)} %get-tuple-element.39.refs_2_), channel_id=1, source_target_pairs={{0,1},{1,0},{2,3},{3,2},{4,5},{5,4},{6,7},{7,6},{8,9},{9,8},{10,11... | collective-permute-start | bytes 1044488 | tf_op jit(solution)/shard_map/ppermute | solution.py:351
  25.9 2.9 %score.7 = (f32[3,136,128]{2,1,0:T(8,128)S(1)}, f32[3,384,128]{2,1,0:T(8,128)S(1)}) custom-call(s32[1]{0:T(128)} %bitcast.2.refs_0_, f32[128,384]{1,0:T(8,128)S(1)} %copy-done.4, f32[384,2048]{1,0:T(8,128)S(1)} %copy-done.1, f32[3,392,128]{2,1,0:T(8,128)S(1)} %collective-permute-done.6.refs_3_.refs_9_, f32[392,128]{1,0:T(8,128)S(1)} %relay.13.refs_4_.refs_3_.refs_6_), custom_call_target="tpu_custom_call" | custom-call | bytes 9990000 | tf_op jit(solution)/shard_map/score/pallas_call | solution.py:45
  28.7 1.6 %collective-permute-start.9 = (f32[3,136,128]{2,1,0:T(8,128)S(1)}, f32[3,136,128]{2,1,0:T(8,128)S(1)}, u32[]{:S(2)}, u32[]{:S(2)}) collective-permute-start(f32[3,136,128]{2,1,0:T(8,128)S(1)} %get-tuple-element.43.refs_2_), channel_id=1, source_target_pairs={{0,1},{1,0},{2,3},{3,2},{4,5},{5,4},{6,7},{7,6},{8,9},{9,8},{10,11... | collective-permute-start | bytes 626696 | tf_op jit(solution)/shard_map/ppermute | solution.py:351
  31.8 3.0 %collective-permute-done.4.refs_3_ = f32[5,136,128]{2,1,0:T(8,128)S(1)} collective-permute-done((f32[5,136,128]{2,1,0:T(8,128)S(1)}, f32[5,136,128]{2,1,0:T(8,128)S(1)}, u32[]{:S(2)}, u32[]{:S(2)}) %collective-permute-start.4) | collective-permute-done | bytes 348192 | tf_op jit(solution)/shard_map/ppermute | solution.py:351
  35.8 3.8 %score.8 = (f32[4,136,128]{2,1,0:T(8,128)S(1)}, f32[4,384,128]{2,1,0:T(8,128)S(1)}) custom-call(s32[1]{0:T(128)} %bitcast.2.refs_0_, f32[128,384]{1,0:T(8,128)S(1)} %copy-done.4, f32[384,2048]{1,0:T(8,128)S(1)} %copy-done.1, f32[392,128]{1,0:T(8,128)S(1)} %relay.12.refs_1_.refs_3_.refs_7_, f32[392,128]{1,0:T(8,128)S(1)} %relay.14.refs_4_.refs_8_, ...), custom_call_target="tpu_custom_call" | custom-call | bytes 13320000 | tf_op jit(solution)/shard_map/score/pallas_call | solution.py:45
  40.6 1.6 %collective-permute-start.17 = (f32[4,136,128]{2,1,0:T(8,128)S(1)}, f32[4,136,128]{2,1,0:T(8,128)S(1)}, u32[]{:S(2)}, u32[]{:S(2)}) collective-permute-start(f32[4,136,128]{2,1,0:T(8,128)S(1)} %get-tuple-element.51.refs_2_), channel_id=1, source_target_pairs={{0,1},{1,0},{2,3},{3,2},{4,5},{5,4},{6,7},{7,6},{8,9},{9,8},{10,11... | collective-permute-start | bytes 835592 | tf_op jit(solution)/shard_map/ppermute | solution.py:351
  43.9 3.8 %score.9 = (f32[4,136,128]{2,1,0:T(8,128)S(1)}, f32[4,384,128]{2,1,0:T(8,128)S(1)}) custom-call(s32[1]{0:T(128)} %bitcast.2.refs_0_, f32[128,384]{1,0:T(8,128)S(1)} %copy-done.4, f32[384,2048]{1,0:T(8,128)S(1)} %copy-done.1, f32[392,128]{1,0:T(8,128)S(1)} %relay.13.refs_4_.refs_3_.refs_6_, f32[392,128]{1,0:T(8,128)S(1)} %relay.15.refs_4_.refs_10_, ...), custom_call_target="tpu_custom_call" | custom-call | bytes 13320000 | tf_op jit(solution)/shard_map/score/pallas_call | solution.py:45
  52.5 1.6 %collective-permute-start.20 = (f32[2,392,128]{2,1,0:T(8,128)S(1)}, f32[2,392,128]{2,1,0:T(8,128)S(1)}, u32[]{:S(2)}, u32[]{:S(2)}) collective-permute-start(f32[2,392,128]{2,1,0:T(8,128)S(1)} %merge.15.refs_4_), channel_id=1, source_target_pairs={{0,4},{2,6},{4,0},{6,2},{8,12},{10,14},{12,8},{14,10},{16,20},{18,... | collective-permute-start | bytes 1204232 | tf_op jit(solution)/shard_map/ppermute | solution.py:293
  54.0 2.5 %collective-permute-done.21.refs_3_ = f32[4,136,128]{2,1,0:T(8,128)S(1)} collective-permute-done((f32[4,136,128]{2,1,0:T(8,128)S(1)}, f32[4,136,128]{2,1,0:T(8,128)S(1)}, u32[]{:S(2)}, u32[]{:S(2)}) %collective-permute-start.21) | collective-permute-done | bytes 278560 | tf_op jit(solution)/shard_map/ppermute | solution.py:351
  59.1 1.6 %collective-permute-start.29 = (f32[392,128]{1,0:T(8,128)S(1)}, f32[392,128]{1,0:T(8,128)S(1)}, u32[]{:S(2)}, u32[]{:S(2)}) collective-permute-start(f32[392,128]{1,0:T(8,128)S(1)} %merge.16.refs_2_), channel_id=1, source_target_pairs={{0,4},{2,6},{4,0},{6,2},{8,12},{10,14},{12,8},{14,10},{16,20},{18,... | collective-permute-start | bytes 602120 | tf_op jit(solution)/shard_map/ppermute | solution.py:293
  60.7 2.3 %collective-permute-start.24 = (f32[2,16,128]{2,1,0:T(8,128)S(1)}, f32[2,16,128]{2,1,0:T(8,128)S(1)}, u32[]{:S(2)}, u32[]{:S(2)}) collective-permute-start(f32[2,16,128]{2,1,0:T(8,128)S(1)} %stats_merge.4.refs_2_.refs_0_), channel_id=1, source_target_pairs={{0,16},{2,18},{4,20},{6,22},{8,24},{10,26},{12,28},{14,30},{16,0},... | collective-permute-start | bytes 49160 | tf_op jit(solution)/shard_map/ppermute | solution.py:293
  63.0 2.5 %collective-permute-done.24.refs_1_ = f32[2,16,128]{2,1,0:T(8,128)S(1)} collective-permute-done((f32[2,16,128]{2,1,0:T(8,128)S(1)}, f32[2,16,128]{2,1,0:T(8,128)S(1)}, u32[]{:S(2)}, u32[]{:S(2)}) %collective-permute-start.24) | collective-permute-done | bytes 16416 | tf_op jit(solution)/shard_map/ppermute | solution.py:293
  66.1 3.2 %collective-permute-done.26.refs_1_ = f32[2,16,128]{2,1,0:T(8,128)S(1)} collective-permute-done((f32[2,16,128]{2,1,0:T(8,128)S(1)}, f32[2,16,128]{2,1,0:T(8,128)S(1)}, u32[]{:S(2)}, u32[]{:S(2)}) %collective-permute-start.26) | collective-permute-done | bytes 16416 | tf_op jit(solution)/shard_map/ppermute | solution.py:293
  69.7 1.7 %collective-permute-start.32 = (f32[392,128]{1,0:T(8,128)S(1)}, f32[392,128]{1,0:T(8,128)S(1)}, u32[]{:S(2)}, u32[]{:S(2)}) collective-permute-start(f32[392,128]{1,0:T(8,128)S(1)} %merge.12.refs_2_), channel_id=1, source_target_pairs={{0,4},{2,6},{4,0},{6,2},{8,12},{10,14},{12,8},{14,10},{16,20},{18,... | collective-permute-start | bytes 602120 | tf_op jit(solution)/shard_map/ppermute | solution.py:293
  71.5 2.2 %collective-permute-start.27 = (f32[392,128]{1,0:T(8,128)S(1)}, f32[392,128]{1,0:T(8,128)S(1)}, u32[]{:S(2)}, u32[]{:S(2)}) collective-permute-start(f32[392,128]{1,0:T(8,128)S(1)} %merge.18.refs_2_), channel_id=1, source_target_pairs={{0,16},{2,18},{4,20},{6,22},{8,24},{10,26},{12,28},{14,30},{16,0},... | collective-permute-start | bytes 602120 | tf_op jit(solution)/shard_map/ppermute | solution.py:293
  73.9 2.3 %collective-permute-start.31 = (f32[392,128]{1,0:T(8,128)S(1)}, f32[392,128]{1,0:T(8,128)S(1)}, u32[]{:S(2)}, u32[]{:S(2)}) collective-permute-start(f32[392,128]{1,0:T(8,128)S(1)} %merge.20.refs_19_), channel_id=1, source_target_pairs={{0,24},{2,26},{4,28},{6,30},{8,16},{10,18},{12,20},{14,22},{16,8},... | collective-permute-start | bytes 602120 | tf_op jit(solution)/shard_map/ppermute | solution.py:293
  76.2 9.8 %gradient.1 = (f32[128,384]{1,0:T(8,128)}, f32[384,2048]{1,0:T(8,128)}) custom-call(f32[2,16,128]{2,1,0:T(8,128)S(1)} %stats_merge.7.refs_2_.refs_0_, f32[392,128]{1,0:T(8,128)S(1)} %copy-done.7, f32[392,128]{1,0:T(8,128)S(1)} %relay.8.refs_1_.refs_2_.refs_3_, f32[392,128]{1,0:T(8,128)S(1)} %relay.9.refs_1_.refs_4_.refs_3_, ...), custom_call_target="tpu_custom_call" | custom-call | bytes 40700000 | tf_op jit(solution)/shard_map/gradient/pallas_call | solution.py:45
  (95 shorter events, 23.6 us)
Async XLA Ops:
  2.4 9.2 %collective-permute-start.1 = (f32[392,128]{1,0:T(8,128)}, f32[392,128]{1,0:T(8,128)S(1)}, u32[]{:S(2)}, u32[]{:S(2)}) collective-permute-start(f32[392,128]{1,0:T(8,128)} %pack.1.refs_1_.refs_3_), channel_id=1, source_target_pairs={{0,2},{2,0},{4,6},{6,4},{8,10},{10,8},{12,14},{14,12},{16,18},{18,... | collective-permute-start | bytes 602120 | tf_op jit(solution)/shard_map/ppermute | solution.py:293
  2.9 14.4 %collective-permute-start = (f32[392,128]{1,0:T(8,128)}, f32[392,128]{1,0:T(8,128)S(1)}, u32[]{:S(2)}, u32[]{:S(2)}) collective-permute-start(f32[392,128]{1,0:T(8,128)} %pack.1.refs_1_.refs_3_), channel_id=1, source_target_pairs={{0,16},{2,18},{4,20},{6,22},{8,24},{10,26},{12,28},{14,30},{16,0},... | collective-permute-start | bytes 602120 | tf_op jit(solution)/shard_map/ppermute | solution.py:293
  6.6 10.8 %collective-permute-start.2 = (f32[392,128]{1,0:T(8,128)}, f32[392,128]{1,0:T(8,128)S(1)}, u32[]{:S(2)}, u32[]{:S(2)}) collective-permute-start(f32[392,128]{1,0:T(8,128)} %pack.1.refs_1_.refs_3_), channel_id=1, source_target_pairs={{0,8},{2,10},{4,12},{6,14},{8,0},{10,2},{12,4},{14,6},{16,24},{18,... | collective-permute-start | bytes 602120 | tf_op jit(solution)/shard_map/ppermute | solution.py:293
  8.2 9.3 %collective-permute-start.3 = (f32[392,128]{1,0:T(8,128)}, f32[392,128]{1,0:T(8,128)S(1)}, u32[]{:S(2)}, u32[]{:S(2)}) collective-permute-start(f32[392,128]{1,0:T(8,128)} %pack.1.refs_1_.refs_3_), channel_id=1, source_target_pairs={{0,4},{2,6},{4,0},{6,2},{8,12},{10,14},{12,8},{14,10},{16,20},{18,... | collective-permute-start | bytes 602120 | tf_op jit(solution)/shard_map/ppermute | solution.py:293
  17.5 8.3 %collective-permute-start.6 = (f32[3,392,128]{2,1,0:T(8,128)S(1)}, f32[3,392,128]{2,1,0:T(8,128)S(1)}, u32[]{:S(2)}, u32[]{:S(2)}) collective-permute-start(f32[3,392,128]{2,1,0:T(8,128)S(1)} %relay.11.refs_8_), channel_id=1, source_target_pairs={{0,2},{2,0},{4,6},{6,4},{8,10},{10,8},{12,14},{14,12},{16,18},{18,... | collective-permute-start | bytes 1806344 | tf_op jit(solution)/shard_map/ppermute | solution.py:293
  17.6 7.9 %collective-permute-start.8 = (f32[392,128]{1,0:T(8,128)S(1)}, f32[392,128]{1,0:T(8,128)S(1)}, u32[]{:S(2)}, u32[]{:S(2)}) collective-permute-start(f32[392,128]{1,0:T(8,128)S(1)} %relay.8.refs_1_.refs_2_.refs_3_), channel_id=1, source_target_pairs={{0,4},{2,6},{4,0},{6,2},{8,12},{10,14},{12,8},{14,10},{16,20},{18,... | collective-permute-start | bytes 602120 | tf_op jit(solution)/shard_map/ppermute | solution.py:293
  18.8 7.1 %collective-permute-start.7 = (f32[392,128]{1,0:T(8,128)S(1)}, f32[392,128]{1,0:T(8,128)S(1)}, u32[]{:S(2)}, u32[]{:S(2)}) collective-permute-start(f32[392,128]{1,0:T(8,128)S(1)} %relay.8.refs_1_.refs_2_.refs_3_), channel_id=1, source_target_pairs={{0,8},{2,10},{4,12},{6,14},{8,0},{10,2},{12,4},{14,6},{16,24},{18,... | collective-permute-start | bytes 602120 | tf_op jit(solution)/shard_map/ppermute | solution.py:293
  20.2 10.1 %collective-permute-start.5 = (f32[392,128]{1,0:T(8,128)S(1)}, f32[392,128]{1,0:T(8,128)S(1)}, u32[]{:S(2)}, u32[]{:S(2)}) collective-permute-start(f32[392,128]{1,0:T(8,128)S(1)} %relay.9.refs_1_.refs_4_.refs_3_), channel_id=1, source_target_pairs={{0,4},{2,6},{4,0},{6,2},{8,12},{10,14},{12,8},{14,10},{16,20},{18,... | collective-permute-start | bytes 602120 | tf_op jit(solution)/shard_map/ppermute | solution.py:293
  23.6 11.1 %collective-permute-start.4 = (f32[5,136,128]{2,1,0:T(8,128)S(1)}, f32[5,136,128]{2,1,0:T(8,128)S(1)}, u32[]{:S(2)}, u32[]{:S(2)}) collective-permute-start(f32[5,136,128]{2,1,0:T(8,128)S(1)} %get-tuple-element.39.refs_2_), channel_id=1, source_target_pairs={{0,1},{1,0},{2,3},{3,2},{4,5},{5,4},{6,7},{7,6},{8,9},{9,8},{10,11... | collective-permute-start | bytes 1044488 | tf_op jit(solution)/shard_map/ppermute | solution.py:351
  28.7 10.9 %collective-permute-start.9 = (f32[3,136,128]{2,1,0:T(8,128)S(1)}, f32[3,136,128]{2,1,0:T(8,128)S(1)}, u32[]{:S(2)}, u32[]{:S(2)}) collective-permute-start(f32[3,136,128]{2,1,0:T(8,128)S(1)} %get-tuple-element.43.refs_2_), channel_id=1, source_target_pairs={{0,1},{1,0},{2,3},{3,2},{4,5},{5,4},{6,7},{7,6},{8,9},{9,8},{10,11... | collective-permute-start | bytes 626696 | tf_op jit(solution)/shard_map/ppermute | solution.py:351
  30.3 5.5 %collective-permute-start.11 = (f32[392,128]{1,0:T(8,128)S(1)}, f32[392,128]{1,0:T(8,128)S(1)}, u32[]{:S(2)}, u32[]{:S(2)}) collective-permute-start(f32[392,128]{1,0:T(8,128)S(1)} %relay.12.refs_1_.refs_3_.refs_7_), channel_id=1, source_target_pairs={{0,2},{2,0},{4,6},{6,4},{8,10},{10,8},{12,14},{14,12},{16,18},{18,... | collective-permute-start | bytes 602120 | tf_op jit(solution)/shard_map/ppermute | solution.py:293
  30.3 5.5 %collective-permute-start.12 = (f32[392,128]{1,0:T(8,128)S(1)}, f32[392,128]{1,0:T(8,128)S(1)}, u32[]{:S(2)}, u32[]{:S(2)}) collective-permute-start(f32[392,128]{1,0:T(8,128)S(1)} %relay.14.refs_4_.refs_8_), channel_id=1, source_target_pairs={{0,2},{2,0},{4,6},{6,4},{8,10},{10,8},{12,14},{14,12},{16,18},{18,... | collective-permute-start | bytes 602120 | tf_op jit(solution)/shard_map/ppermute | solution.py:293
  30.9 8.7 %collective-permute-start.10 = (f32[392,128]{1,0:T(8,128)S(1)}, f32[392,128]{1,0:T(8,128)S(1)}, u32[]{:S(2)}, u32[]{:S(2)}) collective-permute-start(f32[392,128]{1,0:T(8,128)S(1)} %relay.13.refs_4_.refs_3_.refs_6_), channel_id=1, source_target_pairs={{0,4},{2,6},{4,0},{6,2},{8,12},{10,14},{12,8},{14,10},{16,20},{18,... | collective-permute-start | bytes 602120 | tf_op jit(solution)/shard_map/ppermute | solution.py:293
  40.5 8.1 %collective-permute-start.13 = (f32[3,392,128]{2,1,0:T(8,128)S(1)}, f32[3,392,128]{2,1,0:T(8,128)S(1)}, u32[]{:S(2)}, u32[]{:S(2)}) collective-permute-start(f32[3,392,128]{2,1,0:T(8,128)S(1)} %get-tuple-element.46.refs_7_), channel_id=1, source_target_pairs={{0,2},{2,0},{4,6},{6,4},{8,10},{10,8},{12,14},{14,12},{16,18},{18,... | collective-permute-start | bytes 1806344 | tf_op jit(solution)/shard_map/ppermute | solution.py:293
  40.6 9.1 %collective-permute-start.17 = (f32[4,136,128]{2,1,0:T(8,128)S(1)}, f32[4,136,128]{2,1,0:T(8,128)S(1)}, u32[]{:S(2)}, u32[]{:S(2)}) collective-permute-start(f32[4,136,128]{2,1,0:T(8,128)S(1)} %get-tuple-element.51.refs_2_), channel_id=1, source_target_pairs={{0,1},{1,0},{2,3},{3,2},{4,5},{5,4},{6,7},{7,6},{8,9},{9,8},{10,11... | collective-permute-start | bytes 835592 | tf_op jit(solution)/shard_map/ppermute | solution.py:351
  42.7 5.9 %collective-permute-start.14 = (f32[392,128]{1,0:T(8,128)S(1)}, f32[392,128]{1,0:T(8,128)S(1)}, u32[]{:S(2)}, u32[]{:S(2)}) collective-permute-start(f32[392,128]{1,0:T(8,128)S(1)} %get-tuple-element.44.refs_7_), channel_id=1, source_target_pairs={{0,2},{2,0},{4,6},{6,4},{8,10},{10,8},{12,14},{14,12},{16,18},{18,... | collective-permute-start | bytes 602120 | tf_op jit(solution)/shard_map/ppermute | solution.py:293
  47.7 8.9 %collective-permute-start.21 = (f32[4,136,128]{2,1,0:T(8,128)S(1)}, f32[4,136,128]{2,1,0:T(8,128)S(1)}, u32[]{:S(2)}, u32[]{:S(2)}) collective-permute-start(f32[4,136,128]{2,1,0:T(8,128)S(1)} %get-tuple-element.56.refs_2_), channel_id=1, source_target_pairs={{0,1},{1,0},{2,3},{3,2},{4,5},{5,4},{6,7},{7,6},{8,9},{9,8},{10,11... | collective-permute-start | bytes 835592 | tf_op jit(solution)/shard_map/ppermute | solution.py:351
  52.5 19.0 %collective-permute-start.20 = (f32[2,392,128]{2,1,0:T(8,128)S(1)}, f32[2,392,128]{2,1,0:T(8,128)S(1)}, u32[]{:S(2)}, u32[]{:S(2)}) collective-permute-start(f32[2,392,128]{2,1,0:T(8,128)S(1)} %merge.15.refs_4_), channel_id=1, source_target_pairs={{0,4},{2,6},{4,0},{6,2},{8,12},{10,14},{12,8},{14,10},{16,20},{18,... | collective-permute-start | bytes 1204232 | tf_op jit(solution)/shard_map/ppermute | solution.py:293
  58.2 13.2 %collective-permute-start.22 = (f32[392,128]{1,0:T(8,128)S(1)}, f32[392,128]{1,0:T(8,128)S(1)}, u32[]{:S(2)}, u32[]{:S(2)}) collective-permute-start(f32[392,128]{1,0:T(8,128)S(1)} %get-tuple-element.58), channel_id=1, source_target_pairs={{0,2},{2,0},{4,6},{6,4},{8,10},{10,8},{12,14},{14,12},{16,18},{18,... | collective-permute-start | bytes 602120 | tf_op jit(solution)/shard_map/ppermute | solution.py:293
  59.1 14.8 %collective-permute-start.29 = (f32[392,128]{1,0:T(8,128)S(1)}, f32[392,128]{1,0:T(8,128)S(1)}, u32[]{:S(2)}, u32[]{:S(2)}) collective-permute-start(f32[392,128]{1,0:T(8,128)S(1)} %merge.16.refs_2_), channel_id=1, source_target_pairs={{0,4},{2,6},{4,0},{6,2},{8,12},{10,14},{12,8},{14,10},{16,20},{18,... | collective-permute-start | bytes 602120 | tf_op jit(solution)/shard_map/ppermute | solution.py:293
  69.7 6.5 %collective-permute-start.32 = (f32[392,128]{1,0:T(8,128)S(1)}, f32[392,128]{1,0:T(8,128)S(1)}, u32[]{:S(2)}, u32[]{:S(2)}) collective-permute-start(f32[392,128]{1,0:T(8,128)S(1)} %merge.12.refs_2_), channel_id=1, source_target_pairs={{0,4},{2,6},{4,0},{6,2},{8,12},{10,14},{12,8},{14,10},{16,20},{18,... | collective-permute-start | bytes 602120 | tf_op jit(solution)/shard_map/ppermute | solution.py:293
  71.5 15.3 %collective-permute-start.27 = (f32[392,128]{1,0:T(8,128)S(1)}, f32[392,128]{1,0:T(8,128)S(1)}, u32[]{:S(2)}, u32[]{:S(2)}) collective-permute-start(f32[392,128]{1,0:T(8,128)S(1)} %merge.18.refs_2_), channel_id=1, source_target_pairs={{0,16},{2,18},{4,20},{6,22},{8,24},{10,26},{12,28},{14,30},{16,0},... | collective-permute-start | bytes 602120 | tf_op jit(solution)/shard_map/ppermute | solution.py:293
  73.8 13.1 %collective-permute-start.28 = (f32[392,128]{1,0:T(8,128)S(1)}, f32[392,128]{1,0:T(8,128)S(1)}, u32[]{:S(2)}, u32[]{:S(2)}) collective-permute-start(f32[392,128]{1,0:T(8,128)S(1)} %merge.19.refs_2_), channel_id=1, source_target_pairs={{0,8},{2,10},{4,12},{6,14},{8,0},{10,2},{12,4},{14,6},{16,24},{18,... | collective-permute-start | bytes 602120 | tf_op jit(solution)/shard_map/ppermute | solution.py:293
  73.9 12.9 %collective-permute-start.31 = (f32[392,128]{1,0:T(8,128)S(1)}, f32[392,128]{1,0:T(8,128)S(1)}, u32[]{:S(2)}, u32[]{:S(2)}) collective-permute-start(f32[392,128]{1,0:T(8,128)S(1)} %merge.20.refs_19_), channel_id=1, source_target_pairs={{0,24},{2,26},{4,28},{6,30},{8,16},{10,18},{12,20},{14,22},{16,8},... | collective-permute-start | bytes 602120 | tf_op jit(solution)/shard_map/ppermute | solution.py:293
  (17 other events, 57.4 us)

commit v10 on v9

--- a/solution.py
+++ b/solution.py
@@ -343,7 +343,9 @@
             0.9 * len(blocks),
             [smem] + [vmem] * (2 + len(used) + len(early[1])),
         )
-        blocks = blocks + early[0]
+        blocks = [r for r in blocks + early[0] if r % 2 == 0] + [
+            r for r in blocks + early[0] if r % 2
+        ]
         if hold:
             held.append((blocks, (part, found)))
             return
@@ -358,7 +360,7 @@
         k = len(blocks)
         odds = [r for r in blocks if r % 2]
         evens = k - len(odds)
-        stacked = len(odds) > 2
+        stacked = False
         e, *out = line(
             functools.partial(softmax_body, evens if stacked else k, len(got)),
             [shape(k, rows + SLACK, rows)]
@@ -426,6 +428,7 @@
         keep(send(packed, 4 * k), 4 * k)
     keep(send(packed, 2), 2)
     keep(send(packed, 1), 1)
+    line.last = None
     dt = line(flip_body, shape(features, rows), "flip", [document_matrix], 0.1)
     score([0, 1], hold=True)
     forward(2)
@@ -438,8 +441,8 @@
     score([3, 5, 9])
     relay(6)
     share(10, 6)
+    score([10, 6, 11, 7])
     softmax()
-    score([10, 6, 11, 7])
     relay(14)
     share(12, 14)
     softmax()

time: 88.4 us -> 84.8 us (0.959)
  waiting for transfers between devices: 16.6 us -> 12.6 us
  starting transfers between devices: 32.3 us -> 33.5 us
  local copies, waits for them, and re-layouts: 5.61 us -> 4.68 us
    ppermute x4, waiting for transfers between devices: 6.41 us -> 3.29 us  [score(): lax.ppermute(part, 'dim', [(i, (i + s) % depth) for i in range(depth)])]
    ppermute x29 -> x31, starting transfers between devices: 26.7 us -> 28.3 us  [send(): return lax.ppermute(x, 'blk', [(i, i ^ mask) for i in range(n)])]
    unnamed x16 -> x14, local copies, waits for them, and re-layouts: 5.61 us -> 4.68 us
    ppermute x29 -> x31, waiting for transfers between devices: 10.2 us -> 9.31 us  [send(): return lax.ppermute(x, 'blk', [(i, i ^ mask) for i in range(n)])]
  transfers between devices with their start and end apart: 33 -> 35, of which waited for: 13 -> 12; matrix products, arithmetic and copies ran while one was open for 0% -> 0% of each run, Pallas kernels for 33% -> 35%
where the time goes in v10:
time: 84.8 us; the launch traced here: 83.8 us
  starting transfers between devices  33.5 us (40%)
  Pallas kernels  32 us (38%)
  waiting for transfers between devices  12.6 us (15%)
  local copies, waits for them, and re-layouts  4.68 us (6%)
  between operations  1.03 us (1%)
    pallas_call x37, Pallas kernels, __call__(): pl.pallas_call(kernel, out_shape=out_shape, name=name, in_specs=in_specs,...  32 us
    ppermute x31, starting transfers between devices, send(): return lax.ppermute(x, 'blk', [(i, i ^ mask) for i in range(n)])  28.3 us
    ppermute x31, waiting for transfers between devices, send(): return lax.ppermute(x, 'blk', [(i, i ^ mask) for i in range(n)])  9.31 us
    ppermute x4, starting transfers between devices, score(): lax.ppermute(part, 'dim', [(i, (i + s) % depth) for i in range(depth)])  5.19 us
    unnamed x14, local copies, waits for them, and re-layouts  4.68 us
    ppermute x4, waiting for transfers between devices, score(): lax.ppermute(part, 'dim', [(i, (i + s) % depth) for i in range(depth)])  3.29 us
  transfers between devices with their start and end apart: 35, of which 12 were waited for; matrix products, arithmetic and copies ran while one was open for 0% of the time, Pallas kernels for 35%

profile of v10, /device:TPU:0, one launch (start us, length us, event | category | flops | bytes accessed | tf_op | source)
XLA Modules:
  0.0 83.8 jit_solution(10549330539273592599)
XLA Ops:
  0.6 1.8 %pack.1.refs_3_.refs_1_ = f32[392,128]{1,0:T(8,128)} custom-call(f32[128,384]{1,0:T(8,128)} %refs_0_.4, s32[8,128]{1,0:T(8,128)} %bitcast.3, s32[8,128]{1,0:T(8,128)} %bitcast.4), custom_call_target="tpu_custom_call" | custom-call | bytes 6660000 | tf_op jit(solution)/shard_map/pack/pallas_call | solution.py:45
  2.9 3.7 %collective-permute-start = (f32[392,128]{1,0:T(8,128)}, f32[392,128]{1,0:T(8,128)S(1)}, u32[]{:S(2)}, u32[]{:S(2)}) collective-permute-start(f32[392,128]{1,0:T(8,128)} %pack.1.refs_3_.refs_1_), channel_id=1, source_target_pairs={{0,16},{2,18},{4,20},{6,22},{8,24},{10,26},{12,28},{14,30},{16,0},... | collective-permute-start | bytes 602120 | tf_op jit(solution)/shard_map/ppermute | solution.py:293
  6.6 1.6 %collective-permute-start.2 = (f32[392,128]{1,0:T(8,128)}, f32[392,128]{1,0:T(8,128)S(1)}, u32[]{:S(2)}, u32[]{:S(2)}) collective-permute-start(f32[392,128]{1,0:T(8,128)} %pack.1.refs_3_.refs_1_), channel_id=1, source_target_pairs={{0,8},{2,10},{4,12},{6,14},{8,0},{10,2},{12,4},{14,6},{16,24},{18,... | collective-permute-start | bytes 602120 | tf_op jit(solution)/shard_map/ppermute | solution.py:293
  8.2 1.5 %collective-permute-start.3 = (f32[392,128]{1,0:T(8,128)}, f32[392,128]{1,0:T(8,128)S(1)}, u32[]{:S(2)}, u32[]{:S(2)}) collective-permute-start(f32[392,128]{1,0:T(8,128)} %pack.1.refs_3_.refs_1_), channel_id=1, source_target_pairs={{0,4},{2,6},{4,0},{6,2},{8,12},{10,14},{12,8},{14,10},{16,20},{18,... | collective-permute-start | bytes 602120 | tf_op jit(solution)/shard_map/ppermute | solution.py:293
  10.7 1.9 %copy-done = f32[384,2048]{1,0:T(8,128)S(1)} copy-done((f32[384,2048]{1,0:T(8,128)S(1)}, f32[384,2048]{1,0:T(8,128)}, u32[]{:S(2)}) %copy-start) | copy-done | bytes 3145752
  14.5 1.9 %score.5 = (f32[2,136,128]{2,1,0:T(8,128)S(1)}, f32[2,384,128]{2,1,0:T(8,128)S(1)}) custom-call(s32[1]{0:T(128)} %bitcast.refs_0_, f32[128,384]{1,0:T(8,128)S(1)} %copy-done.3, f32[384,2048]{1,0:T(8,128)S(1)} %copy-done, f32[392,128]{1,0:T(8,128)S(1)} %copy-done.5, f32[392,128]{1,0:T(8,128)S(1)} %collective-permute-done.1.refs_4_.refs_5_, ...), custom_call_target="tpu_custom_call" | custom-call | bytes 6660000 | tf_op jit(solution)/shard_map/score/pallas_call | solution.py:45
  17.2 1.6 %collective-permute-start.5 = (f32[392,128]{1,0:T(8,128)S(1)}, f32[392,128]{1,0:T(8,128)S(1)}, u32[]{:S(2)}, u32[]{:S(2)}) collective-permute-start(f32[392,128]{1,0:T(8,128)S(1)} %relay.8.refs_1_.refs_2_.refs_3_), channel_id=1, source_target_pairs={{0,4},{2,6},{4,0},{6,2},{8,12},{10,14},{12,8},{14,10},{16,20},{18,... | collective-permute-start | bytes 602120 | tf_op jit(solution)/shard_map/ppermute | solution.py:293
  20.8 2.9 %score.6 = (f32[5,136,128]{2,1,0:T(8,128)S(1)}, f32[5,384,128]{2,1,0:T(8,128)S(1)}) custom-call(s32[1]{0:T(128)} %bitcast.refs_0_, f32[128,384]{1,0:T(8,128)S(1)} %copy-done.4, f32[384,2048]{1,0:T(8,128)S(1)} %copy-done.1, f32[392,128]{1,0:T(8,128)S(1)} %relay.8.refs_1_.refs_2_.refs_3_, f32[392,128]{1,0:T(8,128)S(1)} %relay.9.refs_1_.refs_4_.refs_3_, ...), custom_call_target="tpu_custom_call" | custom-call | bytes 9990000 | tf_op jit(solution)/shard_map/score/pallas_call | solution.py:45
  23.7 1.6 %collective-permute-start.4 = (f32[5,136,128]{2,1,0:T(8,128)S(1)}, f32[5,136,128]{2,1,0:T(8,128)S(1)}, u32[]{:S(2)}, u32[]{:S(2)}) collective-permute-start(f32[5,136,128]{2,1,0:T(8,128)S(1)} %get-tuple-element.41.refs_2_), channel_id=1, source_target_pairs={{0,1},{1,0},{2,3},{3,2},{4,5},{5,4},{6,7},{7,6},{8,9},{9,8},{10,11... | collective-permute-start | bytes 1044488 | tf_op jit(solution)/shard_map/ppermute | solution.py:353
  25.9 2.9 %score.7 = (f32[3,136,128]{2,1,0:T(8,128)S(1)}, f32[3,384,128]{2,1,0:T(8,128)S(1)}) custom-call(s32[1]{0:T(128)} %bitcast.refs_0_, f32[128,384]{1,0:T(8,128)S(1)} %copy-done.4, f32[384,2048]{1,0:T(8,128)S(1)} %copy-done.1, f32[3,392,128]{2,1,0:T(8,128)S(1)} %collective-permute-done.7.refs_3_.refs_9_, f32[392,128]{1,0:T(8,128)S(1)} %relay.13.refs_4_.refs_3_.refs_6_), custom_call_target="tpu_custom_call" | custom-call | bytes 9990000 | tf_op jit(solution)/shard_map/score/pallas_call | solution.py:45
  29.0 1.6 %collective-permute-start.12 = (f32[392,128]{1,0:T(8,128)S(1)}, f32[392,128]{1,0:T(8,128)S(1)}, u32[]{:S(2)}, u32[]{:S(2)}) collective-permute-start(f32[392,128]{1,0:T(8,128)S(1)} %relay.13.refs_4_.refs_3_.refs_6_), channel_id=1, source_target_pairs={{0,4},{2,6},{4,0},{6,2},{8,12},{10,14},{12,8},{14,10},{16,20},{18,... | collective-permute-start | bytes 602120 | tf_op jit(solution)/shard_map/ppermute | solution.py:293
  30.6 1.5 %collective-permute-start.11 = (f32[3,136,128]{2,1,0:T(8,128)S(1)}, f32[3,136,128]{2,1,0:T(8,128)S(1)}, u32[]{:S(2)}, u32[]{:S(2)}) collective-permute-start(f32[3,136,128]{2,1,0:T(8,128)S(1)} %get-tuple-element.46.refs_2_), channel_id=1, source_target_pairs={{0,1},{1,0},{2,3},{3,2},{4,5},{5,4},{6,7},{7,6},{8,9},{9,8},{10,11... | collective-permute-start | bytes 626696 | tf_op jit(solution)/shard_map/ppermute | solution.py:353
  32.1 3.8 %score.8 = (f32[4,136,128]{2,1,0:T(8,128)S(1)}, f32[4,384,128]{2,1,0:T(8,128)S(1)}) custom-call(s32[1]{0:T(128)} %bitcast.refs_0_, f32[128,384]{1,0:T(8,128)S(1)} %copy-done.4, f32[384,2048]{1,0:T(8,128)S(1)} %copy-done.1, f32[392,128]{1,0:T(8,128)S(1)} %relay.12.refs_1_.refs_3_.refs_7_, f32[392,128]{1,0:T(8,128)S(1)} %relay.14.refs_4_.refs_7_.refs_8_, ...), custom_call_target="tpu_custom_call" | custom-call | bytes 13320000 | tf_op jit(solution)/shard_map/score/pallas_call | solution.py:45
  40.1 3.8 %score.9 = (f32[4,136,128]{2,1,0:T(8,128)S(1)}, f32[4,384,128]{2,1,0:T(8,128)S(1)}) custom-call(s32[1]{0:T(128)} %bitcast.refs_0_, f32[128,384]{1,0:T(8,128)S(1)} %copy-done.4, f32[384,2048]{1,0:T(8,128)S(1)} %copy-done.1, f32[392,128]{1,0:T(8,128)S(1)} %relay.13.refs_4_.refs_3_.refs_6_, f32[392,128]{1,0:T(8,128)S(1)} %relay.15.refs_4_.refs_10_, ...), custom_call_target="tpu_custom_call" | custom-call | bytes 13320000 | tf_op jit(solution)/shard_map/score/pallas_call | solution.py:45
  43.9 1.5 %collective-permute-start.23 = (f32[4,136,128]{2,1,0:T(8,128)S(1)}, f32[4,136,128]{2,1,0:T(8,128)S(1)}, u32[]{:S(2)}, u32[]{:S(2)}) collective-permute-start(f32[4,136,128]{2,1,0:T(8,128)S(1)} %get-tuple-element.60.refs_2_), channel_id=1, source_target_pairs={{0,1},{1,0},{2,3},{3,2},{4,5},{5,4},{6,7},{7,6},{8,9},{9,8},{10,11... | collective-permute-start | bytes 835592 | tf_op jit(solution)/shard_map/ppermute | solution.py:353
  50.1 2.6 %collective-permute-done.23.refs_3_ = f32[4,136,128]{2,1,0:T(8,128)S(1)} collective-permute-done((f32[4,136,128]{2,1,0:T(8,128)S(1)}, f32[4,136,128]{2,1,0:T(8,128)S(1)}, u32[]{:S(2)}, u32[]{:S(2)}) %collective-permute-start.23) | collective-permute-done | bytes 278560 | tf_op jit(solution)/shard_map/ppermute | solution.py:353
  55.2 1.6 %collective-permute-start.31 = (f32[392,128]{1,0:T(8,128)S(1)}, f32[392,128]{1,0:T(8,128)S(1)}, u32[]{:S(2)}, u32[]{:S(2)}) collective-permute-start(f32[392,128]{1,0:T(8,128)S(1)} %merge.16.refs_2_), channel_id=1, source_target_pairs={{0,4},{2,6},{4,0},{6,2},{8,12},{10,14},{12,8},{14,10},{16,20},{18,... | collective-permute-start | bytes 602120 | tf_op jit(solution)/shard_map/ppermute | solution.py:293
  56.8 1.7 %collective-permute-start.26 = (f32[2,16,128]{2,1,0:T(8,128)S(1)}, f32[2,16,128]{2,1,0:T(8,128)S(1)}, u32[]{:S(2)}, u32[]{:S(2)}) collective-permute-start(f32[2,16,128]{2,1,0:T(8,128)S(1)} %stats_merge.4.refs_2_.refs_0_), channel_id=1, source_target_pairs={{0,16},{2,18},{4,20},{6,22},{8,24},{10,26},{12,28},{14,30},{16,0},... | collective-permute-start | bytes 49160 | tf_op jit(solution)/shard_map/ppermute | solution.py:293
  58.5 3.0 %collective-permute-done.26.refs_1_ = f32[2,16,128]{2,1,0:T(8,128)S(1)} collective-permute-done((f32[2,16,128]{2,1,0:T(8,128)S(1)}, f32[2,16,128]{2,1,0:T(8,128)S(1)}, u32[]{:S(2)}, u32[]{:S(2)}) %collective-permute-start.26) | collective-permute-done | bytes 16416 | tf_op jit(solution)/shard_map/ppermute | solution.py:293
  62.9 2.4 %collective-permute-done.28.refs_1_ = f32[2,16,128]{2,1,0:T(8,128)S(1)} collective-permute-done((f32[2,16,128]{2,1,0:T(8,128)S(1)}, f32[2,16,128]{2,1,0:T(8,128)S(1)}, u32[]{:S(2)}, u32[]{:S(2)}) %collective-permute-start.28) | collective-permute-done | bytes 16416 | tf_op jit(solution)/shard_map/ppermute | solution.py:293
  66.0 1.5 %collective-permute-start.34 = (f32[392,128]{1,0:T(8,128)S(1)}, f32[392,128]{1,0:T(8,128)S(1)}, u32[]{:S(2)}, u32[]{:S(2)}) collective-permute-start(f32[392,128]{1,0:T(8,128)S(1)} %merge.12.refs_2_), channel_id=1, source_target_pairs={{0,4},{2,6},{4,0},{6,2},{8,12},{10,14},{12,8},{14,10},{16,20},{18,... | collective-permute-start | bytes 602120 | tf_op jit(solution)/shard_map/ppermute | solution.py:293
  67.6 1.7 %collective-permute-start.29 = (f32[392,128]{1,0:T(8,128)S(1)}, f32[392,128]{1,0:T(8,128)S(1)}, u32[]{:S(2)}, u32[]{:S(2)}) collective-permute-start(f32[392,128]{1,0:T(8,128)S(1)} %merge.18.refs_2_), channel_id=1, source_target_pairs={{0,16},{2,18},{4,20},{6,22},{8,24},{10,26},{12,28},{14,30},{16,0},... | collective-permute-start | bytes 602120 | tf_op jit(solution)/shard_map/ppermute | solution.py:293
  69.3 2.1 %collective-permute-start.30 = (f32[392,128]{1,0:T(8,128)S(1)}, f32[392,128]{1,0:T(8,128)S(1)}, u32[]{:S(2)}, u32[]{:S(2)}) collective-permute-start(f32[392,128]{1,0:T(8,128)S(1)} %merge.19.refs_2_), channel_id=1, source_target_pairs={{0,8},{2,10},{4,12},{6,14},{8,0},{10,2},{12,4},{14,6},{16,24},{18,... | collective-permute-start | bytes 602120 | tf_op jit(solution)/shard_map/ppermute | solution.py:293
  72.5 9.8 %gradient.1 = (f32[128,384]{1,0:T(8,128)}, f32[384,2048]{1,0:T(8,128)}) custom-call(f32[2,16,128]{2,1,0:T(8,128)S(1)} %stats_merge.7.refs_2_.refs_0_, f32[392,128]{1,0:T(8,128)S(1)} %copy-done.6, f32[392,128]{1,0:T(8,128)S(1)} %relay.8.refs_1_.refs_2_.refs_3_, f32[392,128]{1,0:T(8,128)S(1)} %relay.9.refs_1_.refs_4_.refs_3_, ...), custom_call_target="tpu_custom_call" | custom-call | bytes 40700000 | tf_op jit(solution)/shard_map/gradient/pallas_call | solution.py:45
  (97 shorter events, 22.9 us)
Async XLA Ops:
  2.4 8.3 %collective-permute-start.1 = (f32[392,128]{1,0:T(8,128)}, f32[392,128]{1,0:T(8,128)S(1)}, u32[]{:S(2)}, u32[]{:S(2)}) collective-permute-start(f32[392,128]{1,0:T(8,128)} %pack.1.refs_3_.refs_1_), channel_id=1, source_target_pairs={{0,2},{2,0},{4,6},{6,4},{8,10},{10,8},{12,14},{14,12},{16,18},{18,... | collective-permute-start | bytes 602120 | tf_op jit(solution)/shard_map/ppermute | solution.py:293
  2.9 13.9 %collective-permute-start = (f32[392,128]{1,0:T(8,128)}, f32[392,128]{1,0:T(8,128)S(1)}, u32[]{:S(2)}, u32[]{:S(2)}) collective-permute-start(f32[392,128]{1,0:T(8,128)} %pack.1.refs_3_.refs_1_), channel_id=1, source_target_pairs={{0,16},{2,18},{4,20},{6,22},{8,24},{10,26},{12,28},{14,30},{16,0},... | collective-permute-start | bytes 602120 | tf_op jit(solution)/shard_map/ppermute | solution.py:293
  6.6 10.4 %collective-permute-start.2 = (f32[392,128]{1,0:T(8,128)}, f32[392,128]{1,0:T(8,128)S(1)}, u32[]{:S(2)}, u32[]{:S(2)}) collective-permute-start(f32[392,128]{1,0:T(8,128)} %pack.1.refs_3_.refs_1_), channel_id=1, source_target_pairs={{0,8},{2,10},{4,12},{6,14},{8,0},{10,2},{12,4},{14,6},{16,24},{18,... | collective-permute-start | bytes 602120 | tf_op jit(solution)/shard_map/ppermute | solution.py:293
  8.2 8.8 %collective-permute-start.3 = (f32[392,128]{1,0:T(8,128)}, f32[392,128]{1,0:T(8,128)S(1)}, u32[]{:S(2)}, u32[]{:S(2)}) collective-permute-start(f32[392,128]{1,0:T(8,128)} %pack.1.refs_3_.refs_1_), channel_id=1, source_target_pairs={{0,4},{2,6},{4,0},{6,2},{8,12},{10,14},{12,8},{14,10},{16,20},{18,... | collective-permute-start | bytes 602120 | tf_op jit(solution)/shard_map/ppermute | solution.py:293
  17.1 8.8 %collective-permute-start.7 = (f32[3,392,128]{2,1,0:T(8,128)S(1)}, f32[3,392,128]{2,1,0:T(8,128)S(1)}, u32[]{:S(2)}, u32[]{:S(2)}) collective-permute-start(f32[3,392,128]{2,1,0:T(8,128)S(1)} %relay.11.refs_8_), channel_id=1, source_target_pairs={{0,2},{2,0},{4,6},{6,4},{8,10},{10,8},{12,14},{14,12},{16,18},{18,... | collective-permute-start | bytes 1806344 | tf_op jit(solution)/shard_map/ppermute | solution.py:293
  17.2 8.1 %collective-permute-start.5 = (f32[392,128]{1,0:T(8,128)S(1)}, f32[392,128]{1,0:T(8,128)S(1)}, u32[]{:S(2)}, u32[]{:S(2)}) collective-permute-start(f32[392,128]{1,0:T(8,128)S(1)} %relay.8.refs_1_.refs_2_.refs_3_), channel_id=1, source_target_pairs={{0,4},{2,6},{4,0},{6,2},{8,12},{10,14},{12,8},{14,10},{16,20},{18,... | collective-permute-start | bytes 602120 | tf_op jit(solution)/shard_map/ppermute | solution.py:293
  18.8 7.1 %collective-permute-start.8 = (f32[392,128]{1,0:T(8,128)S(1)}, f32[392,128]{1,0:T(8,128)S(1)}, u32[]{:S(2)}, u32[]{:S(2)}) collective-permute-start(f32[392,128]{1,0:T(8,128)S(1)} %relay.8.refs_1_.refs_2_.refs_3_), channel_id=1, source_target_pairs={{0,8},{2,10},{4,12},{6,14},{8,0},{10,2},{12,4},{14,6},{16,24},{18,... | collective-permute-start | bytes 602120 | tf_op jit(solution)/shard_map/ppermute | solution.py:293
  20.2 8.6 %collective-permute-start.6 = (f32[392,128]{1,0:T(8,128)S(1)}, f32[392,128]{1,0:T(8,128)S(1)}, u32[]{:S(2)}, u32[]{:S(2)}) collective-permute-start(f32[392,128]{1,0:T(8,128)S(1)} %relay.9.refs_1_.refs_4_.refs_3_), channel_id=1, source_target_pairs={{0,4},{2,6},{4,0},{6,2},{8,12},{10,14},{12,8},{14,10},{16,20},{18,... | collective-permute-start | bytes 602120 | tf_op jit(solution)/shard_map/ppermute | solution.py:293
  23.7 12.3 %collective-permute-start.4 = (f32[5,136,128]{2,1,0:T(8,128)S(1)}, f32[5,136,128]{2,1,0:T(8,128)S(1)}, u32[]{:S(2)}, u32[]{:S(2)}) collective-permute-start(f32[5,136,128]{2,1,0:T(8,128)S(1)} %get-tuple-element.41.refs_2_), channel_id=1, source_target_pairs={{0,1},{1,0},{2,3},{3,2},{4,5},{5,4},{6,7},{7,6},{8,9},{9,8},{10,11... | collective-permute-start | bytes 1044488 | tf_op jit(solution)/shard_map/ppermute | solution.py:353
  25.3 6.8 %collective-permute-start.9 = (f32[392,128]{1,0:T(8,128)S(1)}, f32[392,128]{1,0:T(8,128)S(1)}, u32[]{:S(2)}, u32[]{:S(2)}) collective-permute-start(f32[392,128]{1,0:T(8,128)S(1)} %relay.12.refs_1_.refs_3_.refs_7_), channel_id=1, source_target_pairs={{0,2},{2,0},{4,6},{6,4},{8,10},{10,8},{12,14},{14,12},{16,18},{18,... | collective-permute-start | bytes 602120 | tf_op jit(solution)/shard_map/ppermute | solution.py:293
  29.0 8.0 %collective-permute-start.12 = (f32[392,128]{1,0:T(8,128)S(1)}, f32[392,128]{1,0:T(8,128)S(1)}, u32[]{:S(2)}, u32[]{:S(2)}) collective-permute-start(f32[392,128]{1,0:T(8,128)S(1)} %relay.13.refs_4_.refs_3_.refs_6_), channel_id=1, source_target_pairs={{0,4},{2,6},{4,0},{6,2},{8,12},{10,14},{12,8},{14,10},{16,20},{18,... | collective-permute-start | bytes 602120 | tf_op jit(solution)/shard_map/ppermute | solution.py:293
  30.6 7.9 %collective-permute-start.11 = (f32[3,136,128]{2,1,0:T(8,128)S(1)}, f32[3,136,128]{2,1,0:T(8,128)S(1)}, u32[]{:S(2)}, u32[]{:S(2)}) collective-permute-start(f32[3,136,128]{2,1,0:T(8,128)S(1)} %get-tuple-element.46.refs_2_), channel_id=1, source_target_pairs={{0,1},{1,0},{2,3},{3,2},{4,5},{5,4},{6,7},{7,6},{8,9},{9,8},{10,11... | collective-permute-start | bytes 626696 | tf_op jit(solution)/shard_map/ppermute | solution.py:353
  32.1 7.5 %collective-permute-start.17 = (f32[392,128]{1,0:T(8,128)S(1)}, f32[392,128]{1,0:T(8,128)S(1)}, u32[]{:S(2)}, u32[]{:S(2)}) collective-permute-start(f32[392,128]{1,0:T(8,128)S(1)} %relay.13.refs_4_.refs_3_.refs_6_), channel_id=1, source_target_pairs={{0,2},{2,0},{4,6},{6,4},{8,10},{10,8},{12,14},{14,12},{16,18},{18,... | collective-permute-start | bytes 602120 | tf_op jit(solution)/shard_map/ppermute | solution.py:293
  37.7 8.6 %collective-permute-start.19 = (f32[4,136,128]{2,1,0:T(8,128)S(1)}, f32[4,136,128]{2,1,0:T(8,128)S(1)}, u32[]{:S(2)}, u32[]{:S(2)}) collective-permute-start(f32[4,136,128]{2,1,0:T(8,128)S(1)} %get-tuple-element.55.refs_2_), channel_id=1, source_target_pairs={{0,1},{1,0},{2,3},{3,2},{4,5},{5,4},{6,7},{7,6},{8,9},{9,8},{10,11... | collective-permute-start | bytes 835592 | tf_op jit(solution)/shard_map/ppermute | solution.py:353
  39.2 6.3 %collective-permute-start.15 = (f32[392,128]{1,0:T(8,128)S(1)}, f32[392,128]{1,0:T(8,128)S(1)}, u32[]{:S(2)}, u32[]{:S(2)}) collective-permute-start(f32[392,128]{1,0:T(8,128)S(1)} %get-tuple-element.52), channel_id=1, source_target_pairs={{0,2},{2,0},{4,6},{6,4},{8,10},{10,8},{12,14},{14,12},{16,18},{18,... | collective-permute-start | bytes 602120 | tf_op jit(solution)/shard_map/ppermute | solution.py:293
  43.9 8.8 %collective-permute-start.23 = (f32[4,136,128]{2,1,0:T(8,128)S(1)}, f32[4,136,128]{2,1,0:T(8,128)S(1)}, u32[]{:S(2)}, u32[]{:S(2)}) collective-permute-start(f32[4,136,128]{2,1,0:T(8,128)S(1)} %get-tuple-element.60.refs_2_), channel_id=1, source_target_pairs={{0,1},{1,0},{2,3},{3,2},{4,5},{5,4},{6,7},{7,6},{8,9},{9,8},{10,11... | collective-permute-start | bytes 835592 | tf_op jit(solution)/shard_map/ppermute | solution.py:353
  49.2 18.3 %collective-permute-start.22 = (f32[2,392,128]{2,1,0:T(8,128)S(1)}, f32[2,392,128]{2,1,0:T(8,128)S(1)}, u32[]{:S(2)}, u32[]{:S(2)}) collective-permute-start(f32[2,392,128]{2,1,0:T(8,128)S(1)} %merge.15.refs_4_), channel_id=1, source_target_pairs={{0,4},{2,6},{4,0},{6,2},{8,12},{10,14},{12,8},{14,10},{16,20},{18,... | collective-permute-start | bytes 1204232 | tf_op jit(solution)/shard_map/ppermute | solution.py:293
  54.3 13.2 %collective-permute-start.24 = (f32[392,128]{1,0:T(8,128)S(1)}, f32[392,128]{1,0:T(8,128)S(1)}, u32[]{:S(2)}, u32[]{:S(2)}) collective-permute-start(f32[392,128]{1,0:T(8,128)S(1)} %get-tuple-element.62), channel_id=1, source_target_pairs={{0,2},{2,0},{4,6},{6,4},{8,10},{10,8},{12,14},{14,12},{16,18},{18,... | collective-permute-start | bytes 602120 | tf_op jit(solution)/shard_map/ppermute | solution.py:293
  55.2 16.2 %collective-permute-start.31 = (f32[392,128]{1,0:T(8,128)S(1)}, f32[392,128]{1,0:T(8,128)S(1)}, u32[]{:S(2)}, u32[]{:S(2)}) collective-permute-start(f32[392,128]{1,0:T(8,128)S(1)} %merge.16.refs_2_), channel_id=1, source_target_pairs={{0,4},{2,6},{4,0},{6,2},{8,12},{10,14},{12,8},{14,10},{16,20},{18,... | collective-permute-start | bytes 602120 | tf_op jit(solution)/shard_map/ppermute | solution.py:293
  65.4 6.1 %collective-permute-start.32 = (f32[2,16,128]{2,1,0:T(8,128)S(1)}, f32[2,16,128]{2,1,0:T(8,128)S(1)}, u32[]{:S(2)}, u32[]{:S(2)}) collective-permute-start(f32[2,16,128]{2,1,0:T(8,128)S(1)} %stats_merge.6.refs_2_.refs_0_), channel_id=1, source_target_pairs={{0,4},{2,6},{4,0},{6,2},{8,12},{10,14},{12,8},{14,10},{16,20},{18,... | collective-permute-start | bytes 49160 | tf_op jit(solution)/shard_map/ppermute | solution.py:293
  66.0 6.5 %collective-permute-start.34 = (f32[392,128]{1,0:T(8,128)S(1)}, f32[392,128]{1,0:T(8,128)S(1)}, u32[]{:S(2)}, u32[]{:S(2)}) collective-permute-start(f32[392,128]{1,0:T(8,128)S(1)} %merge.12.refs_2_), channel_id=1, source_target_pairs={{0,4},{2,6},{4,0},{6,2},{8,12},{10,14},{12,8},{14,10},{16,20},{18,... | collective-permute-start | bytes 602120 | tf_op jit(solution)/shard_map/ppermute | solution.py:293
  67.6 15.3 %collective-permute-start.29 = (f32[392,128]{1,0:T(8,128)S(1)}, f32[392,128]{1,0:T(8,128)S(1)}, u32[]{:S(2)}, u32[]{:S(2)}) collective-permute-start(f32[392,128]{1,0:T(8,128)S(1)} %merge.18.refs_2_), channel_id=1, source_target_pairs={{0,16},{2,18},{4,20},{6,22},{8,24},{10,26},{12,28},{14,30},{16,0},... | collective-permute-start | bytes 602120 | tf_op jit(solution)/shard_map/ppermute | solution.py:293
  69.3 13.6 %collective-permute-start.30 = (f32[392,128]{1,0:T(8,128)S(1)}, f32[392,128]{1,0:T(8,128)S(1)}, u32[]{:S(2)}, u32[]{:S(2)}) collective-permute-start(f32[392,128]{1,0:T(8,128)S(1)} %merge.19.refs_2_), channel_id=1, source_target_pairs={{0,8},{2,10},{4,12},{6,14},{8,0},{10,2},{12,4},{14,6},{16,24},{18,... | collective-permute-start | bytes 602120 | tf_op jit(solution)/shard_map/ppermute | solution.py:293
  71.5 11.4 %collective-permute-start.33 = (f32[392,128]{1,0:T(8,128)S(1)}, f32[392,128]{1,0:T(8,128)S(1)}, u32[]{:S(2)}, u32[]{:S(2)}) collective-permute-start(f32[392,128]{1,0:T(8,128)S(1)} %merge.20.refs_19_), channel_id=1, source_target_pairs={{0,24},{2,26},{4,28},{6,30},{8,16},{10,18},{12,20},{14,22},{16,8},... | collective-permute-start | bytes 602120 | tf_op jit(solution)/shard_map/ppermute | solution.py:293
  (18 other events, 74.2 us)

commit v11 on v10

--- a/solution.py
+++ b/solution.py
@@ -463,6 +463,7 @@
             pair(4 * k - 2, 4 * k - 4)
             beside(k - 1)
     softmax()
+    over_x[0] = (pass_on(over_x[0][0]), None)
 
     totals = line(
         functools.partial(stats_body, [e_place[r] for r in range(n)]),

time: 84.8 us -> 85.3 us (level)
    pallas_call x37 -> x38, Pallas kernels: 32 us -> 32 us  [__call__(): pl.pallas_call(kernel, out_shape=out_shape, name=name, in_specs=in_specs,...]
  transfers between devices with their start and end apart: 35 -> 35, of which waited for: 12 -> 11; matrix products, arithmetic and copies ran while one was open for 0% -> 0% of each run, Pallas kernels for 35% -> 35%
where the time goes in v11:
time: 85.3 us; the launch traced here: 84.4 us
  starting transfers between devices  33.9 us (40%)
  Pallas kernels  32 us (38%)
  waiting for transfers between devices  12.8 us (15%)
  local copies, waits for them, and re-layouts  4.68 us (5%)
  between operations  1.05 us (1%)
    pallas_call x38, Pallas kernels, __call__(): pl.pallas_call(kernel, out_shape=out_shape, name=name, in_specs=in_specs,...  32 us
    ppermute x31, starting transfers between devices, send(): return lax.ppermute(x, 'blk', [(i, i ^ mask) for i in range(n)])  28.7 us
    ppermute x31, waiting for transfers between devices, send(): return lax.ppermute(x, 'blk', [(i, i ^ mask) for i in range(n)])  9.49 us
    ppermute x4, starting transfers between devices, score(): lax.ppermute(part, 'dim', [(i, (i + s) % depth) for i in range(depth)])  5.19 us
    unnamed x14, local copies, waits for them, and re-layouts  4.68 us
    ppermute x4, waiting for transfers between devices, score(): lax.ppermute(part, 'dim', [(i, (i + s) % depth) for i in range(depth)])  3.31 us
  transfers between devices with their start and end apart: 35, of which 11 were waited for; matrix products, arithmetic and copies ran while one was open for 0% of the time, Pallas kernels for 35%

profile of v11, /device:TPU:0, one launch (start us, length us, event | category | flops | bytes accessed | tf_op | source)
XLA Modules:
  0.0 84.4 jit_solution(14979514173563952121)
XLA Ops:
  0.6 1.8 %pack.1.refs_3_.refs_1_ = f32[392,128]{1,0:T(8,128)} custom-call(f32[128,384]{1,0:T(8,128)} %refs_0_.4, s32[8,128]{1,0:T(8,128)} %bitcast.3, s32[8,128]{1,0:T(8,128)} %bitcast.4), custom_call_target="tpu_custom_call" | custom-call | bytes 6660000 | tf_op jit(solution)/shard_map/pack/pallas_call | solution.py:45
  2.9 3.7 %collective-permute-start = (f32[392,128]{1,0:T(8,128)}, f32[392,128]{1,0:T(8,128)S(1)}, u32[]{:S(2)}, u32[]{:S(2)}) collective-permute-start(f32[392,128]{1,0:T(8,128)} %pack.1.refs_3_.refs_1_), channel_id=1, source_target_pairs={{0,16},{2,18},{4,20},{6,22},{8,24},{10,26},{12,28},{14,30},{16,0},... | collective-permute-start | bytes 602120 | tf_op jit(solution)/shard_map/ppermute | solution.py:293
  6.6 1.6 %collective-permute-start.2 = (f32[392,128]{1,0:T(8,128)}, f32[392,128]{1,0:T(8,128)S(1)}, u32[]{:S(2)}, u32[]{:S(2)}) collective-permute-start(f32[392,128]{1,0:T(8,128)} %pack.1.refs_3_.refs_1_), channel_id=1, source_target_pairs={{0,8},{2,10},{4,12},{6,14},{8,0},{10,2},{12,4},{14,6},{16,24},{18,... | collective-permute-start | bytes 602120 | tf_op jit(solution)/shard_map/ppermute | solution.py:293
  10.7 1.9 %copy-done = f32[384,2048]{1,0:T(8,128)S(1)} copy-done((f32[384,2048]{1,0:T(8,128)S(1)}, f32[384,2048]{1,0:T(8,128)}, u32[]{:S(2)}) %copy-start) | copy-done | bytes 3145752
  14.5 1.9 %score.5 = (f32[2,136,128]{2,1,0:T(8,128)S(1)}, f32[2,384,128]{2,1,0:T(8,128)S(1)}) custom-call(s32[1]{0:T(128)} %bitcast.refs_0_, f32[128,384]{1,0:T(8,128)S(1)} %copy-done.3, f32[384,2048]{1,0:T(8,128)S(1)} %copy-done, f32[392,128]{1,0:T(8,128)S(1)} %copy-done.5, f32[392,128]{1,0:T(8,128)S(1)} %collective-permute-done.1.refs_4_.refs_5_, ...), custom_call_target="tpu_custom_call" | custom-call | bytes 6660000 | tf_op jit(solution)/shard_map/score/pallas_call | solution.py:45
  17.2 1.6 %collective-permute-start.5 = (f32[392,128]{1,0:T(8,128)S(1)}, f32[392,128]{1,0:T(8,128)S(1)}, u32[]{:S(2)}, u32[]{:S(2)}) collective-permute-start(f32[392,128]{1,0:T(8,128)S(1)} %relay.9.refs_1_.refs_2_.refs_3_), channel_id=1, source_target_pairs={{0,4},{2,6},{4,0},{6,2},{8,12},{10,14},{12,8},{14,10},{16,20},{18,... | collective-permute-start | bytes 602120 | tf_op jit(solution)/shard_map/ppermute | solution.py:293
  20.8 2.9 %score.6 = (f32[5,136,128]{2,1,0:T(8,128)S(1)}, f32[5,384,128]{2,1,0:T(8,128)S(1)}) custom-call(s32[1]{0:T(128)} %bitcast.refs_0_, f32[128,384]{1,0:T(8,128)S(1)} %copy-done.4, f32[384,2048]{1,0:T(8,128)S(1)} %copy-done.1, f32[392,128]{1,0:T(8,128)S(1)} %relay.9.refs_1_.refs_2_.refs_3_, f32[392,128]{1,0:T(8,128)S(1)} %relay.10.refs_1_.refs_4_.refs_3_, ...), custom_call_target="tpu_custom_call" | custom-call | bytes 9990000 | tf_op jit(solution)/shard_map/score/pallas_call | solution.py:45
  23.7 1.6 %collective-permute-start.4 = (f32[5,136,128]{2,1,0:T(8,128)S(1)}, f32[5,136,128]{2,1,0:T(8,128)S(1)}, u32[]{:S(2)}, u32[]{:S(2)}) collective-permute-start(f32[5,136,128]{2,1,0:T(8,128)S(1)} %get-tuple-element.41.refs_2_), channel_id=1, source_target_pairs={{0,1},{1,0},{2,3},{3,2},{4,5},{5,4},{6,7},{7,6},{8,9},{9,8},{10,11... | collective-permute-start | bytes 1044488 | tf_op jit(solution)/shard_map/ppermute | solution.py:353
  25.9 2.9 %score.7 = (f32[3,136,128]{2,1,0:T(8,128)S(1)}, f32[3,384,128]{2,1,0:T(8,128)S(1)}) custom-call(s32[1]{0:T(128)} %bitcast.refs_0_, f32[128,384]{1,0:T(8,128)S(1)} %copy-done.4, f32[384,2048]{1,0:T(8,128)S(1)} %copy-done.1, f32[3,392,128]{2,1,0:T(8,128)S(1)} %collective-permute-done.7.refs_3_.refs_9_, f32[392,128]{1,0:T(8,128)S(1)} %relay.14.refs_4_.refs_3_.refs_6_), custom_call_target="tpu_custom_call" | custom-call | bytes 9990000 | tf_op jit(solution)/shard_map/score/pallas_call | solution.py:45
  29.0 1.6 %collective-permute-start.12 = (f32[392,128]{1,0:T(8,128)S(1)}, f32[392,128]{1,0:T(8,128)S(1)}, u32[]{:S(2)}, u32[]{:S(2)}) collective-permute-start(f32[392,128]{1,0:T(8,128)S(1)} %relay.14.refs_4_.refs_3_.refs_6_), channel_id=1, source_target_pairs={{0,4},{2,6},{4,0},{6,2},{8,12},{10,14},{12,8},{14,10},{16,20},{18,... | collective-permute-start | bytes 602120 | tf_op jit(solution)/shard_map/ppermute | solution.py:293
  30.6 1.5 %collective-permute-start.11 = (f32[3,136,128]{2,1,0:T(8,128)S(1)}, f32[3,136,128]{2,1,0:T(8,128)S(1)}, u32[]{:S(2)}, u32[]{:S(2)}) collective-permute-start(f32[3,136,128]{2,1,0:T(8,128)S(1)} %get-tuple-element.46.refs_2_), channel_id=1, source_target_pairs={{0,1},{1,0},{2,3},{3,2},{4,5},{5,4},{6,7},{7,6},{8,9},{9,8},{10,11... | collective-permute-start | bytes 626696 | tf_op jit(solution)/shard_map/ppermute | solution.py:353
  32.1 3.8 %score.8 = (f32[4,136,128]{2,1,0:T(8,128)S(1)}, f32[4,384,128]{2,1,0:T(8,128)S(1)}) custom-call(s32[1]{0:T(128)} %bitcast.refs_0_, f32[128,384]{1,0:T(8,128)S(1)} %copy-done.4, f32[384,2048]{1,0:T(8,128)S(1)} %copy-done.1, f32[392,128]{1,0:T(8,128)S(1)} %relay.13.refs_1_.refs_3_.refs_7_, f32[392,128]{1,0:T(8,128)S(1)} %relay.15.refs_4_.refs_7_.refs_8_, ...), custom_call_target="tpu_custom_call" | custom-call | bytes 13320000 | tf_op jit(solution)/shard_map/score/pallas_call | solution.py:45
  40.1 3.8 %score.9 = (f32[4,136,128]{2,1,0:T(8,128)S(1)}, f32[4,384,128]{2,1,0:T(8,128)S(1)}) custom-call(s32[1]{0:T(128)} %bitcast.refs_0_, f32[128,384]{1,0:T(8,128)S(1)} %copy-done.4, f32[384,2048]{1,0:T(8,128)S(1)} %copy-done.1, f32[392,128]{1,0:T(8,128)S(1)} %relay.14.refs_4_.refs_3_.refs_6_, f32[392,128]{1,0:T(8,128)S(1)} %relay.16.refs_4_.refs_10_, ...), custom_call_target="tpu_custom_call" | custom-call | bytes 13320000 | tf_op jit(solution)/shard_map/score/pallas_call | solution.py:45
  43.9 1.5 %collective-permute-start.23 = (f32[4,136,128]{2,1,0:T(8,128)S(1)}, f32[4,136,128]{2,1,0:T(8,128)S(1)}, u32[]{:S(2)}, u32[]{:S(2)}) collective-permute-start(f32[4,136,128]{2,1,0:T(8,128)S(1)} %get-tuple-element.60.refs_2_), channel_id=1, source_target_pairs={{0,1},{1,0},{2,3},{3,2},{4,5},{5,4},{6,7},{7,6},{8,9},{9,8},{10,11... | collective-permute-start | bytes 835592 | tf_op jit(solution)/shard_map/ppermute | solution.py:353
  50.1 2.6 %collective-permute-done.23.refs_3_ = f32[4,136,128]{2,1,0:T(8,128)S(1)} collective-permute-done((f32[4,136,128]{2,1,0:T(8,128)S(1)}, f32[4,136,128]{2,1,0:T(8,128)S(1)}, u32[]{:S(2)}, u32[]{:S(2)}) %collective-permute-start.23) | collective-permute-done | bytes 278560 | tf_op jit(solution)/shard_map/ppermute | solution.py:353
  53.7 2.0 %collective-permute-done.25.refs_0_ = f32[392,128]{1,0:T(8,128)S(1)} collective-permute-done((f32[392,128]{1,0:T(8,128)S(1)}, f32[392,128]{1,0:T(8,128)S(1)}, u32[]{:S(2)}, u32[]{:S(2)}) %collective-permute-start.25) | collective-permute-done | bytes 200736 | tf_op jit(solution)/shard_map/ppermute | solution.py:293
  58.1 1.7 %collective-permute-start.27 = (f32[2,16,128]{2,1,0:T(8,128)S(1)}, f32[2,16,128]{2,1,0:T(8,128)S(1)}, u32[]{:S(2)}, u32[]{:S(2)}) collective-permute-start(f32[2,16,128]{2,1,0:T(8,128)S(1)} %stats_merge.4.refs_2_.refs_0_), channel_id=1, source_target_pairs={{0,16},{2,18},{4,20},{6,22},{8,24},{10,26},{12,28},{14,30},{16,0},... | collective-permute-start | bytes 49160 | tf_op jit(solution)/shard_map/ppermute | solution.py:293
  59.8 2.9 %collective-permute-done.27.refs_1_ = f32[2,16,128]{2,1,0:T(8,128)S(1)} collective-permute-done((f32[2,16,128]{2,1,0:T(8,128)S(1)}, f32[2,16,128]{2,1,0:T(8,128)S(1)}, u32[]{:S(2)}, u32[]{:S(2)}) %collective-permute-start.27) | collective-permute-done | bytes 16416 | tf_op jit(solution)/shard_map/ppermute | solution.py:293
  62.7 1.5 %collective-permute-start.29 = (f32[2,16,128]{2,1,0:T(8,128)S(1)}, f32[2,16,128]{2,1,0:T(8,128)S(1)}, u32[]{:S(2)}, u32[]{:S(2)}) collective-permute-start(f32[2,16,128]{2,1,0:T(8,128)S(1)} %stats_merge.5.refs_0_.refs_2_), channel_id=1, source_target_pairs={{0,8},{2,10},{4,12},{6,14},{8,0},{10,2},{12,4},{14,6},{16,24},{18,... | collective-permute-start | bytes 49160 | tf_op jit(solution)/shard_map/ppermute | solution.py:293
  64.2 2.3 %collective-permute-done.29.refs_1_ = f32[2,16,128]{2,1,0:T(8,128)S(1)} collective-permute-done((f32[2,16,128]{2,1,0:T(8,128)S(1)}, f32[2,16,128]{2,1,0:T(8,128)S(1)}, u32[]{:S(2)}, u32[]{:S(2)}) %collective-permute-start.29) | collective-permute-done | bytes 16416 | tf_op jit(solution)/shard_map/ppermute | solution.py:293
  67.8 1.8 %collective-permute-start.30 = (f32[392,128]{1,0:T(8,128)S(1)}, f32[392,128]{1,0:T(8,128)S(1)}, u32[]{:S(2)}, u32[]{:S(2)}) collective-permute-start(f32[392,128]{1,0:T(8,128)S(1)} %merge.18.refs_2_), channel_id=1, source_target_pairs={{0,16},{2,18},{4,20},{6,22},{8,24},{10,26},{12,28},{14,30},{16,0},... | collective-permute-start | bytes 602120 | tf_op jit(solution)/shard_map/ppermute | solution.py:293
  69.7 2.1 %collective-permute-start.31 = (f32[392,128]{1,0:T(8,128)S(1)}, f32[392,128]{1,0:T(8,128)S(1)}, u32[]{:S(2)}, u32[]{:S(2)}) collective-permute-start(f32[392,128]{1,0:T(8,128)S(1)} %merge.19.refs_2_), channel_id=1, source_target_pairs={{0,8},{2,10},{4,12},{6,14},{8,0},{10,2},{12,4},{14,6},{16,24},{18,... | collective-permute-start | bytes 602120 | tf_op jit(solution)/shard_map/ppermute | solution.py:293
  71.9 1.8 %collective-permute-start.34 = (f32[392,128]{1,0:T(8,128)S(1)}, f32[392,128]{1,0:T(8,128)S(1)}, u32[]{:S(2)}, u32[]{:S(2)}) collective-permute-start(f32[392,128]{1,0:T(8,128)S(1)} %merge.20.refs_19_), channel_id=1, source_target_pairs={{0,24},{2,26},{4,28},{6,30},{8,16},{10,18},{12,20},{14,22},{16,8},... | collective-permute-start | bytes 602120 | tf_op jit(solution)/shard_map/ppermute | solution.py:293
  73.8 9.8 %gradient.1 = (f32[128,384]{1,0:T(8,128)}, f32[384,2048]{1,0:T(8,128)}) custom-call(f32[2,16,128]{2,1,0:T(8,128)S(1)} %stats_merge.7.refs_2_.refs_0_, f32[392,128]{1,0:T(8,128)S(1)} %copy-done.6, f32[392,128]{1,0:T(8,128)S(1)} %relay.9.refs_1_.refs_2_.refs_3_, f32[392,128]{1,0:T(8,128)S(1)} %relay.10.refs_1_.refs_4_.refs_3_, ...), custom_call_target="tpu_custom_call" | custom-call | bytes 40700000 | tf_op jit(solution)/shard_map/gradient/pallas_call | solution.py:45
  (98 shorter events, 22.8 us)
Async XLA Ops:
  2.4 8.3 %collective-permute-start.1 = (f32[392,128]{1,0:T(8,128)}, f32[392,128]{1,0:T(8,128)S(1)}, u32[]{:S(2)}, u32[]{:S(2)}) collective-permute-start(f32[392,128]{1,0:T(8,128)} %pack.1.refs_3_.refs_1_), channel_id=1, source_target_pairs={{0,2},{2,0},{4,6},{6,4},{8,10},{10,8},{12,14},{14,12},{16,18},{18,... | collective-permute-start | bytes 602120 | tf_op jit(solution)/shard_map/ppermute | solution.py:293
  2.9 13.9 %collective-permute-start = (f32[392,128]{1,0:T(8,128)}, f32[392,128]{1,0:T(8,128)S(1)}, u32[]{:S(2)}, u32[]{:S(2)}) collective-permute-start(f32[392,128]{1,0:T(8,128)} %pack.1.refs_3_.refs_1_), channel_id=1, source_target_pairs={{0,16},{2,18},{4,20},{6,22},{8,24},{10,26},{12,28},{14,30},{16,0},... | collective-permute-start | bytes 602120 | tf_op jit(solution)/shard_map/ppermute | solution.py:293
  6.6 10.4 %collective-permute-start.2 = (f32[392,128]{1,0:T(8,128)}, f32[392,128]{1,0:T(8,128)S(1)}, u32[]{:S(2)}, u32[]{:S(2)}) collective-permute-start(f32[392,128]{1,0:T(8,128)} %pack.1.refs_3_.refs_1_), channel_id=1, source_target_pairs={{0,8},{2,10},{4,12},{6,14},{8,0},{10,2},{12,4},{14,6},{16,24},{18,... | collective-permute-start | bytes 602120 | tf_op jit(solution)/shard_map/ppermute | solution.py:293
  8.2 8.8 %collective-permute-start.3 = (f32[392,128]{1,0:T(8,128)}, f32[392,128]{1,0:T(8,128)S(1)}, u32[]{:S(2)}, u32[]{:S(2)}) collective-permute-start(f32[392,128]{1,0:T(8,128)} %pack.1.refs_3_.refs_1_), channel_id=1, source_target_pairs={{0,4},{2,6},{4,0},{6,2},{8,12},{10,14},{12,8},{14,10},{16,20},{18,... | collective-permute-start | bytes 602120 | tf_op jit(solution)/shard_map/ppermute | solution.py:293
  17.1 8.8 %collective-permute-start.7 = (f32[3,392,128]{2,1,0:T(8,128)S(1)}, f32[3,392,128]{2,1,0:T(8,128)S(1)}, u32[]{:S(2)}, u32[]{:S(2)}) collective-permute-start(f32[3,392,128]{2,1,0:T(8,128)S(1)} %relay.12.refs_8_), channel_id=1, source_target_pairs={{0,2},{2,0},{4,6},{6,4},{8,10},{10,8},{12,14},{14,12},{16,18},{18,... | collective-permute-start | bytes 1806344 | tf_op jit(solution)/shard_map/ppermute | solution.py:293
  17.2 8.1 %collective-permute-start.5 = (f32[392,128]{1,0:T(8,128)S(1)}, f32[392,128]{1,0:T(8,128)S(1)}, u32[]{:S(2)}, u32[]{:S(2)}) collective-permute-start(f32[392,128]{1,0:T(8,128)S(1)} %relay.9.refs_1_.refs_2_.refs_3_), channel_id=1, source_target_pairs={{0,4},{2,6},{4,0},{6,2},{8,12},{10,14},{12,8},{14,10},{16,20},{18,... | collective-permute-start | bytes 602120 | tf_op jit(solution)/shard_map/ppermute | solution.py:293
  18.8 7.1 %collective-permute-start.8 = (f32[392,128]{1,0:T(8,128)S(1)}, f32[392,128]{1,0:T(8,128)S(1)}, u32[]{:S(2)}, u32[]{:S(2)}) collective-permute-start(f32[392,128]{1,0:T(8,128)S(1)} %relay.9.refs_1_.refs_2_.refs_3_), channel_id=1, source_target_pairs={{0,8},{2,10},{4,12},{6,14},{8,0},{10,2},{12,4},{14,6},{16,24},{18,... | collective-permute-start | bytes 602120 | tf_op jit(solution)/shard_map/ppermute | solution.py:293
  20.2 8.6 %collective-permute-start.6 = (f32[392,128]{1,0:T(8,128)S(1)}, f32[392,128]{1,0:T(8,128)S(1)}, u32[]{:S(2)}, u32[]{:S(2)}) collective-permute-start(f32[392,128]{1,0:T(8,128)S(1)} %relay.10.refs_1_.refs_4_.refs_3_), channel_id=1, source_target_pairs={{0,4},{2,6},{4,0},{6,2},{8,12},{10,14},{12,8},{14,10},{16,20},{18,... | collective-permute-start | bytes 602120 | tf_op jit(solution)/shard_map/ppermute | solution.py:293
  23.7 12.3 %collective-permute-start.4 = (f32[5,136,128]{2,1,0:T(8,128)S(1)}, f32[5,136,128]{2,1,0:T(8,128)S(1)}, u32[]{:S(2)}, u32[]{:S(2)}) collective-permute-start(f32[5,136,128]{2,1,0:T(8,128)S(1)} %get-tuple-element.41.refs_2_), channel_id=1, source_target_pairs={{0,1},{1,0},{2,3},{3,2},{4,5},{5,4},{6,7},{7,6},{8,9},{9,8},{10,11... | collective-permute-start | bytes 1044488 | tf_op jit(solution)/shard_map/ppermute | solution.py:353
  25.3 6.8 %collective-permute-start.9 = (f32[392,128]{1,0:T(8,128)S(1)}, f32[392,128]{1,0:T(8,128)S(1)}, u32[]{:S(2)}, u32[]{:S(2)}) collective-permute-start(f32[392,128]{1,0:T(8,128)S(1)} %relay.13.refs_1_.refs_3_.refs_7_), channel_id=1, source_target_pairs={{0,2},{2,0},{4,6},{6,4},{8,10},{10,8},{12,14},{14,12},{16,18},{18,... | collective-permute-start | bytes 602120 | tf_op jit(solution)/shard_map/ppermute | solution.py:293
  29.0 8.0 %collective-permute-start.12 = (f32[392,128]{1,0:T(8,128)S(1)}, f32[392,128]{1,0:T(8,128)S(1)}, u32[]{:S(2)}, u32[]{:S(2)}) collective-permute-start(f32[392,128]{1,0:T(8,128)S(1)} %relay.14.refs_4_.refs_3_.refs_6_), channel_id=1, source_target_pairs={{0,4},{2,6},{4,0},{6,2},{8,12},{10,14},{12,8},{14,10},{16,20},{18,... | collective-permute-start | bytes 602120 | tf_op jit(solution)/shard_map/ppermute | solution.py:293
  30.6 7.9 %collective-permute-start.11 = (f32[3,136,128]{2,1,0:T(8,128)S(1)}, f32[3,136,128]{2,1,0:T(8,128)S(1)}, u32[]{:S(2)}, u32[]{:S(2)}) collective-permute-start(f32[3,136,128]{2,1,0:T(8,128)S(1)} %get-tuple-element.46.refs_2_), channel_id=1, source_target_pairs={{0,1},{1,0},{2,3},{3,2},{4,5},{5,4},{6,7},{7,6},{8,9},{9,8},{10,11... | collective-permute-start | bytes 626696 | tf_op jit(solution)/shard_map/ppermute | solution.py:353
  32.1 7.5 %collective-permute-start.17 = (f32[392,128]{1,0:T(8,128)S(1)}, f32[392,128]{1,0:T(8,128)S(1)}, u32[]{:S(2)}, u32[]{:S(2)}) collective-permute-start(f32[392,128]{1,0:T(8,128)S(1)} %relay.14.refs_4_.refs_3_.refs_6_), channel_id=1, source_target_pairs={{0,2},{2,0},{4,6},{6,4},{8,10},{10,8},{12,14},{14,12},{16,18},{18,... | collective-permute-start | bytes 602120 | tf_op jit(solution)/shard_map/ppermute | solution.py:293
  37.7 8.6 %collective-permute-start.19 = (f32[4,136,128]{2,1,0:T(8,128)S(1)}, f32[4,136,128]{2,1,0:T(8,128)S(1)}, u32[]{:S(2)}, u32[]{:S(2)}) collective-permute-start(f32[4,136,128]{2,1,0:T(8,128)S(1)} %get-tuple-element.55.refs_2_), channel_id=1, source_target_pairs={{0,1},{1,0},{2,3},{3,2},{4,5},{5,4},{6,7},{7,6},{8,9},{9,8},{10,11... | collective-permute-start | bytes 835592 | tf_op jit(solution)/shard_map/ppermute | solution.py:353
  39.2 6.3 %collective-permute-start.15 = (f32[392,128]{1,0:T(8,128)S(1)}, f32[392,128]{1,0:T(8,128)S(1)}, u32[]{:S(2)}, u32[]{:S(2)}) collective-permute-start(f32[392,128]{1,0:T(8,128)S(1)} %get-tuple-element.52), channel_id=1, source_target_pairs={{0,2},{2,0},{4,6},{6,4},{8,10},{10,8},{12,14},{14,12},{16,18},{18,... | collective-permute-start | bytes 602120 | tf_op jit(solution)/shard_map/ppermute | solution.py:293
  39.6 6.0 %collective-permute-start.14 = (f32[392,128]{1,0:T(8,128)S(1)}, f32[392,128]{1,0:T(8,128)S(1)}, u32[]{:S(2)}, u32[]{:S(2)}) collective-permute-start(f32[392,128]{1,0:T(8,128)S(1)} %get-tuple-element.50), channel_id=1, source_target_pairs={{0,2},{2,0},{4,6},{6,4},{8,10},{10,8},{12,14},{14,12},{16,18},{18,... | collective-permute-start | bytes 602120 | tf_op jit(solution)/shard_map/ppermute | solution.py:293
  43.9 8.8 %collective-permute-start.23 = (f32[4,136,128]{2,1,0:T(8,128)S(1)}, f32[4,136,128]{2,1,0:T(8,128)S(1)}, u32[]{:S(2)}, u32[]{:S(2)}) collective-permute-start(f32[4,136,128]{2,1,0:T(8,128)S(1)} %get-tuple-element.60.refs_2_), channel_id=1, source_target_pairs={{0,1},{1,0},{2,3},{3,2},{4,5},{5,4},{6,7},{7,6},{8,9},{9,8},{10,11... | collective-permute-start | bytes 835592 | tf_op jit(solution)/shard_map/ppermute | solution.py:353
  47.9 7.8 %collective-permute-start.25 = (f32[392,128]{1,0:T(8,128)S(1)}, f32[392,128]{1,0:T(8,128)S(1)}, u32[]{:S(2)}, u32[]{:S(2)}) collective-permute-start(f32[392,128]{1,0:T(8,128)S(1)} %merge.12.refs_2_), channel_id=1, source_target_pairs={{0,4},{2,6},{4,0},{6,2},{8,12},{10,14},{12,8},{14,10},{16,20},{18,... | collective-permute-start | bytes 602120 | tf_op jit(solution)/shard_map/ppermute | solution.py:293
  49.2 18.6 %collective-permute-start.22 = (f32[2,392,128]{2,1,0:T(8,128)S(1)}, f32[2,392,128]{2,1,0:T(8,128)S(1)}, u32[]{:S(2)}, u32[]{:S(2)}) collective-permute-start(f32[2,392,128]{2,1,0:T(8,128)S(1)} %merge.15.refs_4_), channel_id=1, source_target_pairs={{0,4},{2,6},{4,0},{6,2},{8,12},{10,14},{12,8},{14,10},{16,20},{18,... | collective-permute-start | bytes 1204232 | tf_op jit(solution)/shard_map/ppermute | solution.py:293
  55.9 11.9 %collective-permute-start.24 = (f32[392,128]{1,0:T(8,128)S(1)}, f32[392,128]{1,0:T(8,128)S(1)}, u32[]{:S(2)}, u32[]{:S(2)}) collective-permute-start(f32[392,128]{1,0:T(8,128)S(1)} %get-tuple-element.62), channel_id=1, source_target_pairs={{0,2},{2,0},{4,6},{6,4},{8,10},{10,8},{12,14},{14,12},{16,18},{18,... | collective-permute-start | bytes 602120 | tf_op jit(solution)/shard_map/ppermute | solution.py:293
  57.1 14.7 %collective-permute-start.32 = (f32[392,128]{1,0:T(8,128)S(1)}, f32[392,128]{1,0:T(8,128)S(1)}, u32[]{:S(2)}, u32[]{:S(2)}) collective-permute-start(f32[392,128]{1,0:T(8,128)S(1)} %merge.16.refs_2_), channel_id=1, source_target_pairs={{0,4},{2,6},{4,0},{6,2},{8,12},{10,14},{12,8},{14,10},{16,20},{18,... | collective-permute-start | bytes 602120 | tf_op jit(solution)/shard_map/ppermute | solution.py:293
  67.8 15.7 %collective-permute-start.30 = (f32[392,128]{1,0:T(8,128)S(1)}, f32[392,128]{1,0:T(8,128)S(1)}, u32[]{:S(2)}, u32[]{:S(2)}) collective-permute-start(f32[392,128]{1,0:T(8,128)S(1)} %merge.18.refs_2_), channel_id=1, source_target_pairs={{0,16},{2,18},{4,20},{6,22},{8,24},{10,26},{12,28},{14,30},{16,0},... | collective-permute-start | bytes 602120 | tf_op jit(solution)/shard_map/ppermute | solution.py:293
  69.7 13.9 %collective-permute-start.31 = (f32[392,128]{1,0:T(8,128)S(1)}, f32[392,128]{1,0:T(8,128)S(1)}, u32[]{:S(2)}, u32[]{:S(2)}) collective-permute-start(f32[392,128]{1,0:T(8,128)S(1)} %merge.19.refs_2_), channel_id=1, source_target_pairs={{0,8},{2,10},{4,12},{6,14},{8,0},{10,2},{12,4},{14,6},{16,24},{18,... | collective-permute-start | bytes 602120 | tf_op jit(solution)/shard_map/ppermute | solution.py:293
  71.9 11.7 %collective-permute-start.34 = (f32[392,128]{1,0:T(8,128)S(1)}, f32[392,128]{1,0:T(8,128)S(1)}, u32[]{:S(2)}, u32[]{:S(2)}) collective-permute-start(f32[392,128]{1,0:T(8,128)S(1)} %merge.20.refs_19_), channel_id=1, source_target_pairs={{0,24},{2,26},{4,28},{6,30},{8,16},{10,18},{12,20},{14,22},{16,8},... | collective-permute-start | bytes 602120 | tf_op jit(solution)/shard_map/ppermute | solution.py:293
  (18 other events, 74.3 us)

commit v12 on v10

--- a/solution.py
+++ b/solution.py
@@ -492,6 +492,7 @@
             0.05,
         )
         if mask == 1:
+            over_x[0] = (pass_on(over_x[0][0]), None)
             pair(4 * far - 2)
             beside(far - 1)
     for k in range(3, far):

time: 84.8 us -> 83.6 us (0.986)
  waiting for transfers between devices: 12.6 us -> 11.6 us
    ppermute x31, waiting for transfers between devices: 9.31 us -> 8.32 us  [send(): return lax.ppermute(x, 'blk', [(i, i ^ mask) for i in range(n)])]
    pallas_call x37 -> x38, Pallas kernels: 32 us -> 32 us  [__call__(): pl.pallas_call(kernel, out_shape=out_shape, name=name, in_specs=in_specs,...]
  transfers between devices with their start and end apart: 35 -> 35, of which waited for: 12 -> 11; matrix products, arithmetic and copies ran while one was open for 0% -> 0% of each run, Pallas kernels for 35% -> 35%
where the time goes in v12:
time: 83.6 us; the launch traced here: 83.2 us
  starting transfers between devices  33.8 us (40%)
  Pallas kernels  32 us (38%)
  waiting for transfers between devices  11.6 us (14%)
  local copies, waits for them, and re-layouts  4.68 us (6%)
  between operations  1.04 us (1%)
    pallas_call x38, Pallas kernels, __call__(): pl.pallas_call(kernel, out_shape=out_shape, name=name, in_specs=in_specs,...  32 us
    ppermute x31, starting transfers between devices, send(): return lax.ppermute(x, 'blk', [(i, i ^ mask) for i in range(n)])  28.6 us
    ppermute x31, waiting for transfers between devices, send(): return lax.ppermute(x, 'blk', [(i, i ^ mask) for i in range(n)])  8.32 us
    ppermute x4, starting transfers between devices, score(): lax.ppermute(part, 'dim', [(i, (i + s) % depth) for i in range(depth)])  5.19 us
    unnamed x14, local copies, waits for them, and re-layouts  4.68 us
    ppermute x4, waiting for transfers between devices, score(): lax.ppermute(part, 'dim', [(i, (i + s) % depth) for i in range(depth)])  3.3 us
  transfers between devices with their start and end apart: 35, of which 11 were waited for; matrix products, arithmetic and copies ran while one was open for 0% of the time, Pallas kernels for 35%

profile of v12, /device:TPU:0, one launch (start us, length us, event | category | flops | bytes accessed | tf_op | source)
XLA Modules:
  0.0 83.2 jit_solution(4117014432793738010)
XLA Ops:
  0.6 1.8 %pack.1.refs_3_.refs_1_ = f32[392,128]{1,0:T(8,128)} custom-call(f32[128,384]{1,0:T(8,128)} %refs_0_.4, s32[8,128]{1,0:T(8,128)} %bitcast.3, s32[8,128]{1,0:T(8,128)} %bitcast.4), custom_call_target="tpu_custom_call" | custom-call | bytes 6660000 | tf_op jit(solution)/shard_map/pack/pallas_call | solution.py:45
  2.9 3.7 %collective-permute-start = (f32[392,128]{1,0:T(8,128)}, f32[392,128]{1,0:T(8,128)S(1)}, u32[]{:S(2)}, u32[]{:S(2)}) collective-permute-start(f32[392,128]{1,0:T(8,128)} %pack.1.refs_3_.refs_1_), channel_id=1, source_target_pairs={{0,16},{2,18},{4,20},{6,22},{8,24},{10,26},{12,28},{14,30},{16,0},... | collective-permute-start | bytes 602120 | tf_op jit(solution)/shard_map/ppermute | solution.py:293
  6.6 1.6 %collective-permute-start.2 = (f32[392,128]{1,0:T(8,128)}, f32[392,128]{1,0:T(8,128)S(1)}, u32[]{:S(2)}, u32[]{:S(2)}) collective-permute-start(f32[392,128]{1,0:T(8,128)} %pack.1.refs_3_.refs_1_), channel_id=1, source_target_pairs={{0,8},{2,10},{4,12},{6,14},{8,0},{10,2},{12,4},{14,6},{16,24},{18,... | collective-permute-start | bytes 602120 | tf_op jit(solution)/shard_map/ppermute | solution.py:293
  8.2 1.5 %collective-permute-start.3 = (f32[392,128]{1,0:T(8,128)}, f32[392,128]{1,0:T(8,128)S(1)}, u32[]{:S(2)}, u32[]{:S(2)}) collective-permute-start(f32[392,128]{1,0:T(8,128)} %pack.1.refs_3_.refs_1_), channel_id=1, source_target_pairs={{0,4},{2,6},{4,0},{6,2},{8,12},{10,14},{12,8},{14,10},{16,20},{18,... | collective-permute-start | bytes 602120 | tf_op jit(solution)/shard_map/ppermute | solution.py:293
  10.7 1.9 %copy-done = f32[384,2048]{1,0:T(8,128)S(1)} copy-done((f32[384,2048]{1,0:T(8,128)S(1)}, f32[384,2048]{1,0:T(8,128)}, u32[]{:S(2)}) %copy-start) | copy-done | bytes 3145752
  14.5 1.9 %score.5 = (f32[2,136,128]{2,1,0:T(8,128)S(1)}, f32[2,384,128]{2,1,0:T(8,128)S(1)}) custom-call(s32[1]{0:T(128)} %bitcast.refs_0_, f32[128,384]{1,0:T(8,128)S(1)} %copy-done.3, f32[384,2048]{1,0:T(8,128)S(1)} %copy-done, f32[392,128]{1,0:T(8,128)S(1)} %copy-done.5, f32[392,128]{1,0:T(8,128)S(1)} %collective-permute-done.1.refs_4_.refs_5_, ...), custom_call_target="tpu_custom_call" | custom-call | bytes 6660000 | tf_op jit(solution)/shard_map/score/pallas_call | solution.py:45
  17.2 1.6 %collective-permute-start.5 = (f32[392,128]{1,0:T(8,128)S(1)}, f32[392,128]{1,0:T(8,128)S(1)}, u32[]{:S(2)}, u32[]{:S(2)}) collective-permute-start(f32[392,128]{1,0:T(8,128)S(1)} %relay.9.refs_1_.refs_2_.refs_3_), channel_id=1, source_target_pairs={{0,4},{2,6},{4,0},{6,2},{8,12},{10,14},{12,8},{14,10},{16,20},{18,... | collective-permute-start | bytes 602120 | tf_op jit(solution)/shard_map/ppermute | solution.py:293
  18.8 1.4 %collective-permute-start.8 = (f32[392,128]{1,0:T(8,128)S(1)}, f32[392,128]{1,0:T(8,128)S(1)}, u32[]{:S(2)}, u32[]{:S(2)}) collective-permute-start(f32[392,128]{1,0:T(8,128)S(1)} %relay.9.refs_1_.refs_2_.refs_3_), channel_id=1, source_target_pairs={{0,8},{2,10},{4,12},{6,14},{8,0},{10,2},{12,4},{14,6},{16,24},{18,... | collective-permute-start | bytes 602120 | tf_op jit(solution)/shard_map/ppermute | solution.py:293
  20.8 2.9 %score.6 = (f32[5,136,128]{2,1,0:T(8,128)S(1)}, f32[5,384,128]{2,1,0:T(8,128)S(1)}) custom-call(s32[1]{0:T(128)} %bitcast.refs_0_, f32[128,384]{1,0:T(8,128)S(1)} %copy-done.4, f32[384,2048]{1,0:T(8,128)S(1)} %copy-done.1, f32[392,128]{1,0:T(8,128)S(1)} %relay.9.refs_1_.refs_2_.refs_3_, f32[392,128]{1,0:T(8,128)S(1)} %relay.10.refs_1_.refs_4_.refs_3_, ...), custom_call_target="tpu_custom_call" | custom-call | bytes 9990000 | tf_op jit(solution)/shard_map/score/pallas_call | solution.py:45
  23.7 1.6 %collective-permute-start.4 = (f32[5,136,128]{2,1,0:T(8,128)S(1)}, f32[5,136,128]{2,1,0:T(8,128)S(1)}, u32[]{:S(2)}, u32[]{:S(2)}) collective-permute-start(f32[5,136,128]{2,1,0:T(8,128)S(1)} %get-tuple-element.41.refs_2_), channel_id=1, source_target_pairs={{0,1},{1,0},{2,3},{3,2},{4,5},{5,4},{6,7},{7,6},{8,9},{9,8},{10,11... | collective-permute-start | bytes 1044488 | tf_op jit(solution)/shard_map/ppermute | solution.py:353
  25.9 2.9 %score.7 = (f32[3,136,128]{2,1,0:T(8,128)S(1)}, f32[3,384,128]{2,1,0:T(8,128)S(1)}) custom-call(s32[1]{0:T(128)} %bitcast.refs_0_, f32[128,384]{1,0:T(8,128)S(1)} %copy-done.4, f32[384,2048]{1,0:T(8,128)S(1)} %copy-done.1, f32[3,392,128]{2,1,0:T(8,128)S(1)} %collective-permute-done.7.refs_3_.refs_9_, f32[392,128]{1,0:T(8,128)S(1)} %relay.14.refs_4_.refs_3_.refs_6_), custom_call_target="tpu_custom_call" | custom-call | bytes 9990000 | tf_op jit(solution)/shard_map/score/pallas_call | solution.py:45
  29.0 1.6 %collective-permute-start.12 = (f32[392,128]{1,0:T(8,128)S(1)}, f32[392,128]{1,0:T(8,128)S(1)}, u32[]{:S(2)}, u32[]{:S(2)}) collective-permute-start(f32[392,128]{1,0:T(8,128)S(1)} %relay.14.refs_4_.refs_3_.refs_6_), channel_id=1, source_target_pairs={{0,4},{2,6},{4,0},{6,2},{8,12},{10,14},{12,8},{14,10},{16,20},{18,... | collective-permute-start | bytes 602120 | tf_op jit(solution)/shard_map/ppermute | solution.py:293
  30.6 1.5 %collective-permute-start.11 = (f32[3,136,128]{2,1,0:T(8,128)S(1)}, f32[3,136,128]{2,1,0:T(8,128)S(1)}, u32[]{:S(2)}, u32[]{:S(2)}) collective-permute-start(f32[3,136,128]{2,1,0:T(8,128)S(1)} %get-tuple-element.46.refs_2_), channel_id=1, source_target_pairs={{0,1},{1,0},{2,3},{3,2},{4,5},{5,4},{6,7},{7,6},{8,9},{9,8},{10,11... | collective-permute-start | bytes 626696 | tf_op jit(solution)/shard_map/ppermute | solution.py:353
  32.1 3.8 %score.8 = (f32[4,136,128]{2,1,0:T(8,128)S(1)}, f32[4,384,128]{2,1,0:T(8,128)S(1)}) custom-call(s32[1]{0:T(128)} %bitcast.refs_0_, f32[128,384]{1,0:T(8,128)S(1)} %copy-done.4, f32[384,2048]{1,0:T(8,128)S(1)} %copy-done.1, f32[392,128]{1,0:T(8,128)S(1)} %relay.13.refs_1_.refs_3_.refs_7_, f32[392,128]{1,0:T(8,128)S(1)} %relay.15.refs_4_.refs_7_.refs_8_, ...), custom_call_target="tpu_custom_call" | custom-call | bytes 13320000 | tf_op jit(solution)/shard_map/score/pallas_call | solution.py:45
  40.1 3.8 %score.9 = (f32[4,136,128]{2,1,0:T(8,128)S(1)}, f32[4,384,128]{2,1,0:T(8,128)S(1)}) custom-call(s32[1]{0:T(128)} %bitcast.refs_0_, f32[128,384]{1,0:T(8,128)S(1)} %copy-done.4, f32[384,2048]{1,0:T(8,128)S(1)} %copy-done.1, f32[392,128]{1,0:T(8,128)S(1)} %relay.14.refs_4_.refs_3_.refs_6_, f32[392,128]{1,0:T(8,128)S(1)} %relay.16.refs_4_.refs_10_, ...), custom_call_target="tpu_custom_call" | custom-call | bytes 13320000 | tf_op jit(solution)/shard_map/score/pallas_call | solution.py:45
  43.9 1.5 %collective-permute-start.23 = (f32[4,136,128]{2,1,0:T(8,128)S(1)}, f32[4,136,128]{2,1,0:T(8,128)S(1)}, u32[]{:S(2)}, u32[]{:S(2)}) collective-permute-start(f32[4,136,128]{2,1,0:T(8,128)S(1)} %get-tuple-element.60.refs_2_), channel_id=1, source_target_pairs={{0,1},{1,0},{2,3},{3,2},{4,5},{5,4},{6,7},{7,6},{8,9},{9,8},{10,11... | collective-permute-start | bytes 835592 | tf_op jit(solution)/shard_map/ppermute | solution.py:353
  50.1 2.6 %collective-permute-done.23.refs_3_ = f32[4,136,128]{2,1,0:T(8,128)S(1)} collective-permute-done((f32[4,136,128]{2,1,0:T(8,128)S(1)}, f32[4,136,128]{2,1,0:T(8,128)S(1)}, u32[]{:S(2)}, u32[]{:S(2)}) %collective-permute-start.23) | collective-permute-done | bytes 278560 | tf_op jit(solution)/shard_map/ppermute | solution.py:353
  56.8 1.7 %collective-permute-start.26 = (f32[2,16,128]{2,1,0:T(8,128)S(1)}, f32[2,16,128]{2,1,0:T(8,128)S(1)}, u32[]{:S(2)}, u32[]{:S(2)}) collective-permute-start(f32[2,16,128]{2,1,0:T(8,128)S(1)} %stats_merge.4.refs_1_.refs_0_), channel_id=1, source_target_pairs={{0,16},{2,18},{4,20},{6,22},{8,24},{10,26},{12,28},{14,30},{16,0},... | collective-permute-start | bytes 49160 | tf_op jit(solution)/shard_map/ppermute | solution.py:293
  58.6 3.0 %collective-permute-done.26.refs_1_ = f32[2,16,128]{2,1,0:T(8,128)S(1)} collective-permute-done((f32[2,16,128]{2,1,0:T(8,128)S(1)}, f32[2,16,128]{2,1,0:T(8,128)S(1)}, u32[]{:S(2)}, u32[]{:S(2)}) %collective-permute-start.26) | collective-permute-done | bytes 16416 | tf_op jit(solution)/shard_map/ppermute | solution.py:293
  63.0 2.4 %collective-permute-done.29.refs_1_ = f32[2,16,128]{2,1,0:T(8,128)S(1)} collective-permute-done((f32[2,16,128]{2,1,0:T(8,128)S(1)}, f32[2,16,128]{2,1,0:T(8,128)S(1)}, u32[]{:S(2)}, u32[]{:S(2)}) %collective-permute-start.29) | collective-permute-done | bytes 16416 | tf_op jit(solution)/shard_map/ppermute | solution.py:293
  66.5 1.8 %collective-permute-start.30 = (f32[392,128]{1,0:T(8,128)S(1)}, f32[392,128]{1,0:T(8,128)S(1)}, u32[]{:S(2)}, u32[]{:S(2)}) collective-permute-start(f32[392,128]{1,0:T(8,128)S(1)} %merge.18.refs_2_), channel_id=1, source_target_pairs={{0,16},{2,18},{4,20},{6,22},{8,24},{10,26},{12,28},{14,30},{16,0},... | collective-permute-start | bytes 602120 | tf_op jit(solution)/shard_map/ppermute | solution.py:293
  68.4 2.1 %collective-permute-start.31 = (f32[392,128]{1,0:T(8,128)S(1)}, f32[392,128]{1,0:T(8,128)S(1)}, u32[]{:S(2)}, u32[]{:S(2)}) collective-permute-start(f32[392,128]{1,0:T(8,128)S(1)} %merge.19.refs_2_), channel_id=1, source_target_pairs={{0,8},{2,10},{4,12},{6,14},{8,0},{10,2},{12,4},{14,6},{16,24},{18,... | collective-permute-start | bytes 602120 | tf_op jit(solution)/shard_map/ppermute | solution.py:293
  70.6 1.9 %collective-permute-start.34 = (f32[392,128]{1,0:T(8,128)S(1)}, f32[392,128]{1,0:T(8,128)S(1)}, u32[]{:S(2)}, u32[]{:S(2)}) collective-permute-start(f32[392,128]{1,0:T(8,128)S(1)} %merge.20.refs_19_), channel_id=1, source_target_pairs={{0,24},{2,26},{4,28},{6,30},{8,16},{10,18},{12,20},{14,22},{16,8},... | collective-permute-start | bytes 602120 | tf_op jit(solution)/shard_map/ppermute | solution.py:293
  72.5 9.8 %gradient.1 = (f32[128,384]{1,0:T(8,128)}, f32[384,2048]{1,0:T(8,128)}) custom-call(f32[2,16,128]{2,1,0:T(8,128)S(1)} %stats_merge.7.refs_2_.refs_0_, f32[392,128]{1,0:T(8,128)S(1)} %copy-done.6, f32[392,128]{1,0:T(8,128)S(1)} %relay.9.refs_1_.refs_2_.refs_3_, f32[392,128]{1,0:T(8,128)S(1)} %relay.10.refs_1_.refs_4_.refs_3_, ...), custom_call_target="tpu_custom_call" | custom-call | bytes 40700000 | tf_op jit(solution)/shard_map/gradient/pallas_call | solution.py:45
  (98 shorter events, 21.8 us)
Async XLA Ops:
  2.4 8.3 %collective-permute-start.1 = (f32[392,128]{1,0:T(8,128)}, f32[392,128]{1,0:T(8,128)S(1)}, u32[]{:S(2)}, u32[]{:S(2)}) collective-permute-start(f32[392,128]{1,0:T(8,128)} %pack.1.refs_3_.refs_1_), channel_id=1, source_target_pairs={{0,2},{2,0},{4,6},{6,4},{8,10},{10,8},{12,14},{14,12},{16,18},{18,... | collective-permute-start | bytes 602120 | tf_op jit(solution)/shard_map/ppermute | solution.py:293
  2.9 13.9 %collective-permute-start = (f32[392,128]{1,0:T(8,128)}, f32[392,128]{1,0:T(8,128)S(1)}, u32[]{:S(2)}, u32[]{:S(2)}) collective-permute-start(f32[392,128]{1,0:T(8,128)} %pack.1.refs_3_.refs_1_), channel_id=1, source_target_pairs={{0,16},{2,18},{4,20},{6,22},{8,24},{10,26},{12,28},{14,30},{16,0},... | collective-permute-start | bytes 602120 | tf_op jit(solution)/shard_map/ppermute | solution.py:293
  6.6 10.4 %collective-permute-start.2 = (f32[392,128]{1,0:T(8,128)}, f32[392,128]{1,0:T(8,128)S(1)}, u32[]{:S(2)}, u32[]{:S(2)}) collective-permute-start(f32[392,128]{1,0:T(8,128)} %pack.1.refs_3_.refs_1_), channel_id=1, source_target_pairs={{0,8},{2,10},{4,12},{6,14},{8,0},{10,2},{12,4},{14,6},{16,24},{18,... | collective-permute-start | bytes 602120 | tf_op jit(solution)/shard_map/ppermute | solution.py:293
  8.2 8.8 %collective-permute-start.3 = (f32[392,128]{1,0:T(8,128)}, f32[392,128]{1,0:T(8,128)S(1)}, u32[]{:S(2)}, u32[]{:S(2)}) collective-permute-start(f32[392,128]{1,0:T(8,128)} %pack.1.refs_3_.refs_1_), channel_id=1, source_target_pairs={{0,4},{2,6},{4,0},{6,2},{8,12},{10,14},{12,8},{14,10},{16,20},{18,... | collective-permute-start | bytes 602120 | tf_op jit(solution)/shard_map/ppermute | solution.py:293
  17.1 8.8 %collective-permute-start.7 = (f32[3,392,128]{2,1,0:T(8,128)S(1)}, f32[3,392,128]{2,1,0:T(8,128)S(1)}, u32[]{:S(2)}, u32[]{:S(2)}) collective-permute-start(f32[3,392,128]{2,1,0:T(8,128)S(1)} %relay.12.refs_8_), channel_id=1, source_target_pairs={{0,2},{2,0},{4,6},{6,4},{8,10},{10,8},{12,14},{14,12},{16,18},{18,... | collective-permute-start | bytes 1806344 | tf_op jit(solution)/shard_map/ppermute | solution.py:293
  17.2 8.1 %collective-permute-start.5 = (f32[392,128]{1,0:T(8,128)S(1)}, f32[392,128]{1,0:T(8,128)S(1)}, u32[]{:S(2)}, u32[]{:S(2)}) collective-permute-start(f32[392,128]{1,0:T(8,128)S(1)} %relay.9.refs_1_.refs_2_.refs_3_), channel_id=1, source_target_pairs={{0,4},{2,6},{4,0},{6,2},{8,12},{10,14},{12,8},{14,10},{16,20},{18,... | collective-permute-start | bytes 602120 | tf_op jit(solution)/shard_map/ppermute | solution.py:293
  18.8 7.1 %collective-permute-start.8 = (f32[392,128]{1,0:T(8,128)S(1)}, f32[392,128]{1,0:T(8,128)S(1)}, u32[]{:S(2)}, u32[]{:S(2)}) collective-permute-start(f32[392,128]{1,0:T(8,128)S(1)} %relay.9.refs_1_.refs_2_.refs_3_), channel_id=1, source_target_pairs={{0,8},{2,10},{4,12},{6,14},{8,0},{10,2},{12,4},{14,6},{16,24},{18,... | collective-permute-start | bytes 602120 | tf_op jit(solution)/shard_map/ppermute | solution.py:293
  20.2 8.6 %collective-permute-start.6 = (f32[392,128]{1,0:T(8,128)S(1)}, f32[392,128]{1,0:T(8,128)S(1)}, u32[]{:S(2)}, u32[]{:S(2)}) collective-permute-start(f32[392,128]{1,0:T(8,128)S(1)} %relay.10.refs_1_.refs_4_.refs_3_), channel_id=1, source_target_pairs={{0,4},{2,6},{4,0},{6,2},{8,12},{10,14},{12,8},{14,10},{16,20},{18,... | collective-permute-start | bytes 602120 | tf_op jit(solution)/shard_map/ppermute | solution.py:293
  23.7 12.3 %collective-permute-start.4 = (f32[5,136,128]{2,1,0:T(8,128)S(1)}, f32[5,136,128]{2,1,0:T(8,128)S(1)}, u32[]{:S(2)}, u32[]{:S(2)}) collective-permute-start(f32[5,136,128]{2,1,0:T(8,128)S(1)} %get-tuple-element.41.refs_2_), channel_id=1, source_target_pairs={{0,1},{1,0},{2,3},{3,2},{4,5},{5,4},{6,7},{7,6},{8,9},{9,8},{10,11... | collective-permute-start | bytes 1044488 | tf_op jit(solution)/shard_map/ppermute | solution.py:353
  25.3 6.8 %collective-permute-start.9 = (f32[392,128]{1,0:T(8,128)S(1)}, f32[392,128]{1,0:T(8,128)S(1)}, u32[]{:S(2)}, u32[]{:S(2)}) collective-permute-start(f32[392,128]{1,0:T(8,128)S(1)} %relay.13.refs_1_.refs_3_.refs_7_), channel_id=1, source_target_pairs={{0,2},{2,0},{4,6},{6,4},{8,10},{10,8},{12,14},{14,12},{16,18},{18,... | collective-permute-start | bytes 602120 | tf_op jit(solution)/shard_map/ppermute | solution.py:293
  29.0 8.0 %collective-permute-start.12 = (f32[392,128]{1,0:T(8,128)S(1)}, f32[392,128]{1,0:T(8,128)S(1)}, u32[]{:S(2)}, u32[]{:S(2)}) collective-permute-start(f32[392,128]{1,0:T(8,128)S(1)} %relay.14.refs_4_.refs_3_.refs_6_), channel_id=1, source_target_pairs={{0,4},{2,6},{4,0},{6,2},{8,12},{10,14},{12,8},{14,10},{16,20},{18,... | collective-permute-start | bytes 602120 | tf_op jit(solution)/shard_map/ppermute | solution.py:293
  30.6 7.9 %collective-permute-start.11 = (f32[3,136,128]{2,1,0:T(8,128)S(1)}, f32[3,136,128]{2,1,0:T(8,128)S(1)}, u32[]{:S(2)}, u32[]{:S(2)}) collective-permute-start(f32[3,136,128]{2,1,0:T(8,128)S(1)} %get-tuple-element.46.refs_2_), channel_id=1, source_target_pairs={{0,1},{1,0},{2,3},{3,2},{4,5},{5,4},{6,7},{7,6},{8,9},{9,8},{10,11... | collective-permute-start | bytes 626696 | tf_op jit(solution)/shard_map/ppermute | solution.py:353
  32.1 7.5 %collective-permute-start.17 = (f32[392,128]{1,0:T(8,128)S(1)}, f32[392,128]{1,0:T(8,128)S(1)}, u32[]{:S(2)}, u32[]{:S(2)}) collective-permute-start(f32[392,128]{1,0:T(8,128)S(1)} %relay.14.refs_4_.refs_3_.refs_6_), channel_id=1, source_target_pairs={{0,2},{2,0},{4,6},{6,4},{8,10},{10,8},{12,14},{14,12},{16,18},{18,... | collective-permute-start | bytes 602120 | tf_op jit(solution)/shard_map/ppermute | solution.py:293
  37.7 8.6 %collective-permute-start.19 = (f32[4,136,128]{2,1,0:T(8,128)S(1)}, f32[4,136,128]{2,1,0:T(8,128)S(1)}, u32[]{:S(2)}, u32[]{:S(2)}) collective-permute-start(f32[4,136,128]{2,1,0:T(8,128)S(1)} %get-tuple-element.55.refs_2_), channel_id=1, source_target_pairs={{0,1},{1,0},{2,3},{3,2},{4,5},{5,4},{6,7},{7,6},{8,9},{9,8},{10,11... | collective-permute-start | bytes 835592 | tf_op jit(solution)/shard_map/ppermute | solution.py:353
  39.2 6.3 %collective-permute-start.15 = (f32[392,128]{1,0:T(8,128)S(1)}, f32[392,128]{1,0:T(8,128)S(1)}, u32[]{:S(2)}, u32[]{:S(2)}) collective-permute-start(f32[392,128]{1,0:T(8,128)S(1)} %get-tuple-element.52), channel_id=1, source_target_pairs={{0,2},{2,0},{4,6},{6,4},{8,10},{10,8},{12,14},{14,12},{16,18},{18,... | collective-permute-start | bytes 602120 | tf_op jit(solution)/shard_map/ppermute | solution.py:293
  39.6 6.0 %collective-permute-start.14 = (f32[392,128]{1,0:T(8,128)S(1)}, f32[392,128]{1,0:T(8,128)S(1)}, u32[]{:S(2)}, u32[]{:S(2)}) collective-permute-start(f32[392,128]{1,0:T(8,128)S(1)} %get-tuple-element.50), channel_id=1, source_target_pairs={{0,2},{2,0},{4,6},{6,4},{8,10},{10,8},{12,14},{14,12},{16,18},{18,... | collective-permute-start | bytes 602120 | tf_op jit(solution)/shard_map/ppermute | solution.py:293
  43.9 8.8 %collective-permute-start.23 = (f32[4,136,128]{2,1,0:T(8,128)S(1)}, f32[4,136,128]{2,1,0:T(8,128)S(1)}, u32[]{:S(2)}, u32[]{:S(2)}) collective-permute-start(f32[4,136,128]{2,1,0:T(8,128)S(1)} %get-tuple-element.60.refs_2_), channel_id=1, source_target_pairs={{0,1},{1,0},{2,3},{3,2},{4,5},{5,4},{6,7},{7,6},{8,9},{9,8},{10,11... | collective-permute-start | bytes 835592 | tf_op jit(solution)/shard_map/ppermute | solution.py:353
  47.9 7.8 %collective-permute-start.28 = (f32[392,128]{1,0:T(8,128)S(1)}, f32[392,128]{1,0:T(8,128)S(1)}, u32[]{:S(2)}, u32[]{:S(2)}) collective-permute-start(f32[392,128]{1,0:T(8,128)S(1)} %merge.12.refs_2_), channel_id=1, source_target_pairs={{0,4},{2,6},{4,0},{6,2},{8,12},{10,14},{12,8},{14,10},{16,20},{18,... | collective-permute-start | bytes 602120 | tf_op jit(solution)/shard_map/ppermute | solution.py:293
  49.2 17.3 %collective-permute-start.22 = (f32[2,392,128]{2,1,0:T(8,128)S(1)}, f32[2,392,128]{2,1,0:T(8,128)S(1)}, u32[]{:S(2)}, u32[]{:S(2)}) collective-permute-start(f32[2,392,128]{2,1,0:T(8,128)S(1)} %merge.15.refs_4_), channel_id=1, source_target_pairs={{0,4},{2,6},{4,0},{6,2},{8,12},{10,14},{12,8},{14,10},{16,20},{18,... | collective-permute-start | bytes 1204232 | tf_op jit(solution)/shard_map/ppermute | solution.py:293
  54.3 12.1 %collective-permute-start.24 = (f32[392,128]{1,0:T(8,128)S(1)}, f32[392,128]{1,0:T(8,128)S(1)}, u32[]{:S(2)}, u32[]{:S(2)}) collective-permute-start(f32[392,128]{1,0:T(8,128)S(1)} %get-tuple-element.62), channel_id=1, source_target_pairs={{0,2},{2,0},{4,6},{6,4},{8,10},{10,8},{12,14},{14,12},{16,18},{18,... | collective-permute-start | bytes 602120 | tf_op jit(solution)/shard_map/ppermute | solution.py:293
  55.8 14.7 %collective-permute-start.32 = (f32[392,128]{1,0:T(8,128)S(1)}, f32[392,128]{1,0:T(8,128)S(1)}, u32[]{:S(2)}, u32[]{:S(2)}) collective-permute-start(f32[392,128]{1,0:T(8,128)S(1)} %merge.16.refs_2_), channel_id=1, source_target_pairs={{0,4},{2,6},{4,0},{6,2},{8,12},{10,14},{12,8},{14,10},{16,20},{18,... | collective-permute-start | bytes 602120 | tf_op jit(solution)/shard_map/ppermute | solution.py:293
  66.5 15.8 %collective-permute-start.30 = (f32[392,128]{1,0:T(8,128)S(1)}, f32[392,128]{1,0:T(8,128)S(1)}, u32[]{:S(2)}, u32[]{:S(2)}) collective-permute-start(f32[392,128]{1,0:T(8,128)S(1)} %merge.18.refs_2_), channel_id=1, source_target_pairs={{0,16},{2,18},{4,20},{6,22},{8,24},{10,26},{12,28},{14,30},{16,0},... | collective-permute-start | bytes 602120 | tf_op jit(solution)/shard_map/ppermute | solution.py:293
  68.4 13.9 %collective-permute-start.31 = (f32[392,128]{1,0:T(8,128)S(1)}, f32[392,128]{1,0:T(8,128)S(1)}, u32[]{:S(2)}, u32[]{:S(2)}) collective-permute-start(f32[392,128]{1,0:T(8,128)S(1)} %merge.19.refs_2_), channel_id=1, source_target_pairs={{0,8},{2,10},{4,12},{6,14},{8,0},{10,2},{12,4},{14,6},{16,24},{18,... | collective-permute-start | bytes 602120 | tf_op jit(solution)/shard_map/ppermute | solution.py:293
  70.6 11.7 %collective-permute-start.34 = (f32[392,128]{1,0:T(8,128)S(1)}, f32[392,128]{1,0:T(8,128)S(1)}, u32[]{:S(2)}, u32[]{:S(2)}) collective-permute-start(f32[392,128]{1,0:T(8,128)S(1)} %merge.20.refs_19_), channel_id=1, source_target_pairs={{0,24},{2,26},{4,28},{6,30},{8,16},{10,18},{12,20},{14,22},{16,8},... | collective-permute-start | bytes 602120 | tf_op jit(solution)/shard_map/ppermute | solution.py:293
  (18 other events, 73.9 us)

commit v13 on v12

--- a/solution.py
+++ b/solution.py
@@ -438,10 +438,10 @@
     score([2, 4, 8])
     relay(10)
     forward(3)
-    score([3, 5, 9])
+    score([10, 3, 5, 9])
     relay(6)
     share(10, 6)
-    score([10, 6, 11, 7])
+    score([6, 12, 11, 7])
     softmax()
     relay(14)
     share(12, 14)
@@ -449,7 +449,7 @@
     for k in range(3, far):
         if k + 1 < far:
             forward(k + 1)
-        score([4 * k, 4 * k + 2, 4 * k + 1, 4 * k + 3])
+        score([4 * k + 2 * i for i in range(k == 3, 2)] + [4 * k + 1, 4 * k + 3])
         if k + 1 < far:
             relay(4 * k + 6)
             share(4 * k + 4, 4 * k + 6)

time: 83.6 us -> 83.9 us (level)
  waiting for transfers between devices: 11.6 us -> 12.5 us
    ppermute x31, waiting for transfers between devices: 8.32 us -> 9.62 us  [send(): return lax.ppermute(x, 'blk', [(i, i ^ mask) for i in range(n)])]
  transfers between devices with their start and end apart: 35 -> 35, of which waited for: 11 -> 12; matrix products, arithmetic and copies ran while one was open for 0% -> 0% of each run, Pallas kernels for 35% -> 35%
where the time goes in v13:
time: 83.9 us; the launch traced here: 83.6 us
  starting transfers between devices  33.2 us (40%)
  Pallas kernels  32.1 us (38%)
  waiting for transfers between devices  12.5 us (15%)
  local copies, waits for them, and re-layouts  4.68 us (6%)
  between operations  1.07 us (1%)
    pallas_call x38, Pallas kernels, __call__(): pl.pallas_call(kernel, out_shape=out_shape, name=name, in_specs=in_specs,...  32.1 us
    ppermute x31, starting transfers between devices, send(): return lax.ppermute(x, 'blk', [(i, i ^ mask) for i in range(n)])  28.2 us
    ppermute x31, waiting for transfers between devices, send(): return lax.ppermute(x, 'blk', [(i, i ^ mask) for i in range(n)])  9.62 us
    ppermute x4, starting transfers between devices, score(): lax.ppermute(part, 'dim', [(i, (i + s) % depth) for i in range(depth)])  5.05 us
    unnamed x14, local copies, waits for them, and re-layouts  4.68 us
    ppermute x4, waiting for transfers between devices, score(): lax.ppermute(part, 'dim', [(i, (i + s) % depth) for i in range(depth)])  2.87 us
  transfers between devices with their start and end apart: 35, of which 12 were waited for; matrix products, arithmetic and copies ran while one was open for 0% of the time, Pallas kernels for 35%

profile of v13, /device:TPU:0, one launch (start us, length us, event | category | flops | bytes accessed | tf_op | source)
XLA Modules:
  0.0 83.6 jit_solution(8321872487058349443)
XLA Ops:
  0.6 1.8 %pack.1.refs_3_.refs_1_ = f32[392,128]{1,0:T(8,128)} custom-call(f32[128,384]{1,0:T(8,128)} %refs_0_.4, s32[8,128]{1,0:T(8,128)} %bitcast.3, s32[8,128]{1,0:T(8,128)} %bitcast.4), custom_call_target="tpu_custom_call" | custom-call | bytes 6660000 | tf_op jit(solution)/shard_map/pack/pallas_call | solution.py:45
  2.9 3.7 %collective-permute-start = (f32[392,128]{1,0:T(8,128)}, f32[392,128]{1,0:T(8,128)S(1)}, u32[]{:S(2)}, u32[]{:S(2)}) collective-permute-start(f32[392,128]{1,0:T(8,128)} %pack.1.refs_3_.refs_1_), channel_id=1, source_target_pairs={{0,16},{2,18},{4,20},{6,22},{8,24},{10,26},{12,28},{14,30},{16,0},... | collective-permute-start | bytes 602120 | tf_op jit(solution)/shard_map/ppermute | solution.py:293
  6.6 1.6 %collective-permute-start.2 = (f32[392,128]{1,0:T(8,128)}, f32[392,128]{1,0:T(8,128)S(1)}, u32[]{:S(2)}, u32[]{:S(2)}) collective-permute-start(f32[392,128]{1,0:T(8,128)} %pack.1.refs_3_.refs_1_), channel_id=1, source_target_pairs={{0,8},{2,10},{4,12},{6,14},{8,0},{10,2},{12,4},{14,6},{16,24},{18,... | collective-permute-start | bytes 602120 | tf_op jit(solution)/shard_map/ppermute | solution.py:293
  8.2 1.5 %collective-permute-start.3 = (f32[392,128]{1,0:T(8,128)}, f32[392,128]{1,0:T(8,128)S(1)}, u32[]{:S(2)}, u32[]{:S(2)}) collective-permute-start(f32[392,128]{1,0:T(8,128)} %pack.1.refs_3_.refs_1_), channel_id=1, source_target_pairs={{0,4},{2,6},{4,0},{6,2},{8,12},{10,14},{12,8},{14,10},{16,20},{18,... | collective-permute-start | bytes 602120 | tf_op jit(solution)/shard_map/ppermute | solution.py:293
  10.7 1.9 %copy-done = f32[384,2048]{1,0:T(8,128)S(1)} copy-done((f32[384,2048]{1,0:T(8,128)S(1)}, f32[384,2048]{1,0:T(8,128)}, u32[]{:S(2)}) %copy-start) | copy-done | bytes 3145752
  14.5 1.9 %score.5 = (f32[2,136,128]{2,1,0:T(8,128)S(1)}, f32[2,384,128]{2,1,0:T(8,128)S(1)}) custom-call(s32[1]{0:T(128)} %bitcast.refs_0_, f32[128,384]{1,0:T(8,128)S(1)} %copy-done.3, f32[384,2048]{1,0:T(8,128)S(1)} %copy-done, f32[392,128]{1,0:T(8,128)S(1)} %copy-done.5, f32[392,128]{1,0:T(8,128)S(1)} %collective-permute-done.1.refs_4_.refs_5_, ...), custom_call_target="tpu_custom_call" | custom-call | bytes 6660000 | tf_op jit(solution)/shard_map/score/pallas_call | solution.py:45
  17.2 1.6 %collective-permute-start.6 = (f32[392,128]{1,0:T(8,128)S(1)}, f32[392,128]{1,0:T(8,128)S(1)}, u32[]{:S(2)}, u32[]{:S(2)}) collective-permute-start(f32[392,128]{1,0:T(8,128)S(1)} %relay.9.refs_1_.refs_2_.refs_3_), channel_id=1, source_target_pairs={{0,4},{2,6},{4,0},{6,2},{8,12},{10,14},{12,8},{14,10},{16,20},{18,... | collective-permute-start | bytes 602120 | tf_op jit(solution)/shard_map/ppermute | solution.py:293
  18.8 1.4 %collective-permute-start.5 = (f32[392,128]{1,0:T(8,128)S(1)}, f32[392,128]{1,0:T(8,128)S(1)}, u32[]{:S(2)}, u32[]{:S(2)}) collective-permute-start(f32[392,128]{1,0:T(8,128)S(1)} %relay.9.refs_1_.refs_2_.refs_3_), channel_id=1, source_target_pairs={{0,8},{2,10},{4,12},{6,14},{8,0},{10,2},{12,4},{14,6},{16,24},{18,... | collective-permute-start | bytes 602120 | tf_op jit(solution)/shard_map/ppermute | solution.py:293
  20.8 2.9 %score.6 = (f32[5,136,128]{2,1,0:T(8,128)S(1)}, f32[5,384,128]{2,1,0:T(8,128)S(1)}) custom-call(s32[1]{0:T(128)} %bitcast.refs_0_, f32[128,384]{1,0:T(8,128)S(1)} %copy-done.4, f32[384,2048]{1,0:T(8,128)S(1)} %copy-done.1, f32[392,128]{1,0:T(8,128)S(1)} %relay.9.refs_1_.refs_2_.refs_3_, f32[392,128]{1,0:T(8,128)S(1)} %relay.10.refs_1_.refs_4_.refs_3_, ...), custom_call_target="tpu_custom_call" | custom-call | bytes 9990000 | tf_op jit(solution)/shard_map/score/pallas_call | solution.py:45
  23.6 1.6 %collective-permute-start.4 = (f32[5,136,128]{2,1,0:T(8,128)S(1)}, f32[5,136,128]{2,1,0:T(8,128)S(1)}, u32[]{:S(2)}, u32[]{:S(2)}) collective-permute-start(f32[5,136,128]{2,1,0:T(8,128)S(1)} %get-tuple-element.41.refs_2_), channel_id=1, source_target_pairs={{0,1},{1,0},{2,3},{3,2},{4,5},{5,4},{6,7},{7,6},{8,9},{9,8},{10,11... | collective-permute-start | bytes 1044488 | tf_op jit(solution)/shard_map/ppermute | solution.py:353
  25.9 3.8 %score.7 = (f32[4,136,128]{2,1,0:T(8,128)S(1)}, f32[4,384,128]{2,1,0:T(8,128)S(1)}) custom-call(s32[1]{0:T(128)} %bitcast.refs_0_, f32[128,384]{1,0:T(8,128)S(1)} %copy-done.4, f32[384,2048]{1,0:T(8,128)S(1)} %copy-done.1, f32[392,128]{1,0:T(8,128)S(1)} %relay.13.refs_1_.refs_3_.refs_7_, f32[3,392,128]{2,1,0:T(8,128)S(1)} %collective-permute-done.8.refs_4_.refs_9_, ...), custom_call_target="tpu_custom_call" | custom-call | bytes 13320000 | tf_op jit(solution)/shard_map/score/pallas_call | solution.py:45
  29.8 1.5 %collective-permute-start.12 = (f32[392,128]{1,0:T(8,128)S(1)}, f32[392,128]{1,0:T(8,128)S(1)}, u32[]{:S(2)}, u32[]{:S(2)}) collective-permute-start(f32[392,128]{1,0:T(8,128)S(1)} %relay.14.refs_5_.refs_3_.refs_6_), channel_id=1, source_target_pairs={{0,4},{2,6},{4,0},{6,2},{8,12},{10,14},{12,8},{14,10},{16,20},{18,... | collective-permute-start | bytes 602120 | tf_op jit(solution)/shard_map/ppermute | solution.py:293
  32.6 3.8 %score.8 = (f32[4,136,128]{2,1,0:T(8,128)S(1)}, f32[4,384,128]{2,1,0:T(8,128)S(1)}) custom-call(s32[1]{0:T(128)} %bitcast.refs_0_, f32[128,384]{1,0:T(8,128)S(1)} %copy-done.4, f32[384,2048]{1,0:T(8,128)S(1)} %copy-done.1, f32[392,128]{1,0:T(8,128)S(1)} %relay.14.refs_5_.refs_3_.refs_6_, f32[392,128]{1,0:T(8,128)S(1)} %relay.15.refs_4_.refs_7_.refs_8_, ...), custom_call_target="tpu_custom_call" | custom-call | bytes 13320000 | tf_op jit(solution)/shard_map/score/pallas_call | solution.py:45
  41.2 2.8 %score.9 = (f32[3,136,128]{2,1,0:T(8,128)S(1)}, f32[3,384,128]{2,1,0:T(8,128)S(1)}) custom-call(s32[1]{0:T(128)} %bitcast.refs_0_, f32[128,384]{1,0:T(8,128)S(1)} %copy-done.4, f32[384,2048]{1,0:T(8,128)S(1)} %copy-done.1, f32[392,128]{1,0:T(8,128)S(1)} %relay.16.refs_4_.refs_3_.refs_10_, f32[392,128]{1,0:T(8,128)S(1)} %collective-permute-done.17.refs_4_.refs_13_, ...), custom_call_target="tpu_custom_call" | custom-call | bytes 9990000 | tf_op jit(solution)/shard_map/score/pallas_call | solution.py:45
  44.0 1.4 %collective-permute-start.23 = (f32[3,136,128]{2,1,0:T(8,128)S(1)}, f32[3,136,128]{2,1,0:T(8,128)S(1)}, u32[]{:S(2)}, u32[]{:S(2)}) collective-permute-start(f32[3,136,128]{2,1,0:T(8,128)S(1)} %get-tuple-element.61.refs_2_), channel_id=1, source_target_pairs={{0,1},{1,0},{2,3},{3,2},{4,5},{5,4},{6,7},{7,6},{8,9},{9,8},{10,11... | collective-permute-start | bytes 626696 | tf_op jit(solution)/shard_map/ppermute | solution.py:353
  53.9 2.4 %collective-permute-done.28.refs_0_ = f32[392,128]{1,0:T(8,128)S(1)} collective-permute-done((f32[392,128]{1,0:T(8,128)S(1)}, f32[392,128]{1,0:T(8,128)S(1)}, u32[]{:S(2)}, u32[]{:S(2)}) %collective-permute-start.28) | collective-permute-done | bytes 200736 | tf_op jit(solution)/shard_map/ppermute | solution.py:293
  57.2 2.0 %collective-permute-start.26 = (f32[2,16,128]{2,1,0:T(8,128)S(1)}, f32[2,16,128]{2,1,0:T(8,128)S(1)}, u32[]{:S(2)}, u32[]{:S(2)}) collective-permute-start(f32[2,16,128]{2,1,0:T(8,128)S(1)} %stats_merge.4.refs_1_.refs_0_), channel_id=1, source_target_pairs={{0,16},{2,18},{4,20},{6,22},{8,24},{10,26},{12,28},{14,30},{16,0},... | collective-permute-start | bytes 49160 | tf_op jit(solution)/shard_map/ppermute | solution.py:293
  59.2 2.6 %collective-permute-done.26.refs_1_ = f32[2,16,128]{2,1,0:T(8,128)S(1)} collective-permute-done((f32[2,16,128]{2,1,0:T(8,128)S(1)}, f32[2,16,128]{2,1,0:T(8,128)S(1)}, u32[]{:S(2)}, u32[]{:S(2)}) %collective-permute-start.26) | collective-permute-done | bytes 16416 | tf_op jit(solution)/shard_map/ppermute | solution.py:293
  61.8 1.5 %collective-permute-start.29 = (f32[2,16,128]{2,1,0:T(8,128)S(1)}, f32[2,16,128]{2,1,0:T(8,128)S(1)}, u32[]{:S(2)}, u32[]{:S(2)}) collective-permute-start(f32[2,16,128]{2,1,0:T(8,128)S(1)} %stats_merge.5.refs_0_.refs_2_), channel_id=1, source_target_pairs={{0,8},{2,10},{4,12},{6,14},{8,0},{10,2},{12,4},{14,6},{16,24},{18,... | collective-permute-start | bytes 49160 | tf_op jit(solution)/shard_map/ppermute | solution.py:293
  63.3 2.3 %collective-permute-done.29.refs_1_ = f32[2,16,128]{2,1,0:T(8,128)S(1)} collective-permute-done((f32[2,16,128]{2,1,0:T(8,128)S(1)}, f32[2,16,128]{2,1,0:T(8,128)S(1)}, u32[]{:S(2)}, u32[]{:S(2)}) %collective-permute-start.29) | collective-permute-done | bytes 16416 | tf_op jit(solution)/shard_map/ppermute | solution.py:293
  67.0 1.8 %collective-permute-start.30 = (f32[392,128]{1,0:T(8,128)S(1)}, f32[392,128]{1,0:T(8,128)S(1)}, u32[]{:S(2)}, u32[]{:S(2)}) collective-permute-start(f32[392,128]{1,0:T(8,128)S(1)} %merge.18.refs_2_), channel_id=1, source_target_pairs={{0,16},{2,18},{4,20},{6,22},{8,24},{10,26},{12,28},{14,30},{16,0},... | collective-permute-start | bytes 602120 | tf_op jit(solution)/shard_map/ppermute | solution.py:293
  68.9 2.1 %collective-permute-start.31 = (f32[392,128]{1,0:T(8,128)S(1)}, f32[392,128]{1,0:T(8,128)S(1)}, u32[]{:S(2)}, u32[]{:S(2)}) collective-permute-start(f32[392,128]{1,0:T(8,128)S(1)} %merge.19.refs_2_), channel_id=1, source_target_pairs={{0,8},{2,10},{4,12},{6,14},{8,0},{10,2},{12,4},{14,6},{16,24},{18,... | collective-permute-start | bytes 602120 | tf_op jit(solution)/shard_map/ppermute | solution.py:293
  71.1 1.8 %collective-permute-start.34 = (f32[392,128]{1,0:T(8,128)S(1)}, f32[392,128]{1,0:T(8,128)S(1)}, u32[]{:S(2)}, u32[]{:S(2)}) collective-permute-start(f32[392,128]{1,0:T(8,128)S(1)} %merge.20.refs_19_), channel_id=1, source_target_pairs={{0,24},{2,26},{4,28},{6,30},{8,16},{10,18},{12,20},{14,22},{16,8},... | collective-permute-start | bytes 602120 | tf_op jit(solution)/shard_map/ppermute | solution.py:293
  73.0 9.8 %gradient.1 = (f32[128,384]{1,0:T(8,128)}, f32[384,2048]{1,0:T(8,128)}) custom-call(f32[2,16,128]{2,1,0:T(8,128)S(1)} %stats_merge.7.refs_2_.refs_0_, f32[392,128]{1,0:T(8,128)S(1)} %copy-done.6, f32[392,128]{1,0:T(8,128)S(1)} %relay.9.refs_1_.refs_2_.refs_3_, f32[392,128]{1,0:T(8,128)S(1)} %relay.10.refs_1_.refs_4_.refs_3_, ...), custom_call_target="tpu_custom_call" | custom-call | bytes 40700000 | tf_op jit(solution)/shard_map/gradient/pallas_call | solution.py:45
  (98 shorter events, 23.1 us)
Async XLA Ops:
  2.4 8.3 %collective-permute-start.1 = (f32[392,128]{1,0:T(8,128)}, f32[392,128]{1,0:T(8,128)S(1)}, u32[]{:S(2)}, u32[]{:S(2)}) collective-permute-start(f32[392,128]{1,0:T(8,128)} %pack.1.refs_3_.refs_1_), channel_id=1, source_target_pairs={{0,2},{2,0},{4,6},{6,4},{8,10},{10,8},{12,14},{14,12},{16,18},{18,... | collective-permute-start | bytes 602120 | tf_op jit(solution)/shard_map/ppermute | solution.py:293
  2.9 13.9 %collective-permute-start = (f32[392,128]{1,0:T(8,128)}, f32[392,128]{1,0:T(8,128)S(1)}, u32[]{:S(2)}, u32[]{:S(2)}) collective-permute-start(f32[392,128]{1,0:T(8,128)} %pack.1.refs_3_.refs_1_), channel_id=1, source_target_pairs={{0,16},{2,18},{4,20},{6,22},{8,24},{10,26},{12,28},{14,30},{16,0},... | collective-permute-start | bytes 602120 | tf_op jit(solution)/shard_map/ppermute | solution.py:293
  6.6 10.4 %collective-permute-start.2 = (f32[392,128]{1,0:T(8,128)}, f32[392,128]{1,0:T(8,128)S(1)}, u32[]{:S(2)}, u32[]{:S(2)}) collective-permute-start(f32[392,128]{1,0:T(8,128)} %pack.1.refs_3_.refs_1_), channel_id=1, source_target_pairs={{0,8},{2,10},{4,12},{6,14},{8,0},{10,2},{12,4},{14,6},{16,24},{18,... | collective-permute-start | bytes 602120 | tf_op jit(solution)/shard_map/ppermute | solution.py:293
  8.2 8.8 %collective-permute-start.3 = (f32[392,128]{1,0:T(8,128)}, f32[392,128]{1,0:T(8,128)S(1)}, u32[]{:S(2)}, u32[]{:S(2)}) collective-permute-start(f32[392,128]{1,0:T(8,128)} %pack.1.refs_3_.refs_1_), channel_id=1, source_target_pairs={{0,4},{2,6},{4,0},{6,2},{8,12},{10,14},{12,8},{14,10},{16,20},{18,... | collective-permute-start | bytes 602120 | tf_op jit(solution)/shard_map/ppermute | solution.py:293
  17.1 8.8 %collective-permute-start.8 = (f32[3,392,128]{2,1,0:T(8,128)S(1)}, f32[3,392,128]{2,1,0:T(8,128)S(1)}, u32[]{:S(2)}, u32[]{:S(2)}) collective-permute-start(f32[3,392,128]{2,1,0:T(8,128)S(1)} %relay.12.refs_8_), channel_id=1, source_target_pairs={{0,2},{2,0},{4,6},{6,4},{8,10},{10,8},{12,14},{14,12},{16,18},{18,... | collective-permute-start | bytes 1806344 | tf_op jit(solution)/shard_map/ppermute | solution.py:293
  17.2 8.1 %collective-permute-start.6 = (f32[392,128]{1,0:T(8,128)S(1)}, f32[392,128]{1,0:T(8,128)S(1)}, u32[]{:S(2)}, u32[]{:S(2)}) collective-permute-start(f32[392,128]{1,0:T(8,128)S(1)} %relay.9.refs_1_.refs_2_.refs_3_), channel_id=1, source_target_pairs={{0,4},{2,6},{4,0},{6,2},{8,12},{10,14},{12,8},{14,10},{16,20},{18,... | collective-permute-start | bytes 602120 | tf_op jit(solution)/shard_map/ppermute | solution.py:293
  18.8 7.1 %collective-permute-start.5 = (f32[392,128]{1,0:T(8,128)S(1)}, f32[392,128]{1,0:T(8,128)S(1)}, u32[]{:S(2)}, u32[]{:S(2)}) collective-permute-start(f32[392,128]{1,0:T(8,128)S(1)} %relay.9.refs_1_.refs_2_.refs_3_), channel_id=1, source_target_pairs={{0,8},{2,10},{4,12},{6,14},{8,0},{10,2},{12,4},{14,6},{16,24},{18,... | collective-permute-start | bytes 602120 | tf_op jit(solution)/shard_map/ppermute | solution.py:293
  20.2 9.5 %collective-permute-start.7 = (f32[392,128]{1,0:T(8,128)S(1)}, f32[392,128]{1,0:T(8,128)S(1)}, u32[]{:S(2)}, u32[]{:S(2)}) collective-permute-start(f32[392,128]{1,0:T(8,128)S(1)} %relay.10.refs_1_.refs_4_.refs_3_), channel_id=1, source_target_pairs={{0,4},{2,6},{4,0},{6,2},{8,12},{10,14},{12,8},{14,10},{16,20},{18,... | collective-permute-start | bytes 602120 | tf_op jit(solution)/shard_map/ppermute | solution.py:293
  23.6 12.8 %collective-permute-start.4 = (f32[5,136,128]{2,1,0:T(8,128)S(1)}, f32[5,136,128]{2,1,0:T(8,128)S(1)}, u32[]{:S(2)}, u32[]{:S(2)}) collective-permute-start(f32[5,136,128]{2,1,0:T(8,128)S(1)} %get-tuple-element.41.refs_2_), channel_id=1, source_target_pairs={{0,1},{1,0},{2,3},{3,2},{4,5},{5,4},{6,7},{7,6},{8,9},{9,8},{10,11... | collective-permute-start | bytes 1044488 | tf_op jit(solution)/shard_map/ppermute | solution.py:353
  25.3 7.4 %collective-permute-start.9 = (f32[392,128]{1,0:T(8,128)S(1)}, f32[392,128]{1,0:T(8,128)S(1)}, u32[]{:S(2)}, u32[]{:S(2)}) collective-permute-start(f32[392,128]{1,0:T(8,128)S(1)} %relay.13.refs_1_.refs_3_.refs_7_), channel_id=1, source_target_pairs={{0,2},{2,0},{4,6},{6,4},{8,10},{10,8},{12,14},{14,12},{16,18},{18,... | collective-permute-start | bytes 602120 | tf_op jit(solution)/shard_map/ppermute | solution.py:293
  29.8 7.9 %collective-permute-start.12 = (f32[392,128]{1,0:T(8,128)S(1)}, f32[392,128]{1,0:T(8,128)S(1)}, u32[]{:S(2)}, u32[]{:S(2)}) collective-permute-start(f32[392,128]{1,0:T(8,128)S(1)} %relay.14.refs_5_.refs_3_.refs_6_), channel_id=1, source_target_pairs={{0,4},{2,6},{4,0},{6,2},{8,12},{10,14},{12,8},{14,10},{16,20},{18,... | collective-permute-start | bytes 602120 | tf_op jit(solution)/shard_map/ppermute | solution.py:293
  31.3 8.4 %collective-permute-start.11 = (f32[4,136,128]{2,1,0:T(8,128)S(1)}, f32[4,136,128]{2,1,0:T(8,128)S(1)}, u32[]{:S(2)}, u32[]{:S(2)}) collective-permute-start(f32[4,136,128]{2,1,0:T(8,128)S(1)} %get-tuple-element.46.refs_2_), channel_id=1, source_target_pairs={{0,1},{1,0},{2,3},{3,2},{4,5},{5,4},{6,7},{7,6},{8,9},{9,8},{10,11... | collective-permute-start | bytes 835592 | tf_op jit(solution)/shard_map/ppermute | solution.py:353
  32.6 8.0 %collective-permute-start.17 = (f32[392,128]{1,0:T(8,128)S(1)}, f32[392,128]{1,0:T(8,128)S(1)}, u32[]{:S(2)}, u32[]{:S(2)}) collective-permute-start(f32[392,128]{1,0:T(8,128)S(1)} %relay.14.refs_5_.refs_3_.refs_6_), channel_id=1, source_target_pairs={{0,2},{2,0},{4,6},{6,4},{8,10},{10,8},{12,14},{14,12},{16,18},{18,... | collective-permute-start | bytes 602120 | tf_op jit(solution)/shard_map/ppermute | solution.py:293
  38.3 8.6 %collective-permute-start.19 = (f32[4,136,128]{2,1,0:T(8,128)S(1)}, f32[4,136,128]{2,1,0:T(8,128)S(1)}, u32[]{:S(2)}, u32[]{:S(2)}) collective-permute-start(f32[4,136,128]{2,1,0:T(8,128)S(1)} %get-tuple-element.56.refs_2_), channel_id=1, source_target_pairs={{0,1},{1,0},{2,3},{3,2},{4,5},{5,4},{6,7},{7,6},{8,9},{9,8},{10,11... | collective-permute-start | bytes 835592 | tf_op jit(solution)/shard_map/ppermute | solution.py:353
  39.0 5.1 %collective-permute-start.16 = (f32[392,128]{1,0:T(8,128)S(1)}, f32[392,128]{1,0:T(8,128)S(1)}, u32[]{:S(2)}, u32[]{:S(2)}) collective-permute-start(f32[392,128]{1,0:T(8,128)S(1)} %get-tuple-element.47.refs_1_), channel_id=1, source_target_pairs={{0,2},{2,0},{4,6},{6,4},{8,10},{10,8},{12,14},{14,12},{16,18},{18,... | collective-permute-start | bytes 602120 | tf_op jit(solution)/shard_map/ppermute | solution.py:293
  44.0 7.6 %collective-permute-start.23 = (f32[3,136,128]{2,1,0:T(8,128)S(1)}, f32[3,136,128]{2,1,0:T(8,128)S(1)}, u32[]{:S(2)}, u32[]{:S(2)}) collective-permute-start(f32[3,136,128]{2,1,0:T(8,128)S(1)} %get-tuple-element.61.refs_2_), channel_id=1, source_target_pairs={{0,1},{1,0},{2,3},{3,2},{4,5},{5,4},{6,7},{7,6},{8,9},{9,8},{10,11... | collective-permute-start | bytes 626696 | tf_op jit(solution)/shard_map/ppermute | solution.py:353
  48.4 7.8 %collective-permute-start.28 = (f32[392,128]{1,0:T(8,128)S(1)}, f32[392,128]{1,0:T(8,128)S(1)}, u32[]{:S(2)}, u32[]{:S(2)}) collective-permute-start(f32[392,128]{1,0:T(8,128)S(1)} %merge.12.refs_2_), channel_id=1, source_target_pairs={{0,4},{2,6},{4,0},{6,2},{8,12},{10,14},{12,8},{14,10},{16,20},{18,... | collective-permute-start | bytes 602120 | tf_op jit(solution)/shard_map/ppermute | solution.py:293
  49.7 17.3 %collective-permute-start.22 = (f32[2,392,128]{2,1,0:T(8,128)S(1)}, f32[2,392,128]{2,1,0:T(8,128)S(1)}, u32[]{:S(2)}, u32[]{:S(2)}) collective-permute-start(f32[2,392,128]{2,1,0:T(8,128)S(1)} %merge.15.refs_4_), channel_id=1, source_target_pairs={{0,4},{2,6},{4,0},{6,2},{8,12},{10,14},{12,8},{14,10},{16,20},{18,... | collective-permute-start | bytes 1204232 | tf_op jit(solution)/shard_map/ppermute | solution.py:293
  53.0 14.0 %collective-permute-start.24 = (f32[392,128]{1,0:T(8,128)S(1)}, f32[392,128]{1,0:T(8,128)S(1)}, u32[]{:S(2)}, u32[]{:S(2)}) collective-permute-start(f32[392,128]{1,0:T(8,128)S(1)} %get-tuple-element.62), channel_id=1, source_target_pairs={{0,2},{2,0},{4,6},{6,4},{8,10},{10,8},{12,14},{14,12},{16,18},{18,... | collective-permute-start | bytes 602120 | tf_op jit(solution)/shard_map/ppermute | solution.py:293
  56.3 14.7 %collective-permute-start.32 = (f32[392,128]{1,0:T(8,128)S(1)}, f32[392,128]{1,0:T(8,128)S(1)}, u32[]{:S(2)}, u32[]{:S(2)}) collective-permute-start(f32[392,128]{1,0:T(8,128)S(1)} %merge.16.refs_2_), channel_id=1, source_target_pairs={{0,4},{2,6},{4,0},{6,2},{8,12},{10,14},{12,8},{14,10},{16,20},{18,... | collective-permute-start | bytes 602120 | tf_op jit(solution)/shard_map/ppermute | solution.py:293
  65.6 5.4 %collective-permute-start.33 = (f32[2,16,128]{2,1,0:T(8,128)S(1)}, f32[2,16,128]{2,1,0:T(8,128)S(1)}, u32[]{:S(2)}, u32[]{:S(2)}) collective-permute-start(f32[2,16,128]{2,1,0:T(8,128)S(1)} %stats_merge.6.refs_2_.refs_0_), channel_id=1, source_target_pairs={{0,4},{2,6},{4,0},{6,2},{8,12},{10,14},{12,8},{14,10},{16,20},{18,... | collective-permute-start | bytes 49160 | tf_op jit(solution)/shard_map/ppermute | solution.py:293
  67.0 15.7 %collective-permute-start.30 = (f32[392,128]{1,0:T(8,128)S(1)}, f32[392,128]{1,0:T(8,128)S(1)}, u32[]{:S(2)}, u32[]{:S(2)}) collective-permute-start(f32[392,128]{1,0:T(8,128)S(1)} %merge.18.refs_2_), channel_id=1, source_target_pairs={{0,16},{2,18},{4,20},{6,22},{8,24},{10,26},{12,28},{14,30},{16,0},... | collective-permute-start | bytes 602120 | tf_op jit(solution)/shard_map/ppermute | solution.py:293
  68.9 13.8 %collective-permute-start.31 = (f32[392,128]{1,0:T(8,128)S(1)}, f32[392,128]{1,0:T(8,128)S(1)}, u32[]{:S(2)}, u32[]{:S(2)}) collective-permute-start(f32[392,128]{1,0:T(8,128)S(1)} %merge.19.refs_2_), channel_id=1, source_target_pairs={{0,8},{2,10},{4,12},{6,14},{8,0},{10,2},{12,4},{14,6},{16,24},{18,... | collective-permute-start | bytes 602120 | tf_op jit(solution)/shard_map/ppermute | solution.py:293
  71.1 11.7 %collective-permute-start.34 = (f32[392,128]{1,0:T(8,128)S(1)}, f32[392,128]{1,0:T(8,128)S(1)}, u32[]{:S(2)}, u32[]{:S(2)}) collective-permute-start(f32[392,128]{1,0:T(8,128)S(1)} %merge.20.refs_19_), channel_id=1, source_target_pairs={{0,24},{2,26},{4,28},{6,30},{8,16},{10,18},{12,20},{14,22},{16,8},... | collective-permute-start | bytes 602120 | tf_op jit(solution)/shard_map/ppermute | solution.py:293
  (18 other events, 75.6 us)

commit v14 on v13

--- a/solution.py
+++ b/solution.py
@@ -458,6 +458,7 @@
             beside(0)
         softmax()
         if k == 3:
+            over_x[0] = (pass_on(over_x[0][0]), None)
             beside_all((10, 11), (6, 7))
         else:
             pair(4 * k - 2, 4 * k - 4)
@@ -492,7 +493,6 @@
             0.05,
         )
         if mask == 1:
-            over_x[0] = (pass_on(over_x[0][0]), None)
             pair(4 * far - 2)
             beside(far - 1)
     for k in range(3, far):

time: 83.9 us -> 85 us (1.013); the launches traced: 83.6 us -> 83.7 us
  starting transfers between devices: 33.2 us -> 34.2 us
  waiting for transfers between devices: 12.5 us -> 11.5 us
    ppermute x4, waiting for transfers between devices: 2.87 us -> 0.6 us  [score(): lax.ppermute(part, 'dim', [(i, (i + s) % depth) for i in range(depth)])]
    ppermute x31, waiting for transfers between devices: 9.62 us -> 10.9 us  [send(): return lax.ppermute(x, 'blk', [(i, i ^ mask) for i in range(n)])]
    ppermute x31, starting transfers between devices: 28.2 us -> 29.2 us  [send(): return lax.ppermute(x, 'blk', [(i, i ^ mask) for i in range(n)])]
  transfers between devices with their start and end apart: 35 -> 35, of which waited for: 12 -> 8; matrix products, arithmetic and copies ran while one was open for 0% -> 0% of each run, Pallas kernels for 35% -> 35%
where the time goes in v14:
time: 85 us; the launch traced here: 83.7 us
  starting transfers between devices  34.2 us (40%)
  Pallas kernels  32.2 us (38%)
  waiting for transfers between devices  11.5 us (14%)
  local copies, waits for them, and re-layouts  4.68 us (6%)
  between operations  1.08 us (1%)
    pallas_call x38, Pallas kernels, __call__(): pl.pallas_call(kernel, out_shape=out_shape, name=name, in_specs=in_specs,...  32.2 us
    ppermute x31, starting transfers between devices, send(): return lax.ppermute(x, 'blk', [(i, i ^ mask) for i in range(n)])  29.2 us
    ppermute x31, waiting for transfers between devices, send(): return lax.ppermute(x, 'blk', [(i, i ^ mask) for i in range(n)])  10.9 us
    ppermute x4, starting transfers between devices, score(): lax.ppermute(part, 'dim', [(i, (i + s) % depth) for i in range(depth)])  5.05 us
    unnamed x14, local copies, waits for them, and re-layouts  4.68 us
  transfers between devices with their start and end apart: 35, of which 8 were waited for; matrix products, arithmetic and copies ran while one was open for 0% of the time, Pallas kernels for 35%

profile of v14, /device:TPU:0, one launch (start us, length us, event | category | flops | bytes accessed | tf_op | source)
XLA Modules:
  0.0 83.7 jit_solution(16281187852669924846)
XLA Ops:
  0.6 1.8 %pack.1.refs_3_.refs_1_ = f32[392,128]{1,0:T(8,128)} custom-call(f32[128,384]{1,0:T(8,128)} %refs_0_.4, s32[8,128]{1,0:T(8,128)} %bitcast.3, s32[8,128]{1,0:T(8,128)} %bitcast.4), custom_call_target="tpu_custom_call" | custom-call | bytes 6660000 | tf_op jit(solution)/shard_map/pack/pallas_call | solution.py:45
  2.9 3.7 %collective-permute-start = (f32[392,128]{1,0:T(8,128)}, f32[392,128]{1,0:T(8,128)S(1)}, u32[]{:S(2)}, u32[]{:S(2)}) collective-permute-start(f32[392,128]{1,0:T(8,128)} %pack.1.refs_3_.refs_1_), channel_id=1, source_target_pairs={{0,16},{2,18},{4,20},{6,22},{8,24},{10,26},{12,28},{14,30},{16,0},... | collective-permute-start | bytes 602120 | tf_op jit(solution)/shard_map/ppermute | solution.py:293
  6.6 1.6 %collective-permute-start.2 = (f32[392,128]{1,0:T(8,128)}, f32[392,128]{1,0:T(8,128)S(1)}, u32[]{:S(2)}, u32[]{:S(2)}) collective-permute-start(f32[392,128]{1,0:T(8,128)} %pack.1.refs_3_.refs_1_), channel_id=1, source_target_pairs={{0,8},{2,10},{4,12},{6,14},{8,0},{10,2},{12,4},{14,6},{16,24},{18,... | collective-permute-start | bytes 602120 | tf_op jit(solution)/shard_map/ppermute | solution.py:293
  8.2 1.5 %collective-permute-start.3 = (f32[392,128]{1,0:T(8,128)}, f32[392,128]{1,0:T(8,128)S(1)}, u32[]{:S(2)}, u32[]{:S(2)}) collective-permute-start(f32[392,128]{1,0:T(8,128)} %pack.1.refs_3_.refs_1_), channel_id=1, source_target_pairs={{0,4},{2,6},{4,0},{6,2},{8,12},{10,14},{12,8},{14,10},{16,20},{18,... | collective-permute-start | bytes 602120 | tf_op jit(solution)/shard_map/ppermute | solution.py:293
  10.7 1.9 %copy-done = f32[384,2048]{1,0:T(8,128)S(1)} copy-done((f32[384,2048]{1,0:T(8,128)S(1)}, f32[384,2048]{1,0:T(8,128)}, u32[]{:S(2)}) %copy-start) | copy-done | bytes 3145752
  14.5 1.9 %score.5 = (f32[2,136,128]{2,1,0:T(8,128)S(1)}, f32[2,384,128]{2,1,0:T(8,128)S(1)}) custom-call(s32[1]{0:T(128)} %bitcast.refs_0_, f32[128,384]{1,0:T(8,128)S(1)} %copy-done.3, f32[384,2048]{1,0:T(8,128)S(1)} %copy-done, f32[392,128]{1,0:T(8,128)S(1)} %copy-done.5, f32[392,128]{1,0:T(8,128)S(1)} %collective-permute-done.1.refs_4_.refs_5_, ...), custom_call_target="tpu_custom_call" | custom-call | bytes 6660000 | tf_op jit(solution)/shard_map/score/pallas_call | solution.py:45
  17.2 1.6 %collective-permute-start.6 = (f32[392,128]{1,0:T(8,128)S(1)}, f32[392,128]{1,0:T(8,128)S(1)}, u32[]{:S(2)}, u32[]{:S(2)}) collective-permute-start(f32[392,128]{1,0:T(8,128)S(1)} %relay.9.refs_1_.refs_2_.refs_3_), channel_id=1, source_target_pairs={{0,4},{2,6},{4,0},{6,2},{8,12},{10,14},{12,8},{14,10},{16,20},{18,... | collective-permute-start | bytes 602120 | tf_op jit(solution)/shard_map/ppermute | solution.py:293
  18.8 1.4 %collective-permute-start.5 = (f32[392,128]{1,0:T(8,128)S(1)}, f32[392,128]{1,0:T(8,128)S(1)}, u32[]{:S(2)}, u32[]{:S(2)}) collective-permute-start(f32[392,128]{1,0:T(8,128)S(1)} %relay.9.refs_1_.refs_2_.refs_3_), channel_id=1, source_target_pairs={{0,8},{2,10},{4,12},{6,14},{8,0},{10,2},{12,4},{14,6},{16,24},{18,... | collective-permute-start | bytes 602120 | tf_op jit(solution)/shard_map/ppermute | solution.py:293
  20.8 2.9 %score.6 = (f32[5,136,128]{2,1,0:T(8,128)S(1)}, f32[5,384,128]{2,1,0:T(8,128)S(1)}) custom-call(s32[1]{0:T(128)} %bitcast.refs_0_, f32[128,384]{1,0:T(8,128)S(1)} %copy-done.4, f32[384,2048]{1,0:T(8,128)S(1)} %copy-done.1, f32[392,128]{1,0:T(8,128)S(1)} %relay.9.refs_1_.refs_2_.refs_3_, f32[392,128]{1,0:T(8,128)S(1)} %relay.10.refs_1_.refs_4_.refs_3_, ...), custom_call_target="tpu_custom_call" | custom-call | bytes 9990000 | tf_op jit(solution)/shard_map/score/pallas_call | solution.py:45
  23.6 1.6 %collective-permute-start.4 = (f32[5,136,128]{2,1,0:T(8,128)S(1)}, f32[5,136,128]{2,1,0:T(8,128)S(1)}, u32[]{:S(2)}, u32[]{:S(2)}) collective-permute-start(f32[5,136,128]{2,1,0:T(8,128)S(1)} %get-tuple-element.41.refs_2_), channel_id=1, source_target_pairs={{0,1},{1,0},{2,3},{3,2},{4,5},{5,4},{6,7},{7,6},{8,9},{9,8},{10,11... | collective-permute-start | bytes 1044488 | tf_op jit(solution)/shard_map/ppermute | solution.py:353
  25.9 3.8 %score.7 = (f32[4,136,128]{2,1,0:T(8,128)S(1)}, f32[4,384,128]{2,1,0:T(8,128)S(1)}) custom-call(s32[1]{0:T(128)} %bitcast.refs_0_, f32[128,384]{1,0:T(8,128)S(1)} %copy-done.4, f32[384,2048]{1,0:T(8,128)S(1)} %copy-done.1, f32[392,128]{1,0:T(8,128)S(1)} %relay.13.refs_1_.refs_3_.refs_7_, f32[3,392,128]{2,1,0:T(8,128)S(1)} %collective-permute-done.8.refs_4_.refs_9_, ...), custom_call_target="tpu_custom_call" | custom-call | bytes 13320000 | tf_op jit(solution)/shard_map/score/pallas_call | solution.py:45
  29.8 1.5 %collective-permute-start.12 = (f32[392,128]{1,0:T(8,128)S(1)}, f32[392,128]{1,0:T(8,128)S(1)}, u32[]{:S(2)}, u32[]{:S(2)}) collective-permute-start(f32[392,128]{1,0:T(8,128)S(1)} %relay.14.refs_5_.refs_3_.refs_6_), channel_id=1, source_target_pairs={{0,4},{2,6},{4,0},{6,2},{8,12},{10,14},{12,8},{14,10},{16,20},{18,... | collective-permute-start | bytes 602120 | tf_op jit(solution)/shard_map/ppermute | solution.py:293
  32.6 3.8 %score.8 = (f32[4,136,128]{2,1,0:T(8,128)S(1)}, f32[4,384,128]{2,1,0:T(8,128)S(1)}) custom-call(s32[1]{0:T(128)} %bitcast.refs_0_, f32[128,384]{1,0:T(8,128)S(1)} %copy-done.4, f32[384,2048]{1,0:T(8,128)S(1)} %copy-done.1, f32[392,128]{1,0:T(8,128)S(1)} %relay.14.refs_5_.refs_3_.refs_6_, f32[392,128]{1,0:T(8,128)S(1)} %relay.15.refs_4_.refs_7_.refs_8_, ...), custom_call_target="tpu_custom_call" | custom-call | bytes 13320000 | tf_op jit(solution)/shard_map/score/pallas_call | solution.py:45
  41.2 2.8 %score.9 = (f32[3,136,128]{2,1,0:T(8,128)S(1)}, f32[3,384,128]{2,1,0:T(8,128)S(1)}) custom-call(s32[1]{0:T(128)} %bitcast.refs_0_, f32[128,384]{1,0:T(8,128)S(1)} %copy-done.4, f32[384,2048]{1,0:T(8,128)S(1)} %copy-done.1, f32[392,128]{1,0:T(8,128)S(1)} %relay.16.refs_4_.refs_3_.refs_10_, f32[392,128]{1,0:T(8,128)S(1)} %collective-permute-done.17.refs_4_.refs_13_, ...), custom_call_target="tpu_custom_call" | custom-call | bytes 9990000 | tf_op jit(solution)/shard_map/score/pallas_call | solution.py:45
  44.0 1.4 %collective-permute-start.24 = (f32[3,136,128]{2,1,0:T(8,128)S(1)}, f32[3,136,128]{2,1,0:T(8,128)S(1)}, u32[]{:S(2)}, u32[]{:S(2)}) collective-permute-start(f32[3,136,128]{2,1,0:T(8,128)S(1)} %get-tuple-element.61.refs_2_), channel_id=1, source_target_pairs={{0,1},{1,0},{2,3},{3,2},{4,5},{5,4},{6,7},{7,6},{8,9},{9,8},{10,11... | collective-permute-start | bytes 626696 | tf_op jit(solution)/shard_map/ppermute | solution.py:353
  45.6 1.4 %collective-permute-start.22 = (f32[392,128]{1,0:T(8,128)S(1)}, f32[392,128]{1,0:T(8,128)S(1)}, u32[]{:S(2)}, u32[]{:S(2)}) collective-permute-start(f32[392,128]{1,0:T(8,128)S(1)} %merge.12.refs_2_), channel_id=1, source_target_pairs={{0,4},{2,6},{4,0},{6,2},{8,12},{10,14},{12,8},{14,10},{16,20},{18,... | collective-permute-start | bytes 602120 | tf_op jit(solution)/shard_map/ppermute | solution.py:293
  48.6 4.1 %collective-permute-done.22.refs_0_ = f32[392,128]{1,0:T(8,128)S(1)} collective-permute-done((f32[392,128]{1,0:T(8,128)S(1)}, f32[392,128]{1,0:T(8,128)S(1)}, u32[]{:S(2)}, u32[]{:S(2)}) %collective-permute-start.22) | collective-permute-done | bytes 200736 | tf_op jit(solution)/shard_map/ppermute | solution.py:293
  52.8 1.4 %collective-permute-start.23 = (f32[2,392,128]{2,1,0:T(8,128)S(1)}, f32[2,392,128]{2,1,0:T(8,128)S(1)}, u32[]{:S(2)}, u32[]{:S(2)}) collective-permute-start(f32[2,392,128]{2,1,0:T(8,128)S(1)} %merge.15.refs_4_), channel_id=1, source_target_pairs={{0,4},{2,6},{4,0},{6,2},{8,12},{10,14},{12,8},{14,10},{16,20},{18,... | collective-permute-start | bytes 1204232 | tf_op jit(solution)/shard_map/ppermute | solution.py:293
  57.3 2.2 %collective-permute-start.27 = (f32[2,16,128]{2,1,0:T(8,128)S(1)}, f32[2,16,128]{2,1,0:T(8,128)S(1)}, u32[]{:S(2)}, u32[]{:S(2)}) collective-permute-start(f32[2,16,128]{2,1,0:T(8,128)S(1)} %stats_merge.4.refs_2_.refs_0_), channel_id=1, source_target_pairs={{0,16},{2,18},{4,20},{6,22},{8,24},{10,26},{12,28},{14,30},{16,0},... | collective-permute-start | bytes 49160 | tf_op jit(solution)/shard_map/ppermute | solution.py:293
  59.5 2.5 %collective-permute-done.27.refs_1_ = f32[2,16,128]{2,1,0:T(8,128)S(1)} collective-permute-done((f32[2,16,128]{2,1,0:T(8,128)S(1)}, f32[2,16,128]{2,1,0:T(8,128)S(1)}, u32[]{:S(2)}, u32[]{:S(2)}) %collective-permute-start.27) | collective-permute-done | bytes 16416 | tf_op jit(solution)/shard_map/ppermute | solution.py:293
  63.5 2.4 %collective-permute-done.29.refs_1_ = f32[2,16,128]{2,1,0:T(8,128)S(1)} collective-permute-done((f32[2,16,128]{2,1,0:T(8,128)S(1)}, f32[2,16,128]{2,1,0:T(8,128)S(1)}, u32[]{:S(2)}, u32[]{:S(2)}) %collective-permute-start.29) | collective-permute-done | bytes 16416 | tf_op jit(solution)/shard_map/ppermute | solution.py:293
  67.3 2.6 %collective-permute-start.30 = (f32[392,128]{1,0:T(8,128)S(1)}, f32[392,128]{1,0:T(8,128)S(1)}, u32[]{:S(2)}, u32[]{:S(2)}) collective-permute-start(f32[392,128]{1,0:T(8,128)S(1)} %merge.18.refs_2_), channel_id=1, source_target_pairs={{0,16},{2,18},{4,20},{6,22},{8,24},{10,26},{12,28},{14,30},{16,0},... | collective-permute-start | bytes 602120 | tf_op jit(solution)/shard_map/ppermute | solution.py:293
  71.2 1.9 %collective-permute-start.34 = (f32[392,128]{1,0:T(8,128)S(1)}, f32[392,128]{1,0:T(8,128)S(1)}, u32[]{:S(2)}, u32[]{:S(2)}) collective-permute-start(f32[392,128]{1,0:T(8,128)S(1)} %merge.20.refs_19_), channel_id=1, source_target_pairs={{0,24},{2,26},{4,28},{6,30},{8,16},{10,18},{12,20},{14,22},{16,8},... | collective-permute-start | bytes 602120 | tf_op jit(solution)/shard_map/ppermute | solution.py:293
  73.1 9.8 %gradient.1 = (f32[128,384]{1,0:T(8,128)}, f32[384,2048]{1,0:T(8,128)}) custom-call(f32[2,16,128]{2,1,0:T(8,128)S(1)} %stats_merge.7.refs_2_.refs_0_, f32[392,128]{1,0:T(8,128)S(1)} %copy-done.6, f32[392,128]{1,0:T(8,128)S(1)} %relay.9.refs_1_.refs_2_.refs_3_, f32[392,128]{1,0:T(8,128)S(1)} %relay.10.refs_1_.refs_4_.refs_3_, ...), custom_call_target="tpu_custom_call" | custom-call | bytes 40700000 | tf_op jit(solution)/shard_map/gradient/pallas_call | solution.py:45
  (98 shorter events, 21.2 us)
Async XLA Ops:
  2.4 8.3 %collective-permute-start.1 = (f32[392,128]{1,0:T(8,128)}, f32[392,128]{1,0:T(8,128)S(1)}, u32[]{:S(2)}, u32[]{:S(2)}) collective-permute-start(f32[392,128]{1,0:T(8,128)} %pack.1.refs_3_.refs_1_), channel_id=1, source_target_pairs={{0,2},{2,0},{4,6},{6,4},{8,10},{10,8},{12,14},{14,12},{16,18},{18,... | collective-permute-start | bytes 602120 | tf_op jit(solution)/shard_map/ppermute | solution.py:293
  2.9 13.9 %collective-permute-start = (f32[392,128]{1,0:T(8,128)}, f32[392,128]{1,0:T(8,128)S(1)}, u32[]{:S(2)}, u32[]{:S(2)}) collective-permute-start(f32[392,128]{1,0:T(8,128)} %pack.1.refs_3_.refs_1_), channel_id=1, source_target_pairs={{0,16},{2,18},{4,20},{6,22},{8,24},{10,26},{12,28},{14,30},{16,0},... | collective-permute-start | bytes 602120 | tf_op jit(solution)/shard_map/ppermute | solution.py:293
  6.6 10.4 %collective-permute-start.2 = (f32[392,128]{1,0:T(8,128)}, f32[392,128]{1,0:T(8,128)S(1)}, u32[]{:S(2)}, u32[]{:S(2)}) collective-permute-start(f32[392,128]{1,0:T(8,128)} %pack.1.refs_3_.refs_1_), channel_id=1, source_target_pairs={{0,8},{2,10},{4,12},{6,14},{8,0},{10,2},{12,4},{14,6},{16,24},{18,... | collective-permute-start | bytes 602120 | tf_op jit(solution)/shard_map/ppermute | solution.py:293
  8.2 8.8 %collective-permute-start.3 = (f32[392,128]{1,0:T(8,128)}, f32[392,128]{1,0:T(8,128)S(1)}, u32[]{:S(2)}, u32[]{:S(2)}) collective-permute-start(f32[392,128]{1,0:T(8,128)} %pack.1.refs_3_.refs_1_), channel_id=1, source_target_pairs={{0,4},{2,6},{4,0},{6,2},{8,12},{10,14},{12,8},{14,10},{16,20},{18,... | collective-permute-start | bytes 602120 | tf_op jit(solution)/shard_map/ppermute | solution.py:293
  17.1 8.8 %collective-permute-start.8 = (f32[3,392,128]{2,1,0:T(8,128)S(1)}, f32[3,392,128]{2,1,0:T(8,128)S(1)}, u32[]{:S(2)}, u32[]{:S(2)}) collective-permute-start(f32[3,392,128]{2,1,0:T(8,128)S(1)} %relay.12.refs_8_), channel_id=1, source_target_pairs={{0,2},{2,0},{4,6},{6,4},{8,10},{10,8},{12,14},{14,12},{16,18},{18,... | collective-permute-start | bytes 1806344 | tf_op jit(solution)/shard_map/ppermute | solution.py:293
  17.2 8.1 %collective-permute-start.6 = (f32[392,128]{1,0:T(8,128)S(1)}, f32[392,128]{1,0:T(8,128)S(1)}, u32[]{:S(2)}, u32[]{:S(2)}) collective-permute-start(f32[392,128]{1,0:T(8,128)S(1)} %relay.9.refs_1_.refs_2_.refs_3_), channel_id=1, source_target_pairs={{0,4},{2,6},{4,0},{6,2},{8,12},{10,14},{12,8},{14,10},{16,20},{18,... | collective-permute-start | bytes 602120 | tf_op jit(solution)/shard_map/ppermute | solution.py:293
  18.8 7.1 %collective-permute-start.5 = (f32[392,128]{1,0:T(8,128)S(1)}, f32[392,128]{1,0:T(8,128)S(1)}, u32[]{:S(2)}, u32[]{:S(2)}) collective-permute-start(f32[392,128]{1,0:T(8,128)S(1)} %relay.9.refs_1_.refs_2_.refs_3_), channel_id=1, source_target_pairs={{0,8},{2,10},{4,12},{6,14},{8,0},{10,2},{12,4},{14,6},{16,24},{18,... | collective-permute-start | bytes 602120 | tf_op jit(solution)/shard_map/ppermute | solution.py:293
  20.2 9.5 %collective-permute-start.7 = (f32[392,128]{1,0:T(8,128)S(1)}, f32[392,128]{1,0:T(8,128)S(1)}, u32[]{:S(2)}, u32[]{:S(2)}) collective-permute-start(f32[392,128]{1,0:T(8,128)S(1)} %relay.10.refs_1_.refs_4_.refs_3_), channel_id=1, source_target_pairs={{0,4},{2,6},{4,0},{6,2},{8,12},{10,14},{12,8},{14,10},{16,20},{18,... | collective-permute-start | bytes 602120 | tf_op jit(solution)/shard_map/ppermute | solution.py:293
  23.6 12.8 %collective-permute-start.4 = (f32[5,136,128]{2,1,0:T(8,128)S(1)}, f32[5,136,128]{2,1,0:T(8,128)S(1)}, u32[]{:S(2)}, u32[]{:S(2)}) collective-permute-start(f32[5,136,128]{2,1,0:T(8,128)S(1)} %get-tuple-element.41.refs_2_), channel_id=1, source_target_pairs={{0,1},{1,0},{2,3},{3,2},{4,5},{5,4},{6,7},{7,6},{8,9},{9,8},{10,11... | collective-permute-start | bytes 1044488 | tf_op jit(solution)/shard_map/ppermute | solution.py:353
  25.3 7.4 %collective-permute-start.9 = (f32[392,128]{1,0:T(8,128)S(1)}, f32[392,128]{1,0:T(8,128)S(1)}, u32[]{:S(2)}, u32[]{:S(2)}) collective-permute-start(f32[392,128]{1,0:T(8,128)S(1)} %relay.13.refs_1_.refs_3_.refs_7_), channel_id=1, source_target_pairs={{0,2},{2,0},{4,6},{6,4},{8,10},{10,8},{12,14},{14,12},{16,18},{18,... | collective-permute-start | bytes 602120 | tf_op jit(solution)/shard_map/ppermute | solution.py:293
  29.8 7.9 %collective-permute-start.12 = (f32[392,128]{1,0:T(8,128)S(1)}, f32[392,128]{1,0:T(8,128)S(1)}, u32[]{:S(2)}, u32[]{:S(2)}) collective-permute-start(f32[392,128]{1,0:T(8,128)S(1)} %relay.14.refs_5_.refs_3_.refs_6_), channel_id=1, source_target_pairs={{0,4},{2,6},{4,0},{6,2},{8,12},{10,14},{12,8},{14,10},{16,20},{18,... | collective-permute-start | bytes 602120 | tf_op jit(solution)/shard_map/ppermute | solution.py:293
  31.3 8.4 %collective-permute-start.11 = (f32[4,136,128]{2,1,0:T(8,128)S(1)}, f32[4,136,128]{2,1,0:T(8,128)S(1)}, u32[]{:S(2)}, u32[]{:S(2)}) collective-permute-start(f32[4,136,128]{2,1,0:T(8,128)S(1)} %get-tuple-element.46.refs_2_), channel_id=1, source_target_pairs={{0,1},{1,0},{2,3},{3,2},{4,5},{5,4},{6,7},{7,6},{8,9},{9,8},{10,11... | collective-permute-start | bytes 835592 | tf_op jit(solution)/shard_map/ppermute | solution.py:353
  32.6 8.0 %collective-permute-start.17 = (f32[392,128]{1,0:T(8,128)S(1)}, f32[392,128]{1,0:T(8,128)S(1)}, u32[]{:S(2)}, u32[]{:S(2)}) collective-permute-start(f32[392,128]{1,0:T(8,128)S(1)} %relay.14.refs_5_.refs_3_.refs_6_), channel_id=1, source_target_pairs={{0,2},{2,0},{4,6},{6,4},{8,10},{10,8},{12,14},{14,12},{16,18},{18,... | collective-permute-start | bytes 602120 | tf_op jit(solution)/shard_map/ppermute | solution.py:293
  38.3 8.8 %collective-permute-start.19 = (f32[4,136,128]{2,1,0:T(8,128)S(1)}, f32[4,136,128]{2,1,0:T(8,128)S(1)}, u32[]{:S(2)}, u32[]{:S(2)}) collective-permute-start(f32[4,136,128]{2,1,0:T(8,128)S(1)} %get-tuple-element.56.refs_2_), channel_id=1, source_target_pairs={{0,1},{1,0},{2,3},{3,2},{4,5},{5,4},{6,7},{7,6},{8,9},{9,8},{10,11... | collective-permute-start | bytes 835592 | tf_op jit(solution)/shard_map/ppermute | solution.py:353
  40.6 6.4 %collective-permute-start.14 = (f32[392,128]{1,0:T(8,128)S(1)}, f32[392,128]{1,0:T(8,128)S(1)}, u32[]{:S(2)}, u32[]{:S(2)}) collective-permute-start(f32[392,128]{1,0:T(8,128)S(1)} %get-tuple-element.50), channel_id=1, source_target_pairs={{0,2},{2,0},{4,6},{6,4},{8,10},{10,8},{12,14},{14,12},{16,18},{18,... | collective-permute-start | bytes 602120 | tf_op jit(solution)/shard_map/ppermute | solution.py:293
  41.1 5.9 %collective-permute-start.13 = (f32[392,128]{1,0:T(8,128)S(1)}, f32[392,128]{1,0:T(8,128)S(1)}, u32[]{:S(2)}, u32[]{:S(2)}) collective-permute-start(f32[392,128]{1,0:T(8,128)S(1)} %get-tuple-element.48.refs_6_), channel_id=1, source_target_pairs={{0,2},{2,0},{4,6},{6,4},{8,10},{10,8},{12,14},{14,12},{16,18},{18,... | collective-permute-start | bytes 602120 | tf_op jit(solution)/shard_map/ppermute | solution.py:293
  44.0 10.2 %collective-permute-start.24 = (f32[3,136,128]{2,1,0:T(8,128)S(1)}, f32[3,136,128]{2,1,0:T(8,128)S(1)}, u32[]{:S(2)}, u32[]{:S(2)}) collective-permute-start(f32[3,136,128]{2,1,0:T(8,128)S(1)} %get-tuple-element.61.refs_2_), channel_id=1, source_target_pairs={{0,1},{1,0},{2,3},{3,2},{4,5},{5,4},{6,7},{7,6},{8,9},{9,8},{10,11... | collective-permute-start | bytes 626696 | tf_op jit(solution)/shard_map/ppermute | solution.py:353
  45.6 7.1 %collective-permute-start.22 = (f32[392,128]{1,0:T(8,128)S(1)}, f32[392,128]{1,0:T(8,128)S(1)}, u32[]{:S(2)}, u32[]{:S(2)}) collective-permute-start(f32[392,128]{1,0:T(8,128)S(1)} %merge.12.refs_2_), channel_id=1, source_target_pairs={{0,4},{2,6},{4,0},{6,2},{8,12},{10,14},{12,8},{14,10},{16,20},{18,... | collective-permute-start | bytes 602120 | tf_op jit(solution)/shard_map/ppermute | solution.py:293
  52.8 14.4 %collective-permute-start.23 = (f32[2,392,128]{2,1,0:T(8,128)S(1)}, f32[2,392,128]{2,1,0:T(8,128)S(1)}, u32[]{:S(2)}, u32[]{:S(2)}) collective-permute-start(f32[2,392,128]{2,1,0:T(8,128)S(1)} %merge.15.refs_4_), channel_id=1, source_target_pairs={{0,4},{2,6},{4,0},{6,2},{8,12},{10,14},{12,8},{14,10},{16,20},{18,... | collective-permute-start | bytes 1204232 | tf_op jit(solution)/shard_map/ppermute | solution.py:293
  55.6 11.6 %collective-permute-start.25 = (f32[392,128]{1,0:T(8,128)S(1)}, f32[392,128]{1,0:T(8,128)S(1)}, u32[]{:S(2)}, u32[]{:S(2)}) collective-permute-start(f32[392,128]{1,0:T(8,128)S(1)} %get-tuple-element.62), channel_id=1, source_target_pairs={{0,2},{2,0},{4,6},{6,4},{8,10},{10,8},{12,14},{14,12},{16,18},{18,... | collective-permute-start | bytes 602120 | tf_op jit(solution)/shard_map/ppermute | solution.py:293
  56.6 14.5 %collective-permute-start.32 = (f32[392,128]{1,0:T(8,128)S(1)}, f32[392,128]{1,0:T(8,128)S(1)}, u32[]{:S(2)}, u32[]{:S(2)}) collective-permute-start(f32[392,128]{1,0:T(8,128)S(1)} %merge.16.refs_2_), channel_id=1, source_target_pairs={{0,4},{2,6},{4,0},{6,2},{8,12},{10,14},{12,8},{14,10},{16,20},{18,... | collective-permute-start | bytes 602120 | tf_op jit(solution)/shard_map/ppermute | solution.py:293
  67.3 15.6 %collective-permute-start.30 = (f32[392,128]{1,0:T(8,128)S(1)}, f32[392,128]{1,0:T(8,128)S(1)}, u32[]{:S(2)}, u32[]{:S(2)}) collective-permute-start(f32[392,128]{1,0:T(8,128)S(1)} %merge.18.refs_2_), channel_id=1, source_target_pairs={{0,16},{2,18},{4,20},{6,22},{8,24},{10,26},{12,28},{14,30},{16,0},... | collective-permute-start | bytes 602120 | tf_op jit(solution)/shard_map/ppermute | solution.py:293
  69.9 12.9 %collective-permute-start.31 = (f32[392,128]{1,0:T(8,128)S(1)}, f32[392,128]{1,0:T(8,128)S(1)}, u32[]{:S(2)}, u32[]{:S(2)}) collective-permute-start(f32[392,128]{1,0:T(8,128)S(1)} %merge.19.refs_2_), channel_id=1, source_target_pairs={{0,8},{2,10},{4,12},{6,14},{8,0},{10,2},{12,4},{14,6},{16,24},{18,... | collective-permute-start | bytes 602120 | tf_op jit(solution)/shard_map/ppermute | solution.py:293
  71.2 11.7 %collective-permute-start.34 = (f32[392,128]{1,0:T(8,128)S(1)}, f32[392,128]{1,0:T(8,128)S(1)}, u32[]{:S(2)}, u32[]{:S(2)}) collective-permute-start(f32[392,128]{1,0:T(8,128)S(1)} %merge.20.refs_19_), channel_id=1, source_target_pairs={{0,24},{2,26},{4,28},{6,30},{8,16},{10,18},{12,20},{14,22},{16,8},... | collective-permute-start | bytes 602120 | tf_op jit(solution)/shard_map/ppermute | solution.py:293
  (18 other events, 77.7 us)
